TPU v7x, 32 devices: a whole 2x2x4 slice. The times are simulated.
32 devices in a mesh: dp: 8 (over y, x, core), seq: 4 (over z).
Axes of the slice: x: 2, y: 2, z: 4, core: 2. Of those that a mesh axis runs over, the one named last changes fastest.
Arguments:
- tokens: bfloat16 [8, 512, 1024], P('dp', 'seq'), may hold values from -6 to 6
- positions: int32 [8, 512], P('dp', 'seq'), may hold values from 0 to 4095
- counts: int32 [8, 4], P('dp'), may hold values from 1 to 128, 384 in all within a row
- ln_gain: float32 [1024], replicated, may hold values from 0.1 to 1.9
- w_qkv: bfloat16 [3, 1024, 1024], replicated
- w_out: bfloat16 [1024, 1024], replicated, may hold values from -0.1875 to 0.1875
- d_out: bfloat16 [8, 512, 1024], P('dp', 'seq'), may hold values from -6 to 6
Outputs:
- d_tokens: bfloat16 [8, 512, 1024], P('dp', 'seq')
- grad_qkv: float32 [3, 1024, 1024], P(None, 'seq', 'dp')
- grad_out: float32 [1024, 1024], P('dp', 'seq')
Inputs may be any that keep to these rules, and one draw needn't show every extreme that they name: Each record's counts sum to 384, and the largest of them is 128.
All inputs are finite; a program needn't handle non-finite values.
Results may differ from a plain program's by a relative error of at most 0.0075.
Values may be sent and summed in bfloat16 or wider, within the bound.
No kernel may reach another device: no remote copies, remote signals or barrier semaphores. Data moves between devices by JAX's collectives and lax.ppermute only.
A program may use at most 128 MiB of HBM per device.

v0:
```python
import math

import jax
import jax.numpy as jnp
from jax import lax
from jax.sharding import PartitionSpec as P

HEAD_DIM = 64


EPSILON = 1e-06
MASKED = -1e30


def position_code(places, feature_width):
    half = feature_width // 2
    freqs = jnp.exp(jnp.arange(half, dtype=jnp.float32) * (-math.log(10000.0) / half))
    angle = places.astype(jnp.float32)[:, None] * freqs[None, :]
    return jnp.concatenate([jnp.sin(angle), jnp.cos(angle)], axis=1)


def layer_norm(inputs, places, ln_gain):
    shifted = inputs.astype(jnp.float32) + position_code(places, inputs.shape[1])
    centred = shifted - jnp.mean(shifted, axis=1, keepdims=True)
    inv_std = lax.rsqrt(jnp.mean(centred * centred, axis=1, keepdims=True) + EPSILON)
    standard = centred * inv_std
    normed = (standard * ln_gain).astype(jnp.bfloat16)
    return (normed, standard, inv_std)


def input_grad(query_grad, key_grad, value_grad, masked_grad, w_qkv, standard, inv_std, ln_gain):
    normed_grad = jnp.dot(query_grad, w_qkv[0], preferred_element_type=jnp.float32)
    normed_grad = normed_grad + jnp.dot(key_grad, w_qkv[1], preferred_element_type=jnp.float32)
    normed_grad = normed_grad + jnp.dot(value_grad, w_qkv[2], preferred_element_type=jnp.float32)
    unit_grad = normed_grad * ln_gain
    inner = unit_grad - jnp.mean(unit_grad, axis=1, keepdims=True)
    inner = inner - standard * jnp.mean(unit_grad * standard, axis=1, keepdims=True)
    return (masked_grad.astype(jnp.float32) + inv_std * inner).astype(jnp.bfloat16)


def project(normed, weight):
    return jnp.einsum("td,od->to", normed, weight, preferred_element_type=jnp.float32).astype(
        jnp.bfloat16
    )


def token_sum(left, right):
    return lax.dot_general(
        left, right, (((0,), (0,)), ((), ())), preferred_element_type=jnp.float32
    )


def attention_grads(queries, key_rows, value_rows, attn_grad, key_valid, score_scale):
    total, span = queries.shape
    heads_here = span // HEAD_DIM
    block = math.gcd(512, total)
    blocks = total // block
    key_three = key_rows.reshape(total, heads_here, HEAD_DIM)
    value_three = value_rows.reshape(total, heads_here, HEAD_DIM)
    query_four = queries.reshape(blocks, block, heads_here, HEAD_DIM)
    grad_four = attn_grad.reshape(blocks, block, heads_here, HEAD_DIM)

    def step(carry, item):
        key_acc, value_acc = carry
        query_block, grad_block = item
        scores = (
            jnp.einsum("qhd,khd->hqk", query_block, key_three, preferred_element_type=jnp.float32)
            * score_scale
        )
        scores = jnp.where(key_valid[None, None, :], scores, MASKED)
        peak = jnp.max(scores, axis=2, keepdims=True)
        expo = jnp.exp(scores - peak)
        probs = expo / jnp.sum(expo, axis=2, keepdims=True)
        probs_low = probs.astype(jnp.bfloat16)
        attended = jnp.einsum(
            "hqk,khd->qhd", probs_low, value_three, preferred_element_type=jnp.float32
        )
        delta = jnp.sum(grad_block.astype(jnp.float32) * attended, axis=2)
        prob_grad = jnp.einsum(
            "qhd,khd->hqk", grad_block, value_three, preferred_element_type=jnp.float32
        )
        score_grad = (probs * (prob_grad - jnp.transpose(delta)[:, :, None])).astype(jnp.bfloat16)
        query_grad = jnp.einsum(
            "hqk,khd->qhd", score_grad, key_three, preferred_element_type=jnp.float32
        )
        query_grad = (query_grad * score_scale).astype(jnp.bfloat16)
        key_acc = key_acc + jnp.einsum(
            "hqk,qhd->khd", score_grad, query_block, preferred_element_type=jnp.float32
        )
        value_acc = value_acc + jnp.einsum(
            "hqk,qhd->khd", probs_low, grad_block, preferred_element_type=jnp.float32
        )
        return ((key_acc, value_acc), (attended.astype(jnp.bfloat16), query_grad))

    zeros_acc = jnp.zeros((total, heads_here, HEAD_DIM), jnp.float32)
    sums, outputs = lax.scan(step, (zeros_acc, zeros_acc), (query_four, grad_four))
    attended = outputs[0].reshape(total, span)
    query_grad = outputs[1].reshape(total, span)
    key_grad = (sums[0] * score_scale).astype(jnp.bfloat16).reshape(total, span)
    value_grad = sums[1].astype(jnp.bfloat16).reshape(total, span)
    return (attended, query_grad, key_grad, value_grad)


def shards(tokens, positions, counts, ln_gain, w_qkv, w_out, d_out):
    inputs = tokens[0]
    places = positions[0]
    upstream = d_out[0]
    capacity, feature_width = inputs.shape
    shard_total = lax.axis_size("seq")
    shard_index = lax.axis_index("seq")
    slot_count = capacity * shard_total
    key_valid = jnp.arange(slot_count, dtype=jnp.int32) % capacity < jnp.repeat(counts[0], capacity)
    own_valid = lax.dynamic_slice_in_dim(key_valid, shard_index * capacity, capacity)
    normed, standard, inv_std = layer_norm(inputs, places, ln_gain)
    masked_grad = jnp.where(own_valid[:, None], upstream, jnp.zeros_like(upstream))
    score_scale = HEAD_DIM ** (-0.5)
    factor = 1.0 / math.sqrt(lax.axis_size("dp") * (3 * slot_count // 4))
    head_width = feature_width // shard_total
    normed_all, grad_all = (
        lax.all_gather(normed, "seq", axis=0, tiled=True),
        lax.all_gather(masked_grad, "seq", axis=0, tiled=True),
    )
    local_qkv = lax.dynamic_slice_in_dim(w_qkv, shard_index * head_width, head_width, 1)
    local_out = lax.dynamic_slice_in_dim(w_out, shard_index * head_width, head_width, 1)
    queries = project(normed_all, local_qkv[0])
    key_rows = project(normed_all, local_qkv[1])
    value_rows = project(normed_all, local_qkv[2])
    attn_grad = jnp.dot(grad_all, local_out, preferred_element_type=jnp.float32).astype(
        jnp.bfloat16
    )
    attended, query_grad, key_grad, value_grad = attention_grads(
        queries, key_rows, value_rows, attn_grad, key_valid, score_scale
    )
    term_qkv = jnp.stack(
        [
            token_sum(query_grad, normed_all),
            token_sum(key_grad, normed_all),
            token_sum(value_grad, normed_all),
        ]
    )
    term_out = token_sum(grad_all, attended)
    grad_qkv, grad_out = (
        lax.psum_scatter(term_qkv, "dp", scatter_dimension=2, tiled=True),
        lax.psum_scatter(term_out, "dp", scatter_dimension=0, tiled=True),
    )
    query_rows, key_back, value_back = (
        lax.all_to_all(query_grad, "seq", split_axis=0, concat_axis=1, tiled=True),
        lax.all_to_all(key_grad, "seq", split_axis=0, concat_axis=1, tiled=True),
        lax.all_to_all(value_grad, "seq", split_axis=0, concat_axis=1, tiled=True),
    )
    d_inputs = input_grad(
        query_rows, key_back, value_back, masked_grad, w_qkv, standard, inv_std, ln_gain
    )
    return (d_inputs[None], grad_qkv * factor, grad_out * factor)


def solution(mesh):
    placed = (
        P("dp", "seq", None),
        P("dp", "seq"),
        P("dp", None),
        P(),
        P(),
        P(),
        P("dp", "seq", None),
    )
    return jax.shard_map(
        shards,
        mesh=mesh,
        in_specs=placed,
        out_specs=(P("dp", "seq", None), P(None, "seq", "dp"), P("dp", "seq")),
        check_vma=False,
    )
```

profile of v0, /device:TPU:1, one launch (start us, length us, event | category | flops | bytes accessed | tf_op | source)
XLA Modules:
  0.0 174.2 jit_solution(10269503564292625242)
XLA Ops:
  7.2 0.8 convert_bitcast_fusion
  8.0 1.0 multiply_sine_fusion
  9.0 1.1 fusion.40
  10.1 1.1 multiply_reduce_fusion.2
  11.3 1.8 %multiply_convert_fusion.1 = bf16[128,1024]{1,0:T(8,128)(2,1)} fusion(f32[1024]{0:T(1024)} %param.10, f32[128]{0:T(128)S(1)} %add_rsqrt_fusion, f32[128]{0:T(128)S(1)} %broadcast_multiply_fusion.4, f32[128,512]{1,0:T(8,128)S(1)} %get-tuple-element.28, f32[128,512]{1,0:T(8,128)S(1)} %get-tuple-element.27, bf16[1,128,1024]{2,1,0:T(8,128)(2,1)} %param.7), kind=kLoop, calls=%fused_computation.44 | loop fusion | flops 917504 | bytes 1053696 | tf_op jit(solution)/shard_map/convert_element_type | solution.py:27
  13.1 0.0 all-gather.5.cloned.1.call-start
  13.2 0.7 fusion.30
  13.9 0.1 dynamic_slice.14
  14.0 1.7 bitcast_select_fusion
  15.8 0.0 reduce-scatter.5.cloned.1.call-start
  15.8 27.3 %all-gather.3.cloned.1.call-done = bf16[512,1024]{1,0:T(8,128)(2,1)} async-done(((bf16[128,1024]{1,0:T(8,128)(2,1)}), bf16[512,1024]{1,0:T(8,128)(2,1)}) %all-gather.3.cloned.1.call-update) | async-done | bytes 1048592 | tf_op jit(solution)/shard_map/all_gather | solution.py:120
  43.2 1.8 %convolution_convert_fusion.3 = bf16[512,256]{0,1:T(8,128)(2,1)S(1)} fusion(bf16[512,1024]{1,0:T(8,128)(2,1)} %all-gather.3.cloned.1.call-done, bf16[3,1024,1024]{2,1,0:T(8,128)(2,1)} %param.11, s32[]{:T(128)S(6)} %select_n.30), kind=kOutput, calls=%fused_computation.32 | convolution fusion | flops 268566528 | bytes 1835012 | tf_op jit(solution)/shard_map/td,od->to/dot_general | solution.py:42
  45.0 1.9 %convolution_convert_fusion.4 = bf16[512,256]{0,1:T(8,128)(2,1)S(1)} fusion(bf16[512,1024]{1,0:T(8,128)(2,1)} %all-gather.3.cloned.1.call-done, bf16[3,1024,1024]{2,1,0:T(8,128)(2,1)} %param.11, s32[]{:T(128)S(6)} %add.59, s32[]{:T(128)S(6)} %select_n.30), kind=kOutput, calls=%fused_computation.33 | convolution fusion | flops 268566528 | bytes 1835016 | tf_op jit(solution)/shard_map/td,od->to/dot_general | solution.py:42
  46.9 3.6 %fusion.43 = (f32[4,512]{1,0:T(4,128)S(1)}, f32[4,512,512]{1,2,0:T(8,128)}) fusion(pred[512]{0:T(512)(128)(4,1)S(1)} %fusion.30, bf16[512,4,64]{0,2,1:T(8,128)(2,1)S(1)} %bitcast.129, bf16[512,4,64]{0,2,1:T(8,128)(2,1)S(1)} %bitcast.127), kind=kOutput, calls=%fused_computation.75 | convolution fusion | flops 138412544 | bytes 4727296 | tf_op jit(solution)/shard_map/while/body/eval_jaxpr/sub | solution.py:72
  50.5 4.2 %fusion.14 = bf16[4,512,512]{1,2,0:T(8,128)(2,1)} fusion(f32[4,512,512]{1,2,0:T(8,128)} %get-tuple-element.40, f32[4,512]{1,0:T(4,128)S(1)} %get-tuple-element.29), kind=kLoop, calls=%fused_computation.19 | loop fusion | flops 2097152 | bytes 6299648 | tf_op jit(solution)/shard_map/while/body/eval_jaxpr/convert_element_type | solution.py:74
  54.7 18.0 %all-gather.5.cloned.1.call-done = bf16[512,1024]{1,0:T(8,128)(2,1)} async-done(((bf16[128,1024]{1,0:T(8,128)(2,1)}), bf16[512,1024]{1,0:T(8,128)(2,1)}) %all-gather.5.cloned.1.call-update) | async-done | bytes 1048592 | tf_op jit(solution)/shard_map/all_gather | solution.py:121
  72.8 1.9 %convolution_convert_fusion.2 = bf16[512,256]{0,1:T(8,128)(2,1)S(1)} fusion(bf16[512,1024]{1,0:T(8,128)(2,1)} %all-gather.5.cloned.1.call-done, bf16[1024,1024]{1,0:T(8,128)(2,1)S(1)} %copy-done, s32[]{:T(128)S(6)} %select_n.30), kind=kOutput, calls=%fused_computation.31 | convolution fusion | flops 268566528 | bytes 1835012 | tf_op jit(solution)/shard_map/dot_general | solution.py:128
  74.6 2.3 %convolution_convert_fusion = bf16[4,64,512]{2,1,0:T(8,128)(2,1)S(1)} fusion(bf16[512,4,64]{0,2,1:T(8,128)(2,1)S(1)} %bitcast.124, bf16[4,512,512]{1,2,0:T(8,128)(2,1)} %fusion.14), kind=kOutput, calls=%fused_computation.29 | convolution fusion | flops 134348800 | bytes 2621440 | tf_op jit(solution)/shard_map/while/body/eval_jaxpr/hqk,qhd->khd/dot_general | solution.py:90
  77.0 1.6 convolution_convert_fusion.1
  78.6 0.5 fusion.42
  79.1 1.5 fusion.44
  80.6 0.0 reduce-scatter.3.cloned.1.call-start
  80.6 1.7 convolution_bitcast_fusion
  82.3 3.0 %multiply_convert_fusion = bf16[4,512,512]{1,2,0:T(8,128)(2,1)S(1)} fusion(bf16[512,4,64]{0,2,1:T(8,128)(2,1)S(1)} %bitcast.125, bf16[512,4,64]{0,2,1:T(8,128)(2,1)S(1)} %bitcast.132, f32[4,512]{1,0:T(4,128)S(1)} %bitcast.133, f32[4,512,512]{1,2,0:T(8,128)} %get-tuple-element.40, f32[4,512]{1,0:T(4,128)S(1)} %get-tuple-element.29), kind=kOutput, calls=%fused_computation.1 | convolution fusion | flops 138412032 | bytes 6832128 | tf_op jit(solution)/shard_map/while/body/eval_jaxpr/qhd,khd->hqk/dot_general | solution.py:79
  85.4 0.8 fusion.25
  86.1 0.4 convolution_bitcast_fusion.1
  86.6 0.5 fusion.24
  87.1 0.4 convolution_bitcast_fusion.2
  87.5 1.9 %pad_maximum_fusion = f32[3,256,1024]{2,1,0:T(8,128)} fusion(f32[1,256,1024]{2,1,0:T(8,128)S(1)} %convolution_bitcast_fusion, f32[1,256,1024]{2,1,0:T(8,128)S(1)} %convolution_bitcast_fusion.1, f32[1,256,1024]{2,1,0:T(8,128)S(1)} %convolution_bitcast_fusion.2), kind=kLoop, calls=%fused_computation.5 | loop fusion | flops 1572864 | bytes 6291456 | tf_op jit(solution)/shard_map/stack | solution.py:134
  89.4 0.8 all_to_all.50
  90.1 1.7 copy.22
  91.8 4.0 %all-to-all-start.2 = ((bf16[4,128,256]{1,2,0:T(8,128)(2,1)}), bf16[4,128,256]{1,2,0:T(8,128)(2,1)}, u32[]{:S(2)}, u32[]{:S(2)}) async-start(bf16[4,128,256]{1,2,0:T(8,128)(2,1)} %copy.22), calls=%async_computation.2 | async-start | bytes 524288 | tf_op jit(solution)/shard_map/all_to_all | solution.py:149
  95.9 0.8 all_to_all.46
  96.7 1.7 copy.20
  98.4 5.0 %all-to-all-done.2 = bf16[4,128,256]{1,2,0:T(8,128)(2,1)} async-done(((bf16[4,128,256]{1,2,0:T(8,128)(2,1)}), bf16[4,128,256]{1,2,0:T(8,128)(2,1)}, u32[]{:S(2)}, u32[]{:S(2)}) %all-to-all-start.2) | async-done | bytes 262176 | tf_op jit(solution)/shard_map/all_to_all | solution.py:149
  103.4 4.0 %all-to-all-start.1 = ((bf16[4,128,256]{1,2,0:T(8,128)(2,1)}), bf16[4,128,256]{1,2,0:T(8,128)(2,1)}, u32[]{:S(2)}, u32[]{:S(2)}) async-start(bf16[4,128,256]{1,2,0:T(8,128)(2,1)} %copy.20), calls=%async_computation.1 | async-start | bytes 524288 | tf_op jit(solution)/shard_map/all_to_all | solution.py:148
  107.5 0.1 all_to_all.42
  107.6 0.7 copy.18
  108.3 4.9 %all-to-all-done.1 = bf16[4,128,256]{1,2,0:T(8,128)(2,1)} async-done(((bf16[4,128,256]{1,2,0:T(8,128)(2,1)}), bf16[4,128,256]{1,2,0:T(8,128)(2,1)}, u32[]{:S(2)}, u32[]{:S(2)}) %all-to-all-start.1) | async-done | bytes 262176 | tf_op jit(solution)/shard_map/all_to_all | solution.py:148
  113.2 4.0 %all-to-all-start = ((bf16[4,128,256]{1,2,0:T(8,128)(2,1)}), bf16[4,128,256]{1,2,0:T(8,128)(2,1)}, u32[]{:S(2)}, u32[]{:S(2)}) async-start(bf16[4,128,256]{1,2,0:T(8,128)(2,1)} %copy.18), calls=%async_computation | async-start | bytes 524288 | tf_op jit(solution)/shard_map/all_to_all | solution.py:147
  117.2 2.2 %fusion.2 = f32[128,1024]{1,0:T(8,128)S(1)} fusion(bf16[128,1024]{0,1:T(8,128)(2,1)} %bitcast.24, bf16[3,1024,1024]{2,1,0:T(8,128)(2,1)} %param.11), kind=kOutput, calls=%fused_computation.6 | convolution fusion | flops 268435456 | bytes 2883584 | tf_op jit(solution)/shard_map/dot_general | solution.py:34
  119.4 3.0 %fusion.4 = f32[128,1024]{1,0:T(8,128)} fusion(bf16[128,1024]{0,1:T(8,128)(2,1)} %bitcast.20, bf16[3,1024,1024]{2,1,0:T(8,128)(2,1)} %param.11), kind=kOutput, calls=%fused_computation.8 | convolution fusion | flops 268435456 | bytes 2883584 | tf_op jit(solution)/shard_map/dot_general | solution.py:33
  122.4 0.6 all-to-all-done
  122.9 2.4 %fusion.41 = (f32[128]{0:T(128)S(1)}, f32[128]{0:T(128)S(1)}, f32[128,1024]{1,0:T(8,128)S(1)}) fusion(f32[128]{0:T(128)S(1)} %add_rsqrt_fusion, f32[128]{0:T(128)S(1)} %broadcast_multiply_fusion.4, f32[128,512]{1,0:T(8,128)S(1)} %get-tuple-element.28, f32[128,512]{1,0:T(8,128)S(1)} %get-tuple-element.27, bf16[1,128,1024]{2,1,0:T(8,128)(2,1)S(1)} %copy-done.4, ...), kind=kOutput, calls=%fused_computation.73 | convolution fusion | flops 269876992 | bytes 4724736 | tf_op jit(solution)/shard_map/dot_general | solution.py:32
  125.4 1.0 fusion.29
  126.4 1.6 broadcast_multiply_fusion.1
  128.0 37.9 %reduce-scatter.3.cloned.1.call-done = f32[3,256,128]{2,1,0:T(8,128)} async-done(((f32[3,256,1024]{2,1,0:T(8,128)}), f32[3,256,128]{2,1,0:T(8,128)}) %reduce-scatter.3.cloned.1.call-update) | async-done | bytes 393232 | tf_op jit(solution)/shard_map/reduce_scatter | solution.py:143
  165.9 1.8 %broadcast_multiply_fusion = f32[3,256,128]{2,1,0:T(8,128)} fusion(f32[3,256,128]{2,1,0:T(8,128)} %reduce-scatter.3.cloned.1.call-done), kind=kLoop, calls=%fused_computation.52 | loop fusion | flops 98304 | bytes 786432 | tf_op jit(solution)/shard_map/mul | solution.py:154
  (34 shorter events, 0.2 us)
Async XLA Ops:
  7.2 65.6 %copy-start = (bf16[1024,1024]{1,0:T(8,128)(2,1)S(1)}, bf16[1024,1024]{1,0:T(8,128)(2,1)}, u32[]{:S(2)}) copy-start(bf16[1024,1024]{1,0:T(8,128)(2,1)} %param.12) | copy-start | bytes 6291460
  7.2 36.0 %all-gather.3.cloned.1.call-start = ((), (), s32[]{:S(2)}) async-start(), calls=%async_computation.5 | async-start | bytes 1310720 | tf_op jit(solution)/shard_map/all_gather | solution.py:120
  13.1 59.6 %all-gather.5.cloned.1.call-start = ((), (), s32[]{:S(2)}) async-start(), calls=%async_computation.6 | async-start | bytes 1310720 | tf_op jit(solution)/shard_map/all_gather | solution.py:121
  15.8 110.6 %reduce-scatter.5.cloned.1.call-start = ((), (), s32[]{:S(2)}) async-start(), calls=%async_computation.8 | async-start | bytes 1179648 | tf_op jit(solution)/shard_map/reduce_scatter | solution.py:144
  45.0 5.5 %copy-start.9 = (bf16[512,256]{0,1:T(8,128)(2,1)}, bf16[512,256]{0,1:T(8,128)(2,1)S(1)}, u32[]{:S(2)}) copy-start(bf16[512,256]{0,1:T(8,128)(2,1)S(1)} %convolution_convert_fusion.3) | copy-start | bytes 786436
  46.9 7.8 %copy-start.7 = (bf16[512,256]{0,1:T(8,128)(2,1)}, bf16[512,256]{0,1:T(8,128)(2,1)S(1)}, u32[]{:S(2)}) copy-start(bf16[512,256]{0,1:T(8,128)(2,1)S(1)} %convolution_convert_fusion.4) | copy-start | bytes 786436
  72.8 4.2 %copy-start.2 = (bf16[512,1024]{1,0:T(8,128)(2,1)S(1)}, bf16[512,1024]{1,0:T(8,128)(2,1)}, u32[]{:S(2)}) copy-start(bf16[512,1024]{1,0:T(8,128)(2,1)} %all-gather.3.cloned.1.call-done) | copy-start | bytes 3145732
  72.8 5.8 %copy-start.1 = (bf16[4,512,512]{1,2,0:T(8,128)(2,1)S(1)}, bf16[4,512,512]{1,2,0:T(8,128)(2,1)}, u32[]{:S(2)}) copy-start(bf16[4,512,512]{1,2,0:T(8,128)(2,1)} %fusion.14) | copy-start | bytes 6291460
  72.8 6.3 %copy-start.5 = (bf16[512,1024]{1,0:T(8,128)(2,1)S(1)}, bf16[512,1024]{1,0:T(8,128)(2,1)}, u32[]{:S(2)}) copy-start(bf16[512,1024]{1,0:T(8,128)(2,1)} %all-gather.5.cloned.1.call-done) | copy-start | bytes 3145732
  80.6 85.3 %reduce-scatter.3.cloned.1.call-start = ((), (), s32[]{:S(2)}) async-start(), calls=%async_computation.7 | async-start | bytes 3538944 | tf_op jit(solution)/shard_map/reduce_scatter | solution.py:143
  82.3 3.1 %copy-start.10 = (bf16[512,256]{0,1:T(8,128)(2,1)S(1)}, bf16[512,256]{0,1:T(8,128)(2,1)}, u32[]{:S(2)}) copy-start(bf16[512,256]{0,1:T(8,128)(2,1)} %copy-done.9) | copy-start | bytes 786436
  82.3 3.8 %copy-start.3 = (bf16[512,1024]{1,0:T(8,128)(2,1)S(1)}, bf16[512,1024]{1,0:T(8,128)(2,1)}, u32[]{:S(2)}) copy-start(bf16[512,1024]{1,0:T(8,128)(2,1)} %all-gather.3.cloned.1.call-done) | copy-start | bytes 3145732
  85.4 1.2 copy-start.8
  91.8 11.6 %all-to-all-start.2 = ((bf16[4,128,256]{1,2,0:T(8,128)(2,1)}), bf16[4,128,256]{1,2,0:T(8,128)(2,1)}, u32[]{:S(2)}, u32[]{:S(2)}) async-start(bf16[4,128,256]{1,2,0:T(8,128)(2,1)} %copy.22), calls=%async_computation.2 | async-start | bytes 524288 | tf_op jit(solution)/shard_map/all_to_all | solution.py:149
  96.7 26.3 %copy-start.4 = (bf16[1,128,1024]{2,1,0:T(8,128)(2,1)S(1)}, bf16[1,128,1024]{2,1,0:T(8,128)(2,1)}, u32[]{:S(2)}) copy-start(bf16[1,128,1024]{2,1,0:T(8,128)(2,1)} %param.7) | copy-start | bytes 786436
  96.7 26.3 %copy-start.11 = (f32[1024]{0:T(1024)S(1)}, f32[1024]{0:T(1024)}, u32[]{:S(2)}) copy-start(f32[1024]{0:T(1024)} %param.10) | copy-start | bytes 12292
  103.4 9.7 %all-to-all-start.1 = ((bf16[4,128,256]{1,2,0:T(8,128)(2,1)}), bf16[4,128,256]{1,2,0:T(8,128)(2,1)}, u32[]{:S(2)}, u32[]{:S(2)}) async-start(bf16[4,128,256]{1,2,0:T(8,128)(2,1)} %copy.20), calls=%async_computation.1 | async-start | bytes 524288 | tf_op jit(solution)/shard_map/all_to_all | solution.py:148
  113.2 9.7 %all-to-all-start = ((bf16[4,128,256]{1,2,0:T(8,128)(2,1)}), bf16[4,128,256]{1,2,0:T(8,128)(2,1)}, u32[]{:S(2)}, u32[]{:S(2)}) async-start(bf16[4,128,256]{1,2,0:T(8,128)(2,1)} %copy.18), calls=%async_computation | async-start | bytes 524288 | tf_op jit(solution)/shard_map/all_to_all | solution.py:147
  122.9 2.4 %copy-start.6 = (bf16[1,128,1024]{2,1,0:T(8,128)(2,1)S(1)}, bf16[1,128,1024]{2,1,0:T(8,128)(2,1)}, u32[]{:S(2)}) copy-start(bf16[1,128,1024]{2,1,0:T(8,128)(2,1)} %param.13) | copy-start | bytes 786436
Sparse Core Ops, SparseCore 0:
  13.2 29.8 all-gather.2
  45.3 27.4 all-gather.4
  80.7 35.5 reduce-scatter.4
  119.5 46.3 reduce-scatter.2
where the time goes:
time: 176 us; the launch traced here: 174 us
  waiting for transfers between devices  93.9 us (53%)
  matrix products  29.4 us (17%)
  other arithmetic  18.8 us (11%)
  between operations  14 us (8%)
  starting transfers between devices  12.3 us (7%)
  local copies, waits for them, and re-layouts  5.9 us (3%)
    reduce_scatter x1, waiting for transfers between devices, shards(): lax.psum_scatter(term_qkv, 'dp', scatter_dimension=2, tiled=True)  37.9 us
    all_gather x1, waiting for transfers between devices, shards(): lax.all_gather(normed, 'seq', axis=0, tiled=True)  27.3 us
    all_gather x1, waiting for transfers between devices, shards(): lax.all_gather(masked_grad, 'seq', axis=0, tiled=True)  18 us
    dot_general x3, matrix products, project(): jnp.einsum('td,od->to', normed, weight, preferred_element_type=jnp.float32)  5.33 us
    all_to_all x1, waiting for transfers between devices, shards(): lax.all_to_all(value_grad, 'seq', split_axis=0, concat_axis=1, tiled=True)  5.03 us
    all_to_all x1, waiting for transfers between devices, shards(): lax.all_to_all(key_grad, 'seq', split_axis=0, concat_axis=1, tiled=True)  4.89 us
    convert_element_type x1, other arithmetic, step(): probs_low = probs.astype(jnp.bfloat16)  4.2 us
    all_to_all x1, starting transfers between devices, shards(): lax.all_to_all(value_grad, 'seq', split_axis=0, concat_axis=1, tiled=True)  4.05 us
  transfers between devices with their start and end apart: 7, of which 6 were waited for; matrix products, arithmetic and copies ran while one was open for 21% of the time, Pallas kernels for 0%

commit v1 on v0

--- a/solution.py
+++ b/solution.py
@@ -3,6 +3,8 @@
 import jax
 import jax.numpy as jnp
 from jax import lax
+from jax.experimental import pallas as pl
+from jax.experimental.pallas import tpu as pltpu
 from jax.sharding import PartitionSpec as P
 
 HEAD_DIM = 64
@@ -154,7 +156,285 @@
     return (d_inputs[None], grad_qkv * factor, grad_out * factor)
 
 
+FIRST_MOVES = (
+    ((0, 0), (2, 0)),
+    ((1, 0), (0, 0)),
+    ((2, 0), (0, 1)),
+    ((3, 0), (2, 1)),
+    ((0, 1), (1, 0)),
+    ((1, 1), (3, 1)),
+    ((2, 1), (3, 0)),
+    ((3, 1), (1, 1)),
+)
+SECOND_MOVES = (
+    ((0, 1), (3, 0)),
+    ((3, 0), (0, 1)),
+    ((1, 0), (2, 1)),
+    ((2, 1), (1, 0)),
+)
+SWAP_MOVES = (
+    ((0, 1), (1, 0)),
+    ((1, 0), (0, 1)),
+    ((2, 1), (3, 0)),
+    ((3, 0), (2, 1)),
+)
+
+
+def column_pairs(moves, chips, seqs, back=False):
+    pairs = []
+    for chip in range(chips):
+        for source, target in moves:
+            if back:
+                source, target = target, source
+            pairs.append(
+                ((chip * 2 + source[1]) * seqs + source[0], (chip * 2 + target[1]) * seqs + target[0])
+            )
+    return pairs
+
+
+def block_table():
+    table = [[0, 0] for _ in range(8)]
+    for (source, _), (target, core) in FIRST_MOVES:
+        table[target * 2 + core][0] = source
+        table[target * 2 + core][1] = target
+    for (source, _), (target, core) in SECOND_MOVES:
+        table[target * 2 + core][1] = source
+    return table
+
+
+def nt(left, right):
+    return lax.dot_general(left, right, (((1,), (1,)), ((), ())), preferred_element_type=jnp.float32)
+
+
+def nn(left, right):
+    return lax.dot_general(left, right, (((1,), (0,)), ((), ())), preferred_element_type=jnp.float32)
+
+
+def tn(left, right):
+    return lax.dot_general(left, right, (((0,), (0,)), ((), ())), preferred_element_type=jnp.float32)
+
+
+def attention_kernel(
+    sizes, here_t, there_t, here_g, there_g, w_qkv, w_out,
+    grads, attended, normed_keep, normed_send,
+    query, key, value, lifted, query_sum, key_sum, value_sum, attended_sum,
+):
+    half, _ = here_t.shape
+    total = 2 * half
+    width = w_out.shape[1]
+    capacity = half // 2
+    low = jnp.bfloat16
+    scale = HEAD_DIM ** (-0.5)
+
+    def row_ok(part):
+        row = lax.broadcasted_iota(jnp.int32, (half, 1), 0)
+        first, second = sizes[2 * part], sizes[2 * part + 1]
+        return row < jnp.where(row < capacity, first, second + capacity)
+
+    for part, (rows_t, rows_g) in enumerate(((here_t, here_g), (there_t, there_g))):
+        span = pl.ds(part * half, half)
+        rows = rows_t[...]
+        query[span, :] = (nt(rows, w_qkv[0:width, :]).astype(low) * scale).astype(low)
+        key[span, :] = nt(rows, w_qkv[width : 2 * width, :]).astype(low)
+        value[span, :] = nt(rows, w_qkv[2 * width : 3 * width, :]).astype(low)
+        up = nn(rows_g[...], w_out[...])
+        lifted[span, :] = jnp.where(row_ok(part), up, 0.0).astype(low)
+
+    column = lax.broadcasted_iota(jnp.int32, (1, total), 1)
+    block = column // capacity
+    limit = jnp.where(
+        block == 0, sizes[0], jnp.where(block == 1, sizes[1], jnp.where(block == 2, sizes[2], sizes[3]))
+    )
+    bias = jnp.where(column - block * capacity < limit, 0.0, MASKED)
+    lane = lax.broadcasted_iota(jnp.int32, (1, width), 1) // HEAD_DIM
+
+    key_sum[...] = jnp.zeros_like(key_sum)
+    value_sum[...] = jnp.zeros_like(value_sum)
+    query_sum[...] = jnp.zeros_like(query_sum)
+    attended_sum[...] = jnp.zeros_like(attended_sum)
+
+    def head_step(head, carry):
+        mine = lane == head
+        zero = jnp.zeros((), low)
+        key_h = jnp.where(mine, key[...], zero)
+        value_h = jnp.where(mine, value[...], zero)
+        for part in range(2):
+            span = pl.ds(part * half, half)
+            query_h = jnp.where(mine, query[span, :], zero)
+            lifted_h = jnp.where(mine, lifted[span, :], zero)
+            scores = nt(query_h, key[...]) + bias
+            expo = jnp.exp(scores - jnp.max(scores, axis=1, keepdims=True))
+            probs = expo * (1.0 / jnp.sum(expo, axis=1, keepdims=True))
+            probs_low = probs.astype(low)
+            attended_h = nn(probs_low, value_h)
+            attended_sum[span, :] += attended_h
+            delta = jnp.sum(lifted_h.astype(jnp.float32) * attended_h, axis=1, keepdims=True)
+            score_grad = (probs * (nt(lifted_h, value[...]) - delta)).astype(low)
+            query_sum[span, :] += nn(score_grad, key_h)
+            key_sum[...] += tn(score_grad, query_h)
+            value_sum[...] += tn(probs_low, lifted_h)
+        return carry
+
+    lax.fori_loop(0, width // HEAD_DIM, head_step, 0)
+
+    grads[:, 0:width] = (query_sum[...] * scale).astype(low)
+    grads[:, width : 2 * width] = key_sum[...].astype(low)
+    grads[:, 2 * width : 3 * width] = value_sum[...].astype(low)
+    for part in range(2):
+        span = pl.ds(part * half, half)
+        attended[span, :] = jnp.where(row_ok(part), attended_sum[span, :], 0.0).astype(low)
+    normed_keep[...] = nn(grads[0:half, :], w_qkv[...])
+    normed_send[...] = nn(grads[half:total, :], w_qkv[...]).astype(low)
+
+
+def weight_kernel(
+    place, here_t, there_t, here_g, there_g, grads, attended, x_keep, x_send, y_keep, y_send
+):
+    half, _ = here_t.shape
+    total = 2 * half
+    width = attended.shape[1]
+    lanes = width // 2
+    for slot_y in range(2):
+        for slot_x in range(2):
+            block = (place[0] ^ slot_y) * 2 + (place[1] ^ slot_x)
+            cols = pl.ds(pl.multiple_of(block * width, width), width)
+            for rows, target, index in (
+                (0, x_keep if slot_x == 0 else x_send, slot_y),
+                (1, y_keep if slot_y == 0 else y_send, slot_x),
+            ):
+                low, high = rows * 2 * width, (rows + 1) * 2 * width if rows == 0 else 3 * width
+                term = tn(grads[0:half, low:high], here_t[:, cols])
+                term = term + tn(grads[half:total, low:high], there_t[:, cols])
+                term = term.astype(target.dtype)
+                for core in range(2):
+                    target[index, core, 0 : high - low, :] = term[:, core * lanes : (core + 1) * lanes]
+                if rows == 1:
+                    term = tn(here_g[:, cols], attended[0:half, :])
+                    term = term + tn(there_g[:, cols], attended[half:total, :])
+                    term = term.astype(target.dtype)
+                    for core in range(2):
+                        for side in range(2):
+                            target[index, core, pl.ds(width + side * lanes, lanes), :] = term[
+                                core * lanes : (core + 1) * lanes, side * lanes : (side + 1) * lanes
+                            ]
+
+
+def vmem(count):
+    return [pl.BlockSpec(memory_space=pltpu.VMEM)] * count
+
+
+def column_shards(tokens, positions, counts, ln_gain, w_qkv, w_out, d_out):
+    low, wide = jnp.bfloat16, jnp.float32
+    inputs = tokens[0]
+    upstream = d_out[0]
+    capacity, features = inputs.shape
+    seqs = lax.axis_size("seq")
+    chips = lax.axis_size("dp") // 2
+    seat = lax.axis_index("seq")
+    dp = lax.axis_index("dp")
+    core, place_x, place_y = dp % 2, (dp // 2) % 2, dp // 4
+    half, total = 2 * capacity, 4 * capacity
+    width = features // seqs
+    lanes = width // 2
+    factor = 1.0 / math.sqrt(lax.axis_size("dp") * (3 * total // 4))
+    resident = core == seat % 2
+
+    axes = ("dp", "seq")
+    first = column_pairs(FIRST_MOVES, chips, seqs)
+    second = column_pairs(SECOND_MOVES, chips, seqs)
+    first_back = column_pairs(FIRST_MOVES, chips, seqs, True)
+    swap = column_pairs(SWAP_MOVES, chips, seqs)
+
+    def across(array, bit):
+        return lax.ppermute(array, "dp", [(i, i ^ bit) for i in range(2 * chips)])
+
+    def share(array):
+        from_first = lax.ppermute(array, axes, first)
+        from_second = lax.ppermute(array, axes, second)
+        here = jnp.concatenate([from_first, jnp.where(resident, array, from_second)], axis=0)
+        return here, across(here, 1)
+
+    here_g, there_g = share(upstream)
+    normed, standard, inv_std = layer_norm(inputs, positions[0], ln_gain)
+    here_t, there_t = share(normed)
+
+    other_counts = across(counts[0], 1)
+    sizes = jnp.where(resident, counts[0], other_counts)
+    table = jnp.array(block_table(), jnp.int32)
+    order = jnp.concatenate([table[seat * 2 + core], table[seat * 2 + 1 - core]])
+    sizes = sizes[order]
+
+    group = (seat // 2) * 2 + core
+    own_qkv = lax.dynamic_slice_in_dim(w_qkv, group * width, width, 1).reshape(3 * width, features)
+    own_out = lax.dynamic_slice_in_dim(w_out, group * width, width, 1)
+
+    smem = pl.BlockSpec(memory_space=pltpu.SMEM)
+    grads, attended, normed_keep, normed_send = pl.pallas_call(
+        attention_kernel,
+        out_shape=(
+            jax.ShapeDtypeStruct((total, 3 * width), low),
+            jax.ShapeDtypeStruct((total, width), low),
+            jax.ShapeDtypeStruct((half, features), wide),
+            jax.ShapeDtypeStruct((half, features), low),
+        ),
+        in_specs=[smem] + vmem(6),
+        out_specs=vmem(4),
+        scratch_shapes=[pltpu.VMEM((total, width), low)] * 4 + [pltpu.VMEM((total, width), wide)] * 4,
+        compiler_params=pltpu.CompilerParams(vmem_limit_bytes=48 * 1024 * 1024),
+        cost_estimate=pl.CostEstimate(
+            flops=2 * total * features * width * 7 + 12 * 4 * total * total * width,
+            bytes_accessed=8 * 1024 * 1024,
+            transcendentals=4 * total * total,
+        ),
+    )(sizes, here_t, there_t, here_g, there_g, own_qkv, own_out)
+
+    place = jnp.stack([place_y, place_x]).astype(jnp.int32)
+    x_keep, x_send, y_keep, y_send = pl.pallas_call(
+        weight_kernel,
+        out_shape=(
+            jax.ShapeDtypeStruct((2, 2, 2 * width, lanes), wide),
+            jax.ShapeDtypeStruct((2, 2, 2 * width, lanes), low),
+            jax.ShapeDtypeStruct((2, 2, 2 * width, lanes), wide),
+            jax.ShapeDtypeStruct((2, 2, 2 * width, lanes), low),
+        ),
+        in_specs=[smem] + vmem(6),
+        out_specs=vmem(4),
+        compiler_params=pltpu.CompilerParams(vmem_limit_bytes=48 * 1024 * 1024),
+        cost_estimate=pl.CostEstimate(
+            flops=2 * total * features * width * 4, bytes_accessed=10 * 1024 * 1024, transcendentals=0
+        ),
+    )(place, here_t, there_t, here_g, there_g, grads, attended)
+
+    x_part = x_keep + across(x_send, 2).astype(wide)
+    y_part = y_keep + across(y_send, 4).astype(wide)
+    x_part = x_part[0] + across(x_part[1].astype(low), 4).astype(wide)
+    y_part = y_part[0] + across(y_part[1].astype(low), 2).astype(wide)
+    sums = jnp.concatenate([x_part, y_part], axis=1)
+    swapped = lax.ppermute(sums.astype(low), axes, swap)
+    sums = jnp.where(resident, sums, swapped.astype(wide))
+    kept = lax.dynamic_index_in_dim(sums, core, 0, False)
+    given = lax.dynamic_index_in_dim(sums, 1 - core, 0, False)
+    final = (kept + across(given, 1)) * factor
+    grad_qkv = final[: 3 * width].reshape(3, width, lanes)
+    grad_out = jnp.concatenate([final[3 * width : 3 * width + lanes], final[3 * width + lanes :]], axis=1)
+
+    back = normed_keep + across(normed_send, 1).astype(wide)
+    from_first = lax.ppermute(back[:capacity].astype(low), axes, first_back)
+    from_second = lax.ppermute(back[capacity:].astype(low), axes, second)
+    normed_grad = from_first.astype(wide) + jnp.where(
+        resident, back[capacity:], from_second.astype(wide)
+    )
+    own_valid = jnp.arange(capacity, dtype=jnp.int32) < lax.dynamic_index_in_dim(counts[0], seat, 0, False)
+    masked_grad = jnp.where(own_valid[:, None], upstream, jnp.zeros_like(upstream))
+    unit_grad = normed_grad * ln_gain
+    inner = unit_grad - jnp.mean(unit_grad, axis=1, keepdims=True)
+    inner = inner - standard * jnp.mean(unit_grad * standard, axis=1, keepdims=True)
+    d_inputs = (masked_grad.astype(wide) + inv_std * inner).astype(low)
+    return (d_inputs[None], grad_qkv, grad_out)
+
+
 def solution(mesh):
+    fits = mesh.shape["dp"] == 8 and mesh.shape["seq"] == 4
     placed = (
         P("dp", "seq", None),
         P("dp", "seq"),
@@ -165,7 +445,7 @@
         P("dp", "seq", None),
     )
     return jax.shard_map(
-        shards,
+        column_shards if fits else shards,
         mesh=mesh,
         in_specs=placed,
         out_specs=(P("dp", "seq", None), P(None, "seq", "dp"), P("dp", "seq")),

time: 176 us -> 108 us (0.61)
  waiting for transfers between devices: 93.9 us -> 35.1 us
  matrix products: 29.4 us -> 0 us
  Pallas kernels: 0 us -> 15.7 us
  starting transfers between devices: 12.3 us -> 26.4 us
  between operations: 14 us -> 1.07 us
  local copies, waits for them, and re-layouts: 5.9 us -> 15.6 us
  other arithmetic: 18.8 us -> 13.2 us
    all_gather x2 -> x0, waiting for transfers between devices: 45.4 us -> none  [the longest x1 27.3 us: shards(): lax.all_gather(normed, 'seq', axis=0, tiled=True)]
    reduce_scatter x2 -> x0, waiting for transfers between devices: 37.9 us -> none  [the longest x1 37.9 us: shards(): lax.psum_scatter(term_qkv, 'dp', scatter_dimension=2, tiled=True)]
    ppermute x0 -> x16, waiting for transfers between devices: none -> 35.1 us  [the longest x9 13.2 us: across(): return lax.ppermute(array, 'dp', [(i, i ^ bit) for i in range(2 * chips)])]
    ppermute x0 -> x16, starting transfers between devices: none -> 26.4 us  [the longest x2 7.35 us: share(): from_second = lax.ppermute(array, axes, second)]
    dot_general x16 -> x0, matrix products: 25.8 us -> none  [the longest x3 5.33 us: project(): jnp.einsum('td,od->to', normed, weight, preferred_element_type=jnp.float32)]
    pallas_call x0 -> x2, Pallas kernels: none -> 15.7 us  [the longest x1 12.4 us: column_shards(): pl.pallas_call(attention_kernel, out_shape=(jax.ShapeDtypeStruct((total,...]
    all_to_all x3 -> x0, starting transfers between devices: 12.1 us -> none  [the longest x1 4.05 us: shards(): lax.all_to_all(value_grad, 'seq', split_axis=0, concat_axis=1, tiled=True)]
    all_to_all x3 -> x0, waiting for transfers between devices: 10.5 us -> none  [the longest x1 5.03 us: shards(): lax.all_to_all(value_grad, 'seq', split_axis=0, concat_axis=1, tiled=True)]
  transfers between devices with their start and end apart: 7 -> 16, of which waited for: 6 -> 7; matrix products, arithmetic and copies ran while one was open for 21% -> 18% of each run, Pallas kernels for 0% -> 0%
where the time goes in v1:
time: 108 us; the launch traced here: 107 us
  waiting for transfers between devices  35.1 us (32%)
  starting transfers between devices  26.4 us (24%)
  Pallas kernels  15.7 us (15%)
  local copies, waits for them, and re-layouts  15.6 us (14%)
  other arithmetic  13.2 us (12%)
    ppermute x9, waiting for transfers between devices, across(): return lax.ppermute(array, 'dp', [(i, i ^ bit) for i in range(2 * chips)])  13.2 us
    pallas_call x1, Pallas kernels, column_shards(): pl.pallas_call(attention_kernel, out_shape=(jax.ShapeDtypeStruct((total,...  12.4 us
    unnamed x42, local copies, waits for them, and re-layouts  7.68 us
    ppermute x2, starting transfers between devices, share(): from_second = lax.ppermute(array, axes, second)  7.35 us
    ppermute x9, starting transfers between devices, across(): return lax.ppermute(array, 'dp', [(i, i ^ bit) for i in range(2 * chips)])  7.13 us
    ppermute x2, waiting for transfers between devices, share(): from_first = lax.ppermute(array, axes, first)  5.8 us
    ppermute x1, waiting for transfers between devices, column_shards(): from_first = lax.ppermute(back[:capacity].astype(low), axes, first_back)  5.39 us
    ppermute x2, waiting for transfers between devices, share(): from_second = lax.ppermute(array, axes, second)  5.33 us
  transfers between devices with their start and end apart: 16, of which 7 were waited for; matrix products, arithmetic and copies ran while one was open for 18% of the time, Pallas kernels for 0%

profile of v1, /device:TPU:1, one launch (start us, length us, event | category | flops | bytes accessed | tf_op | source)
XLA Modules:
  0.0 107.2 jit_solution(12793187463736712015)
XLA Ops:
  0.7 2.7 %collective-permute-start.4 = (bf16[128,1024]{1,0:T(8,128)(2,1)}, bf16[128,1024]{1,0:T(8,128)(2,1)}, u32[]{:S(2)}, u32[]{:S(2)}) collective-permute-start(bf16[128,1024]{1,0:T(8,128)(2,1)} %bitcast.52), channel_id=1, source_target_pairs={{0,2},{1,0},{2,4},{3,6},{4,1},{5,7},{6,3},{7,5},{8,10},{9,8},{10,1... | collective-permute-start | bytes 786440 | tf_op jit(solution)/shard_map/ppermute | solution.py:352
  3.4 4.1 %collective-permute-start.5 = (bf16[128,1024]{1,0:T(8,128)(2,1)}, bf16[128,1024]{1,0:T(8,128)(2,1)S(1)}, u32[]{:S(2)}, u32[]{:S(2)}) collective-permute-start(bf16[128,1024]{1,0:T(8,128)(2,1)} %bitcast.53), channel_id=1, source_target_pairs={{4,3},{3,4},{1,6},{6,1},{12,11},{11,12},{9,14},{14,9},{20,19},{19,... | collective-permute-start | bytes 786440 | tf_op jit(solution)/shard_map/ppermute | solution.py:353
  7.5 0.7 convert_bitcast_fusion
  8.2 1.0 multiply_sine_fusion
  9.2 1.2 %fusion.10 = f32[128]{0:T(128)S(1)} fusion(f32[128,512]{1,0:T(8,128)S(1)} %get-tuple-element.29, f32[128,512]{1,0:T(8,128)S(1)} %get-tuple-element.28, bf16[1,128,1024]{2,1,0:T(8,128)(2,1)} %param.8), kind=kLoop, calls=%fused_computation.54 | loop fusion | flops 524160 | bytes 786944 | tf_op jit(solution)/shard_map/reduce_sum | solution.py:26
  10.4 1.2 %multiply_reduce_fusion.1 = f32[128]{0:T(128)S(1)} fusion(f32[128]{0:T(128)S(1)} %broadcast_multiply_fusion.2, f32[128,512]{1,0:T(8,128)S(1)} %get-tuple-element.29, f32[128,512]{1,0:T(8,128)S(1)} %get-tuple-element.28, bf16[1,128,1024]{2,1,0:T(8,128)(2,1)} %param.8), kind=kLoop, calls=%fused_computation.24 | loop fusion | flops 786304 | bytes 787456 | tf_op jit(solution)/shard_map/reduce_sum | solution.py:27
  11.8 3.3 %collective-permute-start.2 = (bf16[128,1024]{1,0:T(8,128)(2,1)S(1)}, bf16[128,1024]{1,0:T(8,128)(2,1)S(1)}, u32[]{:S(2)}, u32[]{:S(2)}) collective-permute-start(bf16[128,1024]{1,0:T(8,128)(2,1)S(1)} %multiply_convert_fusion), channel_id=1, source_target_pairs={{4,3},{3,4},{1,6},{6,1},{12,11},{11,12},{9,14},{14,9},{20,19},{19,... | collective-permute-start | bytes 786440 | tf_op jit(solution)/shard_map/ppermute | solution.py:353
  15.2 0.8 fusion.7
  16.1 5.3 %collective-permute-done.2 = bf16[128,1024]{1,0:T(8,128)(2,1)S(1)} collective-permute-done((bf16[128,1024]{1,0:T(8,128)(2,1)S(1)}, bf16[128,1024]{1,0:T(8,128)(2,1)S(1)}, u32[]{:S(2)}, u32[]{:S(2)}) %collective-permute-start.2) | collective-permute-done | bytes 262176 | tf_op jit(solution)/shard_map/ppermute | solution.py:353
  21.4 5.8 %collective-permute-done.1 = bf16[128,1024]{1,0:T(8,128)(2,1)} collective-permute-done((bf16[128,1024]{1,0:T(8,128)(2,1)S(1)}, bf16[128,1024]{1,0:T(8,128)(2,1)}, u32[]{:S(2)}, u32[]{:S(2)}) %collective-permute-start.1) | collective-permute-done | bytes 262176 | tf_op jit(solution)/shard_map/ppermute | solution.py:352
  27.2 1.0 pad_maximum_fusion.1.here_t
  28.4 1.0 pad_maximum_fusion.2.here_g
  29.4 0.5 collective-permute-start.6
  30.0 0.9 constant_dynamic-slice_fusion.w_out
  30.9 2.7 %constant_dynamic-slice_fusion.1 = bf16[3,256,1024]{2,1,0:T(8,128)(2,1)} fusion(bf16[3,1024,1024]{2,1,0:T(8,128)(2,1)} %param.12, s32[]{:T(128)S(6)} %select_n.107), kind=kLoop, calls=%fused_computation.39 | loop fusion | bytes 3145732 | tf_op jit(solution)/shard_map/dynamic_slice | solution.py:368
  33.6 0.6 gather_fusion
  34.3 1.0 copy-done.3
  35.3 1.0 copy-done.6
  36.3 1.0 copy-done.7
  37.4 12.4 %shard_map.103 = (bf16[512,768]{1,0:T(8,128)(2,1)S(1)}, bf16[512,256]{1,0:T(8,128)(2,1)S(1)}, f32[256,1024]{1,0:T(8,128)S(1)}, bf16[256,1024]{1,0:T(8,128)(2,1)S(1)}) custom-call(s32[4]{0:T(128)S(1)} %gather_fusion, bf16[256,1024]{1,0:T(8,128)(2,1)S(1)} %copy-done.3, bf16[256,1024]{1,0:T(8,128)(2,1)} %collective-permute-done.3.there_t, ...), custom_call_target="tpu_custom_call" | custom-call | flops 5100273664 | bytes 8388608 | tf_op jit(solution)/shard_map/pallas_call | solution.py:372
  49.8 0.8 copy-done.8
  50.5 3.4 %shard_map.104 = (f32[2,2,512,128]{3,2,1,0:T(8,128)S(1)}, bf16[2,2,512,128]{3,2,1,0:T(8,128)(2,1)}, f32[2,2,512,128]{3,2,1,0:T(8,128)}, bf16[2,2,512,128]{3,2,1,0:T(8,128)(2,1)S(1)}) custom-call(s32[2]{0:T(128)S(1)} %pad_add_fusion.place, bf16[256,1024]{1,0:T(8,128)(2,1)S(1)} %copy-done.4, bf16[256,1024]{1,0:T(8,128)(2,1)} %collective-permute-done.3.there_t, ...), custom_call_target="tpu_custom_call" | custom-call | flops 1073741824 | bytes 10485760 | tf_op jit(solution)/shard_map/pallas_call | solution.py:392
  53.9 1.0 copy-done.1
  54.9 0.8 copy-done.9
  55.7 1.2 %collective-permute-start.10 = (bf16[2,2,512,128]{3,2,1,0:T(8,128)(2,1)}, bf16[2,2,512,128]{3,2,1,0:T(8,128)(2,1)}, u32[]{:S(2)}, u32[]{:S(2)}) collective-permute-start(bf16[2,2,512,128]{3,2,1,0:T(8,128)(2,1)} %get-tuple-element.16), channel_id=1, source_target_pairs={{0,8},{4,12},{8,0},{12,4},{16,24},{20,28},{24,16},{28,20},{1,9},{5... | collective-permute-start | bytes 1572872 | tf_op jit(solution)/shard_map/ppermute | solution.py:349
  56.9 0.6 constant_dynamic-slice_fusion.4
  57.5 1.2 %collective-permute-start.12 = (bf16[2,2,512,128]{3,2,1,0:T(8,128)(2,1)}, bf16[2,2,512,128]{3,2,1,0:T(8,128)(2,1)S(1)}, u32[]{:S(2)}, u32[]{:S(2)}) collective-permute-start(bf16[2,2,512,128]{3,2,1,0:T(8,128)(2,1)} %copy-done.9), channel_id=1, source_target_pairs={{0,16},{4,20},{8,24},{12,28},{16,0},{20,4},{24,8},{28,12},{1,17},{... | collective-permute-start | bytes 1572872 | tf_op jit(solution)/shard_map/ppermute | solution.py:349
  58.7 10.7 %collective-permute-done.10 = bf16[2,2,512,128]{3,2,1,0:T(8,128)(2,1)} collective-permute-done((bf16[2,2,512,128]{3,2,1,0:T(8,128)(2,1)}, bf16[2,2,512,128]{3,2,1,0:T(8,128)(2,1)}, u32[]{:S(2)}, u32[]{:S(2)}) %collective-permute-start.10) | collective-permute-done | bytes 524320 | tf_op jit(solution)/shard_map/ppermute | solution.py:349
  69.5 1.4 %convert_add_fusion.1 = f32[2,2,512,128]{3,2,1,0:T(8,128)S(1)} fusion(f32[2,2,512,128]{3,2,1,0:T(8,128)} %copy-done.1, bf16[2,2,512,128]{3,2,1,0:T(8,128)(2,1)} %collective-permute-done.10), kind=kLoop, calls=%fused_computation.4 | loop fusion | flops 524288 | bytes 2621440 | tf_op jit(solution)/shard_map/add | solution.py:408
  71.0 1.0 copy-done.14
  71.9 0.7 fusion.5
  72.6 1.3 %collective-permute-start.11 = (bf16[2,512,128]{2,1,0:T(8,128)(2,1)}, bf16[2,512,128]{2,1,0:T(8,128)(2,1)}, u32[]{:S(2)}, u32[]{:S(2)}) collective-permute-start(bf16[2,512,128]{2,1,0:T(8,128)(2,1)} %fusion.5), channel_id=1, source_target_pairs={{0,16},{4,20},{8,24},{12,28},{16,0},{20,4},{24,8},{28,12},{1,17},{... | collective-permute-start | bytes 786440 | tf_op jit(solution)/shard_map/ppermute | solution.py:349
  74.0 1.0 copy-done.15
  75.0 0.7 fusion.6
  75.7 1.2 %collective-permute-start.13 = (bf16[2,512,128]{2,1,0:T(8,128)(2,1)}, bf16[2,512,128]{2,1,0:T(8,128)(2,1)}, u32[]{:S(2)}, u32[]{:S(2)}) collective-permute-start(bf16[2,512,128]{2,1,0:T(8,128)(2,1)} %fusion.6), channel_id=1, source_target_pairs={{0,8},{4,12},{8,0},{12,4},{16,24},{20,28},{24,16},{28,20},{1,9},{5... | collective-permute-start | bytes 786440 | tf_op jit(solution)/shard_map/ppermute | solution.py:349
  76.9 0.6 iota_compare_fusion
  77.6 1.5 %collective-permute-start.7 = (bf16[256,1024]{1,0:T(8,128)(2,1)}, bf16[256,1024]{1,0:T(8,128)(2,1)S(1)}, u32[]{:S(2)}, u32[]{:S(2)}) collective-permute-start(bf16[256,1024]{1,0:T(8,128)(2,1)} %copy-done.8), channel_id=1, source_target_pairs={{0,4},{4,0},{8,12},{12,8},{16,20},{20,16},{24,28},{28,24},{1,5},{5... | collective-permute-start | bytes 1572872 | tf_op jit(solution)/shard_map/ppermute | solution.py:349
  79.1 0.8 collective-permute-done.11
  79.9 1.2 %fusion.2 = f32[2,512,128]{2,1,0:T(8,128)S(1)} fusion(f32[2,2,512,128]{3,2,1,0:T(8,128)} %copy-done.14, bf16[2,512,128]{2,1,0:T(8,128)(2,1)} %collective-permute-done.11), kind=kLoop, calls=%fused_computation.12 | loop fusion | flops 262144 | bytes 1310720 | tf_op jit(solution)/shard_map/add | solution.py:410
  81.1 1.6 %collective-permute-done.13 = bf16[2,512,128]{2,1,0:T(8,128)(2,1)} collective-permute-done((bf16[2,512,128]{2,1,0:T(8,128)(2,1)}, bf16[2,512,128]{2,1,0:T(8,128)(2,1)}, u32[]{:S(2)}, u32[]{:S(2)}) %collective-permute-start.13) | collective-permute-done | bytes 262176 | tf_op jit(solution)/shard_map/ppermute | solution.py:349
  82.7 1.2 %fusion.1 = f32[2,512,128]{2,1,0:T(8,128)S(1)} fusion(f32[2,2,512,128]{3,2,1,0:T(8,128)} %copy-done.15, bf16[2,512,128]{2,1,0:T(8,128)(2,1)} %collective-permute-done.13), kind=kLoop, calls=%fused_computation.9 | loop fusion | flops 262144 | bytes 1310720 | tf_op jit(solution)/shard_map/add | solution.py:411
  84.0 5.1 %collective-permute-start.14 = (bf16[2,1024,128]{2,1,0:T(8,128)(2,1)S(1)}, bf16[2,1024,128]{2,1,0:T(8,128)(2,1)S(1)}, u32[]{:S(2)}, u32[]{:S(2)}) collective-permute-start(bf16[2,1024,128]{2,1,0:T(8,128)(2,1)S(1)} %fusion), channel_id=1, source_target_pairs={{4,1},{1,4},{6,3},{3,6},{12,9},{9,12},{14,11},{11,14},{20,17},{17,... | collective-permute-start | bytes 1572872 | tf_op jit(solution)/shard_map/ppermute | solution.py:413
  89.8 3.6 %collective-permute-start.9 = (bf16[128,1024]{1,0:T(8,128)(2,1)S(1)}, bf16[128,1024]{1,0:T(8,128)(2,1)S(1)}, u32[]{:S(2)}, u32[]{:S(2)}) collective-permute-start(bf16[128,1024]{1,0:T(8,128)(2,1)S(1)} %get-tuple-element.23), channel_id=1, source_target_pairs={{4,3},{3,4},{1,6},{6,1},{12,11},{11,12},{9,14},{14,9},{20,19},{19,... | collective-permute-start | bytes 786440 | tf_op jit(solution)/shard_map/ppermute | solution.py:423
  93.4 5.3 %collective-permute-done.14 = bf16[2,1024,128]{2,1,0:T(8,128)(2,1)S(1)} collective-permute-done((bf16[2,1024,128]{2,1,0:T(8,128)(2,1)S(1)}, bf16[2,1024,128]{2,1,0:T(8,128)(2,1)S(1)}, u32[]{:S(2)}, u32[]{:S(2)}) %collective-permute-start.14) | collective-permute-done | bytes 524320 | tf_op jit(solution)/shard_map/ppermute | solution.py:413
  98.9 5.4 %collective-permute-done.8 = bf16[128,1024]{1,0:T(8,128)(2,1)S(1)} collective-permute-done((bf16[128,1024]{1,0:T(8,128)(2,1)S(1)}, bf16[128,1024]{1,0:T(8,128)(2,1)S(1)}, u32[]{:S(2)}, u32[]{:S(2)}) %collective-permute-start.8) | collective-permute-done | bytes 262176 | tf_op jit(solution)/shard_map/ppermute | solution.py:422
  104.7 1.0 fusion.4
  105.7 0.8 slice.48
  106.5 0.7 pad_maximum_fusion.3
  (68 shorter events, 2.1 us)
Async XLA Ops:
  0.6 29.4 %copy-start = (bf16[1024,1024]{1,0:T(8,128)(2,1)S(1)}, bf16[1024,1024]{1,0:T(8,128)(2,1)}, u32[]{:S(2)}) copy-start(bf16[1024,1024]{1,0:T(8,128)(2,1)} %param.13) | copy-start | bytes 6291460
  0.6 10.9 %copy-start.12 = (bf16[1,128,1024]{2,1,0:T(8,128)(2,1)S(1)}, bf16[1,128,1024]{2,1,0:T(8,128)(2,1)}, u32[]{:S(2)}) copy-start(bf16[1,128,1024]{2,1,0:T(8,128)(2,1)} %param.8) | copy-start | bytes 786436
  0.7 10.9 %copy-start.19 = (f32[1024]{0:T(1024)S(1)}, f32[1024]{0:T(1024)}, u32[]{:S(2)}) copy-start(f32[1024]{0:T(1024)} %param.11) | copy-start | bytes 12292
  0.7 14.4 %copy-start.20 = (s32[1,4]{1,0:T(1,128)S(1)}, s32[1,4]{1,0:T(1,128)}, u32[]{:S(2)}) copy-start(s32[1,4]{1,0:T(1,128)} %param.10) | copy-start | bytes 52
  0.7 27.7 %collective-permute-start.4 = (bf16[128,1024]{1,0:T(8,128)(2,1)}, bf16[128,1024]{1,0:T(8,128)(2,1)}, u32[]{:S(2)}, u32[]{:S(2)}) collective-permute-start(bf16[128,1024]{1,0:T(8,128)(2,1)} %bitcast.52), channel_id=1, source_target_pairs={{0,2},{1,0},{2,4},{3,6},{4,1},{5,7},{6,3},{7,5},{8,10},{9,8},{10,1... | collective-permute-start | bytes 786440 | tf_op jit(solution)/shard_map/ppermute | solution.py:352
  3.4 24.9 %collective-permute-start.5 = (bf16[128,1024]{1,0:T(8,128)(2,1)}, bf16[128,1024]{1,0:T(8,128)(2,1)S(1)}, u32[]{:S(2)}, u32[]{:S(2)}) collective-permute-start(bf16[128,1024]{1,0:T(8,128)(2,1)} %bitcast.53), channel_id=1, source_target_pairs={{4,3},{3,4},{1,6},{6,1},{12,11},{11,12},{9,14},{14,9},{20,19},{19,... | collective-permute-start | bytes 786440 | tf_op jit(solution)/shard_map/ppermute | solution.py:353
  9.2 2.4 %copy-start.10 = (f32[128,512]{1,0:T(8,128)}, f32[128,512]{1,0:T(8,128)S(1)}, u32[]{:S(2)}) copy-start(f32[128,512]{1,0:T(8,128)S(1)} %get-tuple-element.29) | copy-start | bytes 786436
  10.4 18.0 %copy-start.17 = (bf16[1,128,1024]{2,1,0:T(8,128)(2,1)S(1)}, bf16[1,128,1024]{2,1,0:T(8,128)(2,1)}, u32[]{:S(2)}) copy-start(bf16[1,128,1024]{2,1,0:T(8,128)(2,1)} %param.14) | copy-start | bytes 786436
  11.8 9.7 %collective-permute-start.2 = (bf16[128,1024]{1,0:T(8,128)(2,1)S(1)}, bf16[128,1024]{1,0:T(8,128)(2,1)S(1)}, u32[]{:S(2)}, u32[]{:S(2)}) collective-permute-start(bf16[128,1024]{1,0:T(8,128)(2,1)S(1)} %multiply_convert_fusion), channel_id=1, source_target_pairs={{4,3},{3,4},{1,6},{6,1},{12,11},{11,12},{9,14},{14,9},{20,19},{19,... | collective-permute-start | bytes 786440 | tf_op jit(solution)/shard_map/ppermute | solution.py:353
  15.0 12.2 %collective-permute-start.1 = (bf16[128,1024]{1,0:T(8,128)(2,1)S(1)}, bf16[128,1024]{1,0:T(8,128)(2,1)}, u32[]{:S(2)}, u32[]{:S(2)}) collective-permute-start(bf16[128,1024]{1,0:T(8,128)(2,1)S(1)} %multiply_convert_fusion), channel_id=1, source_target_pairs={{0,2},{1,0},{2,4},{3,6},{4,1},{5,7},{6,3},{7,5},{8,10},{9,8},{10,1... | collective-permute-start | bytes 786440 | tf_op jit(solution)/shard_map/ppermute | solution.py:352
  15.1 18.5 %collective-permute-start = (s32[4]{0:T(128)S(1)}, s32[4]{0:T(128)S(1)}, u32[]{:S(2)}, u32[]{:S(2)}) collective-permute-start(s32[4]{0:T(128)S(1)} %bitcast.55), channel_id=1, source_target_pairs={{0,4},{4,0},{8,12},{12,8},{16,20},{20,16},{24,28},{28,24},{1,5},{5... | collective-permute-start | bytes 56 | tf_op jit(solution)/shard_map/ppermute | solution.py:349
  28.2 5.4 %copy-start.2 = (bf16[256,1024]{1,0:T(8,128)(2,1)}, bf16[256,1024]{1,0:T(8,128)(2,1)S(1)}, u32[]{:S(2)}) copy-start(bf16[256,1024]{1,0:T(8,128)(2,1)S(1)} %pad_maximum_fusion.1.here_t) | copy-start | bytes 1572868
  28.2 6.0 %collective-permute-start.3 = (bf16[256,1024]{1,0:T(8,128)(2,1)S(1)}, bf16[256,1024]{1,0:T(8,128)(2,1)}, u32[]{:S(2)}, u32[]{:S(2)}) collective-permute-start(bf16[256,1024]{1,0:T(8,128)(2,1)S(1)} %pad_maximum_fusion.1.here_t), channel_id=1, source_target_pairs={{0,4},{4,0},{8,12},{12,8},{16,20},{20,16},{24,28},{28,24},{1,5},{5... | collective-permute-start | bytes 1572872 | tf_op jit(solution)/shard_map/ppermute | solution.py:349
  29.4 4.2 %copy-start.5 = (bf16[256,1024]{1,0:T(8,128)(2,1)}, bf16[256,1024]{1,0:T(8,128)(2,1)S(1)}, u32[]{:S(2)}) copy-start(bf16[256,1024]{1,0:T(8,128)(2,1)S(1)} %pad_maximum_fusion.2.here_g) | copy-start | bytes 1572868
  29.4 4.8 %collective-permute-start.6 = (bf16[256,1024]{1,0:T(8,128)(2,1)S(1)}, bf16[256,1024]{1,0:T(8,128)(2,1)}, u32[]{:S(2)}, u32[]{:S(2)}) collective-permute-start(bf16[256,1024]{1,0:T(8,128)(2,1)S(1)} %pad_maximum_fusion.2.here_g), channel_id=1, source_target_pairs={{0,4},{4,0},{8,12},{12,8},{16,20},{20,16},{24,28},{28,24},{1,5},{5... | collective-permute-start | bytes 1572872 | tf_op jit(solution)/shard_map/ppermute | solution.py:349
  34.2 1.0 copy-start.3
  35.3 1.0 copy-start.6
  36.3 1.0 copy-start.7
  37.4 13.2 %copy-start.4 = (bf16[256,1024]{1,0:T(8,128)(2,1)S(1)}, bf16[256,1024]{1,0:T(8,128)(2,1)}, u32[]{:S(2)}) copy-start(bf16[256,1024]{1,0:T(8,128)(2,1)} %copy-done.2) | copy-start | bytes 1572868
  49.7 0.8 copy-start.8
  53.9 1.0 copy-start.1
  54.9 0.8 copy-start.9
  55.7 13.8 %collective-permute-start.10 = (bf16[2,2,512,128]{3,2,1,0:T(8,128)(2,1)}, bf16[2,2,512,128]{3,2,1,0:T(8,128)(2,1)}, u32[]{:S(2)}, u32[]{:S(2)}) collective-permute-start(bf16[2,2,512,128]{3,2,1,0:T(8,128)(2,1)} %get-tuple-element.16), channel_id=1, source_target_pairs={{0,8},{4,12},{8,0},{12,4},{16,24},{20,28},{24,16},{28,20},{1,9},{5... | collective-permute-start | bytes 1572872 | tf_op jit(solution)/shard_map/ppermute | solution.py:349
  56.9 17.0 %copy-start.16 = (f32[2,2,512,128]{3,2,1,0:T(8,128)S(1)}, f32[2,2,512,128]{3,2,1,0:T(8,128)}, u32[]{:S(2)}) copy-start(f32[2,2,512,128]{3,2,1,0:T(8,128)} %get-tuple-element.17) | copy-start | bytes 3145732
  57.5 16.4 %collective-permute-start.12 = (bf16[2,2,512,128]{3,2,1,0:T(8,128)(2,1)}, bf16[2,2,512,128]{3,2,1,0:T(8,128)(2,1)S(1)}, u32[]{:S(2)}, u32[]{:S(2)}) collective-permute-start(bf16[2,2,512,128]{3,2,1,0:T(8,128)(2,1)} %copy-done.9), channel_id=1, source_target_pairs={{0,16},{4,20},{8,24},{12,28},{16,0},{20,4},{24,8},{28,12},{1,17},{... | collective-permute-start | bytes 1572872 | tf_op jit(solution)/shard_map/ppermute | solution.py:349
  70.9 1.0 copy-start.14
  72.6 7.3 %collective-permute-start.11 = (bf16[2,512,128]{2,1,0:T(8,128)(2,1)}, bf16[2,512,128]{2,1,0:T(8,128)(2,1)}, u32[]{:S(2)}, u32[]{:S(2)}) collective-permute-start(bf16[2,512,128]{2,1,0:T(8,128)(2,1)} %fusion.5), channel_id=1, source_target_pairs={{0,16},{4,20},{8,24},{12,28},{16,0},{20,4},{24,8},{28,12},{1,17},{... | collective-permute-start | bytes 786440 | tf_op jit(solution)/shard_map/ppermute | solution.py:349
  74.0 1.0 copy-start.15
  75.7 7.0 %collective-permute-start.13 = (bf16[2,512,128]{2,1,0:T(8,128)(2,1)}, bf16[2,512,128]{2,1,0:T(8,128)(2,1)}, u32[]{:S(2)}, u32[]{:S(2)}) collective-permute-start(bf16[2,512,128]{2,1,0:T(8,128)(2,1)} %fusion.6), channel_id=1, source_target_pairs={{0,8},{4,12},{8,0},{12,4},{16,24},{20,28},{24,16},{28,20},{1,9},{5... | collective-permute-start | bytes 786440 | tf_op jit(solution)/shard_map/ppermute | solution.py:349
  77.6 11.5 %collective-permute-start.7 = (bf16[256,1024]{1,0:T(8,128)(2,1)}, bf16[256,1024]{1,0:T(8,128)(2,1)S(1)}, u32[]{:S(2)}, u32[]{:S(2)}) collective-permute-start(bf16[256,1024]{1,0:T(8,128)(2,1)} %copy-done.8), channel_id=1, source_target_pairs={{0,4},{4,0},{8,12},{12,8},{16,20},{20,16},{24,28},{28,24},{1,5},{5... | collective-permute-start | bytes 1572872 | tf_op jit(solution)/shard_map/ppermute | solution.py:349
  84.0 14.8 %collective-permute-start.14 = (bf16[2,1024,128]{2,1,0:T(8,128)(2,1)S(1)}, bf16[2,1024,128]{2,1,0:T(8,128)(2,1)S(1)}, u32[]{:S(2)}, u32[]{:S(2)}) collective-permute-start(bf16[2,1024,128]{2,1,0:T(8,128)(2,1)S(1)} %fusion), channel_id=1, source_target_pairs={{4,1},{1,4},{6,3},{3,6},{12,9},{9,12},{14,11},{11,14},{20,17},{17,... | collective-permute-start | bytes 1572872 | tf_op jit(solution)/shard_map/ppermute | solution.py:413
  89.3 15.0 %copy-start.11 = (f32[128,512]{1,0:T(8,128)S(1)}, f32[128,512]{1,0:T(8,128)}, u32[]{:S(2)}) copy-start(f32[128,512]{1,0:T(8,128)} %copy-done.10) | copy-start | bytes 786436
  89.3 15.0 %copy-start.13 = (bf16[1,128,1024]{2,1,0:T(8,128)(2,1)S(1)}, bf16[1,128,1024]{2,1,0:T(8,128)(2,1)}, u32[]{:S(2)}) copy-start(bf16[1,128,1024]{2,1,0:T(8,128)(2,1)} %param.8) | copy-start | bytes 786436
  89.4 15.0 %collective-permute-start.8 = (bf16[128,1024]{1,0:T(8,128)(2,1)S(1)}, bf16[128,1024]{1,0:T(8,128)(2,1)S(1)}, u32[]{:S(2)}, u32[]{:S(2)}) collective-permute-start(bf16[128,1024]{1,0:T(8,128)(2,1)S(1)} %get-tuple-element.22), channel_id=1, source_target_pairs={{2,0},{0,1},{4,2},{6,3},{1,4},{7,5},{3,6},{5,7},{10,8},{8,9},{12,1... | collective-permute-start | bytes 786440 | tf_op jit(solution)/shard_map/ppermute | solution.py:422
  89.8 14.5 %collective-permute-start.9 = (bf16[128,1024]{1,0:T(8,128)(2,1)S(1)}, bf16[128,1024]{1,0:T(8,128)(2,1)S(1)}, u32[]{:S(2)}, u32[]{:S(2)}) collective-permute-start(bf16[128,1024]{1,0:T(8,128)(2,1)S(1)} %get-tuple-element.23), channel_id=1, source_target_pairs={{4,3},{3,4},{1,6},{6,1},{12,11},{11,12},{9,14},{14,9},{20,19},{19,... | collective-permute-start | bytes 786440 | tf_op jit(solution)/shard_map/ppermute | solution.py:423
  98.8 5.8 %copy-start.18 = (bf16[1,128,1024]{2,1,0:T(8,128)(2,1)S(1)}, bf16[1,128,1024]{2,1,0:T(8,128)(2,1)}, u32[]{:S(2)}) copy-start(bf16[1,128,1024]{2,1,0:T(8,128)(2,1)} %param.14) | copy-start | bytes 786436
  98.9 6.8 %collective-permute-start.15 = (f32[1024,128]{1,0:T(8,128)S(1)}, f32[1024,128]{1,0:T(8,128)S(1)}, u32[]{:S(2)}, u32[]{:S(2)}) collective-permute-start(f32[1024,128]{1,0:T(8,128)S(1)} %dynamic-slice_bitcast_fusion), channel_id=1, source_target_pairs={{0,4},{4,0},{8,12},{12,8},{16,20},{20,16},{24,28},{28,24},{1,5},{5... | collective-permute-start | bytes 1572872 | tf_op jit(solution)/shard_map/ppermute | solution.py:349

commit v2 on v0

--- a/solution.py
+++ b/solution.py
@@ -3,6 +3,8 @@
 import jax
 import jax.numpy as jnp
 from jax import lax
+from jax.experimental import pallas as pl
+from jax.experimental.pallas import tpu as pltpu
 from jax.sharding import PartitionSpec as P
 
 HEAD_DIM = 64
@@ -154,7 +156,381 @@
     return (d_inputs[None], grad_qkv * factor, grad_out * factor)
 
 
+FIRST_MOVES = (
+    ((0, 0), (2, 0)),
+    ((1, 0), (0, 0)),
+    ((2, 0), (0, 1)),
+    ((3, 0), (2, 1)),
+    ((0, 1), (1, 0)),
+    ((1, 1), (3, 1)),
+    ((2, 1), (3, 0)),
+    ((3, 1), (1, 1)),
+)
+SECOND_MOVES = (
+    ((0, 1), (3, 0)),
+    ((3, 0), (0, 1)),
+    ((1, 0), (2, 1)),
+    ((2, 1), (1, 0)),
+    ((0, 0), (0, 0)),
+    ((1, 1), (1, 1)),
+    ((2, 0), (2, 0)),
+    ((3, 1), (3, 1)),
+)
+HOME_MOVES = (
+    ((0, 0), (0, 1)),
+    ((1, 1), (1, 0)),
+    ((1, 0), (0, 0)),
+    ((0, 1), (1, 1)),
+    ((2, 0), (2, 1)),
+    ((3, 1), (3, 0)),
+    ((3, 0), (2, 0)),
+    ((2, 1), (3, 1)),
+)
+GUEST_MOVES = (
+    ((1, 0), (0, 1)),
+    ((0, 1), (1, 0)),
+    ((3, 0), (2, 1)),
+    ((2, 1), (3, 0)),
+)
+
+
+def column_pairs(moves, chips, seqs, back=False):
+    pairs = []
+    for chip in range(chips):
+        for source, target in moves:
+            if back:
+                source, target = target, source
+            pairs.append(
+                ((chip * 2 + source[1]) * seqs + source[0], (chip * 2 + target[1]) * seqs + target[0])
+            )
+    return pairs
+
+
+def block_table():
+    table = [[0, 0] for _ in range(8)]
+    for place, moves in enumerate((FIRST_MOVES, SECOND_MOVES)):
+        for (source, _), (target, core) in moves:
+            table[target * 2 + core][place] = source
+    return table
+
+
+def nt(left, right):
+    return lax.dot_general(left, right, (((1,), (1,)), ((), ())), preferred_element_type=jnp.float32)
+
+
+def nn(left, right):
+    return lax.dot_general(left, right, (((1,), (0,)), ((), ())), preferred_element_type=jnp.float32)
+
+
+def tn(left, right):
+    return lax.dot_general(left, right, (((0,), (0,)), ((), ())), preferred_element_type=jnp.float32)
+
+
+def valid_slots(info, capacity, axis, total):
+    shape = (total, 1) if axis == 0 else (1, total)
+    slot = lax.broadcasted_iota(jnp.int32, shape, axis)
+    limit = info[0] + jnp.zeros(shape, jnp.int32)
+    for block in range(1, total // capacity):
+        limit = jnp.where(slot >= block * capacity, block * capacity + info[block], limit)
+    return slot < limit
+
+
+def lift_kernel(info, g0, g1, g2, g3, w_out, lifted, rows, weight, sems):
+    capacity = g0.shape[0]
+    width = lifted.shape[0]
+    total = lifted.shape[1]
+    copies = [
+        pltpu.make_async_copy(
+            w_out.at[:, pl.ds(pl.multiple_of(info[4] * width, width), width)], weight, sems.at[4]
+        )
+    ]
+    for block, source in enumerate((g0, g1, g2, g3)):
+        copies.append(
+            pltpu.make_async_copy(source, rows.at[pl.ds(block * capacity, capacity), :], sems.at[block])
+        )
+    for copy in copies:
+        copy.start()
+    for copy in copies:
+        copy.wait()
+    up = nn(rows[...], weight[...])
+    up = jnp.where(valid_slots(info, capacity, 0, total), up, 0.0)
+    lifted[...] = up.T.astype(lifted.dtype)
+
+
+def main_kernel(
+    info, t0, t1, t2, t3, g0, g1, g2, g3, lifted_in, w_qkv,
+    x_send, x_keep, y_send, y_keep, grads,
+    rows_t, rows_g, weight, lifted, query, key, value, stack,
+    x_send_buf, x_keep_buf, y_send_buf, y_keep_buf, in_sems, out_sems,
+):
+    capacity = t0.shape[0]
+    total = rows_t.shape[0]
+    width = lifted.shape[0]
+    lanes = width // 2
+    low = jnp.bfloat16
+    scale = HEAD_DIM ** (-0.5)
+
+    loads = []
+    for block, source in enumerate((t0, t1, t2, t3)):
+        loads.append(
+            pltpu.make_async_copy(
+                source, rows_t.at[pl.ds(block * capacity, capacity), :], in_sems.at[block]
+            )
+        )
+    group = pl.multiple_of(info[4] * width, width)
+    for part in range(3):
+        loads.append(
+            pltpu.make_async_copy(
+                w_qkv.at[part, pl.ds(group, width), :],
+                weight.at[pl.ds(part * width, width), :],
+                in_sems.at[4 + part],
+            )
+        )
+    loads.append(pltpu.make_async_copy(lifted_in, lifted, in_sems.at[7]))
+    for block, source in enumerate((g0, g1, g2, g3)):
+        loads.append(
+            pltpu.make_async_copy(
+                source, rows_g.at[pl.ds(block * capacity, capacity), :], in_sems.at[8 + block]
+            )
+        )
+    for copy in loads:
+        copy.start()
+    for copy in loads[:5]:
+        copy.wait()
+    query[...] = (nt(weight[0:width, :], rows_t[...]).astype(low) * scale).astype(low)
+    loads[5].wait()
+    key[...] = nt(weight[width : 2 * width, :], rows_t[...]).astype(low)
+    loads[6].wait()
+    value[...] = nt(weight[2 * width : 3 * width, :], rows_t[...]).astype(low)
+    loads[7].wait()
+
+    bias = jnp.where(valid_slots(info, capacity, 0, total), 0.0, MASKED)
+    row_ok = valid_slots(info, capacity, 1, total)
+    for head in range(width // HEAD_DIM):
+        span = pl.ds(head * HEAD_DIM, HEAD_DIM)
+        query_h, key_h, value_h, lifted_h = query[span, :], key[span, :], value[span, :], lifted[span, :]
+        scores = tn(key_h, query_h) + bias
+        expo = jnp.exp(scores - jnp.max(scores, axis=0, keepdims=True))
+        probs = expo * (1.0 / jnp.sum(expo, axis=0, keepdims=True))
+        probs_low = probs.astype(low)
+        attended = nn(value_h, probs_low)
+        delta = jnp.sum(lifted_h.astype(jnp.float32) * attended, axis=0, keepdims=True)
+        score_grad = (probs * (tn(value_h, lifted_h) - delta)).astype(low)
+        stack[pl.ds(head * HEAD_DIM, HEAD_DIM), :] = (nn(key_h, score_grad) * scale).astype(low)
+        stack[pl.ds(width + head * HEAD_DIM, HEAD_DIM), :] = nt(query_h, score_grad).astype(low)
+        stack[pl.ds(2 * width + head * HEAD_DIM, HEAD_DIM), :] = nt(lifted_h, probs_low).astype(low)
+        stack[pl.ds(3 * width + head * HEAD_DIM, HEAD_DIM), :] = jnp.where(
+            row_ok, attended, 0.0
+        ).astype(low)
+
+    stores = [
+        pltpu.make_async_copy(stack.at[pl.ds(0, 3 * width), :], grads, out_sems.at[0]),
+        pltpu.make_async_copy(x_send_buf, x_send, out_sems.at[1]),
+        pltpu.make_async_copy(y_send_buf, y_send, out_sems.at[2]),
+        pltpu.make_async_copy(x_keep_buf, x_keep, out_sems.at[3]),
+        pltpu.make_async_copy(y_keep_buf, y_keep, out_sems.at[4]),
+    ]
+    stores[0].start()
+    for copy in loads[8:]:
+        copy.wait()
+    for slot_y, slot_x in ((1, 1), (0, 1), (1, 0), (0, 0)):
+        block = (info[5] ^ slot_y) * 2 + (info[6] ^ slot_x)
+        cols = pl.ds(pl.multiple_of(block * width, width), width)
+        term_t = nn(stack[0 : 3 * width, :], rows_t[:, cols])
+        term_g = nn(stack[3 * width : 4 * width, :], rows_g[:, cols])
+        x_target = x_send_buf if slot_x else x_keep_buf
+        y_target = y_send_buf if slot_y else y_keep_buf
+        for side in range(2):
+            across = slice(side * lanes, (side + 1) * lanes)
+            spot = info[7] ^ side
+            x_target[slot_y, spot, :, :] = term_t[0 : 2 * width, across].astype(x_target.dtype)
+            y_target[slot_x, spot, 0:width, :] = term_t[2 * width : 3 * width, across].astype(y_target.dtype)
+            y_target[slot_x, spot, width : 2 * width, :] = term_g[:, across].astype(y_target.dtype)
+        if (slot_y, slot_x) == (0, 1):
+            stores[1].start()
+        if (slot_y, slot_x) == (1, 0):
+            stores[2].start()
+    stores[3].start()
+    stores[4].start()
+    for copy in stores:
+        copy.wait()
+
+
+def normed_kernel(info, grads_in, w_qkv, keep, send, grads, weight, sems):
+    features = w_qkv.shape[2]
+    total = grads.shape[1]
+    width = grads.shape[0] // 3
+    group = pl.multiple_of(info[4] * width, width)
+    loads = [pltpu.make_async_copy(grads_in, grads, sems.at[3])]
+    for part in range(3):
+        loads.append(
+            pltpu.make_async_copy(
+                w_qkv.at[part, pl.ds(group, width), :],
+                weight.at[pl.ds(part * width, width), :],
+                sems.at[part],
+            )
+        )
+    for copy in loads:
+        copy.start()
+    for copy in loads:
+        copy.wait()
+    send[...] = tn(grads[:, total // 2 : total], weight[...]).astype(send.dtype)
+    keep[...] = tn(grads[:, 0 : total // 2], weight[...])
+
+
+def specs(space, count):
+    return [pl.BlockSpec(memory_space=space)] * count
+
+
+VMEM_BYTES = 56 * 1024 * 1024
+
+
+def column_shards(tokens, positions, counts, ln_gain, w_qkv, w_out, d_out):
+    low, wide = jnp.bfloat16, jnp.float32
+    inputs = tokens[0]
+    upstream = d_out[0]
+    capacity, features = inputs.shape
+    seqs = lax.axis_size("seq")
+    chips = lax.axis_size("dp") // 2
+    seat = lax.axis_index("seq")
+    dp = lax.axis_index("dp")
+    core, place_x, place_y = dp & 1, (dp >> 1) & 1, dp >> 2
+    total = seqs * capacity
+    half = total // 2
+    width = features // seqs
+    lanes = width // 2
+    factor = 1.0 / math.sqrt(lax.axis_size("dp") * (3 * total // 4))
+    guest = core ^ (seat & 1)
+    resident = guest == 0
+
+    axes = ("dp", "seq")
+    first = column_pairs(FIRST_MOVES, chips, seqs)
+    second = column_pairs(SECOND_MOVES, chips, seqs)
+    first_back = column_pairs(FIRST_MOVES, chips, seqs, True)
+    home = column_pairs(HOME_MOVES, chips, seqs)
+    guests = column_pairs(GUEST_MOVES, chips, seqs)
+
+    def across(array, bit):
+        return lax.ppermute(array, "dp", [(i, i ^ bit) for i in range(2 * chips)])
+
+    def share(array):
+        one = lax.ppermute(array, axes, first)
+        two = lax.ppermute(array, axes, second)
+        return one, two, across(one, 1), across(two, 1)
+
+    blocks_g = share(upstream)
+    other_counts = across(counts[0], 1)
+    normed, standard, inv_std = layer_norm(inputs, positions[0], ln_gain)
+    blocks_t = share(normed)
+
+    sizes = jnp.where(resident, counts[0], other_counts)
+    table = jnp.array(block_table(), jnp.int32)
+    order = jnp.concatenate([table[seat * 2 + core], table[seat * 2 + 1 - core]])
+    group = (seat >> 1) * 2 + core
+    info = jnp.concatenate(
+        [sizes[order], jnp.stack([group, place_y, place_x, core ^ 1 ^ guest]).astype(jnp.int32)]
+    )
+
+    params = pltpu.CompilerParams(vmem_limit_bytes=VMEM_BYTES)
+    smem = specs(pltpu.SMEM, 1)
+    lifted = pl.pallas_call(
+        lift_kernel,
+        out_shape=jax.ShapeDtypeStruct((width, total), low),
+        in_specs=smem + specs(pltpu.HBM, 5),
+        out_specs=pl.BlockSpec(memory_space=pltpu.VMEM),
+        scratch_shapes=[
+            pltpu.VMEM((total, features), low),
+            pltpu.VMEM((features, width), low),
+            pltpu.SemaphoreType.DMA((5,)),
+        ],
+        compiler_params=params,
+        cost_estimate=pl.CostEstimate(
+            flops=2 * total * features * width, bytes_accessed=2 * 1024 * 1024, transcendentals=0
+        ),
+    )(info, *blocks_g, w_out)
+
+    send_shape = jax.ShapeDtypeStruct((2, 2, 2 * width, lanes), low)
+    keep_shape = jax.ShapeDtypeStruct((2, 2, 2 * width, lanes), wide)
+    x_send, x_keep, y_send, y_keep, grads = pl.pallas_call(
+        main_kernel,
+        out_shape=(
+            send_shape, keep_shape, send_shape, keep_shape, jax.ShapeDtypeStruct((3 * width, total), low)
+        ),
+        in_specs=smem + specs(pltpu.HBM, 10),
+        out_specs=specs(pltpu.HBM, 5),
+        scratch_shapes=[
+            pltpu.VMEM((total, features), low),
+            pltpu.VMEM((total, features), low),
+            pltpu.VMEM((3 * width, features), low),
+            pltpu.VMEM((width, total), low),
+            pltpu.VMEM((width, total), low),
+            pltpu.VMEM((width, total), low),
+            pltpu.VMEM((width, total), low),
+            pltpu.VMEM((4 * width, total), low),
+            pltpu.VMEM(send_shape.shape, low),
+            pltpu.VMEM(send_shape.shape, wide),
+            pltpu.VMEM(send_shape.shape, low),
+            pltpu.VMEM(send_shape.shape, wide),
+            pltpu.SemaphoreType.DMA((12,)),
+            pltpu.SemaphoreType.DMA((5,)),
+        ],
+        compiler_params=params,
+        cost_estimate=pl.CostEstimate(
+            flops=2 * total * features * width * 7 + 12 * 4 * total * total * HEAD_DIM,
+            bytes_accessed=8 * 1024 * 1024,
+            transcendentals=4 * total * total,
+        ),
+    )(info, *blocks_t, *blocks_g, lifted, w_qkv)
+
+    normed_keep, normed_send = pl.pallas_call(
+        normed_kernel,
+        out_shape=(
+            jax.ShapeDtypeStruct((half, features), wide),
+            jax.ShapeDtypeStruct((half, features), low),
+        ),
+        in_specs=smem + specs(pltpu.HBM, 2),
+        out_specs=specs(pltpu.VMEM, 2),
+        scratch_shapes=[
+            pltpu.VMEM((3 * width, total), low),
+            pltpu.VMEM((3 * width, features), low),
+            pltpu.SemaphoreType.DMA((4,)),
+        ],
+        compiler_params=params,
+        cost_estimate=pl.CostEstimate(
+            flops=2 * total * features * width * 3, bytes_accessed=4 * 1024 * 1024, transcendentals=0
+        ),
+    )(info, grads, w_qkv)
+
+    x_first, y_first = across(x_send, 2), across(y_send, 4)
+    shared = across(normed_send, 1)
+    back_one = (normed_keep[:capacity] + shared[:capacity].astype(wide)).astype(low)
+    back_two = (normed_keep[capacity:] + shared[capacity:].astype(wide)).astype(low)
+    normed_grad = lax.ppermute(back_one, axes, first_back).astype(wide)
+    normed_grad = normed_grad + lax.ppermute(back_two, axes, second).astype(wide)
+
+    x_second = across((x_keep[1] + x_first[1].astype(wide)).astype(low), 4)
+    y_second = across((y_keep[1] + y_first[1].astype(wide)).astype(low), 2)
+    x_part = x_keep[0] + x_first[0].astype(wide) + x_second.astype(wide)
+    y_part = y_keep[0] + y_first[0].astype(wide) + y_second.astype(wide)
+    sums = jnp.concatenate([x_part, y_part], axis=1)
+    from_home = lax.ppermute(sums[0].astype(low), axes, home)
+    from_guest = lax.ppermute(sums[1].astype(low), axes, guests)
+    final = from_home.astype(wide) + jnp.where(resident, sums[1], from_guest.astype(wide))
+    final = final * factor
+    grad_qkv = final[: 3 * width].reshape(3, width, lanes)
+    grad_out = final[3 * width :].T
+
+    own_valid = jnp.arange(capacity, dtype=jnp.int32) < lax.dynamic_index_in_dim(counts[0], seat, 0, False)
+    masked_grad = jnp.where(own_valid[:, None], upstream, jnp.zeros_like(upstream))
+    unit_grad = normed_grad * ln_gain
+    inner = unit_grad - jnp.mean(unit_grad, axis=1, keepdims=True)
+    inner = inner - standard * jnp.mean(unit_grad * standard, axis=1, keepdims=True)
+    d_inputs = (masked_grad.astype(wide) + inv_std * inner).astype(low)
+    return (d_inputs[None], grad_qkv, grad_out)
+
+
 def solution(mesh):
+    fits = mesh.shape["dp"] == 8 and mesh.shape["seq"] == 4
     placed = (
         P("dp", "seq", None),
         P("dp", "seq"),
@@ -165,7 +541,7 @@
         P("dp", "seq", None),
     )
     return jax.shard_map(
-        shards,
+        column_shards if fits else shards,
         mesh=mesh,
         in_specs=placed,
         out_specs=(P("dp", "seq", None), P(None, "seq", "dp"), P("dp", "seq")),

time: 176 us -> 86.7 us (0.49)
  waiting for transfers between devices: 93.9 us -> 22.5 us
  matrix products: 29.4 us -> 0 us
  Pallas kernels: 0 us -> 18.6 us
  starting transfers between devices: 12.3 us -> 25.6 us
  between operations: 14 us -> 0.96 us
  other arithmetic: 18.8 us -> 11.5 us
    all_gather x2 -> x0, waiting for transfers between devices: 45.4 us -> none  [the longest x1 27.3 us: shards(): lax.all_gather(normed, 'seq', axis=0, tiled=True)]
    reduce_scatter x2 -> x0, waiting for transfers between devices: 37.9 us -> none  [the longest x1 37.9 us: shards(): lax.psum_scatter(term_qkv, 'dp', scatter_dimension=2, tiled=True)]
    dot_general x16 -> x0, matrix products: 25.8 us -> none  [the longest x3 5.33 us: project(): jnp.einsum('td,od->to', normed, weight, preferred_element_type=jnp.float32)]
    ppermute x0 -> x18, starting transfers between devices: none -> 25.6 us  [the longest x2 7.35 us: share(): two = lax.ppermute(array, axes, second)]
    ppermute x0 -> x18, waiting for transfers between devices: none -> 22.5 us  [the longest x2 7.46 us: share(): one = lax.ppermute(array, axes, first)]
    pallas_call x0 -> x3, Pallas kernels: none -> 18.6 us  [the longest x1 10.9 us: column_shards(): pl.pallas_call(main_kernel, out_shape=(send_shape, keep_shape, send_shape...]
    all_to_all x3 -> x0, starting transfers between devices: 12.1 us -> none  [the longest x1 4.05 us: shards(): lax.all_to_all(value_grad, 'seq', split_axis=0, concat_axis=1, tiled=True)]
    all_to_all x3 -> x0, waiting for transfers between devices: 10.5 us -> none  [the longest x1 5.03 us: shards(): lax.all_to_all(value_grad, 'seq', split_axis=0, concat_axis=1, tiled=True)]
  transfers between devices with their start and end apart: 7 -> 18, of which waited for: 6 -> 8; matrix products, arithmetic and copies ran while one was open for 21% -> 16% of each run, Pallas kernels for 0% -> 9%
where the time goes in v2:
time: 86.7 us; the launch traced here: 86.2 us
  starting transfers between devices  25.6 us (30%)
  waiting for transfers between devices  22.5 us (26%)
  Pallas kernels  18.6 us (21%)
  other arithmetic  11.5 us (13%)
  local copies, waits for them, and re-layouts  7.06 us (8%)
  between operations  0.96 us (1%)
    pallas_call x1, Pallas kernels, column_shards(): pl.pallas_call(main_kernel, out_shape=(send_shape, keep_shape, send_shape...  10.9 us
    ppermute x2, waiting for transfers between devices, share(): one = lax.ppermute(array, axes, first)  7.46 us
    ppermute x2, starting transfers between devices, share(): two = lax.ppermute(array, axes, second)  7.35 us
    ppermute x10, starting transfers between devices, across(): return lax.ppermute(array, 'dp', [(i, i ^ bit) for i in range(2 * chips)])  6.77 us
    ppermute x1, starting transfers between devices, column_shards(): normed_grad = lax.ppermute(back_one, axes, first_back).astype(wide)  4.59 us
    pallas_call x1, Pallas kernels, column_shards(): pl.pallas_call(normed_kernel, out_shape=(jax.ShapeDtypeStruct((half, feat...  4.43 us
    ppermute x10, waiting for transfers between devices, across(): return lax.ppermute(array, 'dp', [(i, i ^ bit) for i in range(2 * chips)])  4.18 us
    ppermute x1, waiting for transfers between devices, column_shards(): lax.ppermute(back_two, axes, second).astype(wide)  4.08 us
  transfers between devices with their start and end apart: 18, of which 8 were waited for; matrix products, arithmetic and copies ran while one was open for 16% of the time, Pallas kernels for 9%

profile of v2, /device:TPU:1, one launch (start us, length us, event | category | flops | bytes accessed | tf_op | source)
XLA Modules:
  0.0 86.2 jit_solution(296820095026382753)
XLA Ops:
  0.6 2.7 %collective-permute-start.5 = (bf16[128,1024]{1,0:T(8,128)(2,1)}, bf16[128,1024]{1,0:T(8,128)(2,1)S(1)}, u32[]{:S(2)}, u32[]{:S(2)}) collective-permute-start(bf16[128,1024]{1,0:T(8,128)(2,1)} %bitcast.52), channel_id=1, source_target_pairs={{0,2},{1,0},{2,4},{3,6},{4,1},{5,7},{6,3},{7,5},{8,10},{9,8},{10,1... | collective-permute-start | bytes 786440 | tf_op jit(solution)/shard_map/ppermute | solution.py:417
  3.4 3.9 %collective-permute-start.6 = (bf16[128,1024]{1,0:T(8,128)(2,1)}, bf16[128,1024]{1,0:T(8,128)(2,1)S(1)}, u32[]{:S(2)}, u32[]{:S(2)}) collective-permute-start(bf16[128,1024]{1,0:T(8,128)(2,1)} %bitcast.53), channel_id=1, source_target_pairs={{4,3},{3,4},{1,6},{6,1},{0,0},{5,5},{2,2},{7,7},{12,11},{11,12},{9... | collective-permute-start | bytes 786440 | tf_op jit(solution)/shard_map/ppermute | solution.py:418
  7.3 0.7 convert_bitcast_fusion
  8.0 1.0 %multiply_sine_fusion = (f32[128,512]{1,0:T(8,128)S(1)}, f32[128,512]{1,0:T(8,128)S(1)}) fusion(f32[512]{0:T(512)S(1)} %multiply_exponential_fusion, f32[128]{0:T(128)S(1)} %convert_bitcast_fusion), kind=kLoop, calls=%fused_computation.23 | loop fusion | flops 65536 | bytes 526848 | tf_op jit(solution)/shard_map/sin | solution.py:21
  9.0 1.1 %fusion.12 = f32[128]{0:T(128)S(1)} fusion(f32[128,512]{1,0:T(8,128)S(1)} %get-tuple-element.32, f32[128,512]{1,0:T(8,128)S(1)} %get-tuple-element.31, bf16[1,128,1024]{2,1,0:T(8,128)(2,1)} %param.8), kind=kLoop, calls=%fused_computation.46 | loop fusion | flops 524160 | bytes 786944 | tf_op jit(solution)/shard_map/reduce_sum | solution.py:26
  10.1 1.2 %multiply_reduce_fusion.1 = f32[128]{0:T(128)S(1)} fusion(f32[128]{0:T(128)S(1)} %broadcast_multiply_fusion.2, f32[128,512]{1,0:T(8,128)S(1)} %get-tuple-element.32, f32[128,512]{1,0:T(8,128)S(1)} %get-tuple-element.31, bf16[1,128,1024]{2,1,0:T(8,128)(2,1)} %param.8), kind=kLoop, calls=%fused_computation.19 | loop fusion | flops 786304 | bytes 787456 | tf_op jit(solution)/shard_map/reduce_sum | solution.py:27
  11.3 1.1 %multiply_convert_fusion = bf16[128,1024]{1,0:T(8,128)(2,1)S(1)} fusion(f32[1024]{0:T(1024)} %param.11, f32[128]{0:T(128)S(1)} %add_rsqrt_fusion, f32[128]{0:T(128)S(1)} %broadcast_multiply_fusion.2, f32[128,512]{1,0:T(8,128)S(1)} %get-tuple-element.32, f32[128,512]{1,0:T(8,128)S(1)} %get-tuple-element.31, bf16[1,128,1024]{2,1,0:T(8,128)(2,1)} %param.8), kind=kLoop, calls=%fused_computation.18 | loop fusion | flops 917504 | bytes 1053696 | tf_op jit(solution)/shard_map/convert_element_type | solution.py:29
  12.4 3.4 %collective-permute-start.2 = (bf16[128,1024]{1,0:T(8,128)(2,1)S(1)}, bf16[128,1024]{1,0:T(8,128)(2,1)S(1)}, u32[]{:S(2)}, u32[]{:S(2)}) collective-permute-start(bf16[128,1024]{1,0:T(8,128)(2,1)S(1)} %multiply_convert_fusion), channel_id=1, source_target_pairs={{4,3},{3,4},{1,6},{6,1},{0,0},{5,5},{2,2},{7,7},{12,11},{11,12},{9... | collective-permute-start | bytes 786440 | tf_op jit(solution)/shard_map/ppermute | solution.py:418
  16.0 0.8 fusion.9
  16.7 0.1 fusion.11
  16.8 1.8 %collective-permute-done.5.g0 = bf16[128,1024]{1,0:T(8,128)(2,1)S(1)} collective-permute-done((bf16[128,1024]{1,0:T(8,128)(2,1)}, bf16[128,1024]{1,0:T(8,128)(2,1)S(1)}, u32[]{:S(2)}, u32[]{:S(2)}) %collective-permute-start.5) | collective-permute-done | bytes 262176 | tf_op jit(solution)/shard_map/ppermute | solution.py:417
  18.7 0.5 collective-permute-start.8
  19.2 2.9 %collective-permute-done.2.t1 = bf16[128,1024]{1,0:T(8,128)(2,1)S(1)} collective-permute-done((bf16[128,1024]{1,0:T(8,128)(2,1)S(1)}, bf16[128,1024]{1,0:T(8,128)(2,1)S(1)}, u32[]{:S(2)}, u32[]{:S(2)}) %collective-permute-start.2) | collective-permute-done | bytes 262176 | tf_op jit(solution)/shard_map/ppermute | solution.py:418
  22.0 5.6 %collective-permute-done.1.t0 = bf16[128,1024]{1,0:T(8,128)(2,1)S(1)} collective-permute-done((bf16[128,1024]{1,0:T(8,128)(2,1)S(1)}, bf16[128,1024]{1,0:T(8,128)(2,1)S(1)}, u32[]{:S(2)}, u32[]{:S(2)}) %collective-permute-start.1) | collective-permute-done | bytes 262176 | tf_op jit(solution)/shard_map/ppermute | solution.py:417
  27.7 0.7 broadcast_select_fusion
  28.4 0.6 gather_fusion
  29.0 0.7 concatenate.39.info
  29.7 0.7 copy-done.6
  30.4 0.7 copy-done.7
  31.2 3.3 %shard_map.103.lifted_in = bf16[256,512]{1,0:T(8,128)(2,1)} custom-call(s32[8]{0:T(128)} %concatenate.39.info, bf16[128,1024]{1,0:T(8,128)(2,1)} %copy-done.4, bf16[128,1024]{1,0:T(8,128)(2,1)} %copy-done.5, bf16[128,1024]{1,0:T(8,128)(2,1)} %copy-done.6, bf16[128,1024]{1,0:T(8,128)(2,1)} %copy-done.7, bf16[1024,1024]{1,0:T(8,128)(2,1)} %w_out.1), custom_call_target="tpu_custom_call" | custom-call | flops 268435456 | bytes 2097152 | tf_op jit(solution)/shard_map/pallas_call | solution.py:436
  34.5 0.7 copy-done.12
  35.2 0.7 copy-done.13
  35.9 10.9 %shard_map.104 = (bf16[2,2,512,128]{3,2,1,0:T(8,128)(2,1)}, f32[2,2,512,128]{3,2,1,0:T(8,128)}, bf16[2,2,512,128]{3,2,1,0:T(8,128)(2,1)}, f32[2,2,512,128]{3,2,1,0:T(8,128)}, bf16[768,512]{1,0:T(8,128)(2,1)}) custom-call(s32[8]{0:T(128)} %concatenate.39.info, bf16[128,1024]{1,0:T(8,128)(2,1)} %copy-done.11, bf16[128,1024]{1,0:T(8,128)(2,1)} %copy-done.10, ...), custom_call_target="tpu_custom_call" | custom-call | flops 2684354560 | bytes 8388608 | tf_op jit(solution)/shard_map/pallas_call | solution.py:454
  46.8 1.3 %collective-permute-start.12 = (bf16[2,2,512,128]{3,2,1,0:T(8,128)(2,1)}, bf16[2,2,512,128]{3,2,1,0:T(8,128)(2,1)}, u32[]{:S(2)}, u32[]{:S(2)}) collective-permute-start(bf16[2,2,512,128]{3,2,1,0:T(8,128)(2,1)} %get-tuple-element.14), channel_id=1, source_target_pairs={{0,8},{4,12},{8,0},{12,4},{16,24},{20,28},{24,16},{28,20},{1,9},{5... | collective-permute-start | bytes 1572872 | tf_op jit(solution)/shard_map/ppermute | solution.py:414
  48.1 1.2 %collective-permute-start.14 = (bf16[2,2,512,128]{3,2,1,0:T(8,128)(2,1)}, bf16[2,2,512,128]{3,2,1,0:T(8,128)(2,1)S(1)}, u32[]{:S(2)}, u32[]{:S(2)}) collective-permute-start(bf16[2,2,512,128]{3,2,1,0:T(8,128)(2,1)} %get-tuple-element.16), channel_id=1, source_target_pairs={{0,16},{4,20},{8,24},{12,28},{16,0},{20,4},{24,8},{28,12},{1,17},{... | collective-permute-start | bytes 1572872 | tf_op jit(solution)/shard_map/ppermute | solution.py:414
  49.3 0.6 constant_dynamic-slice_fusion.2
  49.9 4.4 %shard_map.105 = (f32[256,1024]{1,0:T(8,128)}, bf16[256,1024]{1,0:T(8,128)(2,1)}) custom-call(s32[8]{0:T(128)} %concatenate.39.info, bf16[768,512]{1,0:T(8,128)(2,1)} %get-tuple-element.10.grads_in, bf16[3,1024,1024]{2,1,0:T(8,128)(2,1)} %w_qkv.3), custom_call_target="tpu_custom_call" | custom-call | flops 805306368 | bytes 4194304 | tf_op jit(solution)/shard_map/pallas_call | solution.py:485
  54.4 1.1 %collective-permute-start.9 = (bf16[256,1024]{1,0:T(8,128)(2,1)}, bf16[256,1024]{1,0:T(8,128)(2,1)S(1)}, u32[]{:S(2)}, u32[]{:S(2)}) collective-permute-start(bf16[256,1024]{1,0:T(8,128)(2,1)} %get-tuple-element.12), channel_id=1, source_target_pairs={{0,4},{4,0},{8,12},{12,8},{16,20},{20,16},{24,28},{28,24},{1,5},{5... | collective-permute-start | bytes 1572872 | tf_op jit(solution)/shard_map/ppermute | solution.py:414
  55.4 0.6 iota_compare_fusion
  56.1 4.2 %collective-permute-done.12 = bf16[2,2,512,128]{3,2,1,0:T(8,128)(2,1)} collective-permute-done((bf16[2,2,512,128]{3,2,1,0:T(8,128)(2,1)}, bf16[2,2,512,128]{3,2,1,0:T(8,128)(2,1)}, u32[]{:S(2)}, u32[]{:S(2)}) %collective-permute-start.12) | collective-permute-done | bytes 524320 | tf_op jit(solution)/shard_map/ppermute | solution.py:414
  60.3 1.0 %fusion.4 = bf16[2,512,128]{2,1,0:T(8,128)(2,1)S(1)} fusion(f32[2,2,512,128]{3,2,1,0:T(8,128)S(1)} %copy-done.2, bf16[2,2,512,128]{3,2,1,0:T(8,128)(2,1)} %collective-permute-done.12), kind=kLoop, calls=%fused_computation.24 | loop fusion | flops 393216 | bytes 1048576 | tf_op jit(solution)/shard_map/convert_element_type | solution.py:511
  61.3 1.3 %collective-permute-start.13 = (bf16[2,512,128]{2,1,0:T(8,128)(2,1)S(1)}, bf16[2,512,128]{2,1,0:T(8,128)(2,1)S(1)}, u32[]{:S(2)}, u32[]{:S(2)}) collective-permute-start(bf16[2,512,128]{2,1,0:T(8,128)(2,1)S(1)} %fusion.4), channel_id=1, source_target_pairs={{0,16},{4,20},{8,24},{12,28},{16,0},{20,4},{24,8},{28,12},{1,17},{... | collective-permute-start | bytes 786440 | tf_op jit(solution)/shard_map/ppermute | solution.py:414
  62.6 1.3 %collective-permute-start.15 = (bf16[2,512,128]{2,1,0:T(8,128)(2,1)S(1)}, bf16[2,512,128]{2,1,0:T(8,128)(2,1)S(1)}, u32[]{:S(2)}, u32[]{:S(2)}) collective-permute-start(bf16[2,512,128]{2,1,0:T(8,128)(2,1)S(1)} %fusion.5), channel_id=1, source_target_pairs={{0,8},{4,12},{8,0},{12,4},{16,24},{20,28},{24,16},{28,20},{1,9},{5... | collective-permute-start | bytes 786440 | tf_op jit(solution)/shard_map/ppermute | solution.py:414
  63.9 1.3 %add_convert_fusion.4 = (bf16[128,1024]{1,0:T(8,128)(2,1)S(1)}, bf16[128,1024]{1,0:T(8,128)(2,1)S(1)}) fusion(f32[256,1024]{1,0:T(8,128)} %get-tuple-element.11, bf16[256,1024]{1,0:T(8,128)(2,1)S(1)} %collective-permute-done.9), kind=kLoop, calls=%fused_computation.17 | loop fusion | flops 786432 | bytes 2097152 | tf_op jit(solution)/shard_map/convert_element_type | solution.py:506
  65.3 4.6 %collective-permute-start.10 = (bf16[128,1024]{1,0:T(8,128)(2,1)S(1)}, bf16[128,1024]{1,0:T(8,128)(2,1)S(1)}, u32[]{:S(2)}, u32[]{:S(2)}) collective-permute-start(bf16[128,1024]{1,0:T(8,128)(2,1)S(1)} %get-tuple-element.25), channel_id=1, source_target_pairs={{2,0},{0,1},{4,2},{6,3},{1,4},{7,5},{3,6},{5,7},{10,8},{8,9},{12,1... | collective-permute-start | bytes 786440 | tf_op jit(solution)/shard_map/ppermute | solution.py:508
  69.9 2.0 %collective-permute-start.11 = (bf16[128,1024]{1,0:T(8,128)(2,1)S(1)}, bf16[128,1024]{1,0:T(8,128)(2,1)S(1)}, u32[]{:S(2)}, u32[]{:S(2)}) collective-permute-start(bf16[128,1024]{1,0:T(8,128)(2,1)S(1)} %get-tuple-element.26), channel_id=1, source_target_pairs={{4,3},{3,4},{1,6},{6,1},{0,0},{5,5},{2,2},{7,7},{12,11},{11,12},{9... | collective-permute-start | bytes 786440 | tf_op jit(solution)/shard_map/ppermute | solution.py:509
  71.9 1.0 %bitcast_add_fusion.1 = f32[2,512,128]{2,1,0:T(8,128)S(1)} fusion(bf16[2,512,128]{2,1,0:T(8,128)(2,1)S(1)} %collective-permute-done.13, f32[2,2,512,128]{3,2,1,0:T(8,128)S(1)} %copy-done.2, bf16[2,2,512,128]{3,2,1,0:T(8,128)(2,1)} %collective-permute-done.12), kind=kLoop, calls=%fused_computation.9 | loop fusion | flops 524288 | bytes 1572864 | tf_op jit(solution)/shard_map/add | solution.py:513
  73.0 0.1 bitcast_add_fusion
  73.2 1.9 %collective-permute-start.17 = (bf16[1024,128]{1,0:T(8,128)(2,1)S(1)}, bf16[1024,128]{1,0:T(8,128)(2,1)S(1)}, u32[]{:S(2)}, u32[]{:S(2)}) collective-permute-start(bf16[1024,128]{1,0:T(8,128)(2,1)S(1)} %get-tuple-element.28), channel_id=1, source_target_pairs={{1,4},{4,1},{3,6},{6,3},{9,12},{12,9},{11,14},{14,11},{17,20},{20,... | collective-permute-start | bytes 786440 | tf_op jit(solution)/shard_map/ppermute | solution.py:517
  75.2 0.2 collective-permute-done.10
  75.4 4.1 %collective-permute-done.11 = bf16[128,1024]{1,0:T(8,128)(2,1)S(1)} collective-permute-done((bf16[128,1024]{1,0:T(8,128)(2,1)S(1)}, bf16[128,1024]{1,0:T(8,128)(2,1)S(1)}, u32[]{:S(2)}, u32[]{:S(2)}) %collective-permute-start.11) | collective-permute-done | bytes 262176 | tf_op jit(solution)/shard_map/ppermute | solution.py:509
  79.5 0.3 fusion.3
  79.8 1.0 %fusion.7 = bf16[1,128,1024]{2,1,0:T(8,128)(2,1)} fusion(f32[128]{0:T(128)S(1)} %get-tuple-element.33, f32[128]{0:T(128)S(1)} %broadcast_multiply_fusion.2, f32[128]{0:T(128)S(1)} %get-tuple-element.34, f32[1024]{0:T(1024)S(1)} %copy-done.8, bf16[128,1024]{1,0:T(8,128)(2,1)S(1)} %collective-permute-done.11, ...), kind=kLoop, calls=%fused_computation.27 | loop fusion | flops 2228224 | bytes 1841280 | tf_op jit(solution)/shard_map/broadcast_in_dim | solution.py:529
  80.8 0.2 collective-permute-done.16
  81.1 3.4 %collective-permute-done.17 = bf16[1024,128]{1,0:T(8,128)(2,1)S(1)} collective-permute-done((bf16[1024,128]{1,0:T(8,128)(2,1)S(1)}, bf16[1024,128]{1,0:T(8,128)(2,1)S(1)}, u32[]{:S(2)}, u32[]{:S(2)}) %collective-permute-start.17) | collective-permute-done | bytes 262176 | tf_op jit(solution)/shard_map/ppermute | solution.py:517
  84.5 0.1 add_multiply_fusion
  84.6 0.8 slice.76
  85.4 0.8 copy.12
  (48 shorter events, 0.5 us)
Async XLA Ops:
  0.6 18.0 %collective-permute-start.5 = (bf16[128,1024]{1,0:T(8,128)(2,1)}, bf16[128,1024]{1,0:T(8,128)(2,1)S(1)}, u32[]{:S(2)}, u32[]{:S(2)}) collective-permute-start(bf16[128,1024]{1,0:T(8,128)(2,1)} %bitcast.52), channel_id=1, source_target_pairs={{0,2},{1,0},{2,4},{3,6},{4,1},{5,7},{6,3},{7,5},{8,10},{9,8},{10,1... | collective-permute-start | bytes 786440 | tf_op jit(solution)/shard_map/ppermute | solution.py:417
  3.4 15.3 %collective-permute-start.6 = (bf16[128,1024]{1,0:T(8,128)(2,1)}, bf16[128,1024]{1,0:T(8,128)(2,1)S(1)}, u32[]{:S(2)}, u32[]{:S(2)}) collective-permute-start(bf16[128,1024]{1,0:T(8,128)(2,1)} %bitcast.53), channel_id=1, source_target_pairs={{4,3},{3,4},{1,6},{6,1},{0,0},{5,5},{2,2},{7,7},{12,11},{11,12},{9... | collective-permute-start | bytes 786440 | tf_op jit(solution)/shard_map/ppermute | solution.py:418
  12.4 9.6 %collective-permute-start.2 = (bf16[128,1024]{1,0:T(8,128)(2,1)S(1)}, bf16[128,1024]{1,0:T(8,128)(2,1)S(1)}, u32[]{:S(2)}, u32[]{:S(2)}) collective-permute-start(bf16[128,1024]{1,0:T(8,128)(2,1)S(1)} %multiply_convert_fusion), channel_id=1, source_target_pairs={{4,3},{3,4},{1,6},{6,1},{0,0},{5,5},{2,2},{7,7},{12,11},{11,12},{9... | collective-permute-start | bytes 786440 | tf_op jit(solution)/shard_map/ppermute | solution.py:418
  15.8 11.9 %collective-permute-start.1 = (bf16[128,1024]{1,0:T(8,128)(2,1)S(1)}, bf16[128,1024]{1,0:T(8,128)(2,1)S(1)}, u32[]{:S(2)}, u32[]{:S(2)}) collective-permute-start(bf16[128,1024]{1,0:T(8,128)(2,1)S(1)} %multiply_convert_fusion), channel_id=1, source_target_pairs={{0,2},{1,0},{2,4},{3,6},{4,1},{5,7},{6,3},{7,5},{8,10},{9,8},{10,1... | collective-permute-start | bytes 786440 | tf_op jit(solution)/shard_map/ppermute | solution.py:417
  15.9 11.8 %collective-permute-start = (s32[4]{0:T(128)}, s32[4]{0:T(128)S(1)}, u32[]{:S(2)}, u32[]{:S(2)}) collective-permute-start(s32[4]{0:T(128)} %bitcast.54), channel_id=1, source_target_pairs={{0,4},{4,0},{8,12},{12,8},{16,20},{20,16},{24,28},{28,24},{1,5},{5... | collective-permute-start | bytes 56 | tf_op jit(solution)/shard_map/ppermute | solution.py:414
  18.7 11.1 %copy-start.4 = (bf16[128,1024]{1,0:T(8,128)(2,1)}, bf16[128,1024]{1,0:T(8,128)(2,1)S(1)}, u32[]{:S(2)}) copy-start(bf16[128,1024]{1,0:T(8,128)(2,1)S(1)} %collective-permute-done.5.g0) | copy-start | bytes 786436
  18.7 11.1 %collective-permute-start.7 = (bf16[128,1024]{1,0:T(8,128)(2,1)S(1)}, bf16[128,1024]{1,0:T(8,128)(2,1)S(1)}, u32[]{:S(2)}, u32[]{:S(2)}) collective-permute-start(bf16[128,1024]{1,0:T(8,128)(2,1)S(1)} %collective-permute-done.5.g0), channel_id=1, source_target_pairs={{0,4},{4,0},{8,12},{12,8},{16,20},{20,16},{24,28},{28,24},{1,5},{5... | collective-permute-start | bytes 786440 | tf_op jit(solution)/shard_map/ppermute | solution.py:414
  18.7 11.1 %copy-start.5 = (bf16[128,1024]{1,0:T(8,128)(2,1)}, bf16[128,1024]{1,0:T(8,128)(2,1)S(1)}, u32[]{:S(2)}) copy-start(bf16[128,1024]{1,0:T(8,128)(2,1)S(1)} %collective-permute-done.6.g1) | copy-start | bytes 786436
  18.7 11.0 %collective-permute-start.8 = (bf16[128,1024]{1,0:T(8,128)(2,1)S(1)}, bf16[128,1024]{1,0:T(8,128)(2,1)S(1)}, u32[]{:S(2)}, u32[]{:S(2)}) collective-permute-start(bf16[128,1024]{1,0:T(8,128)(2,1)S(1)} %collective-permute-done.6.g1), channel_id=1, source_target_pairs={{0,4},{4,0},{8,12},{12,8},{16,20},{20,16},{24,28},{28,24},{1,5},{5... | collective-permute-start | bytes 786440 | tf_op jit(solution)/shard_map/ppermute | solution.py:414
  22.0 12.4 %copy-start.10 = (bf16[128,1024]{1,0:T(8,128)(2,1)}, bf16[128,1024]{1,0:T(8,128)(2,1)S(1)}, u32[]{:S(2)}) copy-start(bf16[128,1024]{1,0:T(8,128)(2,1)S(1)} %collective-permute-done.2.t1) | copy-start | bytes 786436
  22.0 12.4 %collective-permute-start.4 = (bf16[128,1024]{1,0:T(8,128)(2,1)S(1)}, bf16[128,1024]{1,0:T(8,128)(2,1)S(1)}, u32[]{:S(2)}, u32[]{:S(2)}) collective-permute-start(bf16[128,1024]{1,0:T(8,128)(2,1)S(1)} %collective-permute-done.2.t1), channel_id=1, source_target_pairs={{0,4},{4,0},{8,12},{12,8},{16,20},{20,16},{24,28},{28,24},{1,5},{5... | collective-permute-start | bytes 786440 | tf_op jit(solution)/shard_map/ppermute | solution.py:414
  27.7 6.8 %copy-start.11 = (bf16[128,1024]{1,0:T(8,128)(2,1)}, bf16[128,1024]{1,0:T(8,128)(2,1)S(1)}, u32[]{:S(2)}) copy-start(bf16[128,1024]{1,0:T(8,128)(2,1)S(1)} %collective-permute-done.1.t0) | copy-start | bytes 786436
  27.7 6.8 %collective-permute-start.3 = (bf16[128,1024]{1,0:T(8,128)(2,1)S(1)}, bf16[128,1024]{1,0:T(8,128)(2,1)S(1)}, u32[]{:S(2)}, u32[]{:S(2)}) collective-permute-start(bf16[128,1024]{1,0:T(8,128)(2,1)S(1)} %collective-permute-done.1.t0), channel_id=1, source_target_pairs={{0,4},{4,0},{8,12},{12,8},{16,20},{20,16},{24,28},{28,24},{1,5},{5... | collective-permute-start | bytes 786440 | tf_op jit(solution)/shard_map/ppermute | solution.py:414
  29.7 19.6 %copy-start.9 = (s32[1,4]{1,0:T(1,128)S(1)}, s32[1,4]{1,0:T(1,128)}, u32[]{:S(2)}) copy-start(s32[1,4]{1,0:T(1,128)} %param.10) | copy-start | bytes 52
  29.7 0.7 copy-start.6
  30.4 0.7 copy-start.7
  34.5 0.7 copy-start.12
  35.2 0.7 copy-start.13
  46.8 13.5 %copy-start.2 = (f32[2,2,512,128]{3,2,1,0:T(8,128)S(1)}, f32[2,2,512,128]{3,2,1,0:T(8,128)}, u32[]{:S(2)}) copy-start(f32[2,2,512,128]{3,2,1,0:T(8,128)} %get-tuple-element.13) | copy-start | bytes 3145732
  46.8 15.8 %copy-start.1 = (f32[2,2,512,128]{3,2,1,0:T(8,128)S(1)}, f32[2,2,512,128]{3,2,1,0:T(8,128)}, u32[]{:S(2)}) copy-start(f32[2,2,512,128]{3,2,1,0:T(8,128)} %get-tuple-element.15) | copy-start | bytes 3145732
  46.8 13.4 %collective-permute-start.12 = (bf16[2,2,512,128]{3,2,1,0:T(8,128)(2,1)}, bf16[2,2,512,128]{3,2,1,0:T(8,128)(2,1)}, u32[]{:S(2)}, u32[]{:S(2)}) collective-permute-start(bf16[2,2,512,128]{3,2,1,0:T(8,128)(2,1)} %get-tuple-element.14), channel_id=1, source_target_pairs={{0,8},{4,12},{8,0},{12,4},{16,24},{20,28},{24,16},{28,20},{1,9},{5... | collective-permute-start | bytes 1572872 | tf_op jit(solution)/shard_map/ppermute | solution.py:414
  48.1 14.5 %collective-permute-start.14 = (bf16[2,2,512,128]{3,2,1,0:T(8,128)(2,1)}, bf16[2,2,512,128]{3,2,1,0:T(8,128)(2,1)S(1)}, u32[]{:S(2)}, u32[]{:S(2)}) collective-permute-start(bf16[2,2,512,128]{3,2,1,0:T(8,128)(2,1)} %get-tuple-element.16), channel_id=1, source_target_pairs={{0,16},{4,20},{8,24},{12,28},{16,0},{20,4},{24,8},{28,12},{1,17},{... | collective-permute-start | bytes 1572872 | tf_op jit(solution)/shard_map/ppermute | solution.py:414
  49.9 29.6 %copy-start = (bf16[1,128,1024]{2,1,0:T(8,128)(2,1)S(1)}, bf16[1,128,1024]{2,1,0:T(8,128)(2,1)}, u32[]{:S(2)}) copy-start(bf16[1,128,1024]{2,1,0:T(8,128)(2,1)} %param.8) | copy-start | bytes 786436
  49.9 29.6 %copy-start.8 = (f32[1024]{0:T(1024)S(1)}, f32[1024]{0:T(1024)}, u32[]{:S(2)}) copy-start(f32[1024]{0:T(1024)} %param.11) | copy-start | bytes 12292
  54.4 25.4 %copy-start.3 = (bf16[1,128,1024]{2,1,0:T(8,128)(2,1)S(1)}, bf16[1,128,1024]{2,1,0:T(8,128)(2,1)}, u32[]{:S(2)}) copy-start(bf16[1,128,1024]{2,1,0:T(8,128)(2,1)} %param.14) | copy-start | bytes 786436
  54.4 9.6 %collective-permute-start.9 = (bf16[256,1024]{1,0:T(8,128)(2,1)}, bf16[256,1024]{1,0:T(8,128)(2,1)S(1)}, u32[]{:S(2)}, u32[]{:S(2)}) collective-permute-start(bf16[256,1024]{1,0:T(8,128)(2,1)} %get-tuple-element.12), channel_id=1, source_target_pairs={{0,4},{4,0},{8,12},{12,8},{16,20},{20,16},{24,28},{28,24},{1,5},{5... | collective-permute-start | bytes 1572872 | tf_op jit(solution)/shard_map/ppermute | solution.py:414
  61.3 10.7 %collective-permute-start.13 = (bf16[2,512,128]{2,1,0:T(8,128)(2,1)S(1)}, bf16[2,512,128]{2,1,0:T(8,128)(2,1)S(1)}, u32[]{:S(2)}, u32[]{:S(2)}) collective-permute-start(bf16[2,512,128]{2,1,0:T(8,128)(2,1)S(1)} %fusion.4), channel_id=1, source_target_pairs={{0,16},{4,20},{8,24},{12,28},{16,0},{20,4},{24,8},{28,12},{1,17},{... | collective-permute-start | bytes 786440 | tf_op jit(solution)/shard_map/ppermute | solution.py:414
  62.6 10.3 %collective-permute-start.15 = (bf16[2,512,128]{2,1,0:T(8,128)(2,1)S(1)}, bf16[2,512,128]{2,1,0:T(8,128)(2,1)S(1)}, u32[]{:S(2)}, u32[]{:S(2)}) collective-permute-start(bf16[2,512,128]{2,1,0:T(8,128)(2,1)S(1)} %fusion.5), channel_id=1, source_target_pairs={{0,8},{4,12},{8,0},{12,4},{16,24},{20,28},{24,16},{28,20},{1,9},{5... | collective-permute-start | bytes 786440 | tf_op jit(solution)/shard_map/ppermute | solution.py:414
  65.3 10.1 %collective-permute-start.10 = (bf16[128,1024]{1,0:T(8,128)(2,1)S(1)}, bf16[128,1024]{1,0:T(8,128)(2,1)S(1)}, u32[]{:S(2)}, u32[]{:S(2)}) collective-permute-start(bf16[128,1024]{1,0:T(8,128)(2,1)S(1)} %get-tuple-element.25), channel_id=1, source_target_pairs={{2,0},{0,1},{4,2},{6,3},{1,4},{7,5},{3,6},{5,7},{10,8},{8,9},{12,1... | collective-permute-start | bytes 786440 | tf_op jit(solution)/shard_map/ppermute | solution.py:508
  69.9 9.6 %collective-permute-start.11 = (bf16[128,1024]{1,0:T(8,128)(2,1)S(1)}, bf16[128,1024]{1,0:T(8,128)(2,1)S(1)}, u32[]{:S(2)}, u32[]{:S(2)}) collective-permute-start(bf16[128,1024]{1,0:T(8,128)(2,1)S(1)} %get-tuple-element.26), channel_id=1, source_target_pairs={{4,3},{3,4},{1,6},{6,1},{0,0},{5,5},{2,2},{7,7},{12,11},{11,12},{9... | collective-permute-start | bytes 786440 | tf_op jit(solution)/shard_map/ppermute | solution.py:509
  73.2 7.9 %collective-permute-start.16 = (bf16[1024,128]{1,0:T(8,128)(2,1)S(1)}, bf16[1024,128]{1,0:T(8,128)(2,1)S(1)}, u32[]{:S(2)}, u32[]{:S(2)}) collective-permute-start(bf16[1024,128]{1,0:T(8,128)(2,1)S(1)} %get-tuple-element.27), channel_id=1, source_target_pairs={{0,4},{5,1},{1,0},{4,5},{2,6},{7,3},{3,2},{6,7},{8,12},{13,9},{9,8... | collective-permute-start | bytes 786440 | tf_op jit(solution)/shard_map/ppermute | solution.py:516
  73.2 11.3 %collective-permute-start.17 = (bf16[1024,128]{1,0:T(8,128)(2,1)S(1)}, bf16[1024,128]{1,0:T(8,128)(2,1)S(1)}, u32[]{:S(2)}, u32[]{:S(2)}) collective-permute-start(bf16[1024,128]{1,0:T(8,128)(2,1)S(1)} %get-tuple-element.28), channel_id=1, source_target_pairs={{1,4},{4,1},{3,6},{6,3},{9,12},{12,9},{11,14},{14,11},{17,20},{20,... | collective-permute-start | bytes 786440 | tf_op jit(solution)/shard_map/ppermute | solution.py:517

commit v3 on v2

--- a/solution.py
+++ b/solution.py
@@ -235,32 +235,28 @@
     return slot < limit
 
 
-def lift_kernel(info, g0, g1, g2, g3, w_out, lifted, rows, weight, sems):
-    capacity = g0.shape[0]
-    width = lifted.shape[0]
-    total = lifted.shape[1]
-    copies = [
-        pltpu.make_async_copy(
-            w_out.at[:, pl.ds(pl.multiple_of(info[4] * width, width), width)], weight, sems.at[4]
-        )
-    ]
-    for block, source in enumerate((g0, g1, g2, g3)):
+def weight_kernel(info, w_out, w_qkv, own_out, own_qkv, sems):
+    width = own_out.shape[1]
+    group = pl.multiple_of(info[4] * width, width)
+    copies = [pltpu.make_async_copy(w_out.at[:, pl.ds(group, width)], own_out, sems.at[3])]
+    for part in range(3):
         copies.append(
-            pltpu.make_async_copy(source, rows.at[pl.ds(block * capacity, capacity), :], sems.at[block])
+            pltpu.make_async_copy(
+                w_qkv.at[part, pl.ds(group, width), :],
+                own_qkv.at[pl.ds(part * width, width), :],
+                sems.at[part],
+            )
         )
     for copy in copies:
         copy.start()
     for copy in copies:
         copy.wait()
-    up = nn(rows[...], weight[...])
-    up = jnp.where(valid_slots(info, capacity, 0, total), up, 0.0)
-    lifted[...] = up.T.astype(lifted.dtype)
 
 
 def main_kernel(
-    info, t0, t1, t2, t3, g0, g1, g2, g3, lifted_in, w_qkv,
-    x_send, x_keep, y_send, y_keep, grads,
-    rows_t, rows_g, weight, lifted, query, key, value, stack,
+    info, t0, t1, t2, t3, g0, g1, g2, g3, weight_out, weight,
+    x_send, x_keep, y_send, y_keep, grads_here, grads_there,
+    rows_t, rows_g, lifted, query, key, value, stack,
     x_send_buf, x_keep_buf, y_send_buf, y_keep_buf, in_sems, out_sems,
 ):
     capacity = t0.shape[0]
@@ -277,32 +273,24 @@
                 source, rows_t.at[pl.ds(block * capacity, capacity), :], in_sems.at[block]
             )
         )
-    group = pl.multiple_of(info[4] * width, width)
-    for part in range(3):
-        loads.append(
-            pltpu.make_async_copy(
-                w_qkv.at[part, pl.ds(group, width), :],
-                weight.at[pl.ds(part * width, width), :],
-                in_sems.at[4 + part],
-            )
-        )
-    loads.append(pltpu.make_async_copy(lifted_in, lifted, in_sems.at[7]))
     for block, source in enumerate((g0, g1, g2, g3)):
         loads.append(
             pltpu.make_async_copy(
-                source, rows_g.at[pl.ds(block * capacity, capacity), :], in_sems.at[8 + block]
+                source, rows_g.at[pl.ds(block * capacity, capacity), :], in_sems.at[4 + block]
             )
         )
     for copy in loads:
         copy.start()
-    for copy in loads[:5]:
+    for copy in loads[:4]:
         copy.wait()
     query[...] = (nt(weight[0:width, :], rows_t[...]).astype(low) * scale).astype(low)
-    loads[5].wait()
     key[...] = nt(weight[width : 2 * width, :], rows_t[...]).astype(low)
-    loads[6].wait()
     value[...] = nt(weight[2 * width : 3 * width, :], rows_t[...]).astype(low)
-    loads[7].wait()
+    for copy in loads[4:]:
+        copy.wait()
+    up = nn(rows_g[...], weight_out[...])
+    up = jnp.where(valid_slots(info, capacity, 0, total), up, 0.0)
+    lifted[...] = up.T.astype(low)
 
     bias = jnp.where(valid_slots(info, capacity, 0, total), 0.0, MASKED)
     row_ok = valid_slots(info, capacity, 1, total)
@@ -324,65 +312,85 @@
         ).astype(low)
 
     stores = [
-        pltpu.make_async_copy(stack.at[pl.ds(0, 3 * width), :], grads, out_sems.at[0]),
-        pltpu.make_async_copy(x_send_buf, x_send, out_sems.at[1]),
-        pltpu.make_async_copy(y_send_buf, y_send, out_sems.at[2]),
-        pltpu.make_async_copy(x_keep_buf, x_keep, out_sems.at[3]),
-        pltpu.make_async_copy(y_keep_buf, y_keep, out_sems.at[4]),
+        pltpu.make_async_copy(
+            stack.at[pl.ds(0, 3 * width), pl.ds(part * (total // 2), total // 2)],
+            (grads_here, grads_there)[part],
+            out_sems.at[part],
+        )
+        for part in range(2)
     ]
-    stores[0].start()
-    for copy in loads[8:]:
-        copy.wait()
-    for slot_y, slot_x in ((1, 1), (0, 1), (1, 0), (0, 0)):
+    for copy in stores:
+        copy.start()
+    for step, (slot_y, slot_x) in enumerate(((0, 0), (1, 0), (0, 1), (1, 1))):
         block = (info[5] ^ slot_y) * 2 + (info[6] ^ slot_x)
         cols = pl.ds(pl.multiple_of(block * width, width), width)
         term_t = nn(stack[0 : 3 * width, :], rows_t[:, cols])
-        term_g = nn(stack[3 * width : 4 * width, :], rows_g[:, cols])
-        x_target = x_send_buf if slot_x else x_keep_buf
-        y_target = y_send_buf if slot_y else y_keep_buf
+        term_g = nn(stack[3 * width : 4 * width, :], rows_g[:, cols]).T
+        x_target, x_out = (x_send_buf, x_send) if slot_x else (x_keep_buf, x_keep)
+        y_target, y_out = (y_send_buf, y_send) if slot_y else (y_keep_buf, y_keep)
         for side in range(2):
             across = slice(side * lanes, (side + 1) * lanes)
             spot = info[7] ^ side
             x_target[slot_y, spot, :, :] = term_t[0 : 2 * width, across].astype(x_target.dtype)
             y_target[slot_x, spot, 0:width, :] = term_t[2 * width : 3 * width, across].astype(y_target.dtype)
-            y_target[slot_x, spot, width : 2 * width, :] = term_g[:, across].astype(y_target.dtype)
-        if (slot_y, slot_x) == (0, 1):
-            stores[1].start()
-        if (slot_y, slot_x) == (1, 0):
-            stores[2].start()
-    stores[3].start()
-    stores[4].start()
+            for part in range(2):
+                y_target[slot_x, spot, width + part * lanes : width + (part + 1) * lanes, :] = term_g[
+                    across, part * lanes : (part + 1) * lanes
+                ].astype(y_target.dtype)
+        for part, (target, out, index) in enumerate(((x_target, x_out, slot_y), (y_target, y_out, slot_x))):
+            copy = pltpu.make_async_copy(target.at[index], out.at[index], out_sems.at[2 + 2 * step + part])
+            copy.start()
+            stores.append(copy)
     for copy in stores:
         copy.wait()
 
 
-def normed_kernel(info, grads_in, w_qkv, keep, send, grads, weight, sems):
-    features = w_qkv.shape[2]
-    total = grads.shape[1]
-    width = grads.shape[0] // 3
-    group = pl.multiple_of(info[4] * width, width)
-    loads = [pltpu.make_async_copy(grads_in, grads, sems.at[3])]
+def normed_kernel(info, here, there, w_qkv, back_one, back_two, grads, weight, sems):
+    width = here.shape[0] // 3
+    capacity = back_one.shape[0]
+    first = pl.multiple_of((info[4] >> 1) * 2 * width, 2 * width)
+    core = info[4] & 1
+    loads = []
     for part in range(3):
         loads.append(
             pltpu.make_async_copy(
-                w_qkv.at[part, pl.ds(group, width), :],
-                weight.at[pl.ds(part * width, width), :],
+                w_qkv.at[part, pl.ds(first, 2 * width), :],
+                weight.at[pl.ds(part * 2 * width, 2 * width), :],
                 sems.at[part],
             )
         )
+        for place, source, spot in ((0, here, core), (1, there, 1 - core)):
+            loads.append(
+                pltpu.make_async_copy(
+                    source.at[pl.ds(part * width, width), :],
+                    grads.at[pl.ds(pl.multiple_of((part * 2 + spot) * width, width), width), :],
+                    sems.at[3 + part * 2 + place],
+                )
+            )
     for copy in loads:
         copy.start()
     for copy in loads:
         copy.wait()
-    send[...] = tn(grads[:, total // 2 : total], weight[...]).astype(send.dtype)
-    keep[...] = tn(grads[:, 0 : total // 2], weight[...])
+    back_one[...] = tn(grads[:, 0:capacity], weight[...]).astype(back_one.dtype)
+    back_two[...] = tn(grads[:, capacity : 2 * capacity], weight[...]).astype(back_two.dtype)
+
+
+def sum_kernel(x_part, y_part, x_second, y_second, home_send, guest_send, own):
+    half = x_part.shape[1]
+    for rows, part, second in ((0, x_part, x_second), (half, y_part, y_second)):
+        span = pl.ds(rows, half)
+        home_send[span, :] = (part[0] + second[0].astype(part.dtype)).astype(home_send.dtype)
+        total = part[1] + second[1].astype(part.dtype)
+        guest_send[span, :] = total.astype(guest_send.dtype)
+        own[span, :] = total
 
 
 def specs(space, count):
     return [pl.BlockSpec(memory_space=space)] * count
 
 
-VMEM_BYTES = 56 * 1024 * 1024
+VMEM_BYTES = 50 * 1024 * 1024
+MAIN_BYTES = 50 * 1024 * 1024
 
 
 def column_shards(tokens, positions, counts, ln_gain, w_qkv, w_out, d_out):
@@ -413,15 +421,16 @@
     def across(array, bit):
         return lax.ppermute(array, "dp", [(i, i ^ bit) for i in range(2 * chips)])
 
-    def share(array):
-        one = lax.ppermute(array, axes, first)
-        two = lax.ppermute(array, axes, second)
-        return one, two, across(one, 1), across(two, 1)
-
-    blocks_g = share(upstream)
+    def fetch(array):
+        return lax.ppermute(array, axes, first), lax.ppermute(array, axes, second)
+
+    def share(pair):
+        return pair + (across(pair[0], 1), across(pair[1], 1))
+
     other_counts = across(counts[0], 1)
+    blocks_g = share(fetch(upstream))
     normed, standard, inv_std = layer_norm(inputs, positions[0], ln_gain)
-    blocks_t = share(normed)
+    fetched_t = fetch(normed)
 
     sizes = jnp.where(resident, counts[0], other_counts)
     table = jnp.array(block_table(), jnp.int32)
@@ -433,35 +442,34 @@
 
     params = pltpu.CompilerParams(vmem_limit_bytes=VMEM_BYTES)
     smem = specs(pltpu.SMEM, 1)
-    lifted = pl.pallas_call(
-        lift_kernel,
-        out_shape=jax.ShapeDtypeStruct((width, total), low),
-        in_specs=smem + specs(pltpu.HBM, 5),
-        out_specs=pl.BlockSpec(memory_space=pltpu.VMEM),
-        scratch_shapes=[
-            pltpu.VMEM((total, features), low),
-            pltpu.VMEM((features, width), low),
-            pltpu.SemaphoreType.DMA((5,)),
-        ],
+    own_out, own_qkv = pl.pallas_call(
+        weight_kernel,
+        out_shape=(
+            jax.ShapeDtypeStruct((features, width), low),
+            jax.ShapeDtypeStruct((3 * width, features), low),
+        ),
+        in_specs=smem + specs(pl.ANY, 2),
+        out_specs=specs(pltpu.VMEM, 2),
+        scratch_shapes=[pltpu.SemaphoreType.DMA((4,))],
         compiler_params=params,
-        cost_estimate=pl.CostEstimate(
-            flops=2 * total * features * width, bytes_accessed=2 * 1024 * 1024, transcendentals=0
-        ),
-    )(info, *blocks_g, w_out)
+        cost_estimate=pl.CostEstimate(flops=0, bytes_accessed=4 * 1024 * 1024, transcendentals=0),
+    )(info, w_out, w_qkv)
+    fetched_t, blocks_g, own_out, own_qkv = lax.optimization_barrier((fetched_t, blocks_g, own_out, own_qkv))
+    blocks_t = share(fetched_t)
 
     send_shape = jax.ShapeDtypeStruct((2, 2, 2 * width, lanes), low)
     keep_shape = jax.ShapeDtypeStruct((2, 2, 2 * width, lanes), wide)
-    x_send, x_keep, y_send, y_keep, grads = pl.pallas_call(
+    grads_shape = jax.ShapeDtypeStruct((3 * width, half), low)
+    x_send, x_keep, y_send, y_keep, grads_here, grads_there = pl.pallas_call(
         main_kernel,
         out_shape=(
-            send_shape, keep_shape, send_shape, keep_shape, jax.ShapeDtypeStruct((3 * width, total), low)
+            send_shape, keep_shape, send_shape, keep_shape, grads_shape, grads_shape
         ),
-        in_specs=smem + specs(pltpu.HBM, 10),
-        out_specs=specs(pltpu.HBM, 5),
+        in_specs=smem + specs(pl.ANY, 8) + specs(pltpu.VMEM, 2),
+        out_specs=specs(pltpu.HBM, 6),
         scratch_shapes=[
             pltpu.VMEM((total, features), low),
             pltpu.VMEM((total, features), low),
-            pltpu.VMEM((3 * width, features), low),
             pltpu.VMEM((width, total), low),
             pltpu.VMEM((width, total), low),
             pltpu.VMEM((width, total), low),
@@ -471,55 +479,67 @@
             pltpu.VMEM(send_shape.shape, wide),
             pltpu.VMEM(send_shape.shape, low),
             pltpu.VMEM(send_shape.shape, wide),
-            pltpu.SemaphoreType.DMA((12,)),
-            pltpu.SemaphoreType.DMA((5,)),
+            pltpu.SemaphoreType.DMA((8,)),
+            pltpu.SemaphoreType.DMA((10,)),
         ],
-        compiler_params=params,
+        compiler_params=pltpu.CompilerParams(vmem_limit_bytes=MAIN_BYTES),
         cost_estimate=pl.CostEstimate(
             flops=2 * total * features * width * 7 + 12 * 4 * total * total * HEAD_DIM,
             bytes_accessed=8 * 1024 * 1024,
             transcendentals=4 * total * total,
         ),
-    )(info, *blocks_t, *blocks_g, lifted, w_qkv)
-
-    normed_keep, normed_send = pl.pallas_call(
+    )(info, *blocks_t, *blocks_g, own_out, own_qkv)
+
+    x_first, y_first = across(x_send, 2), across(y_send, 4)
+    from_core = across(grads_there, 1)
+    block_shape = jax.ShapeDtypeStruct((capacity, features), low)
+    back_one, back_two = pl.pallas_call(
         normed_kernel,
-        out_shape=(
-            jax.ShapeDtypeStruct((half, features), wide),
-            jax.ShapeDtypeStruct((half, features), low),
-        ),
-        in_specs=smem + specs(pltpu.HBM, 2),
+        out_shape=(block_shape, block_shape),
+        in_specs=smem + specs(pl.ANY, 2) + specs(pltpu.HBM, 1),
         out_specs=specs(pltpu.VMEM, 2),
         scratch_shapes=[
-            pltpu.VMEM((3 * width, total), low),
-            pltpu.VMEM((3 * width, features), low),
-            pltpu.SemaphoreType.DMA((4,)),
+            pltpu.VMEM((6 * width, half), low),
+            pltpu.VMEM((6 * width, features), low),
+            pltpu.SemaphoreType.DMA((9,)),
         ],
         compiler_params=params,
         cost_estimate=pl.CostEstimate(
             flops=2 * total * features * width * 3, bytes_accessed=4 * 1024 * 1024, transcendentals=0
         ),
-    )(info, grads, w_qkv)
-
-    x_first, y_first = across(x_send, 2), across(y_send, 4)
-    shared = across(normed_send, 1)
-    back_one = (normed_keep[:capacity] + shared[:capacity].astype(wide)).astype(low)
-    back_two = (normed_keep[capacity:] + shared[capacity:].astype(wide)).astype(low)
-    normed_grad = lax.ppermute(back_one, axes, first_back).astype(wide)
-    normed_grad = normed_grad + lax.ppermute(back_two, axes, second).astype(wide)
-
+    )(info, grads_here, from_core, w_qkv)
+    home_one = lax.ppermute(back_one, axes, first_back)
+    home_two = lax.ppermute(back_two, axes, second)
     x_second = across((x_keep[1] + x_first[1].astype(wide)).astype(low), 4)
     y_second = across((y_keep[1] + y_first[1].astype(wide)).astype(low), 2)
-    x_part = x_keep[0] + x_first[0].astype(wide) + x_second.astype(wide)
-    y_part = y_keep[0] + y_first[0].astype(wide) + y_second.astype(wide)
-    sums = jnp.concatenate([x_part, y_part], axis=1)
-    from_home = lax.ppermute(sums[0].astype(low), axes, home)
-    from_guest = lax.ppermute(sums[1].astype(low), axes, guests)
-    final = from_home.astype(wide) + jnp.where(resident, sums[1], from_guest.astype(wide))
-    final = final * factor
-    grad_qkv = final[: 3 * width].reshape(3, width, lanes)
-    grad_out = final[3 * width :].T
-
+    x_part = x_keep[0] + x_first[0].astype(wide)
+    y_part = y_keep[0] + y_first[0].astype(wide)
+    x_part, y_part = lax.optimization_barrier((x_part, y_part))
+    home_send, guest_send, own = pl.pallas_call(
+        sum_kernel,
+        out_shape=(
+            jax.ShapeDtypeStruct((4 * width, lanes), low),
+            jax.ShapeDtypeStruct((4 * width, lanes), low),
+            jax.ShapeDtypeStruct((4 * width, lanes), wide),
+        ),
+        in_specs=specs(pltpu.VMEM, 4),
+        out_specs=specs(pltpu.VMEM, 3),
+        compiler_params=pltpu.CompilerParams(vmem_limit_bytes=16 * 1024 * 1024),
+        cost_estimate=pl.CostEstimate(flops=4 * width * 2 * lanes, bytes_accessed=2 * 1024 * 1024, transcendentals=0),
+    )(x_part, y_part, x_second, y_second)
+    from_home = lax.ppermute(home_send, axes, home)
+    from_guest = lax.ppermute(guest_send, axes, guests)
+
+    def finish(low_row, high_row):
+        rest = jnp.where(resident, own[low_row:high_row], from_guest[low_row:high_row].astype(wide))
+        return (from_home[low_row:high_row].astype(wide) + rest) * factor
+
+    grad_qkv = finish(0, 3 * width).reshape(3, width, lanes)
+    grad_out = jnp.concatenate(
+        [finish(3 * width, 3 * width + lanes), finish(3 * width + lanes, 4 * width)], axis=1
+    )
+
+    normed_grad = home_one.astype(wide) + home_two.astype(wide)
     own_valid = jnp.arange(capacity, dtype=jnp.int32) < lax.dynamic_index_in_dim(counts[0], seat, 0, False)
     masked_grad = jnp.where(own_valid[:, None], upstream, jnp.zeros_like(upstream))
     unit_grad = normed_grad * ln_gain

time: 86.7 us -> 75.8 us (0.87)
  waiting for transfers between devices: 22.5 us -> 18.1 us
  other arithmetic: 11.5 us -> 8.01 us
  Pallas kernels: 18.6 us -> 15.9 us
  local copies, waits for them, and re-layouts: 7.06 us -> 4.79 us
  starting transfers between devices: 25.6 us -> 27.6 us
    ppermute x8, starting transfers between devices: 18.8 us -> 23 us  [the longest x4 10.1 us: fetch(): return (lax.ppermute(array, axes, first), lax.ppermute(array, axes, second))]
    ppermute x8, waiting for transfers between devices: 18.3 us -> 14.7 us  [the longest x4 5.64 us: fetch(): return (lax.ppermute(array, axes, first), lax.ppermute(array, axes, second))]
    ppermute x10, starting transfers between devices: 6.77 us -> 4.66 us  [across(): return lax.ppermute(array, 'dp', [(i, i ^ bit) for i in range(2 * chips)])]
    pallas_call x2 -> x3, Pallas kernels: 7.7 us -> 5.89 us  [the longest x1 3.69 us: column_shards(): pl.pallas_call(normed_kernel, out_shape=(block_shape, block_shape), in_sp...]
    unnamed x29 -> x26, local copies, waits for them, and re-layouts: 3.62 us -> 2.05 us
    convert_element_type x2 -> x0, other arithmetic: 1.41 us -> none  [the longest x1 1.34 us: column_shards(): (normed_keep[:capacity] + shared[:capacity].astype(wide)).astype(low)]
    add x2 -> x0, other arithmetic: 1.13 us -> none  [the longest x1 1.04 us: column_shards(): x_part = x_keep[0] + x_first[0].astype(wide) + x_second.astype(wide)]
    convert_element_type x1, other arithmetic: 1.12 us -> 0.14 us  [layer_norm(): normed = (standard * ln_gain).astype(jnp.bfloat16)]
  transfers between devices with their start and end apart: 18 -> 18, of which waited for: 8 -> 9; matrix products, arithmetic and copies ran while one was open for 16% -> 12% of each run, Pallas kernels for 9% -> 8%
where the time goes in v3:
time: 75.8 us; the launch traced here: 75.4 us
  starting transfers between devices  27.6 us (36%)
  waiting for transfers between devices  18.1 us (24%)
  Pallas kernels  15.9 us (21%)
  other arithmetic  8.01 us (11%)
  local copies, waits for them, and re-layouts  4.79 us (6%)
  between operations  0.94 us (1%)
    ppermute x4, starting transfers between devices, fetch(): return (lax.ppermute(array, axes, first), lax.ppermute(array, axes, second))  10.1 us
    pallas_call x1, Pallas kernels, column_shards(): pl.pallas_call(main_kernel, out_shape=(send_shape, keep_shape, send_shape...  10.1 us
    ppermute x4, waiting for transfers between devices, fetch(): return (lax.ppermute(array, axes, first), lax.ppermute(array, axes, second))  5.64 us
    ppermute x1, starting transfers between devices, column_shards(): home_one = lax.ppermute(back_one, axes, first_back)  5.04 us
    ppermute x1, waiting for transfers between devices, column_shards(): home_two = lax.ppermute(back_two, axes, second)  4.67 us
    ppermute x10, starting transfers between devices, across(): return lax.ppermute(array, 'dp', [(i, i ^ bit) for i in range(2 * chips)])  4.66 us
    ppermute x1, starting transfers between devices, column_shards(): from_guest = lax.ppermute(guest_send, axes, guests)  3.99 us
    ppermute x1, waiting for transfers between devices, column_shards(): from_guest = lax.ppermute(guest_send, axes, guests)  3.91 us
  transfers between devices with their start and end apart: 18, of which 9 were waited for; matrix products, arithmetic and copies ran while one was open for 12% of the time, Pallas kernels for 8%

profile of v3, /device:TPU:1, one launch (start us, length us, event | category | flops | bytes accessed | tf_op | source)
XLA Modules:
  0.0 75.4 jit_solution(10312569332458898614)
XLA Ops:
  0.7 2.7 %collective-permute-start.3 = (bf16[128,1024]{1,0:T(8,128)(2,1)}, bf16[128,1024]{1,0:T(8,128)(2,1)S(1)}, u32[]{:S(2)}, u32[]{:S(2)}) collective-permute-start(bf16[128,1024]{1,0:T(8,128)(2,1)} %bitcast.42), channel_id=1, source_target_pairs={{0,2},{1,0},{2,4},{3,6},{4,1},{5,7},{6,3},{7,5},{8,10},{9,8},{10,1... | collective-permute-start | bytes 786440 | tf_op jit(solution)/shard_map/ppermute | solution.py:425
  3.4 4.1 %collective-permute-start.4 = (bf16[128,1024]{1,0:T(8,128)(2,1)}, bf16[128,1024]{1,0:T(8,128)(2,1)S(1)}, u32[]{:S(2)}, u32[]{:S(2)}) collective-permute-start(bf16[128,1024]{1,0:T(8,128)(2,1)} %bitcast.43), channel_id=1, source_target_pairs={{4,3},{3,4},{1,6},{6,1},{0,0},{5,5},{2,2},{7,7},{12,11},{11,12},{9... | collective-permute-start | bytes 786440 | tf_op jit(solution)/shard_map/ppermute | solution.py:425
  7.5 0.7 convert_bitcast_fusion
  8.2 1.0 %multiply_sine_fusion = (f32[128,512]{1,0:T(8,128)S(1)}, f32[128,512]{1,0:T(8,128)S(1)}) fusion(f32[512]{0:T(512)S(1)} %multiply_exponential_fusion, f32[128]{0:T(128)S(1)} %convert_bitcast_fusion), kind=kLoop, calls=%fused_computation.15 | loop fusion | flops 65536 | bytes 526848 | tf_op jit(solution)/shard_map/sin | solution.py:21
  9.2 1.3 %fusion.7 = f32[128]{0:T(128)S(1)} fusion(f32[128,512]{1,0:T(8,128)S(1)} %get-tuple-element.60, f32[128,512]{1,0:T(8,128)S(1)} %get-tuple-element.59, bf16[1,128,1024]{2,1,0:T(8,128)(2,1)} %param.8), kind=kLoop, calls=%fused_computation.38 | loop fusion | flops 524160 | bytes 786944 | tf_op jit(solution)/shard_map/reduce_sum | solution.py:26
  10.5 1.1 %multiply_reduce_fusion.1 = f32[128]{0:T(128)S(1)} fusion(f32[128]{0:T(128)S(1)} %broadcast_multiply_fusion.2, f32[128,512]{1,0:T(8,128)S(1)} %get-tuple-element.60, f32[128,512]{1,0:T(8,128)S(1)} %get-tuple-element.59, bf16[1,128,1024]{2,1,0:T(8,128)(2,1)} %param.8), kind=kLoop, calls=%fused_computation.10 | loop fusion | flops 786304 | bytes 787456 | tf_op jit(solution)/shard_map/reduce_sum | solution.py:27
  11.6 0.1 multiply_convert_fusion
  11.8 3.3 %collective-permute-start.2 = (bf16[128,1024]{1,0:T(8,128)(2,1)S(1)}, bf16[128,1024]{1,0:T(8,128)(2,1)S(1)}, u32[]{:S(2)}, u32[]{:S(2)}) collective-permute-start(bf16[128,1024]{1,0:T(8,128)(2,1)S(1)} %multiply_convert_fusion), channel_id=1, source_target_pairs={{4,3},{3,4},{1,6},{6,1},{0,0},{5,5},{2,2},{7,7},{12,11},{11,12},{9... | collective-permute-start | bytes 786440 | tf_op jit(solution)/shard_map/ppermute | solution.py:425
  15.1 0.1 collective-permute-start.1
  15.1 0.1 collective-permute-start
  15.2 0.8 %fusion.4 = (s32[2,1]{0,1:T(1,128)S(1)}, s32[2,1]{0,1:T(1,128)S(1)}) fusion(s32[8,2]{1,0:T(8,128)} %constant.44.clone, s32[]{:T(128)S(6)} %select_n.56, s32[]{:T(128)S(6)} %select_n.57), kind=kLoop, calls=%fused_computation.29 | loop fusion | bytes 40 | tf_op jit(solution)/shard_map/concatenate | solution.py:437
  16.0 0.1 fusion.6
  16.1 5.4 %collective-permute-done.3.g0 = bf16[128,1024]{1,0:T(8,128)(2,1)S(1)} collective-permute-done((bf16[128,1024]{1,0:T(8,128)(2,1)}, bf16[128,1024]{1,0:T(8,128)(2,1)S(1)}, u32[]{:S(2)}, u32[]{:S(2)}) %collective-permute-start.3) | collective-permute-done | bytes 262176 | tf_op jit(solution)/shard_map/ppermute | solution.py:425
  21.5 0.5 collective-permute-start.6
  22.0 0.6 gather_fusion
  22.7 0.1 concatenate.39.info
  22.8 2.1 %shard_map.103 = (bf16[1024,256]{1,0:T(8,128)(2,1)S(1)}, bf16[768,1024]{1,0:T(8,128)(2,1)S(1)}) custom-call(s32[8]{0:T(128)S(1)} %concatenate.39.info, bf16[1024,1024]{1,0:T(8,128)(2,1)} %w_out.1, bf16[3,1024,1024]{2,1,0:T(8,128)(2,1)} %w_qkv.3), custom_call_target="tpu_custom_call" | custom-call | bytes 4194304 | tf_op jit(solution)/shard_map/pallas_call | solution.py:445
  24.9 1.2 %copy-done = bf16[768,1024]{1,0:T(8,128)(2,1)} copy-done((bf16[768,1024]{1,0:T(8,128)(2,1)}, bf16[768,1024]{1,0:T(8,128)(2,1)S(1)}, u32[]{:S(2)}) %copy-start) | copy-done | bytes 1572888
  26.1 0.8 %copy-done.1 = bf16[1024,256]{1,0:T(8,128)(2,1)} copy-done((bf16[1024,256]{1,0:T(8,128)(2,1)}, bf16[1024,256]{1,0:T(8,128)(2,1)S(1)}, u32[]{:S(2)}) %copy-start.1) | copy-done | bytes 524312
  26.9 0.2 collective-permute-done.1.t0
  27.1 0.5 collective-permute-start.8
  27.6 1.0 %collective-permute-done.7.t2 = bf16[128,1024]{1,0:T(8,128)(2,1)S(1)} collective-permute-done((bf16[128,1024]{1,0:T(8,128)(2,1)S(1)}, bf16[128,1024]{1,0:T(8,128)(2,1)S(1)}, u32[]{:S(2)}, u32[]{:S(2)}) %collective-permute-start.7) | collective-permute-done | bytes 262176 | tf_op jit(solution)/shard_map/ppermute | solution.py:422
  28.7 0.4 collective-permute-done.8.t3
  29.0 10.1 %shard_map.104 = (bf16[2,2,512,128]{3,2,1,0:T(8,128)(2,1)S(1)}, f32[2,2,512,128]{3,2,1,0:T(8,128)}, bf16[2,2,512,128]{3,2,1,0:T(8,128)(2,1)S(1)}, f32[2,2,512,12...) custom-call(s32[8]{0:T(128)S(1)} %concatenate.39.info, ...), custom_call_target="tpu_custom_call" | custom-call | flops 2684354560 | bytes 8388608 | tf_op jit(solution)/shard_map/pallas_call | solution.py:463
  39.1 1.3 %collective-permute-start.12 = (bf16[2,2,512,128]{3,2,1,0:T(8,128)(2,1)S(1)}, bf16[2,2,512,128]{3,2,1,0:T(8,128)(2,1)S(1)}, u32[]{:S(2)}, u32[]{:S(2)}) collective-permute-start(bf16[2,2,512,128]{3,2,1,0:T(8,128)(2,1)S(1)} %get-tuple-element.41), channel_id=1, source_target_pairs={{0,8},{4,12},{8,0},{12,4},{16,24},{20,28},{24,16},{28,20},{1,9},{5... | collective-permute-start | bytes 1572872 | tf_op jit(solution)/shard_map/ppermute | solution.py:422
  40.4 0.4 collective-permute-start.9
  40.8 1.3 %collective-permute-start.13 = (bf16[2,2,512,128]{3,2,1,0:T(8,128)(2,1)S(1)}, bf16[2,2,512,128]{3,2,1,0:T(8,128)(2,1)S(1)}, u32[]{:S(2)}, u32[]{:S(2)}) collective-permute-start(bf16[2,2,512,128]{3,2,1,0:T(8,128)(2,1)S(1)} %get-tuple-element.43), channel_id=1, source_target_pairs={{0,16},{4,20},{8,24},{12,28},{16,0},{20,4},{24,8},{28,12},{1,17},{... | collective-permute-start | bytes 1572872 | tf_op jit(solution)/shard_map/ppermute | solution.py:422
  42.1 1.2 %constant_dynamic-slice_fusion.2 = s32[1,1]{1,0:T(1,128)} fusion(s32[1,4]{1,0:T(1,128)} %param.10, s32[]{:T(128)S(6)} %select_n.52), kind=kLoop, calls=%fused_computation.28 | loop fusion | bytes 12 | tf_op jit(solution)/shard_map/jit(dynamic_index_in_dim)/dynamic_slice | solution.py:543
  43.3 3.7 %shard_map.105 = (bf16[128,1024]{1,0:T(8,128)(2,1)S(1)}, bf16[128,1024]{1,0:T(8,128)(2,1)S(1)}) custom-call(s32[8]{0:T(128)S(1)} %concatenate.39.info, bf16[768,256]{1,0:T(8,128)(2,1)S(1)} %get-tuple-element.36.here, bf16[768,256]{1,0:T(8,128)(2,1)S(1)} %collective-permute-done.9.there, bf16[3,1024,1024]{2,1,0:T(8,128)(2,1)} %w_qkv.3), custom_call_target="tpu_custom_call" | custom-call | flops 805306368 | bytes 4194304 | tf_op jit(solution)/shard_map/pallas_call | solution.py:496
  47.0 5.0 %collective-permute-start.10 = (bf16[128,1024]{1,0:T(8,128)(2,1)S(1)}, bf16[128,1024]{1,0:T(8,128)(2,1)S(1)}, u32[]{:S(2)}, u32[]{:S(2)}) collective-permute-start(bf16[128,1024]{1,0:T(8,128)(2,1)S(1)} %get-tuple-element.38), channel_id=1, source_target_pairs={{2,0},{0,1},{4,2},{6,3},{1,4},{7,5},{3,6},{5,7},{10,8},{8,9},{12,1... | collective-permute-start | bytes 786440 | tf_op jit(solution)/shard_map/ppermute | solution.py:511
  52.1 3.2 %collective-permute-start.11 = (bf16[128,1024]{1,0:T(8,128)(2,1)S(1)}, bf16[128,1024]{1,0:T(8,128)(2,1)S(1)}, u32[]{:S(2)}, u32[]{:S(2)}) collective-permute-start(bf16[128,1024]{1,0:T(8,128)(2,1)S(1)} %get-tuple-element.39), channel_id=1, source_target_pairs={{4,3},{3,4},{1,6},{6,1},{0,0},{5,5},{2,2},{7,7},{12,11},{11,12},{9... | collective-permute-start | bytes 786440 | tf_op jit(solution)/shard_map/ppermute | solution.py:512
  55.3 0.1 fusion.1
  55.4 0.3 collective-permute-start.14
  55.7 0.1 fusion.2
  55.9 0.3 collective-permute-start.15
  56.2 0.6 iota_compare_fusion
  56.8 0.5 collective-permute-done.10
  57.4 4.7 %collective-permute-done.11 = bf16[128,1024]{1,0:T(8,128)(2,1)S(1)} collective-permute-done((bf16[128,1024]{1,0:T(8,128)(2,1)S(1)}, bf16[128,1024]{1,0:T(8,128)(2,1)S(1)}, u32[]{:S(2)}, u32[]{:S(2)}) %collective-permute-start.11) | collective-permute-done | bytes 262176 | tf_op jit(solution)/shard_map/ppermute | solution.py:512
  62.0 0.3 fusion
  62.3 0.2 collective-permute-done.14.x_second
  62.5 1.7 %collective-permute-done.15.y_second = bf16[2,512,128]{2,1,0:T(8,128)(2,1)S(1)} collective-permute-done((bf16[2,512,128]{2,1,0:T(8,128)(2,1)S(1)}, bf16[2,512,128]{2,1,0:T(8,128)(2,1)S(1)}, u32[]{:S(2)}, u32[]{:S(2)}) %collective-permute-start.15) | collective-permute-done | bytes 262176 | tf_op jit(solution)/shard_map/ppermute | solution.py:422
  64.2 0.1 shard_map.106
  64.3 0.6 collective-permute-start.16
  64.9 4.0 %collective-permute-start.17 = (bf16[1024,128]{1,0:T(8,128)(2,1)S(1)}, bf16[1024,128]{1,0:T(8,128)(2,1)S(1)}, u32[]{:S(2)}, u32[]{:S(2)}) collective-permute-start(bf16[1024,128]{1,0:T(8,128)(2,1)S(1)} %get-tuple-element.48), channel_id=1, source_target_pairs={{1,4},{4,1},{3,6},{6,3},{9,12},{12,9},{11,14},{14,11},{17,20},{20,... | collective-permute-start | bytes 786440 | tf_op jit(solution)/shard_map/ppermute | solution.py:531
  68.9 1.0 %fusion.3 = bf16[1,128,1024]{2,1,0:T(8,128)(2,1)} fusion(f32[128]{0:T(128)S(1)} %get-tuple-element.61, f32[128]{0:T(128)S(1)} %broadcast_multiply_fusion.2, f32[128]{0:T(128)S(1)} %get-tuple-element.62, f32[1024]{0:T(1024)S(1)} %copy-done.11, bf16[128,1024]{1,0:T(8,128)(2,1)S(1)} %collective-permute-done.11, ...), kind=kLoop, calls=%fused_computation.18 | loop fusion | flops 2228224 | bytes 1841280 | tf_op jit(solution)/shard_map/broadcast_in_dim | solution.py:549
  69.9 3.9 %collective-permute-done.17 = bf16[1024,128]{1,0:T(8,128)(2,1)S(1)} collective-permute-done((bf16[1024,128]{1,0:T(8,128)(2,1)S(1)}, bf16[1024,128]{1,0:T(8,128)(2,1)S(1)}, u32[]{:S(2)}, u32[]{:S(2)}) %collective-permute-start.17) | collective-permute-done | bytes 262176 | tf_op jit(solution)/shard_map/ppermute | solution.py:531
  73.9 0.7 pad_maximum_fusion
  74.6 0.8 %add_multiply_fusion.1 = f32[768,128]{1,0:T(8,128)} fusion(f32[1024,128]{1,0:T(8,128)S(1)} %get-tuple-element.47, bf16[1024,128]{1,0:T(8,128)(2,1)S(1)} %collective-permute-done.17, bf16[1024,128]{1,0:T(8,128)(2,1)S(1)} %collective-permute-done.16, pred[]{:T(512)S(6)} %eq.3), kind=kLoop, calls=%fused_computation.13 | loop fusion | flops 491520 | bytes 1179649 | tf_op jit(solution)/shard_map/mul | solution.py:535
  (42 shorter events, 0.2 us)
Async XLA Ops:
  0.6 11.0 %copy-start.6 = (bf16[1,128,1024]{2,1,0:T(8,128)(2,1)S(1)}, bf16[1,128,1024]{2,1,0:T(8,128)(2,1)}, u32[]{:S(2)}) copy-start(bf16[1,128,1024]{2,1,0:T(8,128)(2,1)} %param.8) | copy-start | bytes 786436
  0.6 11.0 %copy-start.11 = (f32[1024]{0:T(1024)S(1)}, f32[1024]{0:T(1024)}, u32[]{:S(2)}) copy-start(f32[1024]{0:T(1024)} %param.11) | copy-start | bytes 12292
  0.7 14.5 %copy-start.12 = (s32[1,4]{1,0:T(1,128)S(1)}, s32[1,4]{1,0:T(1,128)}, u32[]{:S(2)}) copy-start(s32[1,4]{1,0:T(1,128)} %param.10) | copy-start | bytes 52
  0.7 20.8 %collective-permute-start.3 = (bf16[128,1024]{1,0:T(8,128)(2,1)}, bf16[128,1024]{1,0:T(8,128)(2,1)S(1)}, u32[]{:S(2)}, u32[]{:S(2)}) collective-permute-start(bf16[128,1024]{1,0:T(8,128)(2,1)} %bitcast.42), channel_id=1, source_target_pairs={{0,2},{1,0},{2,4},{3,6},{4,1},{5,7},{6,3},{7,5},{8,10},{9,8},{10,1... | collective-permute-start | bytes 786440 | tf_op jit(solution)/shard_map/ppermute | solution.py:425
  3.4 18.1 %collective-permute-start.4 = (bf16[128,1024]{1,0:T(8,128)(2,1)}, bf16[128,1024]{1,0:T(8,128)(2,1)S(1)}, u32[]{:S(2)}, u32[]{:S(2)}) collective-permute-start(bf16[128,1024]{1,0:T(8,128)(2,1)} %bitcast.43), channel_id=1, source_target_pairs={{4,3},{3,4},{1,6},{6,1},{0,0},{5,5},{2,2},{7,7},{12,11},{11,12},{9... | collective-permute-start | bytes 786440 | tf_op jit(solution)/shard_map/ppermute | solution.py:425
  9.2 13.5 %copy-start.2 = (f32[128,512]{1,0:T(8,128)}, f32[128,512]{1,0:T(8,128)S(1)}, u32[]{:S(2)}) copy-start(f32[128,512]{1,0:T(8,128)S(1)} %get-tuple-element.59) | copy-start | bytes 786436
  9.2 15.7 %copy-start.4 = (f32[128,512]{1,0:T(8,128)}, f32[128,512]{1,0:T(8,128)S(1)}, u32[]{:S(2)}) copy-start(f32[128,512]{1,0:T(8,128)S(1)} %get-tuple-element.60) | copy-start | bytes 786436
  11.8 15.1 %collective-permute-start.2 = (bf16[128,1024]{1,0:T(8,128)(2,1)S(1)}, bf16[128,1024]{1,0:T(8,128)(2,1)S(1)}, u32[]{:S(2)}, u32[]{:S(2)}) collective-permute-start(bf16[128,1024]{1,0:T(8,128)(2,1)S(1)} %multiply_convert_fusion), channel_id=1, source_target_pairs={{4,3},{3,4},{1,6},{6,1},{0,0},{5,5},{2,2},{7,7},{12,11},{11,12},{9... | collective-permute-start | bytes 786440 | tf_op jit(solution)/shard_map/ppermute | solution.py:425
  15.1 12.1 %collective-permute-start.1 = (bf16[128,1024]{1,0:T(8,128)(2,1)S(1)}, bf16[128,1024]{1,0:T(8,128)(2,1)S(1)}, u32[]{:S(2)}, u32[]{:S(2)}) collective-permute-start(bf16[128,1024]{1,0:T(8,128)(2,1)S(1)} %multiply_convert_fusion), channel_id=1, source_target_pairs={{0,2},{1,0},{2,4},{3,6},{4,1},{5,7},{6,3},{7,5},{8,10},{9,8},{10,1... | collective-permute-start | bytes 786440 | tf_op jit(solution)/shard_map/ppermute | solution.py:425
  15.1 6.9 %collective-permute-start = (s32[4]{0:T(128)S(1)}, s32[4]{0:T(128)S(1)}, u32[]{:S(2)}, u32[]{:S(2)}) collective-permute-start(s32[4]{0:T(128)S(1)} %bitcast.44), channel_id=1, source_target_pairs={{0,4},{4,0},{8,12},{12,8},{16,20},{20,16},{24,28},{28,24},{1,5},{5... | collective-permute-start | bytes 56 | tf_op jit(solution)/shard_map/ppermute | solution.py:422
  21.5 5.6 %collective-permute-start.5 = (bf16[128,1024]{1,0:T(8,128)(2,1)S(1)}, bf16[128,1024]{1,0:T(8,128)(2,1)S(1)}, u32[]{:S(2)}, u32[]{:S(2)}) collective-permute-start(bf16[128,1024]{1,0:T(8,128)(2,1)S(1)} %collective-permute-done.3.g0), channel_id=1, source_target_pairs={{0,4},{4,0},{8,12},{12,8},{16,20},{20,16},{24,28},{28,24},{1,5},{5... | collective-permute-start | bytes 786440 | tf_op jit(solution)/shard_map/ppermute | solution.py:422
  21.5 5.6 %collective-permute-start.6 = (bf16[128,1024]{1,0:T(8,128)(2,1)S(1)}, bf16[128,1024]{1,0:T(8,128)(2,1)S(1)}, u32[]{:S(2)}, u32[]{:S(2)}) collective-permute-start(bf16[128,1024]{1,0:T(8,128)(2,1)S(1)} %collective-permute-done.4.g1), channel_id=1, source_target_pairs={{0,4},{4,0},{8,12},{12,8},{16,20},{20,16},{24,28},{28,24},{1,5},{5... | collective-permute-start | bytes 786440 | tf_op jit(solution)/shard_map/ppermute | solution.py:422
  24.9 1.2 %copy-start = (bf16[768,1024]{1,0:T(8,128)(2,1)}, bf16[768,1024]{1,0:T(8,128)(2,1)S(1)}, u32[]{:S(2)}) copy-start(bf16[768,1024]{1,0:T(8,128)(2,1)S(1)} %get-tuple-element.35.weight) | copy-start | bytes 4718596
  26.1 0.8 %copy-start.1 = (bf16[1024,256]{1,0:T(8,128)(2,1)}, bf16[1024,256]{1,0:T(8,128)(2,1)S(1)}, u32[]{:S(2)}) copy-start(bf16[1024,256]{1,0:T(8,128)(2,1)S(1)} %get-tuple-element.34.weight_out) | copy-start | bytes 1572868
  27.1 1.5 %collective-permute-start.7 = (bf16[128,1024]{1,0:T(8,128)(2,1)S(1)}, bf16[128,1024]{1,0:T(8,128)(2,1)S(1)}, u32[]{:S(2)}, u32[]{:S(2)}) collective-permute-start(bf16[128,1024]{1,0:T(8,128)(2,1)S(1)} %collective-permute-done.1.t0), channel_id=1, source_target_pairs={{0,4},{4,0},{8,12},{12,8},{16,20},{20,16},{24,28},{28,24},{1,5},{5... | collective-permute-start | bytes 786440 | tf_op jit(solution)/shard_map/ppermute | solution.py:422
  27.1 1.9 %collective-permute-start.8 = (bf16[128,1024]{1,0:T(8,128)(2,1)S(1)}, bf16[128,1024]{1,0:T(8,128)(2,1)S(1)}, u32[]{:S(2)}, u32[]{:S(2)}) collective-permute-start(bf16[128,1024]{1,0:T(8,128)(2,1)S(1)} %collective-permute-done.2.t1), channel_id=1, source_target_pairs={{0,4},{4,0},{8,12},{12,8},{16,20},{20,16},{24,28},{28,24},{1,5},{5... | collective-permute-start | bytes 786440 | tf_op jit(solution)/shard_map/ppermute | solution.py:422
  39.1 16.2 %collective-permute-start.12 = (bf16[2,2,512,128]{3,2,1,0:T(8,128)(2,1)S(1)}, bf16[2,2,512,128]{3,2,1,0:T(8,128)(2,1)S(1)}, u32[]{:S(2)}, u32[]{:S(2)}) collective-permute-start(bf16[2,2,512,128]{3,2,1,0:T(8,128)(2,1)S(1)} %get-tuple-element.41), channel_id=1, source_target_pairs={{0,8},{4,12},{8,0},{12,4},{16,24},{20,28},{24,16},{28,20},{1,9},{5... | collective-permute-start | bytes 1572872 | tf_op jit(solution)/shard_map/ppermute | solution.py:422
  40.4 2.9 %collective-permute-start.9 = (bf16[768,256]{1,0:T(8,128)(2,1)S(1)}, bf16[768,256]{1,0:T(8,128)(2,1)S(1)}, u32[]{:S(2)}, u32[]{:S(2)}) collective-permute-start(bf16[768,256]{1,0:T(8,128)(2,1)S(1)} %get-tuple-element.37), channel_id=1, source_target_pairs={{0,4},{4,0},{8,12},{12,8},{16,20},{20,16},{24,28},{28,24},{1,5},{5... | collective-permute-start | bytes 1179656 | tf_op jit(solution)/shard_map/ppermute | solution.py:422
  40.8 14.9 %collective-permute-start.13 = (bf16[2,2,512,128]{3,2,1,0:T(8,128)(2,1)S(1)}, bf16[2,2,512,128]{3,2,1,0:T(8,128)(2,1)S(1)}, u32[]{:S(2)}, u32[]{:S(2)}) collective-permute-start(bf16[2,2,512,128]{3,2,1,0:T(8,128)(2,1)S(1)} %get-tuple-element.43), channel_id=1, source_target_pairs={{0,16},{4,20},{8,24},{12,28},{16,0},{20,4},{24,8},{28,12},{1,17},{... | collective-permute-start | bytes 1572872 | tf_op jit(solution)/shard_map/ppermute | solution.py:422
  43.3 12.0 %copy-start.9 = (f32[2,2,512,128]{3,2,1,0:T(8,128)S(1)}, f32[2,2,512,128]{3,2,1,0:T(8,128)}, u32[]{:S(2)}) copy-start(f32[2,2,512,128]{3,2,1,0:T(8,128)} %get-tuple-element.40) | copy-start | bytes 3145732
  47.0 8.7 %copy-start.8 = (f32[2,2,512,128]{3,2,1,0:T(8,128)S(1)}, f32[2,2,512,128]{3,2,1,0:T(8,128)}, u32[]{:S(2)}) copy-start(f32[2,2,512,128]{3,2,1,0:T(8,128)} %get-tuple-element.42) | copy-start | bytes 3145732
  47.0 10.3 %collective-permute-start.10 = (bf16[128,1024]{1,0:T(8,128)(2,1)S(1)}, bf16[128,1024]{1,0:T(8,128)(2,1)S(1)}, u32[]{:S(2)}, u32[]{:S(2)}) collective-permute-start(bf16[128,1024]{1,0:T(8,128)(2,1)S(1)} %get-tuple-element.38), channel_id=1, source_target_pairs={{2,0},{0,1},{4,2},{6,3},{1,4},{7,5},{3,6},{5,7},{10,8},{8,9},{12,1... | collective-permute-start | bytes 786440 | tf_op jit(solution)/shard_map/ppermute | solution.py:511
  52.1 10.0 %collective-permute-start.11 = (bf16[128,1024]{1,0:T(8,128)(2,1)S(1)}, bf16[128,1024]{1,0:T(8,128)(2,1)S(1)}, u32[]{:S(2)}, u32[]{:S(2)}) collective-permute-start(bf16[128,1024]{1,0:T(8,128)(2,1)S(1)} %get-tuple-element.39), channel_id=1, source_target_pairs={{4,3},{3,4},{1,6},{6,1},{0,0},{5,5},{2,2},{7,7},{12,11},{11,12},{9... | collective-permute-start | bytes 786440 | tf_op jit(solution)/shard_map/ppermute | solution.py:512
  55.3 6.8 %copy-start.3 = (f32[128,512]{1,0:T(8,128)S(1)}, f32[128,512]{1,0:T(8,128)}, u32[]{:S(2)}) copy-start(f32[128,512]{1,0:T(8,128)} %copy-done.2) | copy-start | bytes 786436
  55.3 6.7 %copy-start.5 = (f32[128,512]{1,0:T(8,128)S(1)}, f32[128,512]{1,0:T(8,128)}, u32[]{:S(2)}) copy-start(f32[128,512]{1,0:T(8,128)} %copy-done.4) | copy-start | bytes 786436
  55.3 6.7 %copy-start.7 = (bf16[1,128,1024]{2,1,0:T(8,128)(2,1)S(1)}, bf16[1,128,1024]{2,1,0:T(8,128)(2,1)}, u32[]{:S(2)}) copy-start(bf16[1,128,1024]{2,1,0:T(8,128)(2,1)} %param.8) | copy-start | bytes 786436
  55.4 7.1 %collective-permute-start.14 = (bf16[2,512,128]{2,1,0:T(8,128)(2,1)S(1)}, bf16[2,512,128]{2,1,0:T(8,128)(2,1)S(1)}, u32[]{:S(2)}, u32[]{:S(2)}) collective-permute-start(bf16[2,512,128]{2,1,0:T(8,128)(2,1)S(1)} %get-tuple-element.53), channel_id=1, source_target_pairs={{0,16},{4,20},{8,24},{12,28},{16,0},{20,4},{24,8},{28,12},{1,17},{... | collective-permute-start | bytes 786440 | tf_op jit(solution)/shard_map/ppermute | solution.py:422
  55.7 13.2 %copy-start.10 = (bf16[1,128,1024]{2,1,0:T(8,128)(2,1)S(1)}, bf16[1,128,1024]{2,1,0:T(8,128)(2,1)}, u32[]{:S(2)}) copy-start(bf16[1,128,1024]{2,1,0:T(8,128)(2,1)} %param.14) | copy-start | bytes 786436
  55.9 8.4 %collective-permute-start.15 = (bf16[2,512,128]{2,1,0:T(8,128)(2,1)S(1)}, bf16[2,512,128]{2,1,0:T(8,128)(2,1)S(1)}, u32[]{:S(2)}, u32[]{:S(2)}) collective-permute-start(bf16[2,512,128]{2,1,0:T(8,128)(2,1)S(1)} %get-tuple-element.51), channel_id=1, source_target_pairs={{0,8},{4,12},{8,0},{12,4},{16,24},{20,28},{24,16},{28,20},{1,9},{5... | collective-permute-start | bytes 786440 | tf_op jit(solution)/shard_map/ppermute | solution.py:422
  64.3 5.6 %collective-permute-start.16 = (bf16[1024,128]{1,0:T(8,128)(2,1)S(1)}, bf16[1024,128]{1,0:T(8,128)(2,1)S(1)}, u32[]{:S(2)}, u32[]{:S(2)}) collective-permute-start(bf16[1024,128]{1,0:T(8,128)(2,1)S(1)} %get-tuple-element.46), channel_id=1, source_target_pairs={{0,4},{5,1},{1,0},{4,5},{2,6},{7,3},{3,2},{6,7},{8,12},{13,9},{9,8... | collective-permute-start | bytes 786440 | tf_op jit(solution)/shard_map/ppermute | solution.py:530
  64.9 9.0 %collective-permute-start.17 = (bf16[1024,128]{1,0:T(8,128)(2,1)S(1)}, bf16[1024,128]{1,0:T(8,128)(2,1)S(1)}, u32[]{:S(2)}, u32[]{:S(2)}) collective-permute-start(bf16[1024,128]{1,0:T(8,128)(2,1)S(1)} %get-tuple-element.48), channel_id=1, source_target_pairs={{1,4},{4,1},{3,6},{6,3},{9,12},{12,9},{11,14},{14,11},{17,20},{20,... | collective-permute-start | bytes 786440 | tf_op jit(solution)/shard_map/ppermute | solution.py:531

commit v4 on v3

--- a/solution.py
+++ b/solution.py
@@ -2,6 +2,7 @@
 
 import jax
 import jax.numpy as jnp
+import numpy as np
 from jax import lax
 from jax.experimental import pallas as pl
 from jax.experimental.pallas import tpu as pltpu
@@ -226,18 +227,50 @@
     return lax.dot_general(left, right, (((0,), (0,)), ((), ())), preferred_element_type=jnp.float32)
 
 
-def valid_slots(info, capacity, axis, total):
-    shape = (total, 1) if axis == 0 else (1, total)
-    slot = lax.broadcasted_iota(jnp.int32, shape, axis)
-    limit = info[0] + jnp.zeros(shape, jnp.int32)
-    for block in range(1, total // capacity):
-        limit = jnp.where(slot >= block * capacity, block * capacity + info[block], limit)
-    return slot < limit
-
-
-def weight_kernel(info, w_out, w_qkv, own_out, own_qkv, sems):
+def gather_matrix(sizes, capacity, rows):
+    total = len(sizes) * capacity
+    slot = lax.broadcasted_iota(jnp.int32, (1, total), 1)
+    limit = jnp.zeros((1, total), jnp.int32)
+    shift = jnp.zeros((1, total), jnp.int32)
+    start = 0
+    for block, size in enumerate(sizes):
+        later = slot >= block * capacity
+        limit = jnp.where(later, block * capacity + size, limit)
+        shift = jnp.where(later, start - block * capacity, shift)
+        start = start + size
+    rank = jnp.where(slot < limit, slot + shift, -1)
+    row = lax.broadcasted_iota(jnp.int32, (rows, total), 0)
+    return jnp.where(row == rank, 1.0, 0.0).astype(jnp.bfloat16)
+
+
+def layer_norm_kernel(places, inputs, ln_gain, freqs, normed):
+    rows, features = inputs.shape
+    place = jnp.broadcast_to(places[...].astype(jnp.float32), (rows, rows)).T
+    angle = jnp.concatenate([place] * (features // 2 // rows), axis=1) * freqs[...]
+    shifted = inputs[...].astype(jnp.float32) + jnp.concatenate([jnp.sin(angle), jnp.cos(angle)], axis=1)
+    centred = shifted - jnp.mean(shifted, axis=1, keepdims=True)
+    inv_std = lax.rsqrt(jnp.mean(centred * centred, axis=1, keepdims=True) + EPSILON)
+    normed[...] = (centred * inv_std * ln_gain[...]).astype(normed.dtype)
+
+
+def lift_kernel(info, g0, g1, g2, g3, weight_out, gathered, lifted, rows_g, sems):
+    capacity = g0.shape[0]
+    copies = [
+        pltpu.make_async_copy(source, rows_g.at[pl.ds(block * capacity, capacity), :], sems.at[block])
+        for block, source in enumerate((g0, g1, g2, g3))
+    ]
+    for copy in copies:
+        copy.start()
+    matrix = gather_matrix([info[block] for block in range(4)], capacity, gathered.shape[0])
+    for copy in copies:
+        copy.wait()
+    gathered[...] = nn(matrix, rows_g[...]).astype(gathered.dtype)
+    lifted[...] = nn(gathered[...], weight_out[...]).T.astype(lifted.dtype)
+
+
+def weight_kernel(place, w_out, w_qkv, own_out, own_qkv, sems):
     width = own_out.shape[1]
-    group = pl.multiple_of(info[4] * width, width)
+    group = pl.multiple_of(place[0] * width, width)
     copies = [pltpu.make_async_copy(w_out.at[:, pl.ds(group, width)], own_out, sems.at[3])]
     for part in range(3):
         copies.append(
@@ -254,50 +287,28 @@
 
 
 def main_kernel(
-    info, t0, t1, t2, t3, g0, g1, g2, g3, weight_out, weight,
-    x_send, x_keep, y_send, y_keep, grads_here, grads_there,
-    rows_t, rows_g, lifted, query, key, value, stack,
-    x_send_buf, x_keep_buf, y_send_buf, y_keep_buf, in_sems, out_sems,
+    info, t0, t1, t2, t3, gathered_g, lifted, weight,
+    x_send, x_keep, y_send, y_keep, grads,
+    rows_t, gathered_t, query, key, value, stack,
 ):
     capacity = t0.shape[0]
-    total = rows_t.shape[0]
     width = lifted.shape[0]
     lanes = width // 2
     low = jnp.bfloat16
     scale = HEAD_DIM ** (-0.5)
 
-    loads = []
+    matrix = gather_matrix([info[block] for block in range(4)], capacity, gathered_t.shape[0])
     for block, source in enumerate((t0, t1, t2, t3)):
-        loads.append(
-            pltpu.make_async_copy(
-                source, rows_t.at[pl.ds(block * capacity, capacity), :], in_sems.at[block]
-            )
-        )
-    for block, source in enumerate((g0, g1, g2, g3)):
-        loads.append(
-            pltpu.make_async_copy(
-                source, rows_g.at[pl.ds(block * capacity, capacity), :], in_sems.at[4 + block]
-            )
-        )
-    for copy in loads:
-        copy.start()
-    for copy in loads[:4]:
-        copy.wait()
-    query[...] = (nt(weight[0:width, :], rows_t[...]).astype(low) * scale).astype(low)
-    key[...] = nt(weight[width : 2 * width, :], rows_t[...]).astype(low)
-    value[...] = nt(weight[2 * width : 3 * width, :], rows_t[...]).astype(low)
-    for copy in loads[4:]:
-        copy.wait()
-    up = nn(rows_g[...], weight_out[...])
-    up = jnp.where(valid_slots(info, capacity, 0, total), up, 0.0)
-    lifted[...] = up.T.astype(low)
-
-    bias = jnp.where(valid_slots(info, capacity, 0, total), 0.0, MASKED)
-    row_ok = valid_slots(info, capacity, 1, total)
+        rows_t[pl.ds(block * capacity, capacity), :] = source[...]
+    gathered_t[...] = nn(matrix, rows_t[...]).astype(low)
+    query[...] = (nt(weight[0:width, :], gathered_t[...]).astype(low) * scale).astype(low)
+    key[...] = nt(weight[width : 2 * width, :], gathered_t[...]).astype(low)
+    value[...] = nt(weight[2 * width : 3 * width, :], gathered_t[...]).astype(low)
+
     for head in range(width // HEAD_DIM):
         span = pl.ds(head * HEAD_DIM, HEAD_DIM)
         query_h, key_h, value_h, lifted_h = query[span, :], key[span, :], value[span, :], lifted[span, :]
-        scores = tn(key_h, query_h) + bias
+        scores = tn(key_h, query_h)
         expo = jnp.exp(scores - jnp.max(scores, axis=0, keepdims=True))
         probs = expo * (1.0 / jnp.sum(expo, axis=0, keepdims=True))
         probs_low = probs.astype(low)
@@ -307,27 +318,16 @@
         stack[pl.ds(head * HEAD_DIM, HEAD_DIM), :] = (nn(key_h, score_grad) * scale).astype(low)
         stack[pl.ds(width + head * HEAD_DIM, HEAD_DIM), :] = nt(query_h, score_grad).astype(low)
         stack[pl.ds(2 * width + head * HEAD_DIM, HEAD_DIM), :] = nt(lifted_h, probs_low).astype(low)
-        stack[pl.ds(3 * width + head * HEAD_DIM, HEAD_DIM), :] = jnp.where(
-            row_ok, attended, 0.0
-        ).astype(low)
-
-    stores = [
-        pltpu.make_async_copy(
-            stack.at[pl.ds(0, 3 * width), pl.ds(part * (total // 2), total // 2)],
-            (grads_here, grads_there)[part],
-            out_sems.at[part],
-        )
-        for part in range(2)
-    ]
-    for copy in stores:
-        copy.start()
-    for step, (slot_y, slot_x) in enumerate(((0, 0), (1, 0), (0, 1), (1, 1))):
+        stack[pl.ds(3 * width + head * HEAD_DIM, HEAD_DIM), :] = attended.astype(low)
+
+    grads[...] = stack[0 : 3 * width, :]
+    for slot_y, slot_x in ((0, 0), (1, 0), (0, 1), (1, 1)):
         block = (info[5] ^ slot_y) * 2 + (info[6] ^ slot_x)
         cols = pl.ds(pl.multiple_of(block * width, width), width)
-        term_t = nn(stack[0 : 3 * width, :], rows_t[:, cols])
-        term_g = nn(stack[3 * width : 4 * width, :], rows_g[:, cols]).T
-        x_target, x_out = (x_send_buf, x_send) if slot_x else (x_keep_buf, x_keep)
-        y_target, y_out = (y_send_buf, y_send) if slot_y else (y_keep_buf, y_keep)
+        term_t = nn(stack[0 : 3 * width, :], gathered_t[:, cols])
+        term_g = nn(stack[3 * width : 4 * width, :], gathered_g[:, cols]).T
+        x_target = x_send if slot_x else x_keep
+        y_target = y_send if slot_y else y_keep
         for side in range(2):
             across = slice(side * lanes, (side + 1) * lanes)
             spot = info[7] ^ side
@@ -337,42 +337,38 @@
                 y_target[slot_x, spot, width + part * lanes : width + (part + 1) * lanes, :] = term_g[
                     across, part * lanes : (part + 1) * lanes
                 ].astype(y_target.dtype)
-        for part, (target, out, index) in enumerate(((x_target, x_out, slot_y), (y_target, y_out, slot_x))):
-            copy = pltpu.make_async_copy(target.at[index], out.at[index], out_sems.at[2 + 2 * step + part])
-            copy.start()
-            stores.append(copy)
-    for copy in stores:
-        copy.wait()
-
-
-def normed_kernel(info, here, there, w_qkv, back_one, back_two, grads, weight, sems):
-    width = here.shape[0] // 3
+
+
+def normed_kernel(info, own, other, w_qkv, back_one, back_two, weight, sems):
+    width = own.shape[0] // 3
+    rows = own.shape[1]
     capacity = back_one.shape[0]
     first = pl.multiple_of((info[4] >> 1) * 2 * width, 2 * width)
     core = info[4] & 1
-    loads = []
-    for part in range(3):
-        loads.append(
-            pltpu.make_async_copy(
-                w_qkv.at[part, pl.ds(first, 2 * width), :],
-                weight.at[pl.ds(part * 2 * width, 2 * width), :],
-                sems.at[part],
-            )
-        )
-        for place, source, spot in ((0, here, core), (1, there, 1 - core)):
-            loads.append(
-                pltpu.make_async_copy(
-                    source.at[pl.ds(part * width, width), :],
-                    grads.at[pl.ds(pl.multiple_of((part * 2 + spot) * width, width), width), :],
-                    sems.at[3 + part * 2 + place],
-                )
-            )
+    loads = [
+        pltpu.make_async_copy(
+            w_qkv.at[part, pl.ds(first, 2 * width), :],
+            weight.at[pl.ds(part * 2 * width, 2 * width), :],
+            sems.at[part],
+        )
+        for part in range(3)
+    ]
     for copy in loads:
         copy.start()
-    for copy in loads:
-        copy.wait()
-    back_one[...] = tn(grads[:, 0:capacity], weight[...]).astype(back_one.dtype)
-    back_two[...] = tn(grads[:, capacity : 2 * capacity], weight[...]).astype(back_two.dtype)
+    half = 2 * capacity
+    mine = gather_matrix([info[block] for block in range(4)], capacity, rows)[:, 0:half]
+    theirs = gather_matrix([info[(block + 2) % 4] for block in range(4)], capacity, rows)[:, half:]
+    own_grads = nn(own[...], mine).astype(own.dtype)
+    other_grads = nn(other[...], theirs).astype(own.dtype)
+    total = jnp.zeros((half, weight.shape[1]), jnp.float32)
+    for part in range(3):
+        loads[part].wait()
+        span = slice(part * width, (part + 1) * width)
+        for grads, spot in ((own_grads, core), (other_grads, 1 - core)):
+            place = pl.ds(pl.multiple_of((part * 2 + spot) * width, width), width)
+            total = total + tn(grads[span, :], weight[place, :])
+    back_one[...] = total[0:capacity].astype(back_one.dtype)
+    back_two[...] = total[capacity:half].astype(back_two.dtype)
 
 
 def sum_kernel(x_part, y_part, x_second, y_second, home_send, guest_send, own):
@@ -390,7 +386,8 @@
 
 
 VMEM_BYTES = 50 * 1024 * 1024
-MAIN_BYTES = 50 * 1024 * 1024
+MAIN_BYTES = 28 * 1024 * 1024
+FULL_BYTES = 60 * 1024 * 1024
 
 
 def column_shards(tokens, positions, counts, ln_gain, w_qkv, w_out, d_out):
@@ -422,26 +419,28 @@
         return lax.ppermute(array, "dp", [(i, i ^ bit) for i in range(2 * chips)])
 
     def fetch(array):
-        return lax.ppermute(array, axes, first), lax.ppermute(array, axes, second)
+        two = lax.ppermute(array, axes, second)
+        return lax.ppermute(array, axes, first), two
 
     def share(pair):
         return pair + (across(pair[0], 1), across(pair[1], 1))
 
-    other_counts = across(counts[0], 1)
-    blocks_g = share(fetch(upstream))
-    normed, standard, inv_std = layer_norm(inputs, positions[0], ln_gain)
-    fetched_t = fetch(normed)
-
-    sizes = jnp.where(resident, counts[0], other_counts)
-    table = jnp.array(block_table(), jnp.int32)
-    order = jnp.concatenate([table[seat * 2 + core], table[seat * 2 + 1 - core]])
     group = (seat >> 1) * 2 + core
-    info = jnp.concatenate(
-        [sizes[order], jnp.stack([group, place_y, place_x, core ^ 1 ^ guest]).astype(jnp.int32)]
-    )
-
+    place = jnp.stack([group, place_y, place_x, core ^ 1 ^ guest]).astype(jnp.int32)
     params = pltpu.CompilerParams(vmem_limit_bytes=VMEM_BYTES)
     smem = specs(pltpu.SMEM, 1)
+
+    fetched_g = fetch(upstream)
+    other_counts = across(counts[0], 1)
+    steps = np.arange(features // 2, dtype=np.float32) * np.float32(-math.log(10000.0) / (features // 2))
+    normed = pl.pallas_call(
+        layer_norm_kernel,
+        out_shape=jax.ShapeDtypeStruct((capacity, features), low),
+        in_specs=specs(pltpu.VMEM, 4),
+        out_specs=pl.BlockSpec(memory_space=pltpu.VMEM),
+        compiler_params=pltpu.CompilerParams(vmem_limit_bytes=FULL_BYTES),
+    )(positions, inputs, ln_gain[None], jnp.asarray(np.exp(steps)[None]))
+    fetched_t = fetch(normed)
     own_out, own_qkv = pl.pallas_call(
         weight_kernel,
         out_shape=(
@@ -453,34 +452,55 @@
         scratch_shapes=[pltpu.SemaphoreType.DMA((4,))],
         compiler_params=params,
         cost_estimate=pl.CostEstimate(flops=0, bytes_accessed=4 * 1024 * 1024, transcendentals=0),
-    )(info, w_out, w_qkv)
-    fetched_t, blocks_g, own_out, own_qkv = lax.optimization_barrier((fetched_t, blocks_g, own_out, own_qkv))
+    )(place, w_out, w_qkv)
+    _, standard, inv_std = layer_norm(inputs, positions[0], ln_gain)
+    own_valid = jnp.arange(capacity, dtype=jnp.int32) < lax.dynamic_index_in_dim(counts[0], seat, 0, False)
+    masked_grad = jnp.where(own_valid[:, None], upstream, jnp.zeros_like(upstream))
+
+    sizes = jnp.where(resident, counts[0], other_counts)
+    table = jnp.array(block_table(), jnp.int32)
+    order = jnp.concatenate([table[seat * 2 + core], table[seat * 2 + 1 - core]])
+    info = jnp.concatenate([sizes[order], place])
+
+    fetched_g, info, own_out, own_qkv, masked_grad = lax.optimization_barrier(
+        (fetched_g, info, own_out, own_qkv, masked_grad)
+    )
+    blocks_g = share(fetched_g)
+    fetched_t, blocks_g = lax.optimization_barrier((fetched_t, blocks_g))
+    rows = 3 * total // 4
+    gathered_g, lifted = pl.pallas_call(
+        lift_kernel,
+        out_shape=(
+            jax.ShapeDtypeStruct((rows, features), low),
+            jax.ShapeDtypeStruct((width, rows), low),
+        ),
+        in_specs=smem + specs(pl.ANY, 4) + specs(pltpu.VMEM, 1),
+        out_specs=specs(pltpu.VMEM, 2),
+        scratch_shapes=[pltpu.VMEM((total, features), low), pltpu.SemaphoreType.DMA((4,))],
+        compiler_params=pltpu.CompilerParams(vmem_limit_bytes=MAIN_BYTES),
+        cost_estimate=pl.CostEstimate(
+            flops=2 * rows * features * (width + total), bytes_accessed=3 * 1024 * 1024, transcendentals=0
+        ),
+    )(info, *blocks_g, own_out)
     blocks_t = share(fetched_t)
 
     send_shape = jax.ShapeDtypeStruct((2, 2, 2 * width, lanes), low)
     keep_shape = jax.ShapeDtypeStruct((2, 2, 2 * width, lanes), wide)
-    grads_shape = jax.ShapeDtypeStruct((3 * width, half), low)
-    x_send, x_keep, y_send, y_keep, grads_here, grads_there = pl.pallas_call(
+    grads_shape = jax.ShapeDtypeStruct((3 * width, rows), low)
+    x_send, x_keep, y_send, y_keep, grads = pl.pallas_call(
         main_kernel,
         out_shape=(
-            send_shape, keep_shape, send_shape, keep_shape, grads_shape, grads_shape
-        ),
-        in_specs=smem + specs(pl.ANY, 8) + specs(pltpu.VMEM, 2),
-        out_specs=specs(pltpu.HBM, 6),
+            send_shape, keep_shape, send_shape, keep_shape, grads_shape
+        ),
+        in_specs=smem + specs(pltpu.VMEM, 7),
+        out_specs=specs(pltpu.VMEM, 5),
         scratch_shapes=[
             pltpu.VMEM((total, features), low),
-            pltpu.VMEM((total, features), low),
-            pltpu.VMEM((width, total), low),
-            pltpu.VMEM((width, total), low),
-            pltpu.VMEM((width, total), low),
-            pltpu.VMEM((width, total), low),
-            pltpu.VMEM((4 * width, total), low),
-            pltpu.VMEM(send_shape.shape, low),
-            pltpu.VMEM(send_shape.shape, wide),
-            pltpu.VMEM(send_shape.shape, low),
-            pltpu.VMEM(send_shape.shape, wide),
-            pltpu.SemaphoreType.DMA((8,)),
-            pltpu.SemaphoreType.DMA((10,)),
+            pltpu.VMEM((rows, features), low),
+            pltpu.VMEM((width, rows), low),
+            pltpu.VMEM((width, rows), low),
+            pltpu.VMEM((width, rows), low),
+            pltpu.VMEM((4 * width, rows), low),
         ],
         compiler_params=pltpu.CompilerParams(vmem_limit_bytes=MAIN_BYTES),
         cost_estimate=pl.CostEstimate(
@@ -488,27 +508,27 @@
             bytes_accessed=8 * 1024 * 1024,
             transcendentals=4 * total * total,
         ),
-    )(info, *blocks_t, *blocks_g, own_out, own_qkv)
+    )(info, *blocks_t, gathered_g, lifted, own_qkv)
 
     x_first, y_first = across(x_send, 2), across(y_send, 4)
-    from_core = across(grads_there, 1)
+    from_core = across(grads, 1)
     block_shape = jax.ShapeDtypeStruct((capacity, features), low)
     back_one, back_two = pl.pallas_call(
         normed_kernel,
         out_shape=(block_shape, block_shape),
-        in_specs=smem + specs(pl.ANY, 2) + specs(pltpu.HBM, 1),
+        in_specs=smem + specs(pltpu.VMEM, 2) + specs(pl.ANY, 1),
         out_specs=specs(pltpu.VMEM, 2),
         scratch_shapes=[
-            pltpu.VMEM((6 * width, half), low),
             pltpu.VMEM((6 * width, features), low),
-            pltpu.SemaphoreType.DMA((9,)),
+            pltpu.SemaphoreType.DMA((3,)),
         ],
         compiler_params=params,
         cost_estimate=pl.CostEstimate(
             flops=2 * total * features * width * 3, bytes_accessed=4 * 1024 * 1024, transcendentals=0
         ),
-    )(info, grads_here, from_core, w_qkv)
+    )(info, grads, from_core, w_qkv)
     home_one = lax.ppermute(back_one, axes, first_back)
+    x_first, y_first, home_one, back_two = lax.optimization_barrier((x_first, y_first, home_one, back_two))
     home_two = lax.ppermute(back_two, axes, second)
     x_second = across((x_keep[1] + x_first[1].astype(wide)).astype(low), 4)
     y_second = across((y_keep[1] + y_first[1].astype(wide)).astype(low), 2)
@@ -540,8 +560,6 @@
     )
 
     normed_grad = home_one.astype(wide) + home_two.astype(wide)
-    own_valid = jnp.arange(capacity, dtype=jnp.int32) < lax.dynamic_index_in_dim(counts[0], seat, 0, False)
-    masked_grad = jnp.where(own_valid[:, None], upstream, jnp.zeros_like(upstream))
     unit_grad = normed_grad * ln_gain
     inner = unit_grad - jnp.mean(unit_grad, axis=1, keepdims=True)
     inner = inner - standard * jnp.mean(unit_grad * standard, axis=1, keepdims=True)

time: 75.8 us -> 72.3 us (0.954)
  waiting for transfers between devices: 18.1 us -> 15.3 us
  starting transfers between devices: 27.6 us -> 30 us
  local copies, waits for them, and re-layouts: 4.79 us -> 2.82 us
  other arithmetic: 8.01 us -> 6.15 us
  Pallas kernels: 15.9 us -> 16.8 us
    ppermute x1, waiting for transfers between devices: 4.67 us -> 0.01 us  [column_shards(): home_two = lax.ppermute(back_two, axes, second)]
    pallas_call x0 -> x2, Pallas kernels: none -> 4.61 us  [the longest x1 2.89 us: column_shards(): pl.pallas_call(layer_norm_kernel, out_shape=jax.ShapeDtypeStruct((capacit...]
    pallas_call x1, Pallas kernels: 10.1 us -> 6.64 us  [column_shards(): pl.pallas_call(main_kernel, out_shape=(send_shape, keep_shape, send_shape...]
    unnamed x26 -> x8, local copies, waits for them, and re-layouts: 2.05 us -> 0.02 us
    ppermute x1, starting transfers between devices: 0.6 us -> 2.57 us  [column_shards(): from_home = lax.ppermute(home_send, axes, home)]
    ppermute x1, waiting for transfers between devices: 0.53 us -> 2.19 us  [column_shards(): home_one = lax.ppermute(back_one, axes, first_back)]
    ppermute x1, starting transfers between devices: 3.19 us -> 4.59 us  [column_shards(): home_two = lax.ppermute(back_two, axes, second)]
    ppermute x1, starting transfers between devices: 5.04 us -> 3.75 us  [column_shards(): home_one = lax.ppermute(back_one, axes, first_back)]
  transfers between devices with their start and end apart: 18 -> 18, of which waited for: 9 -> 7; matrix products, arithmetic and copies ran while one was open for 12% -> 10% of each run, Pallas kernels for 8% -> 14%
where the time goes in v4:
time: 72.3 us; the launch traced here: 72 us
  starting transfers between devices  30 us (41%)
  Pallas kernels  16.8 us (23%)
  waiting for transfers between devices  15.3 us (21%)
  other arithmetic  6.15 us (9%)
  local copies, waits for them, and re-layouts  2.82 us (4%)
  between operations  0.88 us (1%)
    ppermute x2, starting transfers between devices, fetch(): two = lax.ppermute(array, axes, second)  6.75 us
    pallas_call x1, Pallas kernels, column_shards(): pl.pallas_call(main_kernel, out_shape=(send_shape, keep_shape, send_shape...  6.64 us
    ppermute x2, waiting for transfers between devices, fetch(): return (lax.ppermute(array, axes, first), two)  5.72 us
    ppermute x1, starting transfers between devices, column_shards(): home_two = lax.ppermute(back_two, axes, second)  4.59 us
    ppermute x10, starting transfers between devices, across(): return lax.ppermute(array, 'dp', [(i, i ^ bit) for i in range(2 * chips)])  4.54 us
    ppermute x1, starting transfers between devices, column_shards(): from_guest = lax.ppermute(guest_send, axes, guests)  4.2 us
    ppermute x10, waiting for transfers between devices, across(): return lax.ppermute(array, 'dp', [(i, i ^ bit) for i in range(2 * chips)])  3.75 us
    ppermute x1, starting transfers between devices, column_shards(): home_one = lax.ppermute(back_one, axes, first_back)  3.75 us
  transfers between devices with their start and end apart: 18, of which 7 were waited for; matrix products, arithmetic and copies ran while one was open for 10% of the time, Pallas kernels for 14%

profile of v4, /device:TPU:1, one launch (start us, length us, event | category | flops | bytes accessed | tf_op | source)
XLA Modules:
  0.0 72.0 jit_solution(372433876044801495)
XLA Ops:
  0.6 2.7 %collective-permute-start = (bf16[128,1024]{1,0:T(8,128)(2,1)}, bf16[128,1024]{1,0:T(8,128)(2,1)S(1)}, u32[]{:S(2)}, u32[]{:S(2)}) collective-permute-start(bf16[128,1024]{1,0:T(8,128)(2,1)} %bitcast.41), channel_id=1, source_target_pairs={{0,2},{1,0},{2,4},{3,6},{4,1},{5,7},{6,3},{7,5},{8,10},{9,8},{10,1... | collective-permute-start | bytes 786440 | tf_op jit(solution)/shard_map/ppermute | solution.py:423
  3.4 3.9 %collective-permute-start.1 = (bf16[128,1024]{1,0:T(8,128)(2,1)}, bf16[128,1024]{1,0:T(8,128)(2,1)S(1)}, u32[]{:S(2)}, u32[]{:S(2)}) collective-permute-start(bf16[128,1024]{1,0:T(8,128)(2,1)} %bitcast.42), channel_id=1, source_target_pairs={{4,3},{3,4},{1,6},{6,1},{0,0},{5,5},{2,2},{7,7},{12,11},{11,12},{9... | collective-permute-start | bytes 786440 | tf_op jit(solution)/shard_map/ppermute | solution.py:422
  7.3 2.9 %shard_map.113 = bf16[128,1024]{1,0:T(8,128)(2,1)} custom-call(s32[1,128]{1,0:T(1,128)} %places.1, bf16[128,1024]{1,0:T(8,128)(2,1)} %bitcast.39, f32[1,1024]{1,0:T(1,128)} %bitcast.43, f32[1,512]{1,0:T(1,128)} %constant.46.clone.freqs), custom_call_target="tpu_custom_call" | custom-call | tf_op jit(solution)/shard_map/pallas_call | solution.py:436
  10.2 0.8 %collective-permute-start.3 = (bf16[128,1024]{1,0:T(8,128)(2,1)}, bf16[128,1024]{1,0:T(8,128)(2,1)S(1)}, u32[]{:S(2)}, u32[]{:S(2)}) collective-permute-start(bf16[128,1024]{1,0:T(8,128)(2,1)} %shard_map.113), channel_id=1, source_target_pairs={{0,2},{1,0},{2,4},{3,6},{4,1},{5,7},{6,3},{7,5},{8,10},{9,8},{10,1... | collective-permute-start | bytes 786440 | tf_op jit(solution)/shard_map/ppermute | solution.py:423
  11.0 2.8 %collective-permute-start.4 = (bf16[128,1024]{1,0:T(8,128)(2,1)}, bf16[128,1024]{1,0:T(8,128)(2,1)S(1)}, u32[]{:S(2)}, u32[]{:S(2)}) collective-permute-start(bf16[128,1024]{1,0:T(8,128)(2,1)} %shard_map.113), channel_id=1, source_target_pairs={{4,3},{3,4},{1,6},{6,1},{0,0},{5,5},{2,2},{7,7},{12,11},{11,12},{9... | collective-permute-start | bytes 786440 | tf_op jit(solution)/shard_map/ppermute | solution.py:422
  13.8 0.1 collective-permute-start.2
  13.9 0.8 %fusion.4 = (s32[2,1]{0,1:T(1,128)S(1)}, s32[2,1]{0,1:T(1,128)S(1)}) fusion(s32[8,2]{1,0:T(8,128)} %constant.47.clone, s32[]{:T(128)S(6)} %select_n.54, s32[]{:T(128)S(6)} %select_n.55), kind=kLoop, calls=%fused_computation.28 | loop fusion | bytes 40 | tf_op jit(solution)/shard_map/concatenate | solution.py:462
  14.7 0.1 fusion.6
  14.8 1.3 %constant_dynamic-slice_fusion = s32[1,1]{1,0:T(1,128)} fusion(s32[1,4]{1,0:T(1,128)} %param.11, s32[]{:T(128)S(6)} %select_n.57), kind=kLoop, calls=%fused_computation.25 | loop fusion | bytes 12 | tf_op jit(solution)/shard_map/jit(dynamic_index_in_dim)/dynamic_slice | solution.py:457
  16.1 0.6 iota_compare_fusion
  16.7 1.0 %broadcast_select_fusion = bf16[128,1024]{1,0:T(8,128)(2,1)S(1)} fusion(pred[128]{0:T(512)(128)(4,1)S(1)} %iota_compare_fusion, bf16[1,128,1024]{2,1,0:T(8,128)(2,1)} %param.15), kind=kLoop, calls=%fused_computation.16 | loop fusion | flops 131072 | bytes 524416 | tf_op jit(solution)/shard_map/jit(_where)/select_n | solution.py:458
  17.8 0.1 pad_add_fusion.place
  17.9 2.1 %shard_map.112 = (bf16[1024,256]{1,0:T(8,128)(2,1)S(1)}, bf16[768,1024]{1,0:T(8,128)(2,1)S(1)}) custom-call(s32[4]{0:T(128)S(1)} %pad_add_fusion.place, bf16[1024,1024]{1,0:T(8,128)(2,1)} %w_out.1, bf16[3,1024,1024]{2,1,0:T(8,128)(2,1)} %w_qkv.3), custom_call_target="tpu_custom_call" | custom-call | bytes 4194304 | tf_op jit(solution)/shard_map/pallas_call | solution.py:444
  20.0 0.6 gather_fusion
  20.7 0.1 concatenate.39.info
  20.7 0.5 collective-permute-start.5
  21.3 0.1 collective-permute-start.6
  21.4 5.7 %collective-permute-done.3.t0 = bf16[128,1024]{1,0:T(8,128)(2,1)S(1)} collective-permute-done((bf16[128,1024]{1,0:T(8,128)(2,1)}, bf16[128,1024]{1,0:T(8,128)(2,1)S(1)}, u32[]{:S(2)}, u32[]{:S(2)}) %collective-permute-start.3) | collective-permute-done | bytes 262176 | tf_op jit(solution)/shard_map/ppermute | solution.py:423
  27.1 0.1 collective-permute-start.7
  27.2 0.5 collective-permute-start.8
  27.7 1.7 %shard_map.114 = (bf16[384,1024]{1,0:T(8,128)(2,1)S(1)}, bf16[256,384]{1,0:T(8,128)(2,1)S(1)}) custom-call(s32[8]{0:T(128)S(1)} %concatenate.39.info, bf16[128,1024]{1,0:T(8,128)(2,1)S(1)} %collective-permute-done.g0, bf16[128,1024]{1,0:T(8,128)(2,1)S(1)} %collective-permute-done.1.g1, bf16[128,1024]{1,0:T(8,128)(2,1)S(1)} %collective-permute-done.5.g2, ...), custom_call_target="tpu_custom_call" | custom-call | flops 603979776 | bytes 3145728 | tf_op jit(solution)/shard_map/pallas_call | solution.py:471
  29.4 6.6 %shard_map.115 = (bf16[2,2,512,128]{3,2,1,0:T(8,128)(2,1)S(1)}, f32[2,2,512,128]{3,2,1,0:T(8,128)S(1)}, bf16[2,2,512,128]{3,2,1,0:T(8,128)(2,1)S(1)}, f32[2,2,512,128]{3,2,1,0:T(8,128)S(1)}, bf16[768,384]{1,0:T(8,128)(2,1)S(1)}) custom-call(s32[8]{0:T(128)S(1)} %concatenate.39.info, bf16[128,1024]{1,0:T(8,128)(2,1)S(1)} %collective-permute-done.3.t0, ...), custom_call_target="tpu_custom_call" | custom-call | flops 2684354560 | bytes 8388608 | tf_op jit(solution)/shard_map/pallas_call | solution.py:490
  36.1 0.1 collective-permute-start.11
  36.3 1.3 %collective-permute-start.10 = (bf16[2,2,512,128]{3,2,1,0:T(8,128)(2,1)S(1)}, bf16[2,2,512,128]{3,2,1,0:T(8,128)(2,1)S(1)}, u32[]{:S(2)}, u32[]{:S(2)}) collective-permute-start(bf16[2,2,512,128]{3,2,1,0:T(8,128)(2,1)S(1)} %get-tuple-element.52), channel_id=1, source_target_pairs={{0,16},{4,20},{8,24},{12,28},{16,0},{20,4},{24,8},{28,12},{1,17},{... | collective-permute-start | bytes 1572872 | tf_op jit(solution)/shard_map/ppermute | solution.py:419
  37.6 1.2 %collective-permute-start.9 = (bf16[2,2,512,128]{3,2,1,0:T(8,128)(2,1)S(1)}, bf16[2,2,512,128]{3,2,1,0:T(8,128)(2,1)S(1)}, u32[]{:S(2)}, u32[]{:S(2)}) collective-permute-start(bf16[2,2,512,128]{3,2,1,0:T(8,128)(2,1)S(1)} %get-tuple-element.51), channel_id=1, source_target_pairs={{0,8},{4,12},{8,0},{12,4},{16,24},{20,28},{24,16},{28,20},{1,9},{5... | collective-permute-start | bytes 1572872 | tf_op jit(solution)/shard_map/ppermute | solution.py:419
  38.8 1.0 %multiply_sine_fusion = (f32[128,512]{1,0:T(8,128)S(1)}, f32[128,512]{1,0:T(8,128)S(1)}) fusion(f32[512]{0:T(512)S(1)} %multiply_exponential_fusion, f32[128]{0:T(128)S(1)} %convert_bitcast_fusion), kind=kLoop, calls=%fused_computation.13 | loop fusion | flops 65536 | bytes 526848 | tf_op jit(solution)/shard_map/sin | solution.py:22
  39.8 3.4 %shard_map.116 = (bf16[128,1024]{1,0:T(8,128)(2,1)S(1)}, bf16[128,1024]{1,0:T(8,128)(2,1)S(1)}) custom-call(s32[8]{0:T(128)S(1)} %concatenate.39.info, bf16[768,384]{1,0:T(8,128)(2,1)S(1)} %get-tuple-element.53.own, bf16[768,384]{1,0:T(8,128)(2,1)S(1)} %collective-permute-done.11.other, bf16[3,1024,1024]{2,1,0:T(8,128)(2,1)} %w_qkv.3), custom_call_target="tpu_custom_call" | custom-call | flops 805306368 | bytes 4194304 | tf_op jit(solution)/shard_map/pallas_call | solution.py:516
  43.2 3.7 %collective-permute-start.12 = (bf16[128,1024]{1,0:T(8,128)(2,1)S(1)}, bf16[128,1024]{1,0:T(8,128)(2,1)S(1)}, u32[]{:S(2)}, u32[]{:S(2)}) collective-permute-start(bf16[128,1024]{1,0:T(8,128)(2,1)S(1)} %get-tuple-element.54), channel_id=1, source_target_pairs={{2,0},{0,1},{4,2},{6,3},{1,4},{7,5},{3,6},{5,7},{10,8},{8,9},{12,1... | collective-permute-start | bytes 786440 | tf_op jit(solution)/shard_map/ppermute | solution.py:530
  46.9 0.1 fusion.7
  47.1 2.3 %collective-permute-done.10 = bf16[2,2,512,128]{3,2,1,0:T(8,128)(2,1)S(1)} collective-permute-done((bf16[2,2,512,128]{3,2,1,0:T(8,128)(2,1)S(1)}, bf16[2,2,512,128]{3,2,1,0:T(8,128)(2,1)S(1)}, u32[]{:S(2)}, u32[]{:S(2)}) %collective-permute-start.10) | collective-permute-done | bytes 524320 | tf_op jit(solution)/shard_map/ppermute | solution.py:419
  49.4 0.9 %collective-permute-done.9 = bf16[2,2,512,128]{3,2,1,0:T(8,128)(2,1)S(1)} collective-permute-done((bf16[2,2,512,128]{3,2,1,0:T(8,128)(2,1)S(1)}, bf16[2,2,512,128]{3,2,1,0:T(8,128)(2,1)S(1)}, u32[]{:S(2)}, u32[]{:S(2)}) %collective-permute-start.9) | collective-permute-done | bytes 524320 | tf_op jit(solution)/shard_map/ppermute | solution.py:419
  50.3 2.2 %collective-permute-done.12 = bf16[128,1024]{1,0:T(8,128)(2,1)S(1)} collective-permute-done((bf16[128,1024]{1,0:T(8,128)(2,1)S(1)}, bf16[128,1024]{1,0:T(8,128)(2,1)S(1)}, u32[]{:S(2)}, u32[]{:S(2)}) %collective-permute-start.12) | collective-permute-done | bytes 262176 | tf_op jit(solution)/shard_map/ppermute | solution.py:530
  52.5 0.1 fusion.2
  52.6 0.3 collective-permute-start.15
  52.9 0.1 fusion.1
  53.0 0.3 collective-permute-start.14
  53.3 4.6 %collective-permute-start.13 = (bf16[128,1024]{1,0:T(8,128)(2,1)S(1)}, bf16[128,1024]{1,0:T(8,128)(2,1)S(1)}, u32[]{:S(2)}, u32[]{:S(2)}) collective-permute-start(bf16[128,1024]{1,0:T(8,128)(2,1)S(1)} %get-tuple-element.57), channel_id=1, source_target_pairs={{4,3},{3,4},{1,6},{6,1},{0,0},{5,5},{2,2},{7,7},{12,11},{11,12},{9... | collective-permute-start | bytes 786440 | tf_op jit(solution)/shard_map/ppermute | solution.py:532
  57.9 0.2 multiply_reduce_fusion.1
  58.1 0.4 collective-permute-done.15.y_second
  58.5 0.1 collective-permute-done.14.x_second
  58.6 0.1 shard_map.117
  58.7 2.6 %collective-permute-start.16 = (bf16[1024,128]{1,0:T(8,128)(2,1)S(1)}, bf16[1024,128]{1,0:T(8,128)(2,1)S(1)}, u32[]{:S(2)}, u32[]{:S(2)}) collective-permute-start(bf16[1024,128]{1,0:T(8,128)(2,1)S(1)} %get-tuple-element.64), channel_id=1, source_target_pairs={{0,4},{5,1},{1,0},{4,5},{2,6},{7,3},{3,2},{6,7},{8,12},{13,9},{9,8... | collective-permute-start | bytes 786440 | tf_op jit(solution)/shard_map/ppermute | solution.py:550
  61.3 4.2 %collective-permute-start.17 = (bf16[1024,128]{1,0:T(8,128)(2,1)S(1)}, bf16[1024,128]{1,0:T(8,128)(2,1)S(1)}, u32[]{:S(2)}, u32[]{:S(2)}) collective-permute-start(bf16[1024,128]{1,0:T(8,128)(2,1)S(1)} %get-tuple-element.66), channel_id=1, source_target_pairs={{1,4},{4,1},{3,6},{6,3},{9,12},{12,9},{11,14},{14,11},{17,20},{20,... | collective-permute-start | bytes 786440 | tf_op jit(solution)/shard_map/ppermute | solution.py:551
  65.5 0.3 fusion
  65.8 1.0 %fusion.3 = bf16[1,128,1024]{2,1,0:T(8,128)(2,1)} fusion(f32[128]{0:T(128)S(1)} %get-tuple-element.79, f32[128]{0:T(128)S(1)} %broadcast_multiply_fusion.2, f32[128]{0:T(128)S(1)} %get-tuple-element.80, f32[1024]{0:T(1024)S(1)} %copy-done.1, bf16[128,1024]{1,0:T(8,128)(2,1)S(1)} %collective-permute-done.13, ...), kind=kLoop, calls=%fused_computation.17 | loop fusion | flops 2097152 | bytes 1841152 | tf_op jit(solution)/shard_map/broadcast_in_dim | solution.py:567
  66.8 3.6 %collective-permute-done.17 = bf16[1024,128]{1,0:T(8,128)(2,1)S(1)} collective-permute-done((bf16[1024,128]{1,0:T(8,128)(2,1)S(1)}, bf16[1024,128]{1,0:T(8,128)(2,1)S(1)}, u32[]{:S(2)}, u32[]{:S(2)}) %collective-permute-start.17) | collective-permute-done | bytes 262176 | tf_op jit(solution)/shard_map/ppermute | solution.py:551
  70.5 0.7 pad_maximum_fusion
  71.2 0.8 %add_multiply_fusion.1 = f32[768,128]{1,0:T(8,128)} fusion(f32[1024,128]{1,0:T(8,128)S(1)} %get-tuple-element.65, bf16[1024,128]{1,0:T(8,128)(2,1)S(1)} %collective-permute-done.17, bf16[1024,128]{1,0:T(8,128)(2,1)S(1)} %collective-permute-done.16, pred[]{:T(512)S(6)} %eq.3), kind=kLoop, calls=%fused_computation.11 | loop fusion | flops 491520 | bytes 1179649 | tf_op jit(solution)/shard_map/mul | solution.py:555
  (27 shorter events, 0.1 us)
Async XLA Ops:
  0.6 20.1 %collective-permute-start = (bf16[128,1024]{1,0:T(8,128)(2,1)}, bf16[128,1024]{1,0:T(8,128)(2,1)S(1)}, u32[]{:S(2)}, u32[]{:S(2)}) collective-permute-start(bf16[128,1024]{1,0:T(8,128)(2,1)} %bitcast.41), channel_id=1, source_target_pairs={{0,2},{1,0},{2,4},{3,6},{4,1},{5,7},{6,3},{7,5},{8,10},{9,8},{10,1... | collective-permute-start | bytes 786440 | tf_op jit(solution)/shard_map/ppermute | solution.py:423
  3.4 17.4 %collective-permute-start.1 = (bf16[128,1024]{1,0:T(8,128)(2,1)}, bf16[128,1024]{1,0:T(8,128)(2,1)S(1)}, u32[]{:S(2)}, u32[]{:S(2)}) collective-permute-start(bf16[128,1024]{1,0:T(8,128)(2,1)} %bitcast.42), channel_id=1, source_target_pairs={{4,3},{3,4},{1,6},{6,1},{0,0},{5,5},{2,2},{7,7},{12,11},{11,12},{9... | collective-permute-start | bytes 786440 | tf_op jit(solution)/shard_map/ppermute | solution.py:422
  10.2 16.9 %collective-permute-start.3 = (bf16[128,1024]{1,0:T(8,128)(2,1)}, bf16[128,1024]{1,0:T(8,128)(2,1)S(1)}, u32[]{:S(2)}, u32[]{:S(2)}) collective-permute-start(bf16[128,1024]{1,0:T(8,128)(2,1)} %shard_map.113), channel_id=1, source_target_pairs={{0,2},{1,0},{2,4},{3,6},{4,1},{5,7},{6,3},{7,5},{8,10},{9,8},{10,1... | collective-permute-start | bytes 786440 | tf_op jit(solution)/shard_map/ppermute | solution.py:423
  11.0 16.1 %collective-permute-start.4 = (bf16[128,1024]{1,0:T(8,128)(2,1)}, bf16[128,1024]{1,0:T(8,128)(2,1)S(1)}, u32[]{:S(2)}, u32[]{:S(2)}) collective-permute-start(bf16[128,1024]{1,0:T(8,128)(2,1)} %shard_map.113), channel_id=1, source_target_pairs={{4,3},{3,4},{1,6},{6,1},{0,0},{5,5},{2,2},{7,7},{12,11},{11,12},{9... | collective-permute-start | bytes 786440 | tf_op jit(solution)/shard_map/ppermute | solution.py:422
  13.8 6.1 %collective-permute-start.2 = (s32[4]{0:T(128)}, s32[4]{0:T(128)S(1)}, u32[]{:S(2)}, u32[]{:S(2)}) collective-permute-start(s32[4]{0:T(128)} %bitcast.44), channel_id=1, source_target_pairs={{0,4},{4,0},{8,12},{12,8},{16,20},{20,16},{24,28},{28,24},{1,5},{5... | collective-permute-start | bytes 56 | tf_op jit(solution)/shard_map/ppermute | solution.py:419
  17.9 2.1 %copy-start.3 = (s32[1,4]{1,0:T(1,128)S(1)}, s32[1,4]{1,0:T(1,128)}, u32[]{:S(2)}) copy-start(s32[1,4]{1,0:T(1,128)} %param.11) | copy-start | bytes 52
  20.7 6.3 %collective-permute-start.5 = (bf16[128,1024]{1,0:T(8,128)(2,1)S(1)}, bf16[128,1024]{1,0:T(8,128)(2,1)S(1)}, u32[]{:S(2)}, u32[]{:S(2)}) collective-permute-start(bf16[128,1024]{1,0:T(8,128)(2,1)S(1)} %collective-permute-done.g0), channel_id=1, source_target_pairs={{0,4},{4,0},{8,12},{12,8},{16,20},{20,16},{24,28},{28,24},{1,5},{5... | collective-permute-start | bytes 786440 | tf_op jit(solution)/shard_map/ppermute | solution.py:419
  21.3 5.8 %collective-permute-start.6 = (bf16[128,1024]{1,0:T(8,128)(2,1)S(1)}, bf16[128,1024]{1,0:T(8,128)(2,1)S(1)}, u32[]{:S(2)}, u32[]{:S(2)}) collective-permute-start(bf16[128,1024]{1,0:T(8,128)(2,1)S(1)} %collective-permute-done.1.g1), channel_id=1, source_target_pairs={{0,4},{4,0},{8,12},{12,8},{16,20},{20,16},{24,28},{28,24},{1,5},{5... | collective-permute-start | bytes 786440 | tf_op jit(solution)/shard_map/ppermute | solution.py:419
  27.1 2.3 %collective-permute-start.7 = (bf16[128,1024]{1,0:T(8,128)(2,1)S(1)}, bf16[128,1024]{1,0:T(8,128)(2,1)S(1)}, u32[]{:S(2)}, u32[]{:S(2)}) collective-permute-start(bf16[128,1024]{1,0:T(8,128)(2,1)S(1)} %collective-permute-done.3.t0), channel_id=1, source_target_pairs={{0,4},{4,0},{8,12},{12,8},{16,20},{20,16},{24,28},{28,24},{1,5},{5... | collective-permute-start | bytes 786440 | tf_op jit(solution)/shard_map/ppermute | solution.py:419
  27.2 2.2 %collective-permute-start.8 = (bf16[128,1024]{1,0:T(8,128)(2,1)S(1)}, bf16[128,1024]{1,0:T(8,128)(2,1)S(1)}, u32[]{:S(2)}, u32[]{:S(2)}) collective-permute-start(bf16[128,1024]{1,0:T(8,128)(2,1)S(1)} %collective-permute-done.4.t1), channel_id=1, source_target_pairs={{0,4},{4,0},{8,12},{12,8},{16,20},{20,16},{24,28},{28,24},{1,5},{5... | collective-permute-start | bytes 786440 | tf_op jit(solution)/shard_map/ppermute | solution.py:419
  29.4 6.8 %copy-start.2 = (s32[1,128]{1,0:T(1,128)S(1)}, s32[1,128]{1,0:T(1,128)}, u32[]{:S(2)}) copy-start(s32[1,128]{1,0:T(1,128)} %places.1) | copy-start | bytes 1540
  36.1 3.7 %collective-permute-start.11 = (bf16[768,384]{1,0:T(8,128)(2,1)S(1)}, bf16[768,384]{1,0:T(8,128)(2,1)S(1)}, u32[]{:S(2)}, u32[]{:S(2)}) collective-permute-start(bf16[768,384]{1,0:T(8,128)(2,1)S(1)} %get-tuple-element.53.own), channel_id=1, source_target_pairs={{0,4},{4,0},{8,12},{12,8},{16,20},{20,16},{24,28},{28,24},{1,5},{5... | collective-permute-start | bytes 1769480 | tf_op jit(solution)/shard_map/ppermute | solution.py:419
  36.3 13.1 %collective-permute-start.10 = (bf16[2,2,512,128]{3,2,1,0:T(8,128)(2,1)S(1)}, bf16[2,2,512,128]{3,2,1,0:T(8,128)(2,1)S(1)}, u32[]{:S(2)}, u32[]{:S(2)}) collective-permute-start(bf16[2,2,512,128]{3,2,1,0:T(8,128)(2,1)S(1)} %get-tuple-element.52), channel_id=1, source_target_pairs={{0,16},{4,20},{8,24},{12,28},{16,0},{20,4},{24,8},{28,12},{1,17},{... | collective-permute-start | bytes 1572872 | tf_op jit(solution)/shard_map/ppermute | solution.py:419
  37.6 12.8 %collective-permute-start.9 = (bf16[2,2,512,128]{3,2,1,0:T(8,128)(2,1)S(1)}, bf16[2,2,512,128]{3,2,1,0:T(8,128)(2,1)S(1)}, u32[]{:S(2)}, u32[]{:S(2)}) collective-permute-start(bf16[2,2,512,128]{3,2,1,0:T(8,128)(2,1)S(1)} %get-tuple-element.51), channel_id=1, source_target_pairs={{0,8},{4,12},{8,0},{12,4},{16,24},{20,28},{24,16},{28,20},{1,9},{5... | collective-permute-start | bytes 1572872 | tf_op jit(solution)/shard_map/ppermute | solution.py:419
  39.8 7.2 %copy-start = (bf16[1,128,1024]{2,1,0:T(8,128)(2,1)S(1)}, bf16[1,128,1024]{2,1,0:T(8,128)(2,1)}, u32[]{:S(2)}) copy-start(bf16[1,128,1024]{2,1,0:T(8,128)(2,1)} %param.9) | copy-start | bytes 786436
  43.2 9.3 %collective-permute-start.12 = (bf16[128,1024]{1,0:T(8,128)(2,1)S(1)}, bf16[128,1024]{1,0:T(8,128)(2,1)S(1)}, u32[]{:S(2)}, u32[]{:S(2)}) collective-permute-start(bf16[128,1024]{1,0:T(8,128)(2,1)S(1)} %get-tuple-element.54), channel_id=1, source_target_pairs={{2,0},{0,1},{4,2},{6,3},{1,4},{7,5},{3,6},{5,7},{10,8},{8,9},{12,1... | collective-permute-start | bytes 786440 | tf_op jit(solution)/shard_map/ppermute | solution.py:530
  52.6 5.9 %collective-permute-start.15 = (bf16[2,512,128]{2,1,0:T(8,128)(2,1)S(1)}, bf16[2,512,128]{2,1,0:T(8,128)(2,1)S(1)}, u32[]{:S(2)}, u32[]{:S(2)}) collective-permute-start(bf16[2,512,128]{2,1,0:T(8,128)(2,1)S(1)} %get-tuple-element.69), channel_id=1, source_target_pairs={{0,8},{4,12},{8,0},{12,4},{16,24},{20,28},{24,16},{28,20},{1,9},{5... | collective-permute-start | bytes 786440 | tf_op jit(solution)/shard_map/ppermute | solution.py:419
  52.9 12.6 %copy-start.1 = (f32[1024]{0:T(1024)S(1)}, f32[1024]{0:T(1024)}, u32[]{:S(2)}) copy-start(f32[1024]{0:T(1024)} %param.12) | copy-start | bytes 12292
  53.0 5.6 %collective-permute-start.14 = (bf16[2,512,128]{2,1,0:T(8,128)(2,1)S(1)}, bf16[2,512,128]{2,1,0:T(8,128)(2,1)S(1)}, u32[]{:S(2)}, u32[]{:S(2)}) collective-permute-start(bf16[2,512,128]{2,1,0:T(8,128)(2,1)S(1)} %get-tuple-element.71), channel_id=1, source_target_pairs={{0,16},{4,20},{8,24},{12,28},{16,0},{20,4},{24,8},{28,12},{1,17},{... | collective-permute-start | bytes 786440 | tf_op jit(solution)/shard_map/ppermute | solution.py:419
  53.3 12.2 %collective-permute-start.13 = (bf16[128,1024]{1,0:T(8,128)(2,1)S(1)}, bf16[128,1024]{1,0:T(8,128)(2,1)S(1)}, u32[]{:S(2)}, u32[]{:S(2)}) collective-permute-start(bf16[128,1024]{1,0:T(8,128)(2,1)S(1)} %get-tuple-element.57), channel_id=1, source_target_pairs={{4,3},{3,4},{1,6},{6,1},{0,0},{5,5},{2,2},{7,7},{12,11},{11,12},{9... | collective-permute-start | bytes 786440 | tf_op jit(solution)/shard_map/ppermute | solution.py:532
  58.7 8.1 %collective-permute-start.16 = (bf16[1024,128]{1,0:T(8,128)(2,1)S(1)}, bf16[1024,128]{1,0:T(8,128)(2,1)S(1)}, u32[]{:S(2)}, u32[]{:S(2)}) collective-permute-start(bf16[1024,128]{1,0:T(8,128)(2,1)S(1)} %get-tuple-element.64), channel_id=1, source_target_pairs={{0,4},{5,1},{1,0},{4,5},{2,6},{7,3},{3,2},{6,7},{8,12},{13,9},{9,8... | collective-permute-start | bytes 786440 | tf_op jit(solution)/shard_map/ppermute | solution.py:550
  61.3 9.2 %collective-permute-start.17 = (bf16[1024,128]{1,0:T(8,128)(2,1)S(1)}, bf16[1024,128]{1,0:T(8,128)(2,1)S(1)}, u32[]{:S(2)}, u32[]{:S(2)}) collective-permute-start(bf16[1024,128]{1,0:T(8,128)(2,1)S(1)} %get-tuple-element.66), channel_id=1, source_target_pairs={{1,4},{4,1},{3,6},{6,3},{9,12},{12,9},{11,14},{14,11},{17,20},{20,... | collective-permute-start | bytes 786440 | tf_op jit(solution)/shard_map/ppermute | solution.py:551

commit v5 on v4

--- a/solution.py
+++ b/solution.py
@@ -453,7 +453,6 @@
         compiler_params=params,
         cost_estimate=pl.CostEstimate(flops=0, bytes_accessed=4 * 1024 * 1024, transcendentals=0),
     )(place, w_out, w_qkv)
-    _, standard, inv_std = layer_norm(inputs, positions[0], ln_gain)
     own_valid = jnp.arange(capacity, dtype=jnp.int32) < lax.dynamic_index_in_dim(counts[0], seat, 0, False)
     masked_grad = jnp.where(own_valid[:, None], upstream, jnp.zeros_like(upstream))
 
@@ -527,6 +526,8 @@
             flops=2 * total * features * width * 3, bytes_accessed=4 * 1024 * 1024, transcendentals=0
         ),
     )(info, grads, from_core, w_qkv)
+    places, back_one = lax.optimization_barrier((positions, back_one))
+    _, standard, inv_std = layer_norm(inputs, places[0], ln_gain)
     home_one = lax.ppermute(back_one, axes, first_back)
     x_first, y_first, home_one, back_two = lax.optimization_barrier((x_first, y_first, home_one, back_two))
     home_two = lax.ppermute(back_two, axes, second)

time: 72.3 us -> 71.3 us (0.986)
  waiting for transfers between devices: 15.3 us -> 13.8 us
    ppermute x1, waiting for transfers between devices: 2.19 us -> 1.21 us  [column_shards(): home_one = lax.ppermute(back_one, axes, first_back)]
    ppermute x1, starting transfers between devices: 2.57 us -> 1.63 us  [column_shards(): from_home = lax.ppermute(home_send, axes, home)]
    ppermute x10, starting transfers between devices: 4.54 us -> 5.33 us  [across(): return lax.ppermute(array, 'dp', [(i, i ^ bit) for i in range(2 * chips)])]
  transfers between devices with their start and end apart: 18 -> 18, of which waited for: 7 -> 5; matrix products, arithmetic and copies ran while one was open for 10% -> 10% of each run, Pallas kernels for 14% -> 14%
where the time goes in v5:
time: 71.3 us; the launch traced here: 70.9 us
  starting transfers between devices  30.4 us (43%)
  Pallas kernels  16.8 us (24%)
  waiting for transfers between devices  13.8 us (19%)
  other arithmetic  6.15 us (9%)
  local copies, waits for them, and re-layouts  2.81 us (4%)
  between operations  0.87 us (1%)
    ppermute x2, starting transfers between devices, fetch(): two = lax.ppermute(array, axes, second)  6.75 us
    pallas_call x1, Pallas kernels, column_shards(): pl.pallas_call(main_kernel, out_shape=(send_shape, keep_shape, send_shape...  6.65 us
    ppermute x2, waiting for transfers between devices, fetch(): return (lax.ppermute(array, axes, first), two)  5.72 us
    ppermute x10, starting transfers between devices, across(): return lax.ppermute(array, 'dp', [(i, i ^ bit) for i in range(2 * chips)])  5.33 us
    ppermute x1, starting transfers between devices, column_shards(): home_two = lax.ppermute(back_two, axes, second)  4.82 us
    ppermute x1, starting transfers between devices, column_shards(): from_guest = lax.ppermute(guest_send, axes, guests)  4.55 us
    ppermute x1, starting transfers between devices, column_shards(): home_one = lax.ppermute(back_one, axes, first_back)  3.74 us
    ppermute x1, waiting for transfers between devices, column_shards(): from_guest = lax.ppermute(guest_send, axes, guests)  3.64 us
  transfers between devices with their start and end apart: 18, of which 5 were waited for; matrix products, arithmetic and copies ran while one was open for 10% of the time, Pallas kernels for 14%

profile of v5, /device:TPU:1, one launch (start us, length us, event | category | flops | bytes accessed | tf_op | source)
XLA Modules:
  0.0 70.9 jit_solution(16774984268521037304)
XLA Ops:
  0.6 2.7 %collective-permute-start = (bf16[128,1024]{1,0:T(8,128)(2,1)}, bf16[128,1024]{1,0:T(8,128)(2,1)S(1)}, u32[]{:S(2)}, u32[]{:S(2)}) collective-permute-start(bf16[128,1024]{1,0:T(8,128)(2,1)} %bitcast.41), channel_id=1, source_target_pairs={{0,2},{1,0},{2,4},{3,6},{4,1},{5,7},{6,3},{7,5},{8,10},{9,8},{10,1... | collective-permute-start | bytes 786440 | tf_op jit(solution)/shard_map/ppermute | solution.py:423
  3.4 3.9 %collective-permute-start.1 = (bf16[128,1024]{1,0:T(8,128)(2,1)}, bf16[128,1024]{1,0:T(8,128)(2,1)S(1)}, u32[]{:S(2)}, u32[]{:S(2)}) collective-permute-start(bf16[128,1024]{1,0:T(8,128)(2,1)} %bitcast.42), channel_id=1, source_target_pairs={{4,3},{3,4},{1,6},{6,1},{0,0},{5,5},{2,2},{7,7},{12,11},{11,12},{9... | collective-permute-start | bytes 786440 | tf_op jit(solution)/shard_map/ppermute | solution.py:422
  7.3 2.9 %shard_map.113 = bf16[128,1024]{1,0:T(8,128)(2,1)} custom-call(s32[1,128]{1,0:T(1,128)} %places.1, bf16[128,1024]{1,0:T(8,128)(2,1)} %bitcast.39, f32[1,1024]{1,0:T(1,128)} %bitcast.43, f32[1,512]{1,0:T(1,128)} %constant.46.clone.freqs), custom_call_target="tpu_custom_call" | custom-call | tf_op jit(solution)/shard_map/pallas_call | solution.py:436
  10.2 0.8 %collective-permute-start.3 = (bf16[128,1024]{1,0:T(8,128)(2,1)}, bf16[128,1024]{1,0:T(8,128)(2,1)S(1)}, u32[]{:S(2)}, u32[]{:S(2)}) collective-permute-start(bf16[128,1024]{1,0:T(8,128)(2,1)} %shard_map.113), channel_id=1, source_target_pairs={{0,2},{1,0},{2,4},{3,6},{4,1},{5,7},{6,3},{7,5},{8,10},{9,8},{10,1... | collective-permute-start | bytes 786440 | tf_op jit(solution)/shard_map/ppermute | solution.py:423
  11.0 2.8 %collective-permute-start.4 = (bf16[128,1024]{1,0:T(8,128)(2,1)}, bf16[128,1024]{1,0:T(8,128)(2,1)S(1)}, u32[]{:S(2)}, u32[]{:S(2)}) collective-permute-start(bf16[128,1024]{1,0:T(8,128)(2,1)} %shard_map.113), channel_id=1, source_target_pairs={{4,3},{3,4},{1,6},{6,1},{0,0},{5,5},{2,2},{7,7},{12,11},{11,12},{9... | collective-permute-start | bytes 786440 | tf_op jit(solution)/shard_map/ppermute | solution.py:422
  13.8 0.1 collective-permute-start.2
  13.9 0.8 %fusion.4 = (s32[2,1]{0,1:T(1,128)S(1)}, s32[2,1]{0,1:T(1,128)S(1)}) fusion(s32[8,2]{1,0:T(8,128)} %constant.47.clone, s32[]{:T(128)S(6)} %select_n.54, s32[]{:T(128)S(6)} %select_n.55), kind=kLoop, calls=%fused_computation.28 | loop fusion | bytes 40 | tf_op jit(solution)/shard_map/concatenate | solution.py:461
  14.7 0.1 fusion.6
  14.8 1.3 %constant_dynamic-slice_fusion = s32[1,1]{1,0:T(1,128)} fusion(s32[1,4]{1,0:T(1,128)} %param.11, s32[]{:T(128)S(6)} %select_n.57), kind=kLoop, calls=%fused_computation.25 | loop fusion | bytes 12 | tf_op jit(solution)/shard_map/jit(dynamic_index_in_dim)/dynamic_slice | solution.py:456
  16.1 0.6 iota_compare_fusion
  16.7 1.0 %broadcast_select_fusion = bf16[128,1024]{1,0:T(8,128)(2,1)S(1)} fusion(pred[128]{0:T(512)(128)(4,1)S(1)} %iota_compare_fusion, bf16[1,128,1024]{2,1,0:T(8,128)(2,1)} %param.15), kind=kLoop, calls=%fused_computation.16 | loop fusion | flops 131072 | bytes 524416 | tf_op jit(solution)/shard_map/jit(_where)/select_n | solution.py:457
  17.8 0.1 pad_add_fusion.place
  17.9 2.1 %shard_map.112 = (bf16[1024,256]{1,0:T(8,128)(2,1)S(1)}, bf16[768,1024]{1,0:T(8,128)(2,1)S(1)}) custom-call(s32[4]{0:T(128)S(1)} %pad_add_fusion.place, bf16[1024,1024]{1,0:T(8,128)(2,1)} %w_out.1, bf16[3,1024,1024]{2,1,0:T(8,128)(2,1)} %w_qkv.3), custom_call_target="tpu_custom_call" | custom-call | bytes 4194304 | tf_op jit(solution)/shard_map/pallas_call | solution.py:444
  20.0 0.0 collective-permute-done.2
  20.0 0.6 gather_fusion
  20.7 0.1 concatenate.39.info
  20.7 0.0 collective-permute-done.g0
  20.7 0.5 collective-permute-start.5
  21.3 0.1 collective-permute-start.6
  21.4 5.7 %collective-permute-done.3.t0 = bf16[128,1024]{1,0:T(8,128)(2,1)S(1)} collective-permute-done((bf16[128,1024]{1,0:T(8,128)(2,1)}, bf16[128,1024]{1,0:T(8,128)(2,1)S(1)}, u32[]{:S(2)}, u32[]{:S(2)}) %collective-permute-start.3) | collective-permute-done | bytes 262176 | tf_op jit(solution)/shard_map/ppermute | solution.py:423
  27.1 0.1 collective-permute-start.7
  27.2 0.5 collective-permute-start.8
  27.7 1.7 %shard_map.114 = (bf16[384,1024]{1,0:T(8,128)(2,1)S(1)}, bf16[256,384]{1,0:T(8,128)(2,1)S(1)}) custom-call(s32[8]{0:T(128)S(1)} %concatenate.39.info, bf16[128,1024]{1,0:T(8,128)(2,1)S(1)} %collective-permute-done.g0, bf16[128,1024]{1,0:T(8,128)(2,1)S(1)} %collective-permute-done.1.g1, bf16[128,1024]{1,0:T(8,128)(2,1)S(1)} %collective-permute-done.5.g2, ...), custom_call_target="tpu_custom_call" | custom-call | flops 603979776 | bytes 3145728 | tf_op jit(solution)/shard_map/pallas_call | solution.py:470
  29.4 6.6 %shard_map.115 = (bf16[2,2,512,128]{3,2,1,0:T(8,128)(2,1)S(1)}, f32[2,2,512,128]{3,2,1,0:T(8,128)S(1)}, bf16[2,2,512,128]{3,2,1,0:T(8,128)(2,1)S(1)}, f32[2,2,512,128]{3,2,1,0:T(8,128)S(1)}, bf16[768,384]{1,0:T(8,128)(2,1)S(1)}) custom-call(s32[8]{0:T(128)S(1)} %concatenate.39.info, bf16[128,1024]{1,0:T(8,128)(2,1)S(1)} %collective-permute-done.3.t0, ...), custom_call_target="tpu_custom_call" | custom-call | flops 2684354560 | bytes 8388608 | tf_op jit(solution)/shard_map/pallas_call | solution.py:489
  36.1 0.1 collective-permute-start.9
  36.2 1.2 %collective-permute-start.10 = (bf16[2,2,512,128]{3,2,1,0:T(8,128)(2,1)S(1)}, bf16[2,2,512,128]{3,2,1,0:T(8,128)(2,1)S(1)}, u32[]{:S(2)}, u32[]{:S(2)}) collective-permute-start(bf16[2,2,512,128]{3,2,1,0:T(8,128)(2,1)S(1)} %get-tuple-element.56), channel_id=1, source_target_pairs={{0,8},{4,12},{8,0},{12,4},{16,24},{20,28},{24,16},{28,20},{1,9},{5... | collective-permute-start | bytes 1572872 | tf_op jit(solution)/shard_map/ppermute | solution.py:419
  37.5 1.2 %collective-permute-start.11 = (bf16[2,2,512,128]{3,2,1,0:T(8,128)(2,1)S(1)}, bf16[2,2,512,128]{3,2,1,0:T(8,128)(2,1)S(1)}, u32[]{:S(2)}, u32[]{:S(2)}) collective-permute-start(bf16[2,2,512,128]{3,2,1,0:T(8,128)(2,1)S(1)} %get-tuple-element.57), channel_id=1, source_target_pairs={{0,16},{4,20},{8,24},{12,28},{16,0},{20,4},{24,8},{28,12},{1,17},{... | collective-permute-start | bytes 1572872 | tf_op jit(solution)/shard_map/ppermute | solution.py:419
  38.7 3.4 %shard_map.116 = (bf16[128,1024]{1,0:T(8,128)(2,1)S(1)}, bf16[128,1024]{1,0:T(8,128)(2,1)S(1)}) custom-call(s32[8]{0:T(128)S(1)} %concatenate.39.info, bf16[768,384]{1,0:T(8,128)(2,1)S(1)} %get-tuple-element.53.own, bf16[768,384]{1,0:T(8,128)(2,1)S(1)} %collective-permute-done.9.other, bf16[3,1024,1024]{2,1,0:T(8,128)(2,1)} %w_qkv.3), custom_call_target="tpu_custom_call" | custom-call | flops 805306368 | bytes 4194304 | tf_op jit(solution)/shard_map/pallas_call | solution.py:515
  42.1 3.7 %collective-permute-start.12 = (bf16[128,1024]{1,0:T(8,128)(2,1)S(1)}, bf16[128,1024]{1,0:T(8,128)(2,1)S(1)}, u32[]{:S(2)}, u32[]{:S(2)}) collective-permute-start(bf16[128,1024]{1,0:T(8,128)(2,1)S(1)} %get-tuple-element.58), channel_id=1, source_target_pairs={{2,0},{0,1},{4,2},{6,3},{1,4},{7,5},{3,6},{5,7},{10,8},{8,9},{12,1... | collective-permute-start | bytes 786440 | tf_op jit(solution)/shard_map/ppermute | solution.py:531
  45.9 1.0 %multiply_sine_fusion = (f32[128,512]{1,0:T(8,128)S(1)}, f32[128,512]{1,0:T(8,128)S(1)}) fusion(f32[512]{0:T(512)S(1)} %multiply_exponential_fusion, f32[128]{0:T(128)S(1)} %convert_bitcast_fusion), kind=kLoop, calls=%fused_computation.13 | loop fusion | flops 65536 | bytes 526848 | tf_op jit(solution)/shard_map/sin | solution.py:22
  46.9 0.1 fusion.7
  47.0 2.3 %collective-permute-done.10 = bf16[2,2,512,128]{3,2,1,0:T(8,128)(2,1)S(1)} collective-permute-done((bf16[2,2,512,128]{3,2,1,0:T(8,128)(2,1)S(1)}, bf16[2,2,512,128]{3,2,1,0:T(8,128)(2,1)S(1)}, u32[]{:S(2)}, u32[]{:S(2)}) %collective-permute-start.10) | collective-permute-done | bytes 524320 | tf_op jit(solution)/shard_map/ppermute | solution.py:419
  49.3 0.9 %collective-permute-done.11 = bf16[2,2,512,128]{3,2,1,0:T(8,128)(2,1)S(1)} collective-permute-done((bf16[2,2,512,128]{3,2,1,0:T(8,128)(2,1)S(1)}, bf16[2,2,512,128]{3,2,1,0:T(8,128)(2,1)S(1)}, u32[]{:S(2)}, u32[]{:S(2)}) %collective-permute-start.11) | collective-permute-done | bytes 524320 | tf_op jit(solution)/shard_map/ppermute | solution.py:419
  50.2 1.2 %collective-permute-done.12 = bf16[128,1024]{1,0:T(8,128)(2,1)S(1)} collective-permute-done((bf16[128,1024]{1,0:T(8,128)(2,1)S(1)}, bf16[128,1024]{1,0:T(8,128)(2,1)S(1)}, u32[]{:S(2)}, u32[]{:S(2)}) %collective-permute-start.12) | collective-permute-done | bytes 262176 | tf_op jit(solution)/shard_map/ppermute | solution.py:531
  51.4 0.1 fusion.2
  51.5 0.3 collective-permute-start.15
  51.9 0.1 fusion.1
  52.0 1.1 %collective-permute-start.14 = (bf16[2,512,128]{2,1,0:T(8,128)(2,1)S(1)}, bf16[2,512,128]{2,1,0:T(8,128)(2,1)S(1)}, u32[]{:S(2)}, u32[]{:S(2)}) collective-permute-start(bf16[2,512,128]{2,1,0:T(8,128)(2,1)S(1)} %get-tuple-element.75), channel_id=1, source_target_pairs={{0,16},{4,20},{8,24},{12,28},{16,0},{20,4},{24,8},{28,12},{1,17},{... | collective-permute-start | bytes 786440 | tf_op jit(solution)/shard_map/ppermute | solution.py:419
  53.1 4.8 %collective-permute-start.13 = (bf16[128,1024]{1,0:T(8,128)(2,1)S(1)}, bf16[128,1024]{1,0:T(8,128)(2,1)S(1)}, u32[]{:S(2)}, u32[]{:S(2)}) collective-permute-start(bf16[128,1024]{1,0:T(8,128)(2,1)S(1)} %get-tuple-element.61), channel_id=1, source_target_pairs={{4,3},{3,4},{1,6},{6,1},{0,0},{5,5},{2,2},{7,7},{12,11},{11,12},{9... | collective-permute-start | bytes 786440 | tf_op jit(solution)/shard_map/ppermute | solution.py:533
  57.9 0.2 multiply_reduce_fusion.1
  58.1 0.1 shard_map.117
  58.2 1.6 %collective-permute-start.16 = (bf16[1024,128]{1,0:T(8,128)(2,1)S(1)}, bf16[1024,128]{1,0:T(8,128)(2,1)S(1)}, u32[]{:S(2)}, u32[]{:S(2)}) collective-permute-start(bf16[1024,128]{1,0:T(8,128)(2,1)S(1)} %get-tuple-element.68), channel_id=1, source_target_pairs={{0,4},{5,1},{1,0},{4,5},{2,6},{7,3},{3,2},{6,7},{8,12},{13,9},{9,8... | collective-permute-start | bytes 786440 | tf_op jit(solution)/shard_map/ppermute | solution.py:551
  59.9 4.5 %collective-permute-start.17 = (bf16[1024,128]{1,0:T(8,128)(2,1)S(1)}, bf16[1024,128]{1,0:T(8,128)(2,1)S(1)}, u32[]{:S(2)}, u32[]{:S(2)}) collective-permute-start(bf16[1024,128]{1,0:T(8,128)(2,1)S(1)} %get-tuple-element.70), channel_id=1, source_target_pairs={{1,4},{4,1},{3,6},{6,3},{9,12},{12,9},{11,14},{14,11},{17,20},{20,... | collective-permute-start | bytes 786440 | tf_op jit(solution)/shard_map/ppermute | solution.py:552
  64.5 0.3 fusion
  64.7 1.0 %fusion.3 = bf16[1,128,1024]{2,1,0:T(8,128)(2,1)} fusion(f32[128]{0:T(128)S(1)} %get-tuple-element.83, f32[128]{0:T(128)S(1)} %broadcast_multiply_fusion.2, f32[128]{0:T(128)S(1)} %get-tuple-element.84, f32[1024]{0:T(1024)S(1)} %copy-done.1, bf16[128,1024]{1,0:T(8,128)(2,1)S(1)} %collective-permute-done.13, ...), kind=kLoop, calls=%fused_computation.17 | loop fusion | flops 2097152 | bytes 1841152 | tf_op jit(solution)/shard_map/broadcast_in_dim | solution.py:568
  65.7 3.6 %collective-permute-done.17 = bf16[1024,128]{1,0:T(8,128)(2,1)S(1)} collective-permute-done((bf16[1024,128]{1,0:T(8,128)(2,1)S(1)}, bf16[1024,128]{1,0:T(8,128)(2,1)S(1)}, u32[]{:S(2)}, u32[]{:S(2)}) %collective-permute-start.17) | collective-permute-done | bytes 262176 | tf_op jit(solution)/shard_map/ppermute | solution.py:552
  69.4 0.7 pad_maximum_fusion
  70.1 0.8 %add_multiply_fusion.1 = f32[768,128]{1,0:T(8,128)} fusion(f32[1024,128]{1,0:T(8,128)S(1)} %get-tuple-element.69, bf16[1024,128]{1,0:T(8,128)(2,1)S(1)} %collective-permute-done.17, bf16[1024,128]{1,0:T(8,128)(2,1)S(1)} %collective-permute-done.16, pred[]{:T(512)S(6)} %eq.3), kind=kLoop, calls=%fused_computation.11 | loop fusion | flops 491520 | bytes 1179649 | tf_op jit(solution)/shard_map/mul | solution.py:556
  (27 shorter events, 0.1 us)
Async XLA Ops:
  0.6 20.1 %collective-permute-start = (bf16[128,1024]{1,0:T(8,128)(2,1)}, bf16[128,1024]{1,0:T(8,128)(2,1)S(1)}, u32[]{:S(2)}, u32[]{:S(2)}) collective-permute-start(bf16[128,1024]{1,0:T(8,128)(2,1)} %bitcast.41), channel_id=1, source_target_pairs={{0,2},{1,0},{2,4},{3,6},{4,1},{5,7},{6,3},{7,5},{8,10},{9,8},{10,1... | collective-permute-start | bytes 786440 | tf_op jit(solution)/shard_map/ppermute | solution.py:423
  3.4 17.4 %collective-permute-start.1 = (bf16[128,1024]{1,0:T(8,128)(2,1)}, bf16[128,1024]{1,0:T(8,128)(2,1)S(1)}, u32[]{:S(2)}, u32[]{:S(2)}) collective-permute-start(bf16[128,1024]{1,0:T(8,128)(2,1)} %bitcast.42), channel_id=1, source_target_pairs={{4,3},{3,4},{1,6},{6,1},{0,0},{5,5},{2,2},{7,7},{12,11},{11,12},{9... | collective-permute-start | bytes 786440 | tf_op jit(solution)/shard_map/ppermute | solution.py:422
  10.2 16.9 %collective-permute-start.3 = (bf16[128,1024]{1,0:T(8,128)(2,1)}, bf16[128,1024]{1,0:T(8,128)(2,1)S(1)}, u32[]{:S(2)}, u32[]{:S(2)}) collective-permute-start(bf16[128,1024]{1,0:T(8,128)(2,1)} %shard_map.113), channel_id=1, source_target_pairs={{0,2},{1,0},{2,4},{3,6},{4,1},{5,7},{6,3},{7,5},{8,10},{9,8},{10,1... | collective-permute-start | bytes 786440 | tf_op jit(solution)/shard_map/ppermute | solution.py:423
  11.0 16.1 %collective-permute-start.4 = (bf16[128,1024]{1,0:T(8,128)(2,1)}, bf16[128,1024]{1,0:T(8,128)(2,1)S(1)}, u32[]{:S(2)}, u32[]{:S(2)}) collective-permute-start(bf16[128,1024]{1,0:T(8,128)(2,1)} %shard_map.113), channel_id=1, source_target_pairs={{4,3},{3,4},{1,6},{6,1},{0,0},{5,5},{2,2},{7,7},{12,11},{11,12},{9... | collective-permute-start | bytes 786440 | tf_op jit(solution)/shard_map/ppermute | solution.py:422
  13.8 6.1 %collective-permute-start.2 = (s32[4]{0:T(128)}, s32[4]{0:T(128)S(1)}, u32[]{:S(2)}, u32[]{:S(2)}) collective-permute-start(s32[4]{0:T(128)} %bitcast.44), channel_id=1, source_target_pairs={{0,4},{4,0},{8,12},{12,8},{16,20},{20,16},{24,28},{28,24},{1,5},{5... | collective-permute-start | bytes 56 | tf_op jit(solution)/shard_map/ppermute | solution.py:419
  17.9 2.1 %copy-start.3 = (s32[1,4]{1,0:T(1,128)S(1)}, s32[1,4]{1,0:T(1,128)}, u32[]{:S(2)}) copy-start(s32[1,4]{1,0:T(1,128)} %param.11) | copy-start | bytes 52
  20.7 6.3 %collective-permute-start.5 = (bf16[128,1024]{1,0:T(8,128)(2,1)S(1)}, bf16[128,1024]{1,0:T(8,128)(2,1)S(1)}, u32[]{:S(2)}, u32[]{:S(2)}) collective-permute-start(bf16[128,1024]{1,0:T(8,128)(2,1)S(1)} %collective-permute-done.g0), channel_id=1, source_target_pairs={{0,4},{4,0},{8,12},{12,8},{16,20},{20,16},{24,28},{28,24},{1,5},{5... | collective-permute-start | bytes 786440 | tf_op jit(solution)/shard_map/ppermute | solution.py:419
  21.3 5.8 %collective-permute-start.6 = (bf16[128,1024]{1,0:T(8,128)(2,1)S(1)}, bf16[128,1024]{1,0:T(8,128)(2,1)S(1)}, u32[]{:S(2)}, u32[]{:S(2)}) collective-permute-start(bf16[128,1024]{1,0:T(8,128)(2,1)S(1)} %collective-permute-done.1.g1), channel_id=1, source_target_pairs={{0,4},{4,0},{8,12},{12,8},{16,20},{20,16},{24,28},{28,24},{1,5},{5... | collective-permute-start | bytes 786440 | tf_op jit(solution)/shard_map/ppermute | solution.py:419
  27.1 2.3 %collective-permute-start.7 = (bf16[128,1024]{1,0:T(8,128)(2,1)S(1)}, bf16[128,1024]{1,0:T(8,128)(2,1)S(1)}, u32[]{:S(2)}, u32[]{:S(2)}) collective-permute-start(bf16[128,1024]{1,0:T(8,128)(2,1)S(1)} %collective-permute-done.3.t0), channel_id=1, source_target_pairs={{0,4},{4,0},{8,12},{12,8},{16,20},{20,16},{24,28},{28,24},{1,5},{5... | collective-permute-start | bytes 786440 | tf_op jit(solution)/shard_map/ppermute | solution.py:419
  27.2 2.2 %collective-permute-start.8 = (bf16[128,1024]{1,0:T(8,128)(2,1)S(1)}, bf16[128,1024]{1,0:T(8,128)(2,1)S(1)}, u32[]{:S(2)}, u32[]{:S(2)}) collective-permute-start(bf16[128,1024]{1,0:T(8,128)(2,1)S(1)} %collective-permute-done.4.t1), channel_id=1, source_target_pairs={{0,4},{4,0},{8,12},{12,8},{16,20},{20,16},{24,28},{28,24},{1,5},{5... | collective-permute-start | bytes 786440 | tf_op jit(solution)/shard_map/ppermute | solution.py:419
  36.1 2.6 %collective-permute-start.9 = (bf16[768,384]{1,0:T(8,128)(2,1)S(1)}, bf16[768,384]{1,0:T(8,128)(2,1)S(1)}, u32[]{:S(2)}, u32[]{:S(2)}) collective-permute-start(bf16[768,384]{1,0:T(8,128)(2,1)S(1)} %get-tuple-element.53.own), channel_id=1, source_target_pairs={{0,4},{4,0},{8,12},{12,8},{16,20},{20,16},{24,28},{28,24},{1,5},{5... | collective-permute-start | bytes 1769480 | tf_op jit(solution)/shard_map/ppermute | solution.py:419
  36.2 13.1 %collective-permute-start.10 = (bf16[2,2,512,128]{3,2,1,0:T(8,128)(2,1)S(1)}, bf16[2,2,512,128]{3,2,1,0:T(8,128)(2,1)S(1)}, u32[]{:S(2)}, u32[]{:S(2)}) collective-permute-start(bf16[2,2,512,128]{3,2,1,0:T(8,128)(2,1)S(1)} %get-tuple-element.56), channel_id=1, source_target_pairs={{0,8},{4,12},{8,0},{12,4},{16,24},{20,28},{24,16},{28,20},{1,9},{5... | collective-permute-start | bytes 1572872 | tf_op jit(solution)/shard_map/ppermute | solution.py:419
  37.5 8.4 %copy-start.2 = (s32[1,128]{1,0:T(1,128)S(1)}, s32[1,128]{1,0:T(1,128)}, u32[]{:S(2)}) copy-start(s32[1,128]{1,0:T(1,128)} %places.1) | copy-start | bytes 1540
  37.5 9.4 %copy-start = (bf16[1,128,1024]{2,1,0:T(8,128)(2,1)S(1)}, bf16[1,128,1024]{2,1,0:T(8,128)(2,1)}, u32[]{:S(2)}) copy-start(bf16[1,128,1024]{2,1,0:T(8,128)(2,1)} %param.9) | copy-start | bytes 786436
  37.5 12.8 %collective-permute-start.11 = (bf16[2,2,512,128]{3,2,1,0:T(8,128)(2,1)S(1)}, bf16[2,2,512,128]{3,2,1,0:T(8,128)(2,1)S(1)}, u32[]{:S(2)}, u32[]{:S(2)}) collective-permute-start(bf16[2,2,512,128]{3,2,1,0:T(8,128)(2,1)S(1)} %get-tuple-element.57), channel_id=1, source_target_pairs={{0,16},{4,20},{8,24},{12,28},{16,0},{20,4},{24,8},{28,12},{1,17},{... | collective-permute-start | bytes 1572872 | tf_op jit(solution)/shard_map/ppermute | solution.py:419
  42.1 9.3 %collective-permute-start.12 = (bf16[128,1024]{1,0:T(8,128)(2,1)S(1)}, bf16[128,1024]{1,0:T(8,128)(2,1)S(1)}, u32[]{:S(2)}, u32[]{:S(2)}) collective-permute-start(bf16[128,1024]{1,0:T(8,128)(2,1)S(1)} %get-tuple-element.58), channel_id=1, source_target_pairs={{2,0},{0,1},{4,2},{6,3},{1,4},{7,5},{3,6},{5,7},{10,8},{8,9},{12,1... | collective-permute-start | bytes 786440 | tf_op jit(solution)/shard_map/ppermute | solution.py:531
  51.5 6.6 %collective-permute-start.15 = (bf16[2,512,128]{2,1,0:T(8,128)(2,1)S(1)}, bf16[2,512,128]{2,1,0:T(8,128)(2,1)S(1)}, u32[]{:S(2)}, u32[]{:S(2)}) collective-permute-start(bf16[2,512,128]{2,1,0:T(8,128)(2,1)S(1)} %get-tuple-element.73), channel_id=1, source_target_pairs={{0,8},{4,12},{8,0},{12,4},{16,24},{20,28},{24,16},{28,20},{1,9},{5... | collective-permute-start | bytes 786440 | tf_op jit(solution)/shard_map/ppermute | solution.py:419
  51.9 12.6 %copy-start.1 = (f32[1024]{0:T(1024)S(1)}, f32[1024]{0:T(1024)}, u32[]{:S(2)}) copy-start(f32[1024]{0:T(1024)} %param.12) | copy-start | bytes 12292
  52.0 6.2 %collective-permute-start.14 = (bf16[2,512,128]{2,1,0:T(8,128)(2,1)S(1)}, bf16[2,512,128]{2,1,0:T(8,128)(2,1)S(1)}, u32[]{:S(2)}, u32[]{:S(2)}) collective-permute-start(bf16[2,512,128]{2,1,0:T(8,128)(2,1)S(1)} %get-tuple-element.75), channel_id=1, source_target_pairs={{0,16},{4,20},{8,24},{12,28},{16,0},{20,4},{24,8},{28,12},{1,17},{... | collective-permute-start | bytes 786440 | tf_op jit(solution)/shard_map/ppermute | solution.py:419
  53.1 11.3 %collective-permute-start.13 = (bf16[128,1024]{1,0:T(8,128)(2,1)S(1)}, bf16[128,1024]{1,0:T(8,128)(2,1)S(1)}, u32[]{:S(2)}, u32[]{:S(2)}) collective-permute-start(bf16[128,1024]{1,0:T(8,128)(2,1)S(1)} %get-tuple-element.61), channel_id=1, source_target_pairs={{4,3},{3,4},{1,6},{6,1},{0,0},{5,5},{2,2},{7,7},{12,11},{11,12},{9... | collective-permute-start | bytes 786440 | tf_op jit(solution)/shard_map/ppermute | solution.py:533
  58.2 7.5 %collective-permute-start.16 = (bf16[1024,128]{1,0:T(8,128)(2,1)S(1)}, bf16[1024,128]{1,0:T(8,128)(2,1)S(1)}, u32[]{:S(2)}, u32[]{:S(2)}) collective-permute-start(bf16[1024,128]{1,0:T(8,128)(2,1)S(1)} %get-tuple-element.68), channel_id=1, source_target_pairs={{0,4},{5,1},{1,0},{4,5},{2,6},{7,3},{3,2},{6,7},{8,12},{13,9},{9,8... | collective-permute-start | bytes 786440 | tf_op jit(solution)/shard_map/ppermute | solution.py:551
  59.9 9.5 %collective-permute-start.17 = (bf16[1024,128]{1,0:T(8,128)(2,1)S(1)}, bf16[1024,128]{1,0:T(8,128)(2,1)S(1)}, u32[]{:S(2)}, u32[]{:S(2)}) collective-permute-start(bf16[1024,128]{1,0:T(8,128)(2,1)S(1)} %get-tuple-element.70), channel_id=1, source_target_pairs={{1,4},{4,1},{3,6},{6,3},{9,12},{12,9},{11,14},{14,11},{17,20},{20,... | collective-permute-start | bytes 786440 | tf_op jit(solution)/shard_map/ppermute | solution.py:552

commit v6 on v5

--- a/solution.py
+++ b/solution.py
@@ -1,3 +1,4 @@
+import functools
 import math
 
 import jax
@@ -253,24 +254,19 @@
     normed[...] = (centred * inv_std * ln_gain[...]).astype(normed.dtype)
 
 
-def lift_kernel(info, g0, g1, g2, g3, weight_out, gathered, lifted, rows_g, sems):
+def lift_kernel(info, g0, g1, g2, g3, weight_out, gathered, lifted, rows_g):
     capacity = g0.shape[0]
-    copies = [
-        pltpu.make_async_copy(source, rows_g.at[pl.ds(block * capacity, capacity), :], sems.at[block])
-        for block, source in enumerate((g0, g1, g2, g3))
-    ]
-    for copy in copies:
-        copy.start()
     matrix = gather_matrix([info[block] for block in range(4)], capacity, gathered.shape[0])
-    for copy in copies:
-        copy.wait()
+    for block, source in enumerate((g0, g1, g2, g3)):
+        rows_g[pl.ds(block * capacity, capacity), :] = source[...]
     gathered[...] = nn(matrix, rows_g[...]).astype(gathered.dtype)
     lifted[...] = nn(gathered[...], weight_out[...]).T.astype(lifted.dtype)
 
 
-def weight_kernel(place, w_out, w_qkv, own_out, own_qkv, sems):
+def weight_kernel(place, w_out, w_qkv, own_out, own_qkv, pair_qkv, sems):
     width = own_out.shape[1]
     group = pl.multiple_of(place[0] * width, width)
+    pair = pl.multiple_of((place[0] >> 1) * 2 * width, 2 * width)
     copies = [pltpu.make_async_copy(w_out.at[:, pl.ds(group, width)], own_out, sems.at[3])]
     for part in range(3):
         copies.append(
@@ -278,6 +274,13 @@
                 w_qkv.at[part, pl.ds(group, width), :],
                 own_qkv.at[pl.ds(part * width, width), :],
                 sems.at[part],
+            )
+        )
+        copies.append(
+            pltpu.make_async_copy(
+                w_qkv.at[part, pl.ds(pair, 2 * width), :],
+                pair_qkv.at[pl.ds(part * 2 * width, 2 * width), :],
+                sems.at[4 + part],
             )
         )
     for copy in copies:
@@ -305,20 +308,26 @@
     key[...] = nt(weight[width : 2 * width, :], gathered_t[...]).astype(low)
     value[...] = nt(weight[2 * width : 3 * width, :], gathered_t[...]).astype(low)
 
+    heads = []
     for head in range(width // HEAD_DIM):
         span = pl.ds(head * HEAD_DIM, HEAD_DIM)
-        query_h, key_h, value_h, lifted_h = query[span, :], key[span, :], value[span, :], lifted[span, :]
-        scores = tn(key_h, query_h)
+        rows_h = query[span, :], key[span, :], value[span, :], lifted[span, :]
+        heads.append(rows_h + (tn(rows_h[1], rows_h[0]), tn(rows_h[2], rows_h[3])))
+    weighted = []
+    for _, _, _, _, scores, _ in heads:
         expo = jnp.exp(scores - jnp.max(scores, axis=0, keepdims=True))
         probs = expo * (1.0 / jnp.sum(expo, axis=0, keepdims=True))
-        probs_low = probs.astype(low)
+        weighted.append((probs, probs.astype(low)))
+    for head, (query_h, key_h, value_h, lifted_h, _, prob_grad) in enumerate(heads):
+        probs, probs_low = weighted[head]
+        spans = [pl.ds(part * width + head * HEAD_DIM, HEAD_DIM) for part in range(4)]
         attended = nn(value_h, probs_low)
         delta = jnp.sum(lifted_h.astype(jnp.float32) * attended, axis=0, keepdims=True)
-        score_grad = (probs * (tn(value_h, lifted_h) - delta)).astype(low)
-        stack[pl.ds(head * HEAD_DIM, HEAD_DIM), :] = (nn(key_h, score_grad) * scale).astype(low)
-        stack[pl.ds(width + head * HEAD_DIM, HEAD_DIM), :] = nt(query_h, score_grad).astype(low)
-        stack[pl.ds(2 * width + head * HEAD_DIM, HEAD_DIM), :] = nt(lifted_h, probs_low).astype(low)
-        stack[pl.ds(3 * width + head * HEAD_DIM, HEAD_DIM), :] = attended.astype(low)
+        score_grad = (probs * (prob_grad - delta)).astype(low)
+        stack[spans[0], :] = (nn(key_h, score_grad) * scale).astype(low)
+        stack[spans[1], :] = nt(query_h, score_grad).astype(low)
+        stack[spans[2], :] = nt(lifted_h, probs_low).astype(low)
+        stack[spans[3], :] = attended.astype(low)
 
     grads[...] = stack[0 : 3 * width, :]
     for slot_y, slot_x in ((0, 0), (1, 0), (0, 1), (1, 1)):
@@ -339,22 +348,11 @@
                 ].astype(y_target.dtype)
 
 
-def normed_kernel(info, own, other, w_qkv, back_one, back_two, weight, sems):
+def normed_kernel(info, own, other, weight, back_one, back_two):
     width = own.shape[0] // 3
     rows = own.shape[1]
     capacity = back_one.shape[0]
-    first = pl.multiple_of((info[4] >> 1) * 2 * width, 2 * width)
     core = info[4] & 1
-    loads = [
-        pltpu.make_async_copy(
-            w_qkv.at[part, pl.ds(first, 2 * width), :],
-            weight.at[pl.ds(part * 2 * width, 2 * width), :],
-            sems.at[part],
-        )
-        for part in range(3)
-    ]
-    for copy in loads:
-        copy.start()
     half = 2 * capacity
     mine = gather_matrix([info[block] for block in range(4)], capacity, rows)[:, 0:half]
     theirs = gather_matrix([info[(block + 2) % 4] for block in range(4)], capacity, rows)[:, half:]
@@ -362,7 +360,6 @@
     other_grads = nn(other[...], theirs).astype(own.dtype)
     total = jnp.zeros((half, weight.shape[1]), jnp.float32)
     for part in range(3):
-        loads[part].wait()
         span = slice(part * width, (part + 1) * width)
         for grads, spot in ((own_grads, core), (other_grads, 1 - core)):
             place = pl.ds(pl.multiple_of((part * 2 + spot) * width, width), width)
@@ -379,6 +376,19 @@
         total = part[1] + second[1].astype(part.dtype)
         guest_send[span, :] = total.astype(guest_send.dtype)
         own[span, :] = total
+
+
+def final_kernel(guest, from_home, from_guest, own, grad_qkv, grad_out, *, factor):
+    rows, lanes = grad_qkv.shape
+
+    def finish(low_row, high_row):
+        span = slice(low_row, high_row)
+        rest = jnp.where(guest[0] == 0, own[span, :], from_guest[span, :].astype(jnp.float32))
+        return (from_home[span, :].astype(jnp.float32) + rest) * factor
+
+    grad_qkv[...] = finish(0, rows)
+    grad_out[:, 0:lanes] = finish(rows, rows + lanes)
+    grad_out[:, lanes : 2 * lanes] = finish(rows + lanes, rows + 2 * lanes)
 
 
 def specs(space, count):
@@ -441,15 +451,16 @@
         compiler_params=pltpu.CompilerParams(vmem_limit_bytes=FULL_BYTES),
     )(positions, inputs, ln_gain[None], jnp.asarray(np.exp(steps)[None]))
     fetched_t = fetch(normed)
-    own_out, own_qkv = pl.pallas_call(
+    own_out, own_qkv, pair_qkv = pl.pallas_call(
         weight_kernel,
         out_shape=(
             jax.ShapeDtypeStruct((features, width), low),
             jax.ShapeDtypeStruct((3 * width, features), low),
+            jax.ShapeDtypeStruct((6 * width, features), low),
         ),
         in_specs=smem + specs(pl.ANY, 2),
-        out_specs=specs(pltpu.VMEM, 2),
-        scratch_shapes=[pltpu.SemaphoreType.DMA((4,))],
+        out_specs=specs(pltpu.VMEM, 3),
+        scratch_shapes=[pltpu.SemaphoreType.DMA((7,))],
         compiler_params=params,
         cost_estimate=pl.CostEstimate(flops=0, bytes_accessed=4 * 1024 * 1024, transcendentals=0),
     )(place, w_out, w_qkv)
@@ -473,9 +484,9 @@
             jax.ShapeDtypeStruct((rows, features), low),
             jax.ShapeDtypeStruct((width, rows), low),
         ),
-        in_specs=smem + specs(pl.ANY, 4) + specs(pltpu.VMEM, 1),
+        in_specs=smem + specs(pltpu.VMEM, 5),
         out_specs=specs(pltpu.VMEM, 2),
-        scratch_shapes=[pltpu.VMEM((total, features), low), pltpu.SemaphoreType.DMA((4,))],
+        scratch_shapes=[pltpu.VMEM((total, features), low)],
         compiler_params=pltpu.CompilerParams(vmem_limit_bytes=MAIN_BYTES),
         cost_estimate=pl.CostEstimate(
             flops=2 * rows * features * (width + total), bytes_accessed=3 * 1024 * 1024, transcendentals=0
@@ -515,17 +526,13 @@
     back_one, back_two = pl.pallas_call(
         normed_kernel,
         out_shape=(block_shape, block_shape),
-        in_specs=smem + specs(pltpu.VMEM, 2) + specs(pl.ANY, 1),
+        in_specs=smem + specs(pltpu.VMEM, 3),
         out_specs=specs(pltpu.VMEM, 2),
-        scratch_shapes=[
-            pltpu.VMEM((6 * width, features), low),
-            pltpu.SemaphoreType.DMA((3,)),
-        ],
-        compiler_params=params,
+        compiler_params=pltpu.CompilerParams(vmem_limit_bytes=MAIN_BYTES),
         cost_estimate=pl.CostEstimate(
             flops=2 * total * features * width * 3, bytes_accessed=4 * 1024 * 1024, transcendentals=0
         ),
-    )(info, grads, from_core, w_qkv)
+    )(info, grads, from_core, pair_qkv)
     places, back_one = lax.optimization_barrier((positions, back_one))
     _, standard, inv_std = layer_norm(inputs, places[0], ln_gain)
     home_one = lax.ppermute(back_one, axes, first_back)
@@ -551,14 +558,17 @@
     from_home = lax.ppermute(home_send, axes, home)
     from_guest = lax.ppermute(guest_send, axes, guests)
 
-    def finish(low_row, high_row):
-        rest = jnp.where(resident, own[low_row:high_row], from_guest[low_row:high_row].astype(wide))
-        return (from_home[low_row:high_row].astype(wide) + rest) * factor
-
-    grad_qkv = finish(0, 3 * width).reshape(3, width, lanes)
-    grad_out = jnp.concatenate(
-        [finish(3 * width, 3 * width + lanes), finish(3 * width + lanes, 4 * width)], axis=1
-    )
+    grad_qkv, grad_out = pl.pallas_call(
+        functools.partial(final_kernel, factor=factor),
+        out_shape=(
+            jax.ShapeDtypeStruct((3 * width, lanes), wide),
+            jax.ShapeDtypeStruct((lanes, width), wide),
+        ),
+        in_specs=smem + specs(pltpu.VMEM, 3),
+        out_specs=specs(pltpu.VMEM, 2),
+        compiler_params=pltpu.CompilerParams(vmem_limit_bytes=8 * 1024 * 1024),
+    )(guest[None].astype(jnp.int32), from_home, from_guest, own)
+    grad_qkv = grad_qkv.reshape(3, width, lanes)
 
     normed_grad = home_one.astype(wide) + home_two.astype(wide)
     unit_grad = normed_grad * ln_gain

time: 71.3 us -> 69 us (0.968)
  waiting for transfers between devices: 13.8 us -> 11.3 us
  other arithmetic: 6.15 us -> 4.65 us
  Pallas kernels: 16.8 us -> 17.9 us
  starting transfers between devices: 30.4 us -> 31.2 us
    ppermute x2, waiting for transfers between devices: 5.72 us -> 2.95 us  [fetch(): return (lax.ppermute(array, axes, first), two)]
    pallas_call x1, Pallas kernels: 2.1 us -> 4.86 us  [column_shards(): pl.pallas_call(weight_kernel, out_shape=(jax.ShapeDtypeStruct((features,...]
    ppermute x10, waiting for transfers between devices: 3.25 us -> 4.68 us  [across(): return lax.ppermute(array, 'dp', [(i, i ^ bit) for i in range(2 * chips)])]
    pallas_call x1, Pallas kernels: 3.39 us -> 1.97 us  [column_shards(): pl.pallas_call(normed_kernel, out_shape=(block_shape, block_shape), in_sp...]
    ppermute x1, waiting for transfers between devices: 1.21 us -> 0.01 us  [column_shards(): home_one = lax.ppermute(back_one, axes, first_back)]
    pallas_call x1, Pallas kernels: 6.65 us -> 5.74 us  [column_shards(): pl.pallas_call(main_kernel, out_shape=(send_shape, keep_shape, send_shape...]
    pallas_call x0 -> x1, Pallas kernels: none -> 0.85 us  [column_shards(): pl.pallas_call(functools.partial(final_kernel, factor=factor), out_shape=...]
    mul x2 -> x0, other arithmetic: 0.84 us -> none  [finish(): return (from_home[low_row:high_row].astype(wide) + rest) * factor]
  transfers between devices with their start and end apart: 18 -> 18, of which waited for: 5 -> 4; matrix products, arithmetic and copies ran while one was open for 10% -> 11% of each run, Pallas kernels for 14% -> 16%
where the time goes in v6:
time: 69 us; the launch traced here: 68.7 us
  starting transfers between devices  31.2 us (45%)
  Pallas kernels  17.9 us (26%)
  waiting for transfers between devices  11.3 us (16%)
  other arithmetic  4.65 us (7%)
  local copies, waits for them, and re-layouts  2.82 us (4%)
  between operations  0.89 us (1%)
    ppermute x2, starting transfers between devices, fetch(): two = lax.ppermute(array, axes, second)  6.75 us
    pallas_call x1, Pallas kernels, column_shards(): pl.pallas_call(main_kernel, out_shape=(send_shape, keep_shape, send_shape...  5.74 us
    ppermute x10, starting transfers between devices, across(): return lax.ppermute(array, 'dp', [(i, i ^ bit) for i in range(2 * chips)])  5.59 us
    ppermute x1, starting transfers between devices, column_shards(): home_two = lax.ppermute(back_two, axes, second)  5.42 us
    pallas_call x1, Pallas kernels, column_shards(): pl.pallas_call(weight_kernel, out_shape=(jax.ShapeDtypeStruct((features,...  4.86 us
    ppermute x10, waiting for transfers between devices, across(): return lax.ppermute(array, 'dp', [(i, i ^ bit) for i in range(2 * chips)])  4.68 us
    ppermute x1, starting transfers between devices, column_shards(): from_guest = lax.ppermute(guest_send, axes, guests)  4.13 us
    ppermute x1, starting transfers between devices, column_shards(): home_one = lax.ppermute(back_one, axes, first_back)  3.73 us
  transfers between devices with their start and end apart: 18, of which 4 were waited for; matrix products, arithmetic and copies ran while one was open for 11% of the time, Pallas kernels for 16%

profile of v6, /device:TPU:1, one launch (start us, length us, event | category | flops | bytes accessed | tf_op | source)
XLA Modules:
  0.0 68.7 jit_solution(9205924628641448053)
XLA Ops:
  0.6 2.7 %collective-permute-start = (bf16[128,1024]{1,0:T(8,128)(2,1)}, bf16[128,1024]{1,0:T(8,128)(2,1)S(1)}, u32[]{:S(2)}, u32[]{:S(2)}) collective-permute-start(bf16[128,1024]{1,0:T(8,128)(2,1)} %bitcast.41), channel_id=1, source_target_pairs={{0,2},{1,0},{2,4},{3,6},{4,1},{5,7},{6,3},{7,5},{8,10},{9,8},{10,1... | collective-permute-start | bytes 786440 | tf_op jit(solution)/shard_map/ppermute | solution.py:433
  3.4 3.9 %collective-permute-start.1 = (bf16[128,1024]{1,0:T(8,128)(2,1)}, bf16[128,1024]{1,0:T(8,128)(2,1)S(1)}, u32[]{:S(2)}, u32[]{:S(2)}) collective-permute-start(bf16[128,1024]{1,0:T(8,128)(2,1)} %bitcast.42), channel_id=1, source_target_pairs={{4,3},{3,4},{1,6},{6,1},{0,0},{5,5},{2,2},{7,7},{12,11},{11,12},{9... | collective-permute-start | bytes 786440 | tf_op jit(solution)/shard_map/ppermute | solution.py:432
  7.3 2.9 %shard_map.113 = bf16[128,1024]{1,0:T(8,128)(2,1)} custom-call(s32[1,128]{1,0:T(1,128)} %places.1, bf16[128,1024]{1,0:T(8,128)(2,1)} %bitcast.40, f32[1,1024]{1,0:T(1,128)} %bitcast.43, f32[1,512]{1,0:T(1,128)} %constant.43.clone.freqs), custom_call_target="tpu_custom_call" | custom-call | tf_op jit(solution)/shard_map/pallas_call | solution.py:446
  10.2 0.8 %collective-permute-start.3 = (bf16[128,1024]{1,0:T(8,128)(2,1)}, bf16[128,1024]{1,0:T(8,128)(2,1)S(1)}, u32[]{:S(2)}, u32[]{:S(2)}) collective-permute-start(bf16[128,1024]{1,0:T(8,128)(2,1)} %shard_map.113), channel_id=1, source_target_pairs={{0,2},{1,0},{2,4},{3,6},{4,1},{5,7},{6,3},{7,5},{8,10},{9,8},{10,1... | collective-permute-start | bytes 786440 | tf_op jit(solution)/shard_map/ppermute | solution.py:433
  11.0 2.8 %collective-permute-start.4 = (bf16[128,1024]{1,0:T(8,128)(2,1)}, bf16[128,1024]{1,0:T(8,128)(2,1)S(1)}, u32[]{:S(2)}, u32[]{:S(2)}) collective-permute-start(bf16[128,1024]{1,0:T(8,128)(2,1)} %shard_map.113), channel_id=1, source_target_pairs={{4,3},{3,4},{1,6},{6,1},{0,0},{5,5},{2,2},{7,7},{12,11},{11,12},{9... | collective-permute-start | bytes 786440 | tf_op jit(solution)/shard_map/ppermute | solution.py:432
  13.8 0.1 collective-permute-start.2
  13.9 0.8 %fusion.4 = (s32[2,1]{0,1:T(1,128)S(1)}, s32[2,1]{0,1:T(1,128)S(1)}) fusion(s32[8,2]{1,0:T(8,128)} %constant.44.clone, s32[]{:T(128)S(6)} %select_n.34, s32[]{:T(128)S(6)} %select_n.35), kind=kLoop, calls=%fused_computation.24 | loop fusion | bytes 40 | tf_op jit(solution)/shard_map/concatenate | solution.py:472
  14.7 0.1 fusion.6
  14.8 1.3 %constant_dynamic-slice_fusion = s32[1,1]{1,0:T(1,128)} fusion(s32[1,4]{1,0:T(1,128)} %param.11, s32[]{:T(128)S(6)} %select_n.37), kind=kLoop, calls=%fused_computation.21 | loop fusion | bytes 12 | tf_op jit(solution)/shard_map/jit(dynamic_index_in_dim)/dynamic_slice | solution.py:467
  16.1 0.6 iota_compare_fusion
  16.7 1.0 %broadcast_select_fusion = bf16[128,1024]{1,0:T(8,128)(2,1)S(1)} fusion(pred[128]{0:T(512)(128)(4,1)S(1)} %iota_compare_fusion, bf16[1,128,1024]{2,1,0:T(8,128)(2,1)} %param.15), kind=kLoop, calls=%fused_computation.15 | loop fusion | flops 131072 | bytes 524416 | tf_op jit(solution)/shard_map/jit(_where)/select_n | solution.py:468
  17.8 0.1 pad_add_fusion.place
  17.9 4.9 %shard_map.112 = (bf16[1024,256]{1,0:T(8,128)(2,1)S(1)}, bf16[768,1024]{1,0:T(8,128)(2,1)S(1)}, bf16[1536,1024]{1,0:T(8,128)(2,1)}) custom-call(s32[4]{0:T(128)S(1)} %pad_add_fusion.place, bf16[1024,1024]{1,0:T(8,128)(2,1)} %w_out.1, bf16[3,1024,1024]{2,1,0:T(8,128)(2,1)} %w_qkv.1), custom_call_target="tpu_custom_call" | custom-call | bytes 4194304 | tf_op jit(solution)/shard_map/pallas_call | solution.py:454
  22.8 0.6 gather_fusion
  23.4 0.1 concatenate.36.info
  23.5 0.0 collective-permute-done.g0
  23.5 0.6 collective-permute-start.5
  24.1 0.1 collective-permute-start.6
  24.1 2.9 %collective-permute-done.3.t0 = bf16[128,1024]{1,0:T(8,128)(2,1)S(1)} collective-permute-done((bf16[128,1024]{1,0:T(8,128)(2,1)}, bf16[128,1024]{1,0:T(8,128)(2,1)S(1)}, u32[]{:S(2)}, u32[]{:S(2)}) %collective-permute-start.3) | collective-permute-done | bytes 262176 | tf_op jit(solution)/shard_map/ppermute | solution.py:433
  27.1 0.0 collective-permute-done.4.t1
  27.1 0.1 collective-permute-start.7
  27.2 0.5 collective-permute-start.8
  27.7 1.5 %shard_map.114 = (bf16[384,1024]{1,0:T(8,128)(2,1)S(1)}, bf16[256,384]{1,0:T(8,128)(2,1)S(1)}) custom-call(s32[8]{0:T(128)S(1)} %concatenate.36.info, bf16[128,1024]{1,0:T(8,128)(2,1)S(1)} %collective-permute-done.g0, bf16[128,1024]{1,0:T(8,128)(2,1)S(1)} %collective-permute-done.1.g1, bf16[128,1024]{1,0:T(8,128)(2,1)S(1)} %collective-permute-done.5.g2, ...), custom_call_target="tpu_custom_call" | custom-call | flops 603979776 | bytes 3145728 | tf_op jit(solution)/shard_map/pallas_call | solution.py:481
  29.2 5.7 %shard_map.115 = (bf16[2,2,512,128]{3,2,1,0:T(8,128)(2,1)S(1)}, f32[2,2,512,128]{3,2,1,0:T(8,128)S(1)}, bf16[2,2,512,128]{3,2,1,0:T(8,128)(2,1)S(1)}, f32[2,2,512,128]{3,2,1,0:T(8,128)S(1)}, bf16[768,384]{1,0:T(8,128)(2,1)S(1)}) custom-call(s32[8]{0:T(128)S(1)} %concatenate.36.info, bf16[128,1024]{1,0:T(8,128)(2,1)S(1)} %collective-permute-done.3.t0, ...), custom_call_target="tpu_custom_call" | custom-call | flops 2684354560 | bytes 8388608 | tf_op jit(solution)/shard_map/pallas_call | solution.py:500
  35.0 0.0 copy-start.3
  35.0 0.0 copy-start.1
  35.0 0.1 collective-permute-start.9
  35.1 1.2 %collective-permute-start.10 = (bf16[2,2,512,128]{3,2,1,0:T(8,128)(2,1)S(1)}, bf16[2,2,512,128]{3,2,1,0:T(8,128)(2,1)S(1)}, u32[]{:S(2)}, u32[]{:S(2)}) collective-permute-start(bf16[2,2,512,128]{3,2,1,0:T(8,128)(2,1)S(1)} %get-tuple-element.60), channel_id=1, source_target_pairs={{0,8},{4,12},{8,0},{12,4},{16,24},{20,28},{24,16},{28,20},{1,9},{5... | collective-permute-start | bytes 1572872 | tf_op jit(solution)/shard_map/ppermute | solution.py:429
  36.4 1.2 %collective-permute-start.11 = (bf16[2,2,512,128]{3,2,1,0:T(8,128)(2,1)S(1)}, bf16[2,2,512,128]{3,2,1,0:T(8,128)(2,1)S(1)}, u32[]{:S(2)}, u32[]{:S(2)}) collective-permute-start(bf16[2,2,512,128]{3,2,1,0:T(8,128)(2,1)S(1)} %get-tuple-element.61), channel_id=1, source_target_pairs={{0,16},{4,20},{8,24},{12,28},{16,0},{20,4},{24,8},{28,12},{1,17},{... | collective-permute-start | bytes 1572872 | tf_op jit(solution)/shard_map/ppermute | solution.py:429
  37.6 2.0 %shard_map.116 = (bf16[128,1024]{1,0:T(8,128)(2,1)S(1)}, bf16[128,1024]{1,0:T(8,128)(2,1)S(1)}) custom-call(s32[8]{0:T(128)S(1)} %concatenate.36.info, bf16[768,384]{1,0:T(8,128)(2,1)S(1)} %get-tuple-element.56.own, bf16[768,384]{1,0:T(8,128)(2,1)S(1)} %collective-permute-done.9.other, bf16[1536,1024]{1,0:T(8,128)(2,1)S(1)} %copy-done), custom_call_target="tpu_custom_call" | custom-call | flops 805306368 | bytes 4194304 | tf_op jit(solution)/shard_map/pallas_call | solution.py:526
  39.6 3.7 %collective-permute-start.12 = (bf16[128,1024]{1,0:T(8,128)(2,1)S(1)}, bf16[128,1024]{1,0:T(8,128)(2,1)S(1)}, u32[]{:S(2)}, u32[]{:S(2)}) collective-permute-start(bf16[128,1024]{1,0:T(8,128)(2,1)S(1)} %get-tuple-element.62), channel_id=1, source_target_pairs={{2,0},{0,1},{4,2},{6,3},{1,4},{7,5},{3,6},{5,7},{10,8},{8,9},{12,1... | collective-permute-start | bytes 786440 | tf_op jit(solution)/shard_map/ppermute | solution.py:538
  43.3 1.0 %multiply_sine_fusion = (f32[128,512]{1,0:T(8,128)S(1)}, f32[128,512]{1,0:T(8,128)S(1)}) fusion(f32[512]{0:T(512)S(1)} %multiply_exponential_fusion, f32[128]{0:T(128)S(1)} %convert_bitcast_fusion), kind=kLoop, calls=%fused_computation.12 | loop fusion | flops 65536 | bytes 526848 | tf_op jit(solution)/shard_map/sin | solution.py:23
  44.3 0.1 fusion.7
  44.5 3.8 %collective-permute-done.10 = bf16[2,2,512,128]{3,2,1,0:T(8,128)(2,1)S(1)} collective-permute-done((bf16[2,2,512,128]{3,2,1,0:T(8,128)(2,1)S(1)}, bf16[2,2,512,128]{3,2,1,0:T(8,128)(2,1)S(1)}, u32[]{:S(2)}, u32[]{:S(2)}) %collective-permute-start.10) | collective-permute-done | bytes 524320 | tf_op jit(solution)/shard_map/ppermute | solution.py:429
  48.2 0.9 %collective-permute-done.11 = bf16[2,2,512,128]{3,2,1,0:T(8,128)(2,1)S(1)} collective-permute-done((bf16[2,2,512,128]{3,2,1,0:T(8,128)(2,1)S(1)}, bf16[2,2,512,128]{3,2,1,0:T(8,128)(2,1)S(1)}, u32[]{:S(2)}, u32[]{:S(2)}) %collective-permute-start.11) | collective-permute-done | bytes 524320 | tf_op jit(solution)/shard_map/ppermute | solution.py:429
  49.1 0.1 fusion.2
  49.2 0.4 collective-permute-start.15
  49.6 0.1 fusion.1
  49.7 1.3 %collective-permute-start.14 = (bf16[2,512,128]{2,1,0:T(8,128)(2,1)S(1)}, bf16[2,512,128]{2,1,0:T(8,128)(2,1)S(1)}, u32[]{:S(2)}, u32[]{:S(2)}) collective-permute-start(bf16[2,512,128]{2,1,0:T(8,128)(2,1)S(1)} %get-tuple-element.81), channel_id=1, source_target_pairs={{0,16},{4,20},{8,24},{12,28},{16,0},{20,4},{24,8},{28,12},{1,17},{... | collective-permute-start | bytes 786440 | tf_op jit(solution)/shard_map/ppermute | solution.py:429
  51.0 5.4 %collective-permute-start.13 = (bf16[128,1024]{1,0:T(8,128)(2,1)S(1)}, bf16[128,1024]{1,0:T(8,128)(2,1)S(1)}, u32[]{:S(2)}, u32[]{:S(2)}) collective-permute-start(bf16[128,1024]{1,0:T(8,128)(2,1)S(1)} %get-tuple-element.65), channel_id=1, source_target_pairs={{4,3},{3,4},{1,6},{6,1},{0,0},{5,5},{2,2},{7,7},{12,11},{11,12},{9... | collective-permute-start | bytes 786440 | tf_op jit(solution)/shard_map/ppermute | solution.py:540
  56.5 0.2 multiply_reduce_fusion.1
  56.7 0.1 shard_map.117
  56.8 2.0 %collective-permute-start.16 = (bf16[1024,128]{1,0:T(8,128)(2,1)S(1)}, bf16[1024,128]{1,0:T(8,128)(2,1)S(1)}, u32[]{:S(2)}, u32[]{:S(2)}) collective-permute-start(bf16[1024,128]{1,0:T(8,128)(2,1)S(1)} %get-tuple-element.72), channel_id=1, source_target_pairs={{0,4},{5,1},{1,0},{4,5},{2,6},{7,3},{3,2},{6,7},{8,12},{13,9},{9,8... | collective-permute-start | bytes 786440 | tf_op jit(solution)/shard_map/ppermute | solution.py:558
  58.8 4.1 %collective-permute-start.17 = (bf16[1024,128]{1,0:T(8,128)(2,1)S(1)}, bf16[1024,128]{1,0:T(8,128)(2,1)S(1)}, u32[]{:S(2)}, u32[]{:S(2)}) collective-permute-start(bf16[1024,128]{1,0:T(8,128)(2,1)S(1)} %get-tuple-element.73), channel_id=1, source_target_pairs={{1,4},{4,1},{3,6},{6,3},{9,12},{12,9},{11,14},{14,11},{17,20},{20,... | collective-permute-start | bytes 786440 | tf_op jit(solution)/shard_map/ppermute | solution.py:559
  62.9 0.3 fusion
  63.2 1.0 %fusion.3 = bf16[1,128,1024]{2,1,0:T(8,128)(2,1)} fusion(f32[128]{0:T(128)S(1)} %get-tuple-element.87, f32[128]{0:T(128)S(1)} %broadcast_multiply_fusion.2, f32[128]{0:T(128)S(1)} %get-tuple-element.88, f32[1024]{0:T(1024)S(1)} %copy-done.2, bf16[128,1024]{1,0:T(8,128)(2,1)S(1)} %collective-permute-done.13, ...), kind=kLoop, calls=%fused_computation.16 | loop fusion | flops 2097152 | bytes 1841152 | tf_op jit(solution)/shard_map/broadcast_in_dim | solution.py:578
  64.2 3.6 %collective-permute-done.17.from_guest = bf16[1024,128]{1,0:T(8,128)(2,1)S(1)} collective-permute-done((bf16[1024,128]{1,0:T(8,128)(2,1)S(1)}, bf16[1024,128]{1,0:T(8,128)(2,1)S(1)}, u32[]{:S(2)}, u32[]{:S(2)}) %collective-permute-start.17) | collective-permute-done | bytes 262176 | tf_op jit(solution)/shard_map/ppermute | solution.py:559
  67.9 0.9 %shard_map.118 = (f32[768,128]{1,0:T(8,128)}, f32[128,256]{1,0:T(8,128)}) custom-call(s32[1]{0:T(128)} %bitcast.14.guest, bf16[1024,128]{1,0:T(8,128)(2,1)S(1)} %collective-permute-done.16.from_home, bf16[1024,128]{1,0:T(8,128)(2,1)S(1)} %collective-permute-done.17.from_guest, f32[1024,128]{1,0:T(8,128)S(1)} %get-tuple-element.74.own), custom_call_target="tpu_custom_call" | custom-call | tf_op jit(solution)/shard_map/pallas_call | solution.py:561
  (27 shorter events, 0.1 us)
Async XLA Ops:
  0.6 22.9 %collective-permute-start = (bf16[128,1024]{1,0:T(8,128)(2,1)}, bf16[128,1024]{1,0:T(8,128)(2,1)S(1)}, u32[]{:S(2)}, u32[]{:S(2)}) collective-permute-start(bf16[128,1024]{1,0:T(8,128)(2,1)} %bitcast.41), channel_id=1, source_target_pairs={{0,2},{1,0},{2,4},{3,6},{4,1},{5,7},{6,3},{7,5},{8,10},{9,8},{10,1... | collective-permute-start | bytes 786440 | tf_op jit(solution)/shard_map/ppermute | solution.py:433
  3.4 20.1 %collective-permute-start.1 = (bf16[128,1024]{1,0:T(8,128)(2,1)}, bf16[128,1024]{1,0:T(8,128)(2,1)S(1)}, u32[]{:S(2)}, u32[]{:S(2)}) collective-permute-start(bf16[128,1024]{1,0:T(8,128)(2,1)} %bitcast.42), channel_id=1, source_target_pairs={{4,3},{3,4},{1,6},{6,1},{0,0},{5,5},{2,2},{7,7},{12,11},{11,12},{9... | collective-permute-start | bytes 786440 | tf_op jit(solution)/shard_map/ppermute | solution.py:432
  10.2 16.9 %collective-permute-start.3 = (bf16[128,1024]{1,0:T(8,128)(2,1)}, bf16[128,1024]{1,0:T(8,128)(2,1)S(1)}, u32[]{:S(2)}, u32[]{:S(2)}) collective-permute-start(bf16[128,1024]{1,0:T(8,128)(2,1)} %shard_map.113), channel_id=1, source_target_pairs={{0,2},{1,0},{2,4},{3,6},{4,1},{5,7},{6,3},{7,5},{8,10},{9,8},{10,1... | collective-permute-start | bytes 786440 | tf_op jit(solution)/shard_map/ppermute | solution.py:433
  11.0 16.1 %collective-permute-start.4 = (bf16[128,1024]{1,0:T(8,128)(2,1)}, bf16[128,1024]{1,0:T(8,128)(2,1)S(1)}, u32[]{:S(2)}, u32[]{:S(2)}) collective-permute-start(bf16[128,1024]{1,0:T(8,128)(2,1)} %shard_map.113), channel_id=1, source_target_pairs={{4,3},{3,4},{1,6},{6,1},{0,0},{5,5},{2,2},{7,7},{12,11},{11,12},{9... | collective-permute-start | bytes 786440 | tf_op jit(solution)/shard_map/ppermute | solution.py:432
  13.8 8.9 %collective-permute-start.2 = (s32[4]{0:T(128)}, s32[4]{0:T(128)S(1)}, u32[]{:S(2)}, u32[]{:S(2)}) collective-permute-start(s32[4]{0:T(128)} %bitcast.44), channel_id=1, source_target_pairs={{0,4},{4,0},{8,12},{12,8},{16,20},{20,16},{24,28},{28,24},{1,5},{5... | collective-permute-start | bytes 56 | tf_op jit(solution)/shard_map/ppermute | solution.py:429
  17.9 4.9 %copy-start.4 = (s32[1,4]{1,0:T(1,128)S(1)}, s32[1,4]{1,0:T(1,128)}, u32[]{:S(2)}) copy-start(s32[1,4]{1,0:T(1,128)} %param.11) | copy-start | bytes 52
  23.5 3.6 %collective-permute-start.5 = (bf16[128,1024]{1,0:T(8,128)(2,1)S(1)}, bf16[128,1024]{1,0:T(8,128)(2,1)S(1)}, u32[]{:S(2)}, u32[]{:S(2)}) collective-permute-start(bf16[128,1024]{1,0:T(8,128)(2,1)S(1)} %collective-permute-done.g0), channel_id=1, source_target_pairs={{0,4},{4,0},{8,12},{12,8},{16,20},{20,16},{24,28},{28,24},{1,5},{5... | collective-permute-start | bytes 786440 | tf_op jit(solution)/shard_map/ppermute | solution.py:429
  24.1 3.0 %collective-permute-start.6 = (bf16[128,1024]{1,0:T(8,128)(2,1)S(1)}, bf16[128,1024]{1,0:T(8,128)(2,1)S(1)}, u32[]{:S(2)}, u32[]{:S(2)}) collective-permute-start(bf16[128,1024]{1,0:T(8,128)(2,1)S(1)} %collective-permute-done.1.g1), channel_id=1, source_target_pairs={{0,4},{4,0},{8,12},{12,8},{16,20},{20,16},{24,28},{28,24},{1,5},{5... | collective-permute-start | bytes 786440 | tf_op jit(solution)/shard_map/ppermute | solution.py:429
  27.1 2.1 %collective-permute-start.7 = (bf16[128,1024]{1,0:T(8,128)(2,1)S(1)}, bf16[128,1024]{1,0:T(8,128)(2,1)S(1)}, u32[]{:S(2)}, u32[]{:S(2)}) collective-permute-start(bf16[128,1024]{1,0:T(8,128)(2,1)S(1)} %collective-permute-done.3.t0), channel_id=1, source_target_pairs={{0,4},{4,0},{8,12},{12,8},{16,20},{20,16},{24,28},{28,24},{1,5},{5... | collective-permute-start | bytes 786440 | tf_op jit(solution)/shard_map/ppermute | solution.py:429
  27.2 2.0 %collective-permute-start.8 = (bf16[128,1024]{1,0:T(8,128)(2,1)S(1)}, bf16[128,1024]{1,0:T(8,128)(2,1)S(1)}, u32[]{:S(2)}, u32[]{:S(2)}) collective-permute-start(bf16[128,1024]{1,0:T(8,128)(2,1)S(1)} %collective-permute-done.4.t1), channel_id=1, source_target_pairs={{0,4},{4,0},{8,12},{12,8},{16,20},{20,16},{24,28},{28,24},{1,5},{5... | collective-permute-start | bytes 786440 | tf_op jit(solution)/shard_map/ppermute | solution.py:429
  29.2 8.4 %copy-start = (bf16[1536,1024]{1,0:T(8,128)(2,1)S(1)}, bf16[1536,1024]{1,0:T(8,128)(2,1)}, u32[]{:S(2)}) copy-start(bf16[1536,1024]{1,0:T(8,128)(2,1)} %get-tuple-element.57.weight) | copy-start | bytes 9437188
  35.0 8.4 %copy-start.3 = (s32[1,128]{1,0:T(1,128)S(1)}, s32[1,128]{1,0:T(1,128)}, u32[]{:S(2)}) copy-start(s32[1,128]{1,0:T(1,128)} %places.1) | copy-start | bytes 1540
  35.0 9.3 %copy-start.1 = (bf16[1,128,1024]{2,1,0:T(8,128)(2,1)S(1)}, bf16[1,128,1024]{2,1,0:T(8,128)(2,1)}, u32[]{:S(2)}) copy-start(bf16[1,128,1024]{2,1,0:T(8,128)(2,1)} %param.9) | copy-start | bytes 786436
  35.0 2.6 %collective-permute-start.9 = (bf16[768,384]{1,0:T(8,128)(2,1)S(1)}, bf16[768,384]{1,0:T(8,128)(2,1)S(1)}, u32[]{:S(2)}, u32[]{:S(2)}) collective-permute-start(bf16[768,384]{1,0:T(8,128)(2,1)S(1)} %get-tuple-element.56.own), channel_id=1, source_target_pairs={{0,4},{4,0},{8,12},{12,8},{16,20},{20,16},{24,28},{28,24},{1,5},{5... | collective-permute-start | bytes 1769480 | tf_op jit(solution)/shard_map/ppermute | solution.py:429
  35.1 13.1 %collective-permute-start.10 = (bf16[2,2,512,128]{3,2,1,0:T(8,128)(2,1)S(1)}, bf16[2,2,512,128]{3,2,1,0:T(8,128)(2,1)S(1)}, u32[]{:S(2)}, u32[]{:S(2)}) collective-permute-start(bf16[2,2,512,128]{3,2,1,0:T(8,128)(2,1)S(1)} %get-tuple-element.60), channel_id=1, source_target_pairs={{0,8},{4,12},{8,0},{12,4},{16,24},{20,28},{24,16},{28,20},{1,9},{5... | collective-permute-start | bytes 1572872 | tf_op jit(solution)/shard_map/ppermute | solution.py:429
  36.4 12.8 %collective-permute-start.11 = (bf16[2,2,512,128]{3,2,1,0:T(8,128)(2,1)S(1)}, bf16[2,2,512,128]{3,2,1,0:T(8,128)(2,1)S(1)}, u32[]{:S(2)}, u32[]{:S(2)}) collective-permute-start(bf16[2,2,512,128]{3,2,1,0:T(8,128)(2,1)S(1)} %get-tuple-element.61), channel_id=1, source_target_pairs={{0,16},{4,20},{8,24},{12,28},{16,0},{20,4},{24,8},{28,12},{1,17},{... | collective-permute-start | bytes 1572872 | tf_op jit(solution)/shard_map/ppermute | solution.py:429
  39.6 9.5 %collective-permute-start.12 = (bf16[128,1024]{1,0:T(8,128)(2,1)S(1)}, bf16[128,1024]{1,0:T(8,128)(2,1)S(1)}, u32[]{:S(2)}, u32[]{:S(2)}) collective-permute-start(bf16[128,1024]{1,0:T(8,128)(2,1)S(1)} %get-tuple-element.62), channel_id=1, source_target_pairs={{2,0},{0,1},{4,2},{6,3},{1,4},{7,5},{3,6},{5,7},{10,8},{8,9},{12,1... | collective-permute-start | bytes 786440 | tf_op jit(solution)/shard_map/ppermute | solution.py:538
  49.1 13.8 %copy-start.2 = (f32[1024]{0:T(1024)S(1)}, f32[1024]{0:T(1024)}, u32[]{:S(2)}) copy-start(f32[1024]{0:T(1024)} %param.12) | copy-start | bytes 12292
  49.2 7.4 %collective-permute-start.15 = (bf16[2,512,128]{2,1,0:T(8,128)(2,1)S(1)}, bf16[2,512,128]{2,1,0:T(8,128)(2,1)S(1)}, u32[]{:S(2)}, u32[]{:S(2)}) collective-permute-start(bf16[2,512,128]{2,1,0:T(8,128)(2,1)S(1)} %get-tuple-element.79), channel_id=1, source_target_pairs={{0,8},{4,12},{8,0},{12,4},{16,24},{20,28},{24,16},{28,20},{1,9},{5... | collective-permute-start | bytes 786440 | tf_op jit(solution)/shard_map/ppermute | solution.py:429
  49.7 7.0 %collective-permute-start.14 = (bf16[2,512,128]{2,1,0:T(8,128)(2,1)S(1)}, bf16[2,512,128]{2,1,0:T(8,128)(2,1)S(1)}, u32[]{:S(2)}, u32[]{:S(2)}) collective-permute-start(bf16[2,512,128]{2,1,0:T(8,128)(2,1)S(1)} %get-tuple-element.81), channel_id=1, source_target_pairs={{0,16},{4,20},{8,24},{12,28},{16,0},{20,4},{24,8},{28,12},{1,17},{... | collective-permute-start | bytes 786440 | tf_op jit(solution)/shard_map/ppermute | solution.py:429
  51.0 11.9 %collective-permute-start.13 = (bf16[128,1024]{1,0:T(8,128)(2,1)S(1)}, bf16[128,1024]{1,0:T(8,128)(2,1)S(1)}, u32[]{:S(2)}, u32[]{:S(2)}) collective-permute-start(bf16[128,1024]{1,0:T(8,128)(2,1)S(1)} %get-tuple-element.65), channel_id=1, source_target_pairs={{4,3},{3,4},{1,6},{6,1},{0,0},{5,5},{2,2},{7,7},{12,11},{11,12},{9... | collective-permute-start | bytes 786440 | tf_op jit(solution)/shard_map/ppermute | solution.py:540
  56.8 7.5 %collective-permute-start.16 = (bf16[1024,128]{1,0:T(8,128)(2,1)S(1)}, bf16[1024,128]{1,0:T(8,128)(2,1)S(1)}, u32[]{:S(2)}, u32[]{:S(2)}) collective-permute-start(bf16[1024,128]{1,0:T(8,128)(2,1)S(1)} %get-tuple-element.72), channel_id=1, source_target_pairs={{0,4},{5,1},{1,0},{4,5},{2,6},{7,3},{3,2},{6,7},{8,12},{13,9},{9,8... | collective-permute-start | bytes 786440 | tf_op jit(solution)/shard_map/ppermute | solution.py:558
  58.8 9.1 %collective-permute-start.17 = (bf16[1024,128]{1,0:T(8,128)(2,1)S(1)}, bf16[1024,128]{1,0:T(8,128)(2,1)S(1)}, u32[]{:S(2)}, u32[]{:S(2)}) collective-permute-start(bf16[1024,128]{1,0:T(8,128)(2,1)S(1)} %get-tuple-element.73), channel_id=1, source_target_pairs={{1,4},{4,1},{3,6},{6,3},{9,12},{12,9},{11,14},{14,11},{17,20},{20,... | collective-permute-start | bytes 786440 | tf_op jit(solution)/shard_map/ppermute | solution.py:559

commit v7 on v6

--- a/solution.py
+++ b/solution.py
@@ -228,20 +228,15 @@
     return lax.dot_general(left, right, (((0,), (0,)), ((), ())), preferred_element_type=jnp.float32)
 
 
-def gather_matrix(sizes, capacity, rows):
-    total = len(sizes) * capacity
-    slot = lax.broadcasted_iota(jnp.int32, (1, total), 1)
-    limit = jnp.zeros((1, total), jnp.int32)
-    shift = jnp.zeros((1, total), jnp.int32)
-    start = 0
-    for block, size in enumerate(sizes):
-        later = slot >= block * capacity
-        limit = jnp.where(later, block * capacity + size, limit)
-        shift = jnp.where(later, start - block * capacity, shift)
-        start = start + size
-    rank = jnp.where(slot < limit, slot + shift, -1)
-    row = lax.broadcasted_iota(jnp.int32, (rows, total), 0)
-    return jnp.where(row == rank, 1.0, 0.0).astype(jnp.bfloat16)
+def seats():
+    seat, dp = lax.axis_index("seq"), lax.axis_index("dp")
+    core = dp & 1
+    return (seat >> 1) * 2 + core, core, core ^ (seat & 1), dp >> 2, (dp >> 1) & 1
+
+
+def gather_matrix(rank, rows):
+    row = lax.broadcasted_iota(jnp.int32, (rows, rank.shape[1]), 0)
+    return jnp.where(row == rank[...], 1.0, 0.0).astype(jnp.bfloat16)
 
 
 def layer_norm_kernel(places, inputs, ln_gain, freqs, normed):
@@ -254,19 +249,49 @@
     normed[...] = (centred * inv_std * ln_gain[...]).astype(normed.dtype)
 
 
-def lift_kernel(info, g0, g1, g2, g3, weight_out, gathered, lifted, rows_g):
+def slot_kernel(counts, other_counts, table, upstream, rank, own_rank, other_rank, masked):
+    capacity = upstream.shape[0]
+    half = own_rank.shape[1]
+    seat = lax.axis_index("seq")
+    _, core, guest, _, _ = seats()
+    sizes = []
+    for block in range(rank.shape[1] // capacity):
+        holder = core if block < 2 else 1 - core
+        source = table[(seat * 2 + holder) * 2 + block % 2]
+        sizes.append(jnp.where(guest == 0, counts[source], other_counts[source]))
+    slot = lax.broadcasted_iota(jnp.int32, rank.shape, 1)
+    limit = jnp.zeros(rank.shape, jnp.int32)
+    shift = jnp.zeros(rank.shape, jnp.int32)
+    start = 0
+    for block, size in enumerate(sizes):
+        later = slot >= block * capacity
+        limit = jnp.where(later, block * capacity + size, limit)
+        shift = jnp.where(later, start - block * capacity, shift)
+        start = start + size
+    here = jnp.where(slot < limit, slot + shift, -1)
+    rank[...] = here
+    here = here[:, 0:half]
+    own_rank[...] = here
+    other_rank[...] = jnp.where(here >= 0, here + sizes[2] + sizes[3], -1)
+    row = lax.broadcasted_iota(jnp.int32, (capacity, 1), 0)
+    rows = upstream[...].astype(jnp.float32)
+    masked[...] = jnp.where(row < counts[seat], rows, 0.0).astype(masked.dtype)
+
+
+def lift_kernel(rank, g0, g1, g2, g3, weight_out, gathered, lifted, rows_g):
     capacity = g0.shape[0]
-    matrix = gather_matrix([info[block] for block in range(4)], capacity, gathered.shape[0])
+    matrix = gather_matrix(rank, gathered.shape[0])
     for block, source in enumerate((g0, g1, g2, g3)):
         rows_g[pl.ds(block * capacity, capacity), :] = source[...]
     gathered[...] = nn(matrix, rows_g[...]).astype(gathered.dtype)
     lifted[...] = nn(gathered[...], weight_out[...]).T.astype(lifted.dtype)
 
 
-def weight_kernel(place, w_out, w_qkv, own_out, own_qkv, pair_qkv, sems):
+def weight_kernel(w_out, w_qkv, own_out, own_qkv, pair_qkv, sems):
     width = own_out.shape[1]
-    group = pl.multiple_of(place[0] * width, width)
-    pair = pl.multiple_of((place[0] >> 1) * 2 * width, 2 * width)
+    head_group = seats()[0]
+    group = pl.multiple_of(head_group * width, width)
+    pair = pl.multiple_of((head_group >> 1) * 2 * width, 2 * width)
     copies = [pltpu.make_async_copy(w_out.at[:, pl.ds(group, width)], own_out, sems.at[3])]
     for part in range(3):
         copies.append(
@@ -290,7 +315,7 @@
 
 
 def main_kernel(
-    info, t0, t1, t2, t3, gathered_g, lifted, weight,
+    rank, t0, t1, t2, t3, gathered_g, lifted, weight,
     x_send, x_keep, y_send, y_keep, grads,
     rows_t, gathered_t, query, key, value, stack,
 ):
@@ -300,7 +325,8 @@
     low = jnp.bfloat16
     scale = HEAD_DIM ** (-0.5)
 
-    matrix = gather_matrix([info[block] for block in range(4)], capacity, gathered_t.shape[0])
+    _, core, guest, place_y, place_x = seats()
+    matrix = gather_matrix(rank, gathered_t.shape[0])
     for block, source in enumerate((t0, t1, t2, t3)):
         rows_t[pl.ds(block * capacity, capacity), :] = source[...]
     gathered_t[...] = nn(matrix, rows_t[...]).astype(low)
@@ -331,7 +357,7 @@
 
     grads[...] = stack[0 : 3 * width, :]
     for slot_y, slot_x in ((0, 0), (1, 0), (0, 1), (1, 1)):
-        block = (info[5] ^ slot_y) * 2 + (info[6] ^ slot_x)
+        block = (place_y ^ slot_y) * 2 + (place_x ^ slot_x)
         cols = pl.ds(pl.multiple_of(block * width, width), width)
         term_t = nn(stack[0 : 3 * width, :], gathered_t[:, cols])
         term_g = nn(stack[3 * width : 4 * width, :], gathered_g[:, cols]).T
@@ -339,7 +365,7 @@
         y_target = y_send if slot_y else y_keep
         for side in range(2):
             across = slice(side * lanes, (side + 1) * lanes)
-            spot = info[7] ^ side
+            spot = core ^ 1 ^ guest ^ side
             x_target[slot_y, spot, :, :] = term_t[0 : 2 * width, across].astype(x_target.dtype)
             y_target[slot_x, spot, 0:width, :] = term_t[2 * width : 3 * width, across].astype(y_target.dtype)
             for part in range(2):
@@ -348,14 +374,14 @@
                 ].astype(y_target.dtype)
 
 
-def normed_kernel(info, own, other, weight, back_one, back_two):
+def normed_kernel(own_rank, other_rank, own, other, weight, back_one, back_two):
     width = own.shape[0] // 3
     rows = own.shape[1]
     capacity = back_one.shape[0]
-    core = info[4] & 1
+    core = seats()[1]
     half = 2 * capacity
-    mine = gather_matrix([info[block] for block in range(4)], capacity, rows)[:, 0:half]
-    theirs = gather_matrix([info[(block + 2) % 4] for block in range(4)], capacity, rows)[:, half:]
+    mine = gather_matrix(own_rank, rows)
+    theirs = gather_matrix(other_rank, rows)
     own_grads = nn(own[...], mine).astype(own.dtype)
     other_grads = nn(other[...], theirs).astype(own.dtype)
     total = jnp.zeros((half, weight.shape[1]), jnp.float32)
@@ -378,12 +404,13 @@
         own[span, :] = total
 
 
-def final_kernel(guest, from_home, from_guest, own, grad_qkv, grad_out, *, factor):
+def final_kernel(from_home, from_guest, own, grad_qkv, grad_out, *, factor):
     rows, lanes = grad_qkv.shape
+    guest = seats()[2]
 
     def finish(low_row, high_row):
         span = slice(low_row, high_row)
-        rest = jnp.where(guest[0] == 0, own[span, :], from_guest[span, :].astype(jnp.float32))
+        rest = jnp.where(guest == 0, own[span, :], from_guest[span, :].astype(jnp.float32))
         return (from_home[span, :].astype(jnp.float32) + rest) * factor
 
     grad_qkv[...] = finish(0, rows)
@@ -409,14 +436,12 @@
     chips = lax.axis_size("dp") // 2
     seat = lax.axis_index("seq")
     dp = lax.axis_index("dp")
-    core, place_x, place_y = dp & 1, (dp >> 1) & 1, dp >> 2
+    core = dp & 1
     total = seqs * capacity
     half = total // 2
     width = features // seqs
     lanes = width // 2
     factor = 1.0 / math.sqrt(lax.axis_size("dp") * (3 * total // 4))
-    guest = core ^ (seat & 1)
-    resident = guest == 0
 
     axes = ("dp", "seq")
     first = column_pairs(FIRST_MOVES, chips, seqs)
@@ -435,10 +460,7 @@
     def share(pair):
         return pair + (across(pair[0], 1), across(pair[1], 1))
 
-    group = (seat >> 1) * 2 + core
-    place = jnp.stack([group, place_y, place_x, core ^ 1 ^ guest]).astype(jnp.int32)
     params = pltpu.CompilerParams(vmem_limit_bytes=VMEM_BYTES)
-    smem = specs(pltpu.SMEM, 1)
 
     fetched_g = fetch(upstream)
     other_counts = across(counts[0], 1)
@@ -458,22 +480,28 @@
             jax.ShapeDtypeStruct((3 * width, features), low),
             jax.ShapeDtypeStruct((6 * width, features), low),
         ),
-        in_specs=smem + specs(pl.ANY, 2),
+        in_specs=specs(pl.ANY, 2),
         out_specs=specs(pltpu.VMEM, 3),
         scratch_shapes=[pltpu.SemaphoreType.DMA((7,))],
         compiler_params=params,
         cost_estimate=pl.CostEstimate(flops=0, bytes_accessed=4 * 1024 * 1024, transcendentals=0),
-    )(place, w_out, w_qkv)
-    own_valid = jnp.arange(capacity, dtype=jnp.int32) < lax.dynamic_index_in_dim(counts[0], seat, 0, False)
-    masked_grad = jnp.where(own_valid[:, None], upstream, jnp.zeros_like(upstream))
-
-    sizes = jnp.where(resident, counts[0], other_counts)
-    table = jnp.array(block_table(), jnp.int32)
-    order = jnp.concatenate([table[seat * 2 + core], table[seat * 2 + 1 - core]])
-    info = jnp.concatenate([sizes[order], place])
-
-    fetched_g, info, own_out, own_qkv, masked_grad = lax.optimization_barrier(
-        (fetched_g, info, own_out, own_qkv, masked_grad)
+    )(w_out, w_qkv)
+    table = [block for pair in block_table() for block in pair]
+    rank, own_rank, other_rank, masked_grad = pl.pallas_call(
+        slot_kernel,
+        out_shape=(
+            jax.ShapeDtypeStruct((1, total), jnp.int32),
+            jax.ShapeDtypeStruct((1, half), jnp.int32),
+            jax.ShapeDtypeStruct((1, half), jnp.int32),
+            jax.ShapeDtypeStruct((capacity, features), low),
+        ),
+        in_specs=specs(pltpu.SMEM, 3) + specs(pltpu.VMEM, 1),
+        out_specs=specs(pltpu.VMEM, 4),
+        compiler_params=pltpu.CompilerParams(vmem_limit_bytes=MAIN_BYTES),
+    )(counts[0], other_counts, jnp.array(table, jnp.int32), upstream)
+
+    fetched_g, rank, own_rank, other_rank, own_out, own_qkv, masked_grad = lax.optimization_barrier(
+        (fetched_g, rank, own_rank, other_rank, own_out, own_qkv, masked_grad)
     )
     blocks_g = share(fetched_g)
     fetched_t, blocks_g = lax.optimization_barrier((fetched_t, blocks_g))
@@ -484,14 +512,14 @@
             jax.ShapeDtypeStruct((rows, features), low),
             jax.ShapeDtypeStruct((width, rows), low),
         ),
-        in_specs=smem + specs(pltpu.VMEM, 5),
+        in_specs=specs(pltpu.VMEM, 6),
         out_specs=specs(pltpu.VMEM, 2),
         scratch_shapes=[pltpu.VMEM((total, features), low)],
         compiler_params=pltpu.CompilerParams(vmem_limit_bytes=MAIN_BYTES),
         cost_estimate=pl.CostEstimate(
             flops=2 * rows * features * (width + total), bytes_accessed=3 * 1024 * 1024, transcendentals=0
         ),
-    )(info, *blocks_g, own_out)
+    )(rank, *blocks_g, own_out)
     blocks_t = share(fetched_t)
 
     send_shape = jax.ShapeDtypeStruct((2, 2, 2 * width, lanes), low)
@@ -502,7 +530,7 @@
         out_shape=(
             send_shape, keep_shape, send_shape, keep_shape, grads_shape
         ),
-        in_specs=smem + specs(pltpu.VMEM, 7),
+        in_specs=specs(pltpu.VMEM, 8),
         out_specs=specs(pltpu.VMEM, 5),
         scratch_shapes=[
             pltpu.VMEM((total, features), low),
@@ -518,7 +546,7 @@
             bytes_accessed=8 * 1024 * 1024,
             transcendentals=4 * total * total,
         ),
-    )(info, *blocks_t, gathered_g, lifted, own_qkv)
+    )(rank, *blocks_t, gathered_g, lifted, own_qkv)
 
     x_first, y_first = across(x_send, 2), across(y_send, 4)
     from_core = across(grads, 1)
@@ -526,13 +554,13 @@
     back_one, back_two = pl.pallas_call(
         normed_kernel,
         out_shape=(block_shape, block_shape),
-        in_specs=smem + specs(pltpu.VMEM, 3),
+        in_specs=specs(pltpu.VMEM, 5),
         out_specs=specs(pltpu.VMEM, 2),
         compiler_params=pltpu.CompilerParams(vmem_limit_bytes=MAIN_BYTES),
         cost_estimate=pl.CostEstimate(
             flops=2 * total * features * width * 3, bytes_accessed=4 * 1024 * 1024, transcendentals=0
         ),
-    )(info, grads, from_core, pair_qkv)
+    )(own_rank, other_rank, grads, from_core, pair_qkv)
     places, back_one = lax.optimization_barrier((positions, back_one))
     _, standard, inv_std = layer_norm(inputs, places[0], ln_gain)
     home_one = lax.ppermute(back_one, axes, first_back)
@@ -564,10 +592,10 @@
             jax.ShapeDtypeStruct((3 * width, lanes), wide),
             jax.ShapeDtypeStruct((lanes, width), wide),
         ),
-        in_specs=smem + specs(pltpu.VMEM, 3),
+        in_specs=specs(pltpu.VMEM, 3),
         out_specs=specs(pltpu.VMEM, 2),
         compiler_params=pltpu.CompilerParams(vmem_limit_bytes=8 * 1024 * 1024),
-    )(guest[None].astype(jnp.int32), from_home, from_guest, own)
+    )(from_home, from_guest, own)
     grad_qkv = grad_qkv.reshape(3, width, lanes)
 
     normed_grad = home_one.astype(wide) + home_two.astype(wide)

time: 69 us -> 68.1 us (0.987)
  waiting for transfers between devices: 11.3 us -> 16.8 us
  local copies, waits for them, and re-layouts: 2.82 us -> 0.04 us
  other arithmetic: 4.65 us -> 2.82 us
  Pallas kernels: 17.9 us -> 16.4 us
    ppermute x2, waiting for transfers between devices: 2.95 us -> 7.47 us  [fetch(): return (lax.ppermute(array, axes, first), two)]
    dynamic_slice x1 -> x0, local copies, waits for them, and re-layouts: 1.3 us -> none  [column_shards(): lax.dynamic_index_in_dim(counts[0], seat, 0, False)]
    select_n x3 -> x0, other arithmetic: 1.12 us -> none  [the longest x1 1.04 us: column_shards(): jnp.where(own_valid[:, None], upstream, jnp.zeros_like(upstream))]
    ppermute x10, waiting for transfers between devices: 4.68 us -> 5.72 us  [across(): return lax.ppermute(array, 'dp', [(i, i ^ bit) for i in range(2 * chips)])]
    concatenate x2 -> x0, local copies, waits for them, and re-layouts: 0.86 us -> none  [the longest x1 0.78 us: column_shards(): jnp.concatenate([table[seat * 2 + core], table[seat * 2 + 1 - core]])]
  transfers between devices with their start and end apart: 18 -> 18, of which waited for: 4 -> 5; matrix products, arithmetic and copies ran while one was open for 11% -> 4% of each run, Pallas kernels for 16% -> 15%
where the time goes in v7:
time: 68.1 us; the launch traced here: 67.9 us
  starting transfers between devices  31 us (46%)
  waiting for transfers between devices  16.8 us (25%)
  Pallas kernels  16.4 us (24%)
  other arithmetic  2.82 us (4%)
  between operations  0.88 us (1%)
    ppermute x2, waiting for transfers between devices, fetch(): return (lax.ppermute(array, axes, first), two)  7.47 us
    ppermute x2, starting transfers between devices, fetch(): two = lax.ppermute(array, axes, second)  6.75 us
    ppermute x10, waiting for transfers between devices, across(): return lax.ppermute(array, 'dp', [(i, i ^ bit) for i in range(2 * chips)])  5.72 us
    ppermute x10, starting transfers between devices, across(): return lax.ppermute(array, 'dp', [(i, i ^ bit) for i in range(2 * chips)])  5.61 us
    ppermute x1, starting transfers between devices, column_shards(): home_two = lax.ppermute(back_two, axes, second)  5.38 us
    pallas_call x1, Pallas kernels, column_shards(): pl.pallas_call(main_kernel, out_shape=(send_shape, keep_shape, send_shape...  5.19 us
    pallas_call x1, Pallas kernels, column_shards(): pl.pallas_call(weight_kernel, out_shape=(jax.ShapeDtypeStruct((features,...  4.31 us
    ppermute x1, starting transfers between devices, column_shards(): from_guest = lax.ppermute(guest_send, axes, guests)  4.21 us
  transfers between devices with their start and end apart: 18, of which 5 were waited for; matrix products, arithmetic and copies ran while one was open for 4% of the time, Pallas kernels for 15%

profile of v7, /device:TPU:1, one launch (start us, length us, event | category | flops | bytes accessed | tf_op | source)
XLA Modules:
  0.0 67.9 jit_solution(5804283727311147175)
XLA Ops:
  0.6 2.7 %collective-permute-start = (bf16[128,1024]{1,0:T(8,128)(2,1)}, bf16[128,1024]{1,0:T(8,128)(2,1)S(1)}, u32[]{:S(2)}, u32[]{:S(2)}) collective-permute-start(bf16[128,1024]{1,0:T(8,128)(2,1)} %bitcast.26), channel_id=1, source_target_pairs={{0,2},{1,0},{2,4},{3,6},{4,1},{5,7},{6,3},{7,5},{8,10},{9,8},{10,1... | collective-permute-start | bytes 786440 | tf_op jit(solution)/shard_map/ppermute | solution.py:458
  3.4 3.9 %collective-permute-start.1 = (bf16[128,1024]{1,0:T(8,128)(2,1)}, bf16[128,1024]{1,0:T(8,128)(2,1)S(1)}, u32[]{:S(2)}, u32[]{:S(2)}) collective-permute-start(bf16[128,1024]{1,0:T(8,128)(2,1)} %bitcast.27), channel_id=1, source_target_pairs={{4,3},{3,4},{1,6},{6,1},{0,0},{5,5},{2,2},{7,7},{12,11},{11,12},{9... | collective-permute-start | bytes 786440 | tf_op jit(solution)/shard_map/ppermute | solution.py:457
  7.3 2.9 %shard_map.114 = bf16[128,1024]{1,0:T(8,128)(2,1)} custom-call(s32[1,128]{1,0:T(1,128)} %places.1, bf16[128,1024]{1,0:T(8,128)(2,1)} %bitcast.31, f32[1,1024]{1,0:T(1,128)} %bitcast.32, f32[1,512]{1,0:T(1,128)} %constant.16.clone.freqs), custom_call_target="tpu_custom_call" | custom-call | tf_op jit(solution)/shard_map/pallas_call | solution.py:468
  10.2 0.8 %collective-permute-start.3 = (bf16[128,1024]{1,0:T(8,128)(2,1)}, bf16[128,1024]{1,0:T(8,128)(2,1)S(1)}, u32[]{:S(2)}, u32[]{:S(2)}) collective-permute-start(bf16[128,1024]{1,0:T(8,128)(2,1)} %shard_map.114), channel_id=1, source_target_pairs={{0,2},{1,0},{2,4},{3,6},{4,1},{5,7},{6,3},{7,5},{8,10},{9,8},{10,1... | collective-permute-start | bytes 786440 | tf_op jit(solution)/shard_map/ppermute | solution.py:458
  11.0 2.8 %collective-permute-start.4 = (bf16[128,1024]{1,0:T(8,128)(2,1)}, bf16[128,1024]{1,0:T(8,128)(2,1)S(1)}, u32[]{:S(2)}, u32[]{:S(2)}) collective-permute-start(bf16[128,1024]{1,0:T(8,128)(2,1)} %shard_map.114), channel_id=1, source_target_pairs={{4,3},{3,4},{1,6},{6,1},{0,0},{5,5},{2,2},{7,7},{12,11},{11,12},{9... | collective-permute-start | bytes 786440 | tf_op jit(solution)/shard_map/ppermute | solution.py:457
  13.8 0.0 copy-start.1
  13.9 0.0 copy-start.2
  13.9 0.0 copy-start.3
  13.9 0.1 collective-permute-start.2
  14.0 4.3 %shard_map.113 = (bf16[1024,256]{1,0:T(8,128)(2,1)S(1)}, bf16[768,1024]{1,0:T(8,128)(2,1)S(1)}, bf16[1536,1024]{1,0:T(8,128)(2,1)}) custom-call(bf16[1024,1024]{1,0:T(8,128)(2,1)} %w_out.1, bf16[3,1024,1024]{2,1,0:T(8,128)(2,1)} %w_qkv.1), custom_call_target="tpu_custom_call" | custom-call | bytes 4194304 | tf_op jit(solution)/shard_map/pallas_call | solution.py:476
  18.3 0.6 shard_map.112
  19.0 0.0 collective-permute-done.1.g1
  19.0 0.6 collective-permute-start.5
  19.5 0.1 collective-permute-start.6
  19.6 7.5 %collective-permute-done.3.t0 = bf16[128,1024]{1,0:T(8,128)(2,1)S(1)} collective-permute-done((bf16[128,1024]{1,0:T(8,128)(2,1)}, bf16[128,1024]{1,0:T(8,128)(2,1)S(1)}, u32[]{:S(2)}, u32[]{:S(2)}) %collective-permute-start.3) | collective-permute-done | bytes 262176 | tf_op jit(solution)/shard_map/ppermute | solution.py:458
  27.1 0.0 collective-permute-done.4.t1
  27.1 0.0 collective-permute-done.5.g2
  27.1 0.0 collective-permute-done.6.g3
  27.1 0.1 collective-permute-start.7
  27.2 0.5 collective-permute-start.8
  27.7 1.0 %shard_map.115 = (bf16[384,1024]{1,0:T(8,128)(2,1)S(1)}, bf16[256,384]{1,0:T(8,128)(2,1)S(1)}) custom-call(s32[1,512]{1,0:T(1,128)S(1)} %get-tuple-element.55.rank, bf16[128,1024]{1,0:T(8,128)(2,1)S(1)} %collective-permute-done.g0, bf16[128,1024]{1,0:T(8,128)(2,1)S(1)} %collective-permute-done.1.g1, bf16[128,1024]{1,0:T(8,128)(2,1)S(1)} %collective-permute-done.5.g2, ...), custom_call_target="tpu_custom_call" | custom-call | flops 603979776 | bytes 3145728 | tf_op jit(solution)/shard_map/pallas_call | solution.py:509
  28.7 0.0 collective-permute-done.7.t2
  28.7 0.4 collective-permute-done.8.t3
  29.1 5.2 %shard_map.116 = (bf16[2,2,512,128]{3,2,1,0:T(8,128)(2,1)S(1)}, f32[2,2,512,128]{3,2,1,0:T(8,128)S(1)}, bf16[2,2,512,128]{3,2,1,0:T(8,128)(2,1)S(1)}, f32[2,2,512,128]{3,2,1,0:T(8,128)S(1)}, bf16[768,384]{1,0:T(8,128)(2,1)S(1)}) custom-call(s32[1,512]{1,0:T(1,128)S(1)} %get-tuple-element.55.rank, bf16[128,1024]{1,0:T(8,128)(2,1)S(1)} %collective-permute-done.3.t0, ...), custom_call_target="tpu_custom_call" | custom-call | flops 2684354560 | bytes 8388608 | tf_op jit(solution)/shard_map/pallas_call | solution.py:528
  34.3 0.0 copy-start.6
  34.3 0.0 copy-start.4
  34.3 0.2 collective-permute-start.9
  34.5 1.2 %collective-permute-start.10 = (bf16[2,2,512,128]{3,2,1,0:T(8,128)(2,1)S(1)}, bf16[2,2,512,128]{3,2,1,0:T(8,128)(2,1)S(1)}, u32[]{:S(2)}, u32[]{:S(2)}) collective-permute-start(bf16[2,2,512,128]{3,2,1,0:T(8,128)(2,1)S(1)} %get-tuple-element.72), channel_id=1, source_target_pairs={{0,8},{4,12},{8,0},{12,4},{16,24},{20,28},{24,16},{28,20},{1,9},{5... | collective-permute-start | bytes 1572872 | tf_op jit(solution)/shard_map/ppermute | solution.py:454
  35.7 1.2 %collective-permute-start.11 = (bf16[2,2,512,128]{3,2,1,0:T(8,128)(2,1)S(1)}, bf16[2,2,512,128]{3,2,1,0:T(8,128)(2,1)S(1)}, u32[]{:S(2)}, u32[]{:S(2)}) collective-permute-start(bf16[2,2,512,128]{3,2,1,0:T(8,128)(2,1)S(1)} %get-tuple-element.73), channel_id=1, source_target_pairs={{0,16},{4,20},{8,24},{12,28},{16,0},{20,4},{24,8},{28,12},{1,17},{... | collective-permute-start | bytes 1572872 | tf_op jit(solution)/shard_map/ppermute | solution.py:454
  36.9 1.5 %shard_map.117 = (bf16[128,1024]{1,0:T(8,128)(2,1)S(1)}, bf16[128,1024]{1,0:T(8,128)(2,1)S(1)}) custom-call(s32[1,256]{1,0:T(1,128)S(1)} %get-tuple-element.53.own_rank, s32[1,256]{1,0:T(1,128)S(1)} %get-tuple-element.54.other_rank, bf16[768,384]{1,0:T(8,128)(2,1)S(1)} %get-tuple-element.68.own, bf16[768,384]{1,0:T(8,128)(2,1)S(1)} %collective-permute-done.9.other, ...), custom_call_target="tpu_custom_call" | custom-call | flops 805306368 | bytes 4194304 | tf_op jit(solution)/shard_map/pallas_call | solution.py:554
  38.4 3.7 %collective-permute-start.12 = (bf16[128,1024]{1,0:T(8,128)(2,1)S(1)}, bf16[128,1024]{1,0:T(8,128)(2,1)S(1)}, u32[]{:S(2)}, u32[]{:S(2)}) collective-permute-start(bf16[128,1024]{1,0:T(8,128)(2,1)S(1)} %get-tuple-element.74), channel_id=1, source_target_pairs={{2,0},{0,1},{4,2},{6,3},{1,4},{7,5},{3,6},{5,7},{10,8},{8,9},{12,1... | collective-permute-start | bytes 786440 | tf_op jit(solution)/shard_map/ppermute | solution.py:566
  42.1 1.0 %multiply_sine_fusion = (f32[128,512]{1,0:T(8,128)S(1)}, f32[128,512]{1,0:T(8,128)S(1)}) fusion(f32[512]{0:T(512)S(1)} %multiply_exponential_fusion, f32[128]{0:T(128)S(1)} %convert_bitcast_fusion), kind=kLoop, calls=%fused_computation.11 | loop fusion | flops 65536 | bytes 526848 | tf_op jit(solution)/shard_map/sin | solution.py:23
  43.1 0.1 fusion.4
  43.2 4.4 %collective-permute-done.10 = bf16[2,2,512,128]{3,2,1,0:T(8,128)(2,1)S(1)} collective-permute-done((bf16[2,2,512,128]{3,2,1,0:T(8,128)(2,1)S(1)}, bf16[2,2,512,128]{3,2,1,0:T(8,128)(2,1)S(1)}, u32[]{:S(2)}, u32[]{:S(2)}) %collective-permute-start.10) | collective-permute-done | bytes 524320 | tf_op jit(solution)/shard_map/ppermute | solution.py:454
  47.6 0.9 %collective-permute-done.11 = bf16[2,2,512,128]{3,2,1,0:T(8,128)(2,1)S(1)} collective-permute-done((bf16[2,2,512,128]{3,2,1,0:T(8,128)(2,1)S(1)}, bf16[2,2,512,128]{3,2,1,0:T(8,128)(2,1)S(1)}, u32[]{:S(2)}, u32[]{:S(2)}) %collective-permute-start.11) | collective-permute-done | bytes 524320 | tf_op jit(solution)/shard_map/ppermute | solution.py:454
  48.5 0.1 fusion.2
  48.6 0.4 collective-permute-start.15
  49.0 0.1 fusion.1
  49.1 1.3 %collective-permute-start.14 = (bf16[2,512,128]{2,1,0:T(8,128)(2,1)S(1)}, bf16[2,512,128]{2,1,0:T(8,128)(2,1)S(1)}, u32[]{:S(2)}, u32[]{:S(2)}) collective-permute-start(bf16[2,512,128]{2,1,0:T(8,128)(2,1)S(1)} %get-tuple-element.93), channel_id=1, source_target_pairs={{0,16},{4,20},{8,24},{12,28},{16,0},{20,4},{24,8},{28,12},{1,17},{... | collective-permute-start | bytes 786440 | tf_op jit(solution)/shard_map/ppermute | solution.py:454
  50.4 5.4 %collective-permute-start.13 = (bf16[128,1024]{1,0:T(8,128)(2,1)S(1)}, bf16[128,1024]{1,0:T(8,128)(2,1)S(1)}, u32[]{:S(2)}, u32[]{:S(2)}) collective-permute-start(bf16[128,1024]{1,0:T(8,128)(2,1)S(1)} %get-tuple-element.77), channel_id=1, source_target_pairs={{4,3},{3,4},{1,6},{6,1},{0,0},{5,5},{2,2},{7,7},{12,11},{11,12},{9... | collective-permute-start | bytes 786440 | tf_op jit(solution)/shard_map/ppermute | solution.py:568
  55.8 0.2 multiply_reduce_fusion.1
  56.0 0.1 shard_map.118
  56.1 1.8 %collective-permute-start.16 = (bf16[1024,128]{1,0:T(8,128)(2,1)S(1)}, bf16[1024,128]{1,0:T(8,128)(2,1)S(1)}, u32[]{:S(2)}, u32[]{:S(2)}) collective-permute-start(bf16[1024,128]{1,0:T(8,128)(2,1)S(1)} %get-tuple-element.84), channel_id=1, source_target_pairs={{0,4},{5,1},{1,0},{4,5},{2,6},{7,3},{3,2},{6,7},{8,12},{13,9},{9,8... | collective-permute-start | bytes 786440 | tf_op jit(solution)/shard_map/ppermute | solution.py:586
  57.9 4.2 %collective-permute-start.17 = (bf16[1024,128]{1,0:T(8,128)(2,1)S(1)}, bf16[1024,128]{1,0:T(8,128)(2,1)S(1)}, u32[]{:S(2)}, u32[]{:S(2)}) collective-permute-start(bf16[1024,128]{1,0:T(8,128)(2,1)S(1)} %get-tuple-element.85), channel_id=1, source_target_pairs={{1,4},{4,1},{3,6},{6,3},{9,12},{12,9},{11,14},{14,11},{17,20},{20,... | collective-permute-start | bytes 786440 | tf_op jit(solution)/shard_map/ppermute | solution.py:587
  62.1 0.3 fusion
  62.4 1.0 %fusion.3 = bf16[1,128,1024]{2,1,0:T(8,128)(2,1)} fusion(f32[128]{0:T(128)S(1)} %get-tuple-element.97, f32[128]{0:T(128)S(1)} %broadcast_multiply_fusion.2, f32[128]{0:T(128)S(1)} %get-tuple-element.98, f32[1024]{0:T(1024)S(1)} %copy-done.5, bf16[128,1024]{1,0:T(8,128)(2,1)S(1)} %collective-permute-done.13, ...), kind=kLoop, calls=%fused_computation.14 | loop fusion | flops 2097152 | bytes 1841152 | tf_op jit(solution)/shard_map/broadcast_in_dim | solution.py:606
  63.4 3.6 %collective-permute-done.17.from_guest = bf16[1024,128]{1,0:T(8,128)(2,1)S(1)} collective-permute-done((bf16[1024,128]{1,0:T(8,128)(2,1)S(1)}, bf16[1024,128]{1,0:T(8,128)(2,1)S(1)}, u32[]{:S(2)}, u32[]{:S(2)}) %collective-permute-start.17) | collective-permute-done | bytes 262176 | tf_op jit(solution)/shard_map/ppermute | solution.py:587
  67.1 0.9 %shard_map.119 = (f32[768,128]{1,0:T(8,128)}, f32[128,256]{1,0:T(8,128)}) custom-call(bf16[1024,128]{1,0:T(8,128)(2,1)S(1)} %collective-permute-done.16.from_home, bf16[1024,128]{1,0:T(8,128)(2,1)S(1)} %collective-permute-done.17.from_guest, f32[1024,128]{1,0:T(8,128)S(1)} %get-tuple-element.86.own), custom_call_target="tpu_custom_call" | custom-call | tf_op jit(solution)/shard_map/pallas_call | solution.py:589
  (22 shorter events, 0.1 us)
Async XLA Ops:
  0.6 18.3 %collective-permute-start = (bf16[128,1024]{1,0:T(8,128)(2,1)}, bf16[128,1024]{1,0:T(8,128)(2,1)S(1)}, u32[]{:S(2)}, u32[]{:S(2)}) collective-permute-start(bf16[128,1024]{1,0:T(8,128)(2,1)} %bitcast.26), channel_id=1, source_target_pairs={{0,2},{1,0},{2,4},{3,6},{4,1},{5,7},{6,3},{7,5},{8,10},{9,8},{10,1... | collective-permute-start | bytes 786440 | tf_op jit(solution)/shard_map/ppermute | solution.py:458
  3.4 15.6 %collective-permute-start.1 = (bf16[128,1024]{1,0:T(8,128)(2,1)}, bf16[128,1024]{1,0:T(8,128)(2,1)S(1)}, u32[]{:S(2)}, u32[]{:S(2)}) collective-permute-start(bf16[128,1024]{1,0:T(8,128)(2,1)} %bitcast.27), channel_id=1, source_target_pairs={{4,3},{3,4},{1,6},{6,1},{0,0},{5,5},{2,2},{7,7},{12,11},{11,12},{9... | collective-permute-start | bytes 786440 | tf_op jit(solution)/shard_map/ppermute | solution.py:457
  10.2 16.9 %collective-permute-start.3 = (bf16[128,1024]{1,0:T(8,128)(2,1)}, bf16[128,1024]{1,0:T(8,128)(2,1)S(1)}, u32[]{:S(2)}, u32[]{:S(2)}) collective-permute-start(bf16[128,1024]{1,0:T(8,128)(2,1)} %shard_map.114), channel_id=1, source_target_pairs={{0,2},{1,0},{2,4},{3,6},{4,1},{5,7},{6,3},{7,5},{8,10},{9,8},{10,1... | collective-permute-start | bytes 786440 | tf_op jit(solution)/shard_map/ppermute | solution.py:458
  11.0 16.1 %collective-permute-start.4 = (bf16[128,1024]{1,0:T(8,128)(2,1)}, bf16[128,1024]{1,0:T(8,128)(2,1)S(1)}, u32[]{:S(2)}, u32[]{:S(2)}) collective-permute-start(bf16[128,1024]{1,0:T(8,128)(2,1)} %shard_map.114), channel_id=1, source_target_pairs={{4,3},{3,4},{1,6},{6,1},{0,0},{5,5},{2,2},{7,7},{12,11},{11,12},{9... | collective-permute-start | bytes 786440 | tf_op jit(solution)/shard_map/ppermute | solution.py:457
  13.8 4.4 %copy-start.1 = (bf16[1,128,1024]{2,1,0:T(8,128)(2,1)S(1)}, bf16[1,128,1024]{2,1,0:T(8,128)(2,1)}, u32[]{:S(2)}) copy-start(bf16[1,128,1024]{2,1,0:T(8,128)(2,1)} %param.15) | copy-start | bytes 786436
  13.9 4.4 %copy-start.2 = (s32[1,4]{1,0:T(1,128)S(1)}, s32[1,4]{1,0:T(1,128)}, u32[]{:S(2)}) copy-start(s32[1,4]{1,0:T(1,128)} %param.11) | copy-start | bytes 52
  13.9 4.4 %copy-start.3 = (s32[16]{0:T(128)S(1)}, s32[16]{0:T(128)}, u32[]{:S(2)}) copy-start(s32[16]{0:T(128)} %constant.17.clone.table) | copy-start | bytes 196
  13.9 4.4 %collective-permute-start.2 = (s32[4]{0:T(128)}, s32[4]{0:T(128)S(1)}, u32[]{:S(2)}, u32[]{:S(2)}) collective-permute-start(s32[4]{0:T(128)} %bitcast.29), channel_id=1, source_target_pairs={{0,4},{4,0},{8,12},{12,8},{16,20},{20,16},{24,28},{28,24},{1,5},{5... | collective-permute-start | bytes 56 | tf_op jit(solution)/shard_map/ppermute | solution.py:454
  19.0 8.1 %collective-permute-start.5 = (bf16[128,1024]{1,0:T(8,128)(2,1)S(1)}, bf16[128,1024]{1,0:T(8,128)(2,1)S(1)}, u32[]{:S(2)}, u32[]{:S(2)}) collective-permute-start(bf16[128,1024]{1,0:T(8,128)(2,1)S(1)} %collective-permute-done.g0), channel_id=1, source_target_pairs={{0,4},{4,0},{8,12},{12,8},{16,20},{20,16},{24,28},{28,24},{1,5},{5... | collective-permute-start | bytes 786440 | tf_op jit(solution)/shard_map/ppermute | solution.py:454
  19.5 7.6 %collective-permute-start.6 = (bf16[128,1024]{1,0:T(8,128)(2,1)S(1)}, bf16[128,1024]{1,0:T(8,128)(2,1)S(1)}, u32[]{:S(2)}, u32[]{:S(2)}) collective-permute-start(bf16[128,1024]{1,0:T(8,128)(2,1)S(1)} %collective-permute-done.1.g1), channel_id=1, source_target_pairs={{0,4},{4,0},{8,12},{12,8},{16,20},{20,16},{24,28},{28,24},{1,5},{5... | collective-permute-start | bytes 786440 | tf_op jit(solution)/shard_map/ppermute | solution.py:454
  27.1 1.6 %collective-permute-start.7 = (bf16[128,1024]{1,0:T(8,128)(2,1)S(1)}, bf16[128,1024]{1,0:T(8,128)(2,1)S(1)}, u32[]{:S(2)}, u32[]{:S(2)}) collective-permute-start(bf16[128,1024]{1,0:T(8,128)(2,1)S(1)} %collective-permute-done.3.t0), channel_id=1, source_target_pairs={{0,4},{4,0},{8,12},{12,8},{16,20},{20,16},{24,28},{28,24},{1,5},{5... | collective-permute-start | bytes 786440 | tf_op jit(solution)/shard_map/ppermute | solution.py:454
  27.2 1.9 %collective-permute-start.8 = (bf16[128,1024]{1,0:T(8,128)(2,1)S(1)}, bf16[128,1024]{1,0:T(8,128)(2,1)S(1)}, u32[]{:S(2)}, u32[]{:S(2)}) collective-permute-start(bf16[128,1024]{1,0:T(8,128)(2,1)S(1)} %collective-permute-done.4.t1), channel_id=1, source_target_pairs={{0,4},{4,0},{8,12},{12,8},{16,20},{20,16},{24,28},{28,24},{1,5},{5... | collective-permute-start | bytes 786440 | tf_op jit(solution)/shard_map/ppermute | solution.py:454
  29.1 7.9 %copy-start = (bf16[1536,1024]{1,0:T(8,128)(2,1)S(1)}, bf16[1536,1024]{1,0:T(8,128)(2,1)}, u32[]{:S(2)}) copy-start(bf16[1536,1024]{1,0:T(8,128)(2,1)} %get-tuple-element.69.weight) | copy-start | bytes 9437188
  34.3 7.8 %copy-start.6 = (s32[1,128]{1,0:T(1,128)S(1)}, s32[1,128]{1,0:T(1,128)}, u32[]{:S(2)}) copy-start(s32[1,128]{1,0:T(1,128)} %places.1) | copy-start | bytes 1540
  34.3 8.8 %copy-start.4 = (bf16[1,128,1024]{2,1,0:T(8,128)(2,1)S(1)}, bf16[1,128,1024]{2,1,0:T(8,128)(2,1)}, u32[]{:S(2)}) copy-start(bf16[1,128,1024]{2,1,0:T(8,128)(2,1)} %param.9) | copy-start | bytes 786436
  34.3 2.6 %collective-permute-start.9 = (bf16[768,384]{1,0:T(8,128)(2,1)S(1)}, bf16[768,384]{1,0:T(8,128)(2,1)S(1)}, u32[]{:S(2)}, u32[]{:S(2)}) collective-permute-start(bf16[768,384]{1,0:T(8,128)(2,1)S(1)} %get-tuple-element.68.own), channel_id=1, source_target_pairs={{0,4},{4,0},{8,12},{12,8},{16,20},{20,16},{24,28},{28,24},{1,5},{5... | collective-permute-start | bytes 1769480 | tf_op jit(solution)/shard_map/ppermute | solution.py:454
  34.5 13.1 %collective-permute-start.10 = (bf16[2,2,512,128]{3,2,1,0:T(8,128)(2,1)S(1)}, bf16[2,2,512,128]{3,2,1,0:T(8,128)(2,1)S(1)}, u32[]{:S(2)}, u32[]{:S(2)}) collective-permute-start(bf16[2,2,512,128]{3,2,1,0:T(8,128)(2,1)S(1)} %get-tuple-element.72), channel_id=1, source_target_pairs={{0,8},{4,12},{8,0},{12,4},{16,24},{20,28},{24,16},{28,20},{1,9},{5... | collective-permute-start | bytes 1572872 | tf_op jit(solution)/shard_map/ppermute | solution.py:454
  35.7 12.8 %collective-permute-start.11 = (bf16[2,2,512,128]{3,2,1,0:T(8,128)(2,1)S(1)}, bf16[2,2,512,128]{3,2,1,0:T(8,128)(2,1)S(1)}, u32[]{:S(2)}, u32[]{:S(2)}) collective-permute-start(bf16[2,2,512,128]{3,2,1,0:T(8,128)(2,1)S(1)} %get-tuple-element.73), channel_id=1, source_target_pairs={{0,16},{4,20},{8,24},{12,28},{16,0},{20,4},{24,8},{28,12},{1,17},{... | collective-permute-start | bytes 1572872 | tf_op jit(solution)/shard_map/ppermute | solution.py:454
  38.4 10.1 %collective-permute-start.12 = (bf16[128,1024]{1,0:T(8,128)(2,1)S(1)}, bf16[128,1024]{1,0:T(8,128)(2,1)S(1)}, u32[]{:S(2)}, u32[]{:S(2)}) collective-permute-start(bf16[128,1024]{1,0:T(8,128)(2,1)S(1)} %get-tuple-element.74), channel_id=1, source_target_pairs={{2,0},{0,1},{4,2},{6,3},{1,4},{7,5},{3,6},{5,7},{10,8},{8,9},{12,1... | collective-permute-start | bytes 786440 | tf_op jit(solution)/shard_map/ppermute | solution.py:566
  48.5 13.6 %copy-start.5 = (f32[1024]{0:T(1024)S(1)}, f32[1024]{0:T(1024)}, u32[]{:S(2)}) copy-start(f32[1024]{0:T(1024)} %param.12) | copy-start | bytes 12292
  48.6 7.4 %collective-permute-start.15 = (bf16[2,512,128]{2,1,0:T(8,128)(2,1)S(1)}, bf16[2,512,128]{2,1,0:T(8,128)(2,1)S(1)}, u32[]{:S(2)}, u32[]{:S(2)}) collective-permute-start(bf16[2,512,128]{2,1,0:T(8,128)(2,1)S(1)} %get-tuple-element.91), channel_id=1, source_target_pairs={{0,8},{4,12},{8,0},{12,4},{16,24},{20,28},{24,16},{28,20},{1,9},{5... | collective-permute-start | bytes 786440 | tf_op jit(solution)/shard_map/ppermute | solution.py:454
  49.1 6.9 %collective-permute-start.14 = (bf16[2,512,128]{2,1,0:T(8,128)(2,1)S(1)}, bf16[2,512,128]{2,1,0:T(8,128)(2,1)S(1)}, u32[]{:S(2)}, u32[]{:S(2)}) collective-permute-start(bf16[2,512,128]{2,1,0:T(8,128)(2,1)S(1)} %get-tuple-element.93), channel_id=1, source_target_pairs={{0,16},{4,20},{8,24},{12,28},{16,0},{20,4},{24,8},{28,12},{1,17},{... | collective-permute-start | bytes 786440 | tf_op jit(solution)/shard_map/ppermute | solution.py:454
  50.4 11.7 %collective-permute-start.13 = (bf16[128,1024]{1,0:T(8,128)(2,1)S(1)}, bf16[128,1024]{1,0:T(8,128)(2,1)S(1)}, u32[]{:S(2)}, u32[]{:S(2)}) collective-permute-start(bf16[128,1024]{1,0:T(8,128)(2,1)S(1)} %get-tuple-element.77), channel_id=1, source_target_pairs={{4,3},{3,4},{1,6},{6,1},{0,0},{5,5},{2,2},{7,7},{12,11},{11,12},{9... | collective-permute-start | bytes 786440 | tf_op jit(solution)/shard_map/ppermute | solution.py:568
  56.1 7.3 %collective-permute-start.16 = (bf16[1024,128]{1,0:T(8,128)(2,1)S(1)}, bf16[1024,128]{1,0:T(8,128)(2,1)S(1)}, u32[]{:S(2)}, u32[]{:S(2)}) collective-permute-start(bf16[1024,128]{1,0:T(8,128)(2,1)S(1)} %get-tuple-element.84), channel_id=1, source_target_pairs={{0,4},{5,1},{1,0},{4,5},{2,6},{7,3},{3,2},{6,7},{8,12},{13,9},{9,8... | collective-permute-start | bytes 786440 | tf_op jit(solution)/shard_map/ppermute | solution.py:586
  57.9 9.2 %collective-permute-start.17 = (bf16[1024,128]{1,0:T(8,128)(2,1)S(1)}, bf16[1024,128]{1,0:T(8,128)(2,1)S(1)}, u32[]{:S(2)}, u32[]{:S(2)}) collective-permute-start(bf16[1024,128]{1,0:T(8,128)(2,1)S(1)} %get-tuple-element.85), channel_id=1, source_target_pairs={{1,4},{4,1},{3,6},{6,3},{9,12},{12,9},{11,14},{14,11},{17,20},{20,... | collective-permute-start | bytes 786440 | tf_op jit(solution)/shard_map/ppermute | solution.py:587

commit v8 on v7

--- a/solution.py
+++ b/solution.py
@@ -394,28 +394,33 @@
     back_two[...] = total[capacity:half].astype(back_two.dtype)
 
 
-def sum_kernel(x_part, y_part, x_second, y_second, home_send, guest_send, own):
-    half = x_part.shape[1]
-    for rows, part, second in ((0, x_part, x_second), (half, y_part, y_second)):
-        span = pl.ds(rows, half)
-        home_send[span, :] = (part[0] + second[0].astype(part.dtype)).astype(home_send.dtype)
-        total = part[1] + second[1].astype(part.dtype)
-        guest_send[span, :] = total.astype(guest_send.dtype)
-        own[span, :] = total
-
-
-def final_kernel(from_home, from_guest, own, grad_qkv, grad_out, *, factor):
+def split_kernel(keep, first, _, home_send, guest_send, own):
+    for slot in range(keep.shape[0]):
+        home_send[slot] = (keep[slot, 0] + first[slot, 0].astype(keep.dtype)).astype(home_send.dtype)
+        total = keep[slot, 1] + first[slot, 1].astype(keep.dtype)
+        guest_send[slot] = total.astype(guest_send.dtype)
+        own[slot] = total
+
+
+def joined(from_home, from_guest, own, wide=jnp.float32):
+    guest = seats()[2]
+    return from_home.astype(wide) + jnp.where(guest == 0, own, from_guest.astype(wide))
+
+
+def turn_kernel(from_home, from_guest, own, keep, send):
+    keep[...] = joined(from_home[0], from_guest[0], own[0])
+    send[...] = joined(from_home[1], from_guest[1], own[1]).astype(send.dtype)
+
+
+def final_kernel(from_home, from_guest, own, keep, last, grad_qkv, grad_out, *, factor):
+    half = own.shape[0]
     rows, lanes = grad_qkv.shape
-    guest = seats()[2]
-
-    def finish(low_row, high_row):
-        span = slice(low_row, high_row)
-        rest = jnp.where(guest == 0, own[span, :], from_guest[span, :].astype(jnp.float32))
-        return (from_home[span, :].astype(jnp.float32) + rest) * factor
-
-    grad_qkv[...] = finish(0, rows)
-    grad_out[:, 0:lanes] = finish(rows, rows + lanes)
-    grad_out[:, lanes : 2 * lanes] = finish(rows + lanes, rows + 2 * lanes)
+    grad_qkv[0:half, :] = joined(from_home[...], from_guest[...], own[...]) * factor
+    rest = (keep[...] + last[...].astype(keep.dtype)) * factor
+    grad_qkv[half:rows, :] = rest[0 : rows - half]
+    for part in range(2):
+        low_row = rows - half + part * lanes
+        grad_out[:, part * lanes : (part + 1) * lanes] = rest[low_row : low_row + lanes]
 
 
 def specs(space, count):
@@ -564,38 +569,56 @@
     places, back_one = lax.optimization_barrier((positions, back_one))
     _, standard, inv_std = layer_norm(inputs, places[0], ln_gain)
     home_one = lax.ppermute(back_one, axes, first_back)
-    x_first, y_first, home_one, back_two = lax.optimization_barrier((x_first, y_first, home_one, back_two))
+    token = across(back_one[:16], 1)
+    x_first, y_first, token = lax.optimization_barrier((x_first, y_first, token))
     home_two = lax.ppermute(back_two, axes, second)
     x_second = across((x_keep[1] + x_first[1].astype(wide)).astype(low), 4)
-    y_second = across((y_keep[1] + y_first[1].astype(wide)).astype(low), 2)
     x_part = x_keep[0] + x_first[0].astype(wide)
-    y_part = y_keep[0] + y_first[0].astype(wide)
-    x_part, y_part = lax.optimization_barrier((x_part, y_part))
-    home_send, guest_send, own = pl.pallas_call(
-        sum_kernel,
+    small = pltpu.CompilerParams(vmem_limit_bytes=12 * 1024 * 1024)
+    part_shape = (2, 2 * width, lanes)
+
+    def split(keep, first, token):
+        return pl.pallas_call(
+            split_kernel,
+            out_shape=tuple(
+                jax.ShapeDtypeStruct(keep.shape[:1] + keep.shape[2:], dtype) for dtype in (low, low, wide)
+            ),
+            in_specs=specs(pltpu.VMEM, 2) + specs(pl.ANY, 1),
+            out_specs=specs(pltpu.VMEM, 3),
+            compiler_params=small,
+        )(keep, first, token)
+
+    y_home, y_guest, y_own = split(y_keep, y_first, token)
+    from_home = lax.ppermute(y_home, axes, home)
+    from_guest = lax.ppermute(y_guest, axes, guests)
+    y_part, y_send_last = pl.pallas_call(
+        turn_kernel,
         out_shape=(
-            jax.ShapeDtypeStruct((4 * width, lanes), low),
-            jax.ShapeDtypeStruct((4 * width, lanes), low),
-            jax.ShapeDtypeStruct((4 * width, lanes), wide),
-        ),
-        in_specs=specs(pltpu.VMEM, 4),
-        out_specs=specs(pltpu.VMEM, 3),
-        compiler_params=pltpu.CompilerParams(vmem_limit_bytes=16 * 1024 * 1024),
-        cost_estimate=pl.CostEstimate(flops=4 * width * 2 * lanes, bytes_accessed=2 * 1024 * 1024, transcendentals=0),
-    )(x_part, y_part, x_second, y_second)
-    from_home = lax.ppermute(home_send, axes, home)
-    from_guest = lax.ppermute(guest_send, axes, guests)
-
+            jax.ShapeDtypeStruct(part_shape[1:], wide),
+            jax.ShapeDtypeStruct(part_shape[1:], low),
+        ),
+        in_specs=specs(pltpu.VMEM, 3),
+        out_specs=specs(pltpu.VMEM, 2),
+        compiler_params=small,
+    )(from_home, from_guest, y_own)
+    y_last = across(y_send_last, 2)
+    x_home, x_guest, x_own = split(x_part[None], x_second[None], token)
     grad_qkv, grad_out = pl.pallas_call(
         functools.partial(final_kernel, factor=factor),
         out_shape=(
             jax.ShapeDtypeStruct((3 * width, lanes), wide),
             jax.ShapeDtypeStruct((lanes, width), wide),
         ),
-        in_specs=specs(pltpu.VMEM, 3),
+        in_specs=specs(pltpu.VMEM, 5),
         out_specs=specs(pltpu.VMEM, 2),
-        compiler_params=pltpu.CompilerParams(vmem_limit_bytes=8 * 1024 * 1024),
-    )(from_home, from_guest, own)
+        compiler_params=small,
+    )(
+        lax.ppermute(x_home[0], axes, home),
+        lax.ppermute(x_guest[0], axes, guests),
+        x_own[0],
+        y_part,
+        y_last,
+    )
     grad_qkv = grad_qkv.reshape(3, width, lanes)
 
     normed_grad = home_one.astype(wide) + home_two.astype(wide)

time: 68.1 us -> 67.4 us (0.990)
  waiting for transfers between devices: 16.8 us -> 15.3 us
  starting transfers between devices: 31 us -> 31.7 us
    ppermute x2 -> x4, starting transfers between devices: 5.98 us -> 9.41 us  [the longest x1 3.94 us: column_shards(): lax.ppermute(x_guest[0], axes, guests)]
    ppermute x10 -> x11, waiting for transfers between devices: 5.72 us -> 2.72 us  [across(): return lax.ppermute(array, 'dp', [(i, i ^ bit) for i in range(2 * chips)])]
    ppermute x1, starting transfers between devices: 5.38 us -> 2.73 us  [column_shards(): home_two = lax.ppermute(back_two, axes, second)]
    ppermute x2 -> x4, waiting for transfers between devices: 3.62 us -> 5.05 us  [the longest x1 3.42 us: column_shards(): from_guest = lax.ppermute(y_guest, axes, guests)]
    ppermute x10 -> x11, starting transfers between devices: 5.61 us -> 5.6 us  [across(): return lax.ppermute(array, 'dp', [(i, i ^ bit) for i in range(2 * chips)])]
  transfers between devices with their start and end apart: 18 -> 21, of which waited for: 5 -> 6; matrix products, arithmetic and copies ran while one was open for 4% -> 4% of each run, Pallas kernels for 15% -> 16%
where the time goes in v8:
time: 67.4 us; the launch traced here: 67.2 us
  starting transfers between devices  31.7 us (47%)
  Pallas kernels  16.5 us (24%)
  waiting for transfers between devices  15.3 us (23%)
  other arithmetic  2.76 us (4%)
  between operations  0.9 us (1%)
    ppermute x2, waiting for transfers between devices, fetch(): return (lax.ppermute(array, axes, first), two)  7.47 us
    ppermute x2, starting transfers between devices, fetch(): two = lax.ppermute(array, axes, second)  6.75 us
    ppermute x11, starting transfers between devices, across(): return lax.ppermute(array, 'dp', [(i, i ^ bit) for i in range(2 * chips)])  5.6 us
    pallas_call x1, Pallas kernels, column_shards(): pl.pallas_call(main_kernel, out_shape=(send_shape, keep_shape, send_shape...  5.18 us
    pallas_call x1, Pallas kernels, column_shards(): pl.pallas_call(weight_kernel, out_shape=(jax.ShapeDtypeStruct((features,...  4.31 us
    ppermute x1, starting transfers between devices, column_shards(): lax.ppermute(x_guest[0], axes, guests)  3.94 us
    ppermute x1, starting transfers between devices, column_shards(): home_one = lax.ppermute(back_one, axes, first_back)  3.68 us
    ppermute x2, starting transfers between devices, fetch(): return (lax.ppermute(array, axes, first), two)  3.56 us
  transfers between devices with their start and end apart: 21, of which 6 were waited for; matrix products, arithmetic and copies ran while one was open for 4% of the time, Pallas kernels for 16%

profile of v8, /device:TPU:1, one launch (start us, length us, event | category | flops | bytes accessed | tf_op | source)
XLA Modules:
  0.0 67.2 jit_solution(1162632397068603413)
XLA Ops:
  0.6 2.7 %collective-permute-start = (bf16[128,1024]{1,0:T(8,128)(2,1)}, bf16[128,1024]{1,0:T(8,128)(2,1)S(1)}, u32[]{:S(2)}, u32[]{:S(2)}) collective-permute-start(bf16[128,1024]{1,0:T(8,128)(2,1)} %bitcast.26), channel_id=1, source_target_pairs={{0,2},{1,0},{2,4},{3,6},{4,1},{5,7},{6,3},{7,5},{8,10},{9,8},{10,1... | collective-permute-start | bytes 786440 | tf_op jit(solution)/shard_map/ppermute | solution.py:463
  3.4 3.9 %collective-permute-start.1 = (bf16[128,1024]{1,0:T(8,128)(2,1)}, bf16[128,1024]{1,0:T(8,128)(2,1)S(1)}, u32[]{:S(2)}, u32[]{:S(2)}) collective-permute-start(bf16[128,1024]{1,0:T(8,128)(2,1)} %bitcast.27), channel_id=1, source_target_pairs={{4,3},{3,4},{1,6},{6,1},{0,0},{5,5},{2,2},{7,7},{12,11},{11,12},{9... | collective-permute-start | bytes 786440 | tf_op jit(solution)/shard_map/ppermute | solution.py:462
  7.3 2.9 %shard_map.114 = bf16[128,1024]{1,0:T(8,128)(2,1)} custom-call(s32[1,128]{1,0:T(1,128)} %places.1, bf16[128,1024]{1,0:T(8,128)(2,1)} %bitcast.33, f32[1,1024]{1,0:T(1,128)} %bitcast.34, f32[1,512]{1,0:T(1,128)} %constant.16.clone.freqs), custom_call_target="tpu_custom_call" | custom-call | tf_op jit(solution)/shard_map/pallas_call | solution.py:473
  10.2 0.8 %collective-permute-start.3 = (bf16[128,1024]{1,0:T(8,128)(2,1)}, bf16[128,1024]{1,0:T(8,128)(2,1)S(1)}, u32[]{:S(2)}, u32[]{:S(2)}) collective-permute-start(bf16[128,1024]{1,0:T(8,128)(2,1)} %shard_map.114), channel_id=1, source_target_pairs={{0,2},{1,0},{2,4},{3,6},{4,1},{5,7},{6,3},{7,5},{8,10},{9,8},{10,1... | collective-permute-start | bytes 786440 | tf_op jit(solution)/shard_map/ppermute | solution.py:463
  11.0 2.8 %collective-permute-start.4 = (bf16[128,1024]{1,0:T(8,128)(2,1)}, bf16[128,1024]{1,0:T(8,128)(2,1)S(1)}, u32[]{:S(2)}, u32[]{:S(2)}) collective-permute-start(bf16[128,1024]{1,0:T(8,128)(2,1)} %shard_map.114), channel_id=1, source_target_pairs={{4,3},{3,4},{1,6},{6,1},{0,0},{5,5},{2,2},{7,7},{12,11},{11,12},{9... | collective-permute-start | bytes 786440 | tf_op jit(solution)/shard_map/ppermute | solution.py:462
  13.8 0.0 copy-start.1
  13.9 0.0 copy-start.2
  13.9 0.0 copy-start.3
  13.9 0.1 collective-permute-start.2
  14.0 4.3 %shard_map.113 = (bf16[1024,256]{1,0:T(8,128)(2,1)S(1)}, bf16[768,1024]{1,0:T(8,128)(2,1)S(1)}, bf16[1536,1024]{1,0:T(8,128)(2,1)}) custom-call(bf16[1024,1024]{1,0:T(8,128)(2,1)} %w_out.1, bf16[3,1024,1024]{2,1,0:T(8,128)(2,1)} %w_qkv.1), custom_call_target="tpu_custom_call" | custom-call | bytes 4194304 | tf_op jit(solution)/shard_map/pallas_call | solution.py:481
  18.3 0.6 shard_map.112
  19.0 0.6 collective-permute-start.5
  19.5 0.1 collective-permute-start.6
  19.6 7.5 %collective-permute-done.3.t0 = bf16[128,1024]{1,0:T(8,128)(2,1)S(1)} collective-permute-done((bf16[128,1024]{1,0:T(8,128)(2,1)}, bf16[128,1024]{1,0:T(8,128)(2,1)S(1)}, u32[]{:S(2)}, u32[]{:S(2)}) %collective-permute-start.3) | collective-permute-done | bytes 262176 | tf_op jit(solution)/shard_map/ppermute | solution.py:463
  27.1 0.1 collective-permute-start.7
  27.2 0.5 collective-permute-start.8
  27.7 1.0 %shard_map.115 = (bf16[384,1024]{1,0:T(8,128)(2,1)S(1)}, bf16[256,384]{1,0:T(8,128)(2,1)S(1)}) custom-call(s32[1,512]{1,0:T(1,128)S(1)} %get-tuple-element.57.rank, bf16[128,1024]{1,0:T(8,128)(2,1)S(1)} %collective-permute-done.g0, bf16[128,1024]{1,0:T(8,128)(2,1)S(1)} %collective-permute-done.1.g1, bf16[128,1024]{1,0:T(8,128)(2,1)S(1)} %collective-permute-done.5.g2, ...), custom_call_target="tpu_custom_call" | custom-call | flops 603979776 | bytes 3145728 | tf_op jit(solution)/shard_map/pallas_call | solution.py:514
  28.6 0.0 collective-permute-done.7.t2
  28.7 0.4 collective-permute-done.8.t3
  29.1 5.2 %shard_map.116 = (bf16[2,2,512,128]{3,2,1,0:T(8,128)(2,1)S(1)}, f32[2,2,512,128]{3,2,1,0:T(8,128)S(1)}, bf16[2,2,512,128]{3,2,1,0:T(8,128)(2,1)S(1)}, f32[2,2,512,128]{3,2,1,0:T(8,128)S(1)}, bf16[768,384]{1,0:T(8,128)(2,1)S(1)}) custom-call(s32[1,512]{1,0:T(1,128)S(1)} %get-tuple-element.57.rank, bf16[128,1024]{1,0:T(8,128)(2,1)S(1)} %collective-permute-done.3.t0, ...), custom_call_target="tpu_custom_call" | custom-call | flops 2684354560 | bytes 8388608 | tf_op jit(solution)/shard_map/pallas_call | solution.py:533
  34.3 0.0 copy-start.4
  34.3 0.2 collective-permute-start.9
  34.5 1.2 %collective-permute-start.12 = (bf16[2,2,512,128]{3,2,1,0:T(8,128)(2,1)S(1)}, bf16[2,2,512,128]{3,2,1,0:T(8,128)(2,1)S(1)}, u32[]{:S(2)}, u32[]{:S(2)}) collective-permute-start(bf16[2,2,512,128]{3,2,1,0:T(8,128)(2,1)S(1)} %get-tuple-element.77), channel_id=1, source_target_pairs={{0,8},{4,12},{8,0},{12,4},{16,24},{20,28},{24,16},{28,20},{1,9},{5... | collective-permute-start | bytes 1572872 | tf_op jit(solution)/shard_map/ppermute | solution.py:459
  35.7 1.2 %collective-permute-start.13 = (bf16[2,2,512,128]{3,2,1,0:T(8,128)(2,1)S(1)}, bf16[2,2,512,128]{3,2,1,0:T(8,128)(2,1)S(1)}, u32[]{:S(2)}, u32[]{:S(2)}) collective-permute-start(bf16[2,2,512,128]{3,2,1,0:T(8,128)(2,1)S(1)} %get-tuple-element.78), channel_id=1, source_target_pairs={{0,16},{4,20},{8,24},{12,28},{16,0},{20,4},{24,8},{28,12},{1,17},{... | collective-permute-start | bytes 1572872 | tf_op jit(solution)/shard_map/ppermute | solution.py:459
  36.9 1.5 %shard_map.117 = (bf16[128,1024]{1,0:T(8,128)(2,1)S(1)}, bf16[128,1024]{1,0:T(8,128)(2,1)S(1)}) custom-call(s32[1,256]{1,0:T(1,128)S(1)} %get-tuple-element.55.own_rank, s32[1,256]{1,0:T(1,128)S(1)} %get-tuple-element.56.other_rank, bf16[768,384]{1,0:T(8,128)(2,1)S(1)} %get-tuple-element.70.own, bf16[768,384]{1,0:T(8,128)(2,1)S(1)} %collective-permute-done.9.other, ...), custom_call_target="tpu_custom_call" | custom-call | flops 805306368 | bytes 4194304 | tf_op jit(solution)/shard_map/pallas_call | solution.py:559
  38.4 0.0 copy-start.5
  38.4 3.7 %collective-permute-start.10 = (bf16[128,1024]{1,0:T(8,128)(2,1)S(1)}, bf16[128,1024]{1,0:T(8,128)(2,1)S(1)}, u32[]{:S(2)}, u32[]{:S(2)}) collective-permute-start(bf16[128,1024]{1,0:T(8,128)(2,1)S(1)} %get-tuple-element.74), channel_id=1, source_target_pairs={{2,0},{0,1},{4,2},{6,3},{1,4},{7,5},{3,6},{5,7},{10,8},{8,9},{12,1... | collective-permute-start | bytes 786440 | tf_op jit(solution)/shard_map/ppermute | solution.py:571
  42.1 2.7 %collective-permute-start.11 = (bf16[128,1024]{1,0:T(8,128)(2,1)S(1)}, bf16[128,1024]{1,0:T(8,128)(2,1)S(1)}, u32[]{:S(2)}, u32[]{:S(2)}) collective-permute-start(bf16[128,1024]{1,0:T(8,128)(2,1)S(1)} %get-tuple-element.75), channel_id=1, source_target_pairs={{4,3},{3,4},{1,6},{6,1},{0,0},{5,5},{2,2},{7,7},{12,11},{11,12},{9... | collective-permute-start | bytes 786440 | tf_op jit(solution)/shard_map/ppermute | solution.py:574
  44.9 1.0 %multiply_sine_fusion = (f32[128,512]{1,0:T(8,128)S(1)}, f32[128,512]{1,0:T(8,128)S(1)}) fusion(f32[512]{0:T(512)S(1)} %multiply_exponential_fusion, f32[128]{0:T(128)S(1)} %convert_bitcast_fusion), kind=kLoop, calls=%fused_computation.9 | loop fusion | flops 65536 | bytes 526848 | tf_op jit(solution)/shard_map/sin | solution.py:23
  45.9 0.1 fusion.3
  46.0 0.2 multiply_reduce_fusion.1
  46.2 1.4 %collective-permute-done.12 = bf16[2,2,512,128]{3,2,1,0:T(8,128)(2,1)S(1)} collective-permute-done((bf16[2,2,512,128]{3,2,1,0:T(8,128)(2,1)S(1)}, bf16[2,2,512,128]{3,2,1,0:T(8,128)(2,1)S(1)}, u32[]{:S(2)}, u32[]{:S(2)}) %collective-permute-start.12) | collective-permute-done | bytes 524320 | tf_op jit(solution)/shard_map/ppermute | solution.py:459
  47.6 0.9 %collective-permute-done.13.first = bf16[2,2,512,128]{3,2,1,0:T(8,128)(2,1)S(1)} collective-permute-done((bf16[2,2,512,128]{3,2,1,0:T(8,128)(2,1)S(1)}, bf16[2,2,512,128]{3,2,1,0:T(8,128)(2,1)S(1)}, u32[]{:S(2)}, u32[]{:S(2)}) %collective-permute-start.13) | collective-permute-done | bytes 524320 | tf_op jit(solution)/shard_map/ppermute | solution.py:459
  48.5 0.1 shard_map.119
  48.6 2.3 %collective-permute-start.18 = (bf16[2,512,128]{2,1,0:T(8,128)(2,1)S(1)}, bf16[2,512,128]{2,1,0:T(8,128)(2,1)S(1)}, u32[]{:S(2)}, u32[]{:S(2)}) collective-permute-start(bf16[2,512,128]{2,1,0:T(8,128)(2,1)S(1)} %get-tuple-element.86), channel_id=1, source_target_pairs={{0,4},{5,1},{1,0},{4,5},{2,6},{7,3},{3,2},{6,7},{8,12},{13,9},{9,8... | collective-permute-start | bytes 786440 | tf_op jit(solution)/shard_map/ppermute | solution.py:592
  50.9 3.1 %collective-permute-start.19 = (bf16[2,512,128]{2,1,0:T(8,128)(2,1)S(1)}, bf16[2,512,128]{2,1,0:T(8,128)(2,1)S(1)}, u32[]{:S(2)}, u32[]{:S(2)}) collective-permute-start(bf16[2,512,128]{2,1,0:T(8,128)(2,1)S(1)} %get-tuple-element.87), channel_id=1, source_target_pairs={{1,4},{4,1},{3,6},{6,3},{9,12},{12,9},{11,14},{14,11},{17,20},{20,... | collective-permute-start | bytes 786440 | tf_op jit(solution)/shard_map/ppermute | solution.py:593
  54.0 0.1 fusion.1
  54.1 1.3 %collective-permute-start.15 = (bf16[2,512,128]{2,1,0:T(8,128)(2,1)S(1)}, bf16[2,512,128]{2,1,0:T(8,128)(2,1)S(1)}, u32[]{:S(2)}, u32[]{:S(2)}) collective-permute-start(bf16[2,512,128]{2,1,0:T(8,128)(2,1)S(1)} %get-tuple-element.95), channel_id=1, source_target_pairs={{0,16},{4,20},{8,24},{12,28},{16,0},{20,4},{24,8},{28,12},{1,17},{... | collective-permute-start | bytes 786440 | tf_op jit(solution)/shard_map/ppermute | solution.py:459
  55.4 0.3 fusion
  55.7 3.4 %collective-permute-done.19.from_guest = bf16[2,512,128]{2,1,0:T(8,128)(2,1)S(1)} collective-permute-done((bf16[2,512,128]{2,1,0:T(8,128)(2,1)S(1)}, bf16[2,512,128]{2,1,0:T(8,128)(2,1)S(1)}, u32[]{:S(2)}, u32[]{:S(2)}) %collective-permute-start.19) | collective-permute-done | bytes 262176 | tf_op jit(solution)/shard_map/ppermute | solution.py:593
  59.2 0.1 shard_map.120
  59.3 0.4 collective-permute-start.20
  59.6 0.1 shard_map.118
  59.7 0.1 collective-permute-start.16
  59.8 3.9 %collective-permute-start.17 = (bf16[512,128]{1,0:T(8,128)(2,1)S(1)}, bf16[512,128]{1,0:T(8,128)(2,1)S(1)}, u32[]{:S(2)}, u32[]{:S(2)}) collective-permute-start(bf16[512,128]{1,0:T(8,128)(2,1)S(1)} %bitcast.31), channel_id=1, source_target_pairs={{1,4},{4,1},{3,6},{6,3},{9,12},{12,9},{11,14},{14,11},{17,20},{20,... | collective-permute-start | bytes 393224 | tf_op jit(solution)/shard_map/ppermute | solution.py:617
  63.7 1.0 %fusion.2 = bf16[1,128,1024]{2,1,0:T(8,128)(2,1)} fusion(f32[128]{0:T(128)S(1)} %get-tuple-element.99, f32[128]{0:T(128)S(1)} %broadcast_multiply_fusion.2, f32[128]{0:T(128)S(1)} %get-tuple-element.100, f32[1024]{0:T(1024)S(1)} %copy-done.5, bf16[128,1024]{1,0:T(8,128)(2,1)S(1)} %collective-permute-done.11, ...), kind=kLoop, calls=%fused_computation.11 | loop fusion | flops 2097152 | bytes 1841152 | tf_op jit(solution)/shard_map/broadcast_in_dim | solution.py:629
  64.7 1.6 %collective-permute-done.17.from_guest = bf16[512,128]{1,0:T(8,128)(2,1)S(1)} collective-permute-done((bf16[512,128]{1,0:T(8,128)(2,1)S(1)}, bf16[512,128]{1,0:T(8,128)(2,1)S(1)}, u32[]{:S(2)}, u32[]{:S(2)}) %collective-permute-start.17) | collective-permute-done | bytes 131104 | tf_op jit(solution)/shard_map/ppermute | solution.py:617
  66.3 0.9 %shard_map.121 = (f32[768,128]{1,0:T(8,128)}, f32[128,256]{1,0:T(8,128)}) custom-call(bf16[512,128]{1,0:T(8,128)(2,1)S(1)} %collective-permute-done.16.from_home, bf16[512,128]{1,0:T(8,128)(2,1)S(1)} %collective-permute-done.17.from_guest, f32[512,128]{1,0:T(8,128)S(1)} %bitcast.25, f32[512,128]{1,0:T(8,128)S(1)} %get-tuple-element.89.keep, ...), custom_call_target="tpu_custom_call" | custom-call | tf_op jit(solution)/shard_map/pallas_call | solution.py:606
  (30 shorter events, 0.1 us)
Async XLA Ops:
  0.6 18.3 %collective-permute-start = (bf16[128,1024]{1,0:T(8,128)(2,1)}, bf16[128,1024]{1,0:T(8,128)(2,1)S(1)}, u32[]{:S(2)}, u32[]{:S(2)}) collective-permute-start(bf16[128,1024]{1,0:T(8,128)(2,1)} %bitcast.26), channel_id=1, source_target_pairs={{0,2},{1,0},{2,4},{3,6},{4,1},{5,7},{6,3},{7,5},{8,10},{9,8},{10,1... | collective-permute-start | bytes 786440 | tf_op jit(solution)/shard_map/ppermute | solution.py:463
  3.4 15.6 %collective-permute-start.1 = (bf16[128,1024]{1,0:T(8,128)(2,1)}, bf16[128,1024]{1,0:T(8,128)(2,1)S(1)}, u32[]{:S(2)}, u32[]{:S(2)}) collective-permute-start(bf16[128,1024]{1,0:T(8,128)(2,1)} %bitcast.27), channel_id=1, source_target_pairs={{4,3},{3,4},{1,6},{6,1},{0,0},{5,5},{2,2},{7,7},{12,11},{11,12},{9... | collective-permute-start | bytes 786440 | tf_op jit(solution)/shard_map/ppermute | solution.py:462
  10.2 16.9 %collective-permute-start.3 = (bf16[128,1024]{1,0:T(8,128)(2,1)}, bf16[128,1024]{1,0:T(8,128)(2,1)S(1)}, u32[]{:S(2)}, u32[]{:S(2)}) collective-permute-start(bf16[128,1024]{1,0:T(8,128)(2,1)} %shard_map.114), channel_id=1, source_target_pairs={{0,2},{1,0},{2,4},{3,6},{4,1},{5,7},{6,3},{7,5},{8,10},{9,8},{10,1... | collective-permute-start | bytes 786440 | tf_op jit(solution)/shard_map/ppermute | solution.py:463
  11.0 16.1 %collective-permute-start.4 = (bf16[128,1024]{1,0:T(8,128)(2,1)}, bf16[128,1024]{1,0:T(8,128)(2,1)S(1)}, u32[]{:S(2)}, u32[]{:S(2)}) collective-permute-start(bf16[128,1024]{1,0:T(8,128)(2,1)} %shard_map.114), channel_id=1, source_target_pairs={{4,3},{3,4},{1,6},{6,1},{0,0},{5,5},{2,2},{7,7},{12,11},{11,12},{9... | collective-permute-start | bytes 786440 | tf_op jit(solution)/shard_map/ppermute | solution.py:462
  13.8 4.5 %copy-start.1 = (bf16[1,128,1024]{2,1,0:T(8,128)(2,1)S(1)}, bf16[1,128,1024]{2,1,0:T(8,128)(2,1)}, u32[]{:S(2)}) copy-start(bf16[1,128,1024]{2,1,0:T(8,128)(2,1)} %param.15) | copy-start | bytes 786436
  13.9 4.4 %copy-start.2 = (s32[1,4]{1,0:T(1,128)S(1)}, s32[1,4]{1,0:T(1,128)}, u32[]{:S(2)}) copy-start(s32[1,4]{1,0:T(1,128)} %param.11) | copy-start | bytes 52
  13.9 4.4 %copy-start.3 = (s32[16]{0:T(128)S(1)}, s32[16]{0:T(128)}, u32[]{:S(2)}) copy-start(s32[16]{0:T(128)} %constant.17.clone.table) | copy-start | bytes 196
  13.9 4.4 %collective-permute-start.2 = (s32[4]{0:T(128)}, s32[4]{0:T(128)S(1)}, u32[]{:S(2)}, u32[]{:S(2)}) collective-permute-start(s32[4]{0:T(128)} %bitcast.29), channel_id=1, source_target_pairs={{0,4},{4,0},{8,12},{12,8},{16,20},{20,16},{24,28},{28,24},{1,5},{5... | collective-permute-start | bytes 56 | tf_op jit(solution)/shard_map/ppermute | solution.py:459
  19.0 8.1 %collective-permute-start.5 = (bf16[128,1024]{1,0:T(8,128)(2,1)S(1)}, bf16[128,1024]{1,0:T(8,128)(2,1)S(1)}, u32[]{:S(2)}, u32[]{:S(2)}) collective-permute-start(bf16[128,1024]{1,0:T(8,128)(2,1)S(1)} %collective-permute-done.g0), channel_id=1, source_target_pairs={{0,4},{4,0},{8,12},{12,8},{16,20},{20,16},{24,28},{28,24},{1,5},{5... | collective-permute-start | bytes 786440 | tf_op jit(solution)/shard_map/ppermute | solution.py:459
  19.5 7.6 %collective-permute-start.6 = (bf16[128,1024]{1,0:T(8,128)(2,1)S(1)}, bf16[128,1024]{1,0:T(8,128)(2,1)S(1)}, u32[]{:S(2)}, u32[]{:S(2)}) collective-permute-start(bf16[128,1024]{1,0:T(8,128)(2,1)S(1)} %collective-permute-done.1.g1), channel_id=1, source_target_pairs={{0,4},{4,0},{8,12},{12,8},{16,20},{20,16},{24,28},{28,24},{1,5},{5... | collective-permute-start | bytes 786440 | tf_op jit(solution)/shard_map/ppermute | solution.py:459
  27.1 1.6 %collective-permute-start.7 = (bf16[128,1024]{1,0:T(8,128)(2,1)S(1)}, bf16[128,1024]{1,0:T(8,128)(2,1)S(1)}, u32[]{:S(2)}, u32[]{:S(2)}) collective-permute-start(bf16[128,1024]{1,0:T(8,128)(2,1)S(1)} %collective-permute-done.3.t0), channel_id=1, source_target_pairs={{0,4},{4,0},{8,12},{12,8},{16,20},{20,16},{24,28},{28,24},{1,5},{5... | collective-permute-start | bytes 786440 | tf_op jit(solution)/shard_map/ppermute | solution.py:459
  27.2 1.9 %collective-permute-start.8 = (bf16[128,1024]{1,0:T(8,128)(2,1)S(1)}, bf16[128,1024]{1,0:T(8,128)(2,1)S(1)}, u32[]{:S(2)}, u32[]{:S(2)}) collective-permute-start(bf16[128,1024]{1,0:T(8,128)(2,1)S(1)} %collective-permute-done.4.t1), channel_id=1, source_target_pairs={{0,4},{4,0},{8,12},{12,8},{16,20},{20,16},{24,28},{28,24},{1,5},{5... | collective-permute-start | bytes 786440 | tf_op jit(solution)/shard_map/ppermute | solution.py:459
  29.1 7.9 %copy-start = (bf16[1536,1024]{1,0:T(8,128)(2,1)S(1)}, bf16[1536,1024]{1,0:T(8,128)(2,1)}, u32[]{:S(2)}) copy-start(bf16[1536,1024]{1,0:T(8,128)(2,1)} %get-tuple-element.71.weight) | copy-start | bytes 9437188
  34.3 7.9 %copy-start.6 = (s32[1,128]{1,0:T(1,128)S(1)}, s32[1,128]{1,0:T(1,128)}, u32[]{:S(2)}) copy-start(s32[1,128]{1,0:T(1,128)} %places.1) | copy-start | bytes 1540
  34.3 11.6 %copy-start.4 = (bf16[1,128,1024]{2,1,0:T(8,128)(2,1)S(1)}, bf16[1,128,1024]{2,1,0:T(8,128)(2,1)}, u32[]{:S(2)}) copy-start(bf16[1,128,1024]{2,1,0:T(8,128)(2,1)} %param.9) | copy-start | bytes 786436
  34.3 2.7 %collective-permute-start.9 = (bf16[768,384]{1,0:T(8,128)(2,1)S(1)}, bf16[768,384]{1,0:T(8,128)(2,1)S(1)}, u32[]{:S(2)}, u32[]{:S(2)}) collective-permute-start(bf16[768,384]{1,0:T(8,128)(2,1)S(1)} %get-tuple-element.70.own), channel_id=1, source_target_pairs={{0,4},{4,0},{8,12},{12,8},{16,20},{20,16},{24,28},{28,24},{1,5},{5... | collective-permute-start | bytes 1769480 | tf_op jit(solution)/shard_map/ppermute | solution.py:459
  34.5 13.1 %collective-permute-start.12 = (bf16[2,2,512,128]{3,2,1,0:T(8,128)(2,1)S(1)}, bf16[2,2,512,128]{3,2,1,0:T(8,128)(2,1)S(1)}, u32[]{:S(2)}, u32[]{:S(2)}) collective-permute-start(bf16[2,2,512,128]{3,2,1,0:T(8,128)(2,1)S(1)} %get-tuple-element.77), channel_id=1, source_target_pairs={{0,8},{4,12},{8,0},{12,4},{16,24},{20,28},{24,16},{28,20},{1,9},{5... | collective-permute-start | bytes 1572872 | tf_op jit(solution)/shard_map/ppermute | solution.py:459
  35.7 12.8 %collective-permute-start.13 = (bf16[2,2,512,128]{3,2,1,0:T(8,128)(2,1)S(1)}, bf16[2,2,512,128]{3,2,1,0:T(8,128)(2,1)S(1)}, u32[]{:S(2)}, u32[]{:S(2)}) collective-permute-start(bf16[2,2,512,128]{3,2,1,0:T(8,128)(2,1)S(1)} %get-tuple-element.78), channel_id=1, source_target_pairs={{0,16},{4,20},{8,24},{12,28},{16,0},{20,4},{24,8},{28,12},{1,17},{... | collective-permute-start | bytes 1572872 | tf_op jit(solution)/shard_map/ppermute | solution.py:459
  38.4 17.0 %copy-start.5 = (f32[1024]{0:T(1024)S(1)}, f32[1024]{0:T(1024)}, u32[]{:S(2)}) copy-start(f32[1024]{0:T(1024)} %param.12) | copy-start | bytes 12292
  38.4 17.0 %collective-permute-start.10 = (bf16[128,1024]{1,0:T(8,128)(2,1)S(1)}, bf16[128,1024]{1,0:T(8,128)(2,1)S(1)}, u32[]{:S(2)}, u32[]{:S(2)}) collective-permute-start(bf16[128,1024]{1,0:T(8,128)(2,1)S(1)} %get-tuple-element.74), channel_id=1, source_target_pairs={{2,0},{0,1},{4,2},{6,3},{1,4},{7,5},{3,6},{5,7},{10,8},{8,9},{12,1... | collective-permute-start | bytes 786440 | tf_op jit(solution)/shard_map/ppermute | solution.py:571
  42.1 6.4 %collective-permute-start.14 = (bf16[16,1024]{1,0:T(8,128)(2,1)S(1)}, bf16[16,1024]{1,0:T(8,128)(2,1)S(1)}, u32[]{:S(2)}, u32[]{:S(2)}) collective-permute-start(bf16[16,1024]{1,0:T(8,128)(2,1)S(1)} %slice.16), channel_id=1, source_target_pairs={{0,4},{4,0},{8,12},{12,8},{16,20},{20,16},{24,28},{28,24},{1,5},{5... | collective-permute-start | bytes 98312 | tf_op jit(solution)/shard_map/ppermute | solution.py:459
  42.1 13.3 %collective-permute-start.11 = (bf16[128,1024]{1,0:T(8,128)(2,1)S(1)}, bf16[128,1024]{1,0:T(8,128)(2,1)S(1)}, u32[]{:S(2)}, u32[]{:S(2)}) collective-permute-start(bf16[128,1024]{1,0:T(8,128)(2,1)S(1)} %get-tuple-element.75), channel_id=1, source_target_pairs={{4,3},{3,4},{1,6},{6,1},{0,0},{5,5},{2,2},{7,7},{12,11},{11,12},{9... | collective-permute-start | bytes 786440 | tf_op jit(solution)/shard_map/ppermute | solution.py:574
  48.6 7.1 %collective-permute-start.18 = (bf16[2,512,128]{2,1,0:T(8,128)(2,1)S(1)}, bf16[2,512,128]{2,1,0:T(8,128)(2,1)S(1)}, u32[]{:S(2)}, u32[]{:S(2)}) collective-permute-start(bf16[2,512,128]{2,1,0:T(8,128)(2,1)S(1)} %get-tuple-element.86), channel_id=1, source_target_pairs={{0,4},{5,1},{1,0},{4,5},{2,6},{7,3},{3,2},{6,7},{8,12},{13,9},{9,8... | collective-permute-start | bytes 786440 | tf_op jit(solution)/shard_map/ppermute | solution.py:592
  50.9 8.2 %collective-permute-start.19 = (bf16[2,512,128]{2,1,0:T(8,128)(2,1)S(1)}, bf16[2,512,128]{2,1,0:T(8,128)(2,1)S(1)}, u32[]{:S(2)}, u32[]{:S(2)}) collective-permute-start(bf16[2,512,128]{2,1,0:T(8,128)(2,1)S(1)} %get-tuple-element.87), channel_id=1, source_target_pairs={{1,4},{4,1},{3,6},{6,3},{9,12},{12,9},{11,14},{14,11},{17,20},{20,... | collective-permute-start | bytes 786440 | tf_op jit(solution)/shard_map/ppermute | solution.py:593
  54.1 5.5 %collective-permute-start.15 = (bf16[2,512,128]{2,1,0:T(8,128)(2,1)S(1)}, bf16[2,512,128]{2,1,0:T(8,128)(2,1)S(1)}, u32[]{:S(2)}, u32[]{:S(2)}) collective-permute-start(bf16[2,512,128]{2,1,0:T(8,128)(2,1)S(1)} %get-tuple-element.95), channel_id=1, source_target_pairs={{0,16},{4,20},{8,24},{12,28},{16,0},{20,4},{24,8},{28,12},{1,17},{... | collective-permute-start | bytes 786440 | tf_op jit(solution)/shard_map/ppermute | solution.py:459
  59.3 5.5 %collective-permute-start.20 = (bf16[512,128]{1,0:T(8,128)(2,1)S(1)}, bf16[512,128]{1,0:T(8,128)(2,1)S(1)}, u32[]{:S(2)}, u32[]{:S(2)}) collective-permute-start(bf16[512,128]{1,0:T(8,128)(2,1)S(1)} %get-tuple-element.90), channel_id=1, source_target_pairs={{0,8},{4,12},{8,0},{12,4},{16,24},{20,28},{24,16},{28,20},{1,9},{5... | collective-permute-start | bytes 393224 | tf_op jit(solution)/shard_map/ppermute | solution.py:459
  59.7 5.0 %collective-permute-start.16 = (bf16[512,128]{1,0:T(8,128)(2,1)S(1)}, bf16[512,128]{1,0:T(8,128)(2,1)S(1)}, u32[]{:S(2)}, u32[]{:S(2)}) collective-permute-start(bf16[512,128]{1,0:T(8,128)(2,1)S(1)} %bitcast.32), channel_id=1, source_target_pairs={{0,4},{5,1},{1,0},{4,5},{2,6},{7,3},{3,2},{6,7},{8,12},{13,9},{9,8... | collective-permute-start | bytes 393224 | tf_op jit(solution)/shard_map/ppermute | solution.py:616
  59.8 6.6 %collective-permute-start.17 = (bf16[512,128]{1,0:T(8,128)(2,1)S(1)}, bf16[512,128]{1,0:T(8,128)(2,1)S(1)}, u32[]{:S(2)}, u32[]{:S(2)}) collective-permute-start(bf16[512,128]{1,0:T(8,128)(2,1)S(1)} %bitcast.31), channel_id=1, source_target_pairs={{1,4},{4,1},{3,6},{6,3},{9,12},{12,9},{11,14},{14,11},{17,20},{20,... | collective-permute-start | bytes 393224 | tf_op jit(solution)/shard_map/ppermute | solution.py:617

commit v9 on v8

--- a/solution.py
+++ b/solution.py
@@ -396,8 +396,9 @@
 
 def split_kernel(keep, first, _, home_send, guest_send, own):
     for slot in range(keep.shape[0]):
-        home_send[slot] = (keep[slot, 0] + first[slot, 0].astype(keep.dtype)).astype(home_send.dtype)
-        total = keep[slot, 1] + first[slot, 1].astype(keep.dtype)
+        home_sum = keep[slot, 0].astype(own.dtype) + first[slot, 0].astype(own.dtype)
+        home_send[slot] = home_sum.astype(home_send.dtype)
+        total = keep[slot, 1].astype(own.dtype) + first[slot, 1].astype(own.dtype)
         guest_send[slot] = total.astype(guest_send.dtype)
         own[slot] = total
 
@@ -528,7 +529,7 @@
     blocks_t = share(fetched_t)
 
     send_shape = jax.ShapeDtypeStruct((2, 2, 2 * width, lanes), low)
-    keep_shape = jax.ShapeDtypeStruct((2, 2, 2 * width, lanes), wide)
+    keep_shape = send_shape
     grads_shape = jax.ShapeDtypeStruct((3 * width, rows), low)
     x_send, x_keep, y_send, y_keep, grads = pl.pallas_call(
         main_kernel,
@@ -572,8 +573,8 @@
     token = across(back_one[:16], 1)
     x_first, y_first, token = lax.optimization_barrier((x_first, y_first, token))
     home_two = lax.ppermute(back_two, axes, second)
-    x_second = across((x_keep[1] + x_first[1].astype(wide)).astype(low), 4)
-    x_part = x_keep[0] + x_first[0].astype(wide)
+    x_second = across((x_keep[1].astype(wide) + x_first[1].astype(wide)).astype(low), 4)
+    x_part = x_keep[0].astype(wide) + x_first[0].astype(wide)
     small = pltpu.CompilerParams(vmem_limit_bytes=12 * 1024 * 1024)
     part_shape = (2, 2 * width, lanes)
 

time: 67.4 us -> 67.5 us (level)
  no operation moved by 1% of the time
where the time goes in v9:
time: 67.5 us; the launch traced here: 67.3 us
  starting transfers between devices  31.7 us (47%)
  Pallas kernels  16.5 us (24%)
  waiting for transfers between devices  15.3 us (23%)
  other arithmetic  2.76 us (4%)
  between operations  0.9 us (1%)
    ppermute x2, waiting for transfers between devices, fetch(): return (lax.ppermute(array, axes, first), two)  7.47 us
    ppermute x2, starting transfers between devices, fetch(): two = lax.ppermute(array, axes, second)  6.75 us
    ppermute x11, starting transfers between devices, across(): return lax.ppermute(array, 'dp', [(i, i ^ bit) for i in range(2 * chips)])  5.56 us
    pallas_call x1, Pallas kernels, column_shards(): pl.pallas_call(main_kernel, out_shape=(send_shape, keep_shape, send_shape...  5.18 us
    pallas_call x1, Pallas kernels, column_shards(): pl.pallas_call(weight_kernel, out_shape=(jax.ShapeDtypeStruct((features,...  4.31 us
    ppermute x1, starting transfers between devices, column_shards(): lax.ppermute(x_guest[0], axes, guests)  3.98 us
    ppermute x1, starting transfers between devices, column_shards(): home_one = lax.ppermute(back_one, axes, first_back)  3.71 us
    ppermute x2, starting transfers between devices, fetch(): return (lax.ppermute(array, axes, first), two)  3.56 us
  transfers between devices with their start and end apart: 21, of which 6 were waited for; matrix products, arithmetic and copies ran while one was open for 4% of the time, Pallas kernels for 16%

profile of v9, /device:TPU:1, one launch (start us, length us, event | category | flops | bytes accessed | tf_op | source)
XLA Modules:
  0.0 67.3 jit_solution(4880169893985326749)
XLA Ops:
  0.6 2.7 %collective-permute-start = (bf16[128,1024]{1,0:T(8,128)(2,1)}, bf16[128,1024]{1,0:T(8,128)(2,1)S(1)}, u32[]{:S(2)}, u32[]{:S(2)}) collective-permute-start(bf16[128,1024]{1,0:T(8,128)(2,1)} %bitcast.26), channel_id=1, source_target_pairs={{0,2},{1,0},{2,4},{3,6},{4,1},{5,7},{6,3},{7,5},{8,10},{9,8},{10,1... | collective-permute-start | bytes 786440 | tf_op jit(solution)/shard_map/ppermute | solution.py:464
  3.4 3.9 %collective-permute-start.1 = (bf16[128,1024]{1,0:T(8,128)(2,1)}, bf16[128,1024]{1,0:T(8,128)(2,1)S(1)}, u32[]{:S(2)}, u32[]{:S(2)}) collective-permute-start(bf16[128,1024]{1,0:T(8,128)(2,1)} %bitcast.27), channel_id=1, source_target_pairs={{4,3},{3,4},{1,6},{6,1},{0,0},{5,5},{2,2},{7,7},{12,11},{11,12},{9... | collective-permute-start | bytes 786440 | tf_op jit(solution)/shard_map/ppermute | solution.py:463
  7.3 2.9 %shard_map.114 = bf16[128,1024]{1,0:T(8,128)(2,1)} custom-call(s32[1,128]{1,0:T(1,128)} %places.1, bf16[128,1024]{1,0:T(8,128)(2,1)} %bitcast.33, f32[1,1024]{1,0:T(1,128)} %bitcast.34, f32[1,512]{1,0:T(1,128)} %constant.16.clone.freqs), custom_call_target="tpu_custom_call" | custom-call | tf_op jit(solution)/shard_map/pallas_call | solution.py:474
  10.2 0.8 %collective-permute-start.3 = (bf16[128,1024]{1,0:T(8,128)(2,1)}, bf16[128,1024]{1,0:T(8,128)(2,1)S(1)}, u32[]{:S(2)}, u32[]{:S(2)}) collective-permute-start(bf16[128,1024]{1,0:T(8,128)(2,1)} %shard_map.114), channel_id=1, source_target_pairs={{0,2},{1,0},{2,4},{3,6},{4,1},{5,7},{6,3},{7,5},{8,10},{9,8},{10,1... | collective-permute-start | bytes 786440 | tf_op jit(solution)/shard_map/ppermute | solution.py:464
  11.0 2.8 %collective-permute-start.4 = (bf16[128,1024]{1,0:T(8,128)(2,1)}, bf16[128,1024]{1,0:T(8,128)(2,1)S(1)}, u32[]{:S(2)}, u32[]{:S(2)}) collective-permute-start(bf16[128,1024]{1,0:T(8,128)(2,1)} %shard_map.114), channel_id=1, source_target_pairs={{4,3},{3,4},{1,6},{6,1},{0,0},{5,5},{2,2},{7,7},{12,11},{11,12},{9... | collective-permute-start | bytes 786440 | tf_op jit(solution)/shard_map/ppermute | solution.py:463
  13.8 0.0 copy-start.1
  13.9 0.0 copy-start.2
  13.9 0.0 copy-start.3
  13.9 0.1 collective-permute-start.2
  14.0 4.3 %shard_map.113 = (bf16[1024,256]{1,0:T(8,128)(2,1)S(1)}, bf16[768,1024]{1,0:T(8,128)(2,1)S(1)}, bf16[1536,1024]{1,0:T(8,128)(2,1)}) custom-call(bf16[1024,1024]{1,0:T(8,128)(2,1)} %w_out.1, bf16[3,1024,1024]{2,1,0:T(8,128)(2,1)} %w_qkv.1), custom_call_target="tpu_custom_call" | custom-call | bytes 4194304 | tf_op jit(solution)/shard_map/pallas_call | solution.py:482
  18.3 0.6 shard_map.112
  19.0 0.6 collective-permute-start.5
  19.5 0.1 collective-permute-start.6
  19.6 7.5 %collective-permute-done.3.t0 = bf16[128,1024]{1,0:T(8,128)(2,1)S(1)} collective-permute-done((bf16[128,1024]{1,0:T(8,128)(2,1)}, bf16[128,1024]{1,0:T(8,128)(2,1)S(1)}, u32[]{:S(2)}, u32[]{:S(2)}) %collective-permute-start.3) | collective-permute-done | bytes 262176 | tf_op jit(solution)/shard_map/ppermute | solution.py:464
  27.1 0.1 collective-permute-start.7
  27.2 0.5 collective-permute-start.8
  27.7 1.0 %shard_map.115 = (bf16[384,1024]{1,0:T(8,128)(2,1)S(1)}, bf16[256,384]{1,0:T(8,128)(2,1)S(1)}) custom-call(s32[1,512]{1,0:T(1,128)S(1)} %get-tuple-element.57.rank, bf16[128,1024]{1,0:T(8,128)(2,1)S(1)} %collective-permute-done.g0, bf16[128,1024]{1,0:T(8,128)(2,1)S(1)} %collective-permute-done.1.g1, bf16[128,1024]{1,0:T(8,128)(2,1)S(1)} %collective-permute-done.5.g2, ...), custom_call_target="tpu_custom_call" | custom-call | flops 603979776 | bytes 3145728 | tf_op jit(solution)/shard_map/pallas_call | solution.py:515
  28.6 0.0 collective-permute-done.7.t2
  28.7 0.4 collective-permute-done.8.t3
  29.1 5.2 %shard_map.116 = (bf16[2,2,512,128]{3,2,1,0:T(8,128)(2,1)S(1)}, bf16[2,2,512,128]{3,2,1,0:T(8,128)(2,1)S(1)}, bf16[2,2,512,128]{3,2,1,0:T(8,128)(2,1)S(1)}, bf16...) custom-call(s32[1,512]{1,0:T(1,128)S(1)} %get-tuple-element.57.rank, ...), custom_call_target="tpu_custom_call" | custom-call | flops 2684354560 | bytes 8388608 | tf_op jit(solution)/shard_map/pallas_call | solution.py:534
  34.3 0.0 copy-start.4
  34.3 0.2 collective-permute-start.9
  34.5 1.2 %collective-permute-start.12 = (bf16[2,2,512,128]{3,2,1,0:T(8,128)(2,1)S(1)}, bf16[2,2,512,128]{3,2,1,0:T(8,128)(2,1)S(1)}, u32[]{:S(2)}, u32[]{:S(2)}) collective-permute-start(bf16[2,2,512,128]{3,2,1,0:T(8,128)(2,1)S(1)} %get-tuple-element.77), channel_id=1, source_target_pairs={{0,8},{4,12},{8,0},{12,4},{16,24},{20,28},{24,16},{28,20},{1,9},{5... | collective-permute-start | bytes 1572872 | tf_op jit(solution)/shard_map/ppermute | solution.py:460
  35.7 1.2 %collective-permute-start.13 = (bf16[2,2,512,128]{3,2,1,0:T(8,128)(2,1)S(1)}, bf16[2,2,512,128]{3,2,1,0:T(8,128)(2,1)S(1)}, u32[]{:S(2)}, u32[]{:S(2)}) collective-permute-start(bf16[2,2,512,128]{3,2,1,0:T(8,128)(2,1)S(1)} %get-tuple-element.78), channel_id=1, source_target_pairs={{0,16},{4,20},{8,24},{12,28},{16,0},{20,4},{24,8},{28,12},{1,17},{... | collective-permute-start | bytes 1572872 | tf_op jit(solution)/shard_map/ppermute | solution.py:460
  36.9 1.4 %shard_map.117 = (bf16[128,1024]{1,0:T(8,128)(2,1)S(1)}, bf16[128,1024]{1,0:T(8,128)(2,1)S(1)}) custom-call(s32[1,256]{1,0:T(1,128)S(1)} %get-tuple-element.55.own_rank, s32[1,256]{1,0:T(1,128)S(1)} %get-tuple-element.56.other_rank, bf16[768,384]{1,0:T(8,128)(2,1)S(1)} %get-tuple-element.70.own, bf16[768,384]{1,0:T(8,128)(2,1)S(1)} %collective-permute-done.9.other, ...), custom_call_target="tpu_custom_call" | custom-call | flops 805306368 | bytes 4194304 | tf_op jit(solution)/shard_map/pallas_call | solution.py:560
  38.4 0.0 copy-start.5
  38.4 3.7 %collective-permute-start.10 = (bf16[128,1024]{1,0:T(8,128)(2,1)S(1)}, bf16[128,1024]{1,0:T(8,128)(2,1)S(1)}, u32[]{:S(2)}, u32[]{:S(2)}) collective-permute-start(bf16[128,1024]{1,0:T(8,128)(2,1)S(1)} %get-tuple-element.74), channel_id=1, source_target_pairs={{2,0},{0,1},{4,2},{6,3},{1,4},{7,5},{3,6},{5,7},{10,8},{8,9},{12,1... | collective-permute-start | bytes 786440 | tf_op jit(solution)/shard_map/ppermute | solution.py:572
  42.1 2.7 %collective-permute-start.11 = (bf16[128,1024]{1,0:T(8,128)(2,1)S(1)}, bf16[128,1024]{1,0:T(8,128)(2,1)S(1)}, u32[]{:S(2)}, u32[]{:S(2)}) collective-permute-start(bf16[128,1024]{1,0:T(8,128)(2,1)S(1)} %get-tuple-element.75), channel_id=1, source_target_pairs={{4,3},{3,4},{1,6},{6,1},{0,0},{5,5},{2,2},{7,7},{12,11},{11,12},{9... | collective-permute-start | bytes 786440 | tf_op jit(solution)/shard_map/ppermute | solution.py:575
  44.8 1.0 %multiply_sine_fusion = (f32[128,512]{1,0:T(8,128)S(1)}, f32[128,512]{1,0:T(8,128)S(1)}) fusion(f32[512]{0:T(512)S(1)} %multiply_exponential_fusion, f32[128]{0:T(128)S(1)} %convert_bitcast_fusion), kind=kLoop, calls=%fused_computation.9 | loop fusion | flops 65536 | bytes 526848 | tf_op jit(solution)/shard_map/sin | solution.py:23
  45.8 0.1 fusion.3
  46.0 0.2 multiply_reduce_fusion.1
  46.2 1.4 %collective-permute-done.12 = bf16[2,2,512,128]{3,2,1,0:T(8,128)(2,1)S(1)} collective-permute-done((bf16[2,2,512,128]{3,2,1,0:T(8,128)(2,1)S(1)}, bf16[2,2,512,128]{3,2,1,0:T(8,128)(2,1)S(1)}, u32[]{:S(2)}, u32[]{:S(2)}) %collective-permute-start.12) | collective-permute-done | bytes 524320 | tf_op jit(solution)/shard_map/ppermute | solution.py:460
  47.6 0.9 %collective-permute-done.13.first = bf16[2,2,512,128]{3,2,1,0:T(8,128)(2,1)S(1)} collective-permute-done((bf16[2,2,512,128]{3,2,1,0:T(8,128)(2,1)S(1)}, bf16[2,2,512,128]{3,2,1,0:T(8,128)(2,1)S(1)}, u32[]{:S(2)}, u32[]{:S(2)}) %collective-permute-start.13) | collective-permute-done | bytes 524320 | tf_op jit(solution)/shard_map/ppermute | solution.py:460
  48.5 0.1 shard_map.119
  48.6 2.3 %collective-permute-start.18 = (bf16[2,512,128]{2,1,0:T(8,128)(2,1)S(1)}, bf16[2,512,128]{2,1,0:T(8,128)(2,1)S(1)}, u32[]{:S(2)}, u32[]{:S(2)}) collective-permute-start(bf16[2,512,128]{2,1,0:T(8,128)(2,1)S(1)} %get-tuple-element.86), channel_id=1, source_target_pairs={{0,4},{5,1},{1,0},{4,5},{2,6},{7,3},{3,2},{6,7},{8,12},{13,9},{9,8... | collective-permute-start | bytes 786440 | tf_op jit(solution)/shard_map/ppermute | solution.py:593
  50.9 3.1 %collective-permute-start.19 = (bf16[2,512,128]{2,1,0:T(8,128)(2,1)S(1)}, bf16[2,512,128]{2,1,0:T(8,128)(2,1)S(1)}, u32[]{:S(2)}, u32[]{:S(2)}) collective-permute-start(bf16[2,512,128]{2,1,0:T(8,128)(2,1)S(1)} %get-tuple-element.87), channel_id=1, source_target_pairs={{1,4},{4,1},{3,6},{6,3},{9,12},{12,9},{11,14},{14,11},{17,20},{20,... | collective-permute-start | bytes 786440 | tf_op jit(solution)/shard_map/ppermute | solution.py:594
  54.0 0.1 fusion.1
  54.2 1.3 %collective-permute-start.15 = (bf16[2,512,128]{2,1,0:T(8,128)(2,1)S(1)}, bf16[2,512,128]{2,1,0:T(8,128)(2,1)S(1)}, u32[]{:S(2)}, u32[]{:S(2)}) collective-permute-start(bf16[2,512,128]{2,1,0:T(8,128)(2,1)S(1)} %get-tuple-element.95), channel_id=1, source_target_pairs={{0,16},{4,20},{8,24},{12,28},{16,0},{20,4},{24,8},{28,12},{1,17},{... | collective-permute-start | bytes 786440 | tf_op jit(solution)/shard_map/ppermute | solution.py:460
  55.5 0.3 fusion
  55.8 3.4 %collective-permute-done.19.from_guest = bf16[2,512,128]{2,1,0:T(8,128)(2,1)S(1)} collective-permute-done((bf16[2,512,128]{2,1,0:T(8,128)(2,1)S(1)}, bf16[2,512,128]{2,1,0:T(8,128)(2,1)S(1)}, u32[]{:S(2)}, u32[]{:S(2)}) %collective-permute-start.19) | collective-permute-done | bytes 262176 | tf_op jit(solution)/shard_map/ppermute | solution.py:594
  59.2 0.1 shard_map.120
  59.3 0.3 collective-permute-start.20
  59.6 0.1 shard_map.118
  59.7 0.1 collective-permute-start.16
  59.8 4.0 %collective-permute-start.17 = (bf16[512,128]{1,0:T(8,128)(2,1)S(1)}, bf16[512,128]{1,0:T(8,128)(2,1)S(1)}, u32[]{:S(2)}, u32[]{:S(2)}) collective-permute-start(bf16[512,128]{1,0:T(8,128)(2,1)S(1)} %bitcast.31), channel_id=1, source_target_pairs={{1,4},{4,1},{3,6},{6,3},{9,12},{12,9},{11,14},{14,11},{17,20},{20,... | collective-permute-start | bytes 393224 | tf_op jit(solution)/shard_map/ppermute | solution.py:618
  63.8 1.0 %fusion.2 = bf16[1,128,1024]{2,1,0:T(8,128)(2,1)} fusion(f32[128]{0:T(128)S(1)} %get-tuple-element.99, f32[128]{0:T(128)S(1)} %broadcast_multiply_fusion.2, f32[128]{0:T(128)S(1)} %get-tuple-element.100, f32[1024]{0:T(1024)S(1)} %copy-done.5, bf16[128,1024]{1,0:T(8,128)(2,1)S(1)} %collective-permute-done.11, ...), kind=kLoop, calls=%fused_computation.11 | loop fusion | flops 2097152 | bytes 1841152 | tf_op jit(solution)/shard_map/broadcast_in_dim | solution.py:630
  64.8 1.6 %collective-permute-done.17.from_guest = bf16[512,128]{1,0:T(8,128)(2,1)S(1)} collective-permute-done((bf16[512,128]{1,0:T(8,128)(2,1)S(1)}, bf16[512,128]{1,0:T(8,128)(2,1)S(1)}, u32[]{:S(2)}, u32[]{:S(2)}) %collective-permute-start.17) | collective-permute-done | bytes 131104 | tf_op jit(solution)/shard_map/ppermute | solution.py:618
  66.4 0.9 %shard_map.121 = (f32[768,128]{1,0:T(8,128)}, f32[128,256]{1,0:T(8,128)}) custom-call(bf16[512,128]{1,0:T(8,128)(2,1)S(1)} %collective-permute-done.16.from_home, bf16[512,128]{1,0:T(8,128)(2,1)S(1)} %collective-permute-done.17.from_guest, f32[512,128]{1,0:T(8,128)S(1)} %bitcast.25, f32[512,128]{1,0:T(8,128)S(1)} %get-tuple-element.89.keep, ...), custom_call_target="tpu_custom_call" | custom-call | tf_op jit(solution)/shard_map/pallas_call | solution.py:607
  (30 shorter events, 0.1 us)
Async XLA Ops:
  0.6 18.3 %collective-permute-start = (bf16[128,1024]{1,0:T(8,128)(2,1)}, bf16[128,1024]{1,0:T(8,128)(2,1)S(1)}, u32[]{:S(2)}, u32[]{:S(2)}) collective-permute-start(bf16[128,1024]{1,0:T(8,128)(2,1)} %bitcast.26), channel_id=1, source_target_pairs={{0,2},{1,0},{2,4},{3,6},{4,1},{5,7},{6,3},{7,5},{8,10},{9,8},{10,1... | collective-permute-start | bytes 786440 | tf_op jit(solution)/shard_map/ppermute | solution.py:464
  3.4 15.6 %collective-permute-start.1 = (bf16[128,1024]{1,0:T(8,128)(2,1)}, bf16[128,1024]{1,0:T(8,128)(2,1)S(1)}, u32[]{:S(2)}, u32[]{:S(2)}) collective-permute-start(bf16[128,1024]{1,0:T(8,128)(2,1)} %bitcast.27), channel_id=1, source_target_pairs={{4,3},{3,4},{1,6},{6,1},{0,0},{5,5},{2,2},{7,7},{12,11},{11,12},{9... | collective-permute-start | bytes 786440 | tf_op jit(solution)/shard_map/ppermute | solution.py:463
  10.2 16.9 %collective-permute-start.3 = (bf16[128,1024]{1,0:T(8,128)(2,1)}, bf16[128,1024]{1,0:T(8,128)(2,1)S(1)}, u32[]{:S(2)}, u32[]{:S(2)}) collective-permute-start(bf16[128,1024]{1,0:T(8,128)(2,1)} %shard_map.114), channel_id=1, source_target_pairs={{0,2},{1,0},{2,4},{3,6},{4,1},{5,7},{6,3},{7,5},{8,10},{9,8},{10,1... | collective-permute-start | bytes 786440 | tf_op jit(solution)/shard_map/ppermute | solution.py:464
  11.0 16.1 %collective-permute-start.4 = (bf16[128,1024]{1,0:T(8,128)(2,1)}, bf16[128,1024]{1,0:T(8,128)(2,1)S(1)}, u32[]{:S(2)}, u32[]{:S(2)}) collective-permute-start(bf16[128,1024]{1,0:T(8,128)(2,1)} %shard_map.114), channel_id=1, source_target_pairs={{4,3},{3,4},{1,6},{6,1},{0,0},{5,5},{2,2},{7,7},{12,11},{11,12},{9... | collective-permute-start | bytes 786440 | tf_op jit(solution)/shard_map/ppermute | solution.py:463
  13.8 4.5 %copy-start.1 = (bf16[1,128,1024]{2,1,0:T(8,128)(2,1)S(1)}, bf16[1,128,1024]{2,1,0:T(8,128)(2,1)}, u32[]{:S(2)}) copy-start(bf16[1,128,1024]{2,1,0:T(8,128)(2,1)} %param.15) | copy-start | bytes 786436
  13.9 4.4 %copy-start.2 = (s32[1,4]{1,0:T(1,128)S(1)}, s32[1,4]{1,0:T(1,128)}, u32[]{:S(2)}) copy-start(s32[1,4]{1,0:T(1,128)} %param.11) | copy-start | bytes 52
  13.9 4.4 %copy-start.3 = (s32[16]{0:T(128)S(1)}, s32[16]{0:T(128)}, u32[]{:S(2)}) copy-start(s32[16]{0:T(128)} %constant.17.clone.table) | copy-start | bytes 196
  13.9 4.4 %collective-permute-start.2 = (s32[4]{0:T(128)}, s32[4]{0:T(128)S(1)}, u32[]{:S(2)}, u32[]{:S(2)}) collective-permute-start(s32[4]{0:T(128)} %bitcast.29), channel_id=1, source_target_pairs={{0,4},{4,0},{8,12},{12,8},{16,20},{20,16},{24,28},{28,24},{1,5},{5... | collective-permute-start | bytes 56 | tf_op jit(solution)/shard_map/ppermute | solution.py:460
  19.0 8.1 %collective-permute-start.5 = (bf16[128,1024]{1,0:T(8,128)(2,1)S(1)}, bf16[128,1024]{1,0:T(8,128)(2,1)S(1)}, u32[]{:S(2)}, u32[]{:S(2)}) collective-permute-start(bf16[128,1024]{1,0:T(8,128)(2,1)S(1)} %collective-permute-done.g0), channel_id=1, source_target_pairs={{0,4},{4,0},{8,12},{12,8},{16,20},{20,16},{24,28},{28,24},{1,5},{5... | collective-permute-start | bytes 786440 | tf_op jit(solution)/shard_map/ppermute | solution.py:460
  19.5 7.6 %collective-permute-start.6 = (bf16[128,1024]{1,0:T(8,128)(2,1)S(1)}, bf16[128,1024]{1,0:T(8,128)(2,1)S(1)}, u32[]{:S(2)}, u32[]{:S(2)}) collective-permute-start(bf16[128,1024]{1,0:T(8,128)(2,1)S(1)} %collective-permute-done.1.g1), channel_id=1, source_target_pairs={{0,4},{4,0},{8,12},{12,8},{16,20},{20,16},{24,28},{28,24},{1,5},{5... | collective-permute-start | bytes 786440 | tf_op jit(solution)/shard_map/ppermute | solution.py:460
  27.1 1.6 %collective-permute-start.7 = (bf16[128,1024]{1,0:T(8,128)(2,1)S(1)}, bf16[128,1024]{1,0:T(8,128)(2,1)S(1)}, u32[]{:S(2)}, u32[]{:S(2)}) collective-permute-start(bf16[128,1024]{1,0:T(8,128)(2,1)S(1)} %collective-permute-done.3.t0), channel_id=1, source_target_pairs={{0,4},{4,0},{8,12},{12,8},{16,20},{20,16},{24,28},{28,24},{1,5},{5... | collective-permute-start | bytes 786440 | tf_op jit(solution)/shard_map/ppermute | solution.py:460
  27.2 1.9 %collective-permute-start.8 = (bf16[128,1024]{1,0:T(8,128)(2,1)S(1)}, bf16[128,1024]{1,0:T(8,128)(2,1)S(1)}, u32[]{:S(2)}, u32[]{:S(2)}) collective-permute-start(bf16[128,1024]{1,0:T(8,128)(2,1)S(1)} %collective-permute-done.4.t1), channel_id=1, source_target_pairs={{0,4},{4,0},{8,12},{12,8},{16,20},{20,16},{24,28},{28,24},{1,5},{5... | collective-permute-start | bytes 786440 | tf_op jit(solution)/shard_map/ppermute | solution.py:460
  29.1 7.9 %copy-start = (bf16[1536,1024]{1,0:T(8,128)(2,1)S(1)}, bf16[1536,1024]{1,0:T(8,128)(2,1)}, u32[]{:S(2)}) copy-start(bf16[1536,1024]{1,0:T(8,128)(2,1)} %get-tuple-element.71.weight) | copy-start | bytes 9437188
  34.3 7.9 %copy-start.6 = (s32[1,128]{1,0:T(1,128)S(1)}, s32[1,128]{1,0:T(1,128)}, u32[]{:S(2)}) copy-start(s32[1,128]{1,0:T(1,128)} %places.1) | copy-start | bytes 1540
  34.3 11.6 %copy-start.4 = (bf16[1,128,1024]{2,1,0:T(8,128)(2,1)S(1)}, bf16[1,128,1024]{2,1,0:T(8,128)(2,1)}, u32[]{:S(2)}) copy-start(bf16[1,128,1024]{2,1,0:T(8,128)(2,1)} %param.9) | copy-start | bytes 786436
  34.3 2.7 %collective-permute-start.9 = (bf16[768,384]{1,0:T(8,128)(2,1)S(1)}, bf16[768,384]{1,0:T(8,128)(2,1)S(1)}, u32[]{:S(2)}, u32[]{:S(2)}) collective-permute-start(bf16[768,384]{1,0:T(8,128)(2,1)S(1)} %get-tuple-element.70.own), channel_id=1, source_target_pairs={{0,4},{4,0},{8,12},{12,8},{16,20},{20,16},{24,28},{28,24},{1,5},{5... | collective-permute-start | bytes 1769480 | tf_op jit(solution)/shard_map/ppermute | solution.py:460
  34.5 13.1 %collective-permute-start.12 = (bf16[2,2,512,128]{3,2,1,0:T(8,128)(2,1)S(1)}, bf16[2,2,512,128]{3,2,1,0:T(8,128)(2,1)S(1)}, u32[]{:S(2)}, u32[]{:S(2)}) collective-permute-start(bf16[2,2,512,128]{3,2,1,0:T(8,128)(2,1)S(1)} %get-tuple-element.77), channel_id=1, source_target_pairs={{0,8},{4,12},{8,0},{12,4},{16,24},{20,28},{24,16},{28,20},{1,9},{5... | collective-permute-start | bytes 1572872 | tf_op jit(solution)/shard_map/ppermute | solution.py:460
  35.7 12.8 %collective-permute-start.13 = (bf16[2,2,512,128]{3,2,1,0:T(8,128)(2,1)S(1)}, bf16[2,2,512,128]{3,2,1,0:T(8,128)(2,1)S(1)}, u32[]{:S(2)}, u32[]{:S(2)}) collective-permute-start(bf16[2,2,512,128]{3,2,1,0:T(8,128)(2,1)S(1)} %get-tuple-element.78), channel_id=1, source_target_pairs={{0,16},{4,20},{8,24},{12,28},{16,0},{20,4},{24,8},{28,12},{1,17},{... | collective-permute-start | bytes 1572872 | tf_op jit(solution)/shard_map/ppermute | solution.py:460
  38.4 17.1 %copy-start.5 = (f32[1024]{0:T(1024)S(1)}, f32[1024]{0:T(1024)}, u32[]{:S(2)}) copy-start(f32[1024]{0:T(1024)} %param.12) | copy-start | bytes 12292
  38.4 17.1 %collective-permute-start.10 = (bf16[128,1024]{1,0:T(8,128)(2,1)S(1)}, bf16[128,1024]{1,0:T(8,128)(2,1)S(1)}, u32[]{:S(2)}, u32[]{:S(2)}) collective-permute-start(bf16[128,1024]{1,0:T(8,128)(2,1)S(1)} %get-tuple-element.74), channel_id=1, source_target_pairs={{2,0},{0,1},{4,2},{6,3},{1,4},{7,5},{3,6},{5,7},{10,8},{8,9},{12,1... | collective-permute-start | bytes 786440 | tf_op jit(solution)/shard_map/ppermute | solution.py:572
  42.1 6.4 %collective-permute-start.14 = (bf16[16,1024]{1,0:T(8,128)(2,1)S(1)}, bf16[16,1024]{1,0:T(8,128)(2,1)S(1)}, u32[]{:S(2)}, u32[]{:S(2)}) collective-permute-start(bf16[16,1024]{1,0:T(8,128)(2,1)S(1)} %slice.16), channel_id=1, source_target_pairs={{0,4},{4,0},{8,12},{12,8},{16,20},{20,16},{24,28},{28,24},{1,5},{5... | collective-permute-start | bytes 98312 | tf_op jit(solution)/shard_map/ppermute | solution.py:460
  42.1 13.3 %collective-permute-start.11 = (bf16[128,1024]{1,0:T(8,128)(2,1)S(1)}, bf16[128,1024]{1,0:T(8,128)(2,1)S(1)}, u32[]{:S(2)}, u32[]{:S(2)}) collective-permute-start(bf16[128,1024]{1,0:T(8,128)(2,1)S(1)} %get-tuple-element.75), channel_id=1, source_target_pairs={{4,3},{3,4},{1,6},{6,1},{0,0},{5,5},{2,2},{7,7},{12,11},{11,12},{9... | collective-permute-start | bytes 786440 | tf_op jit(solution)/shard_map/ppermute | solution.py:575
  48.6 7.1 %collective-permute-start.18 = (bf16[2,512,128]{2,1,0:T(8,128)(2,1)S(1)}, bf16[2,512,128]{2,1,0:T(8,128)(2,1)S(1)}, u32[]{:S(2)}, u32[]{:S(2)}) collective-permute-start(bf16[2,512,128]{2,1,0:T(8,128)(2,1)S(1)} %get-tuple-element.86), channel_id=1, source_target_pairs={{0,4},{5,1},{1,0},{4,5},{2,6},{7,3},{3,2},{6,7},{8,12},{13,9},{9,8... | collective-permute-start | bytes 786440 | tf_op jit(solution)/shard_map/ppermute | solution.py:593
  50.9 8.2 %collective-permute-start.19 = (bf16[2,512,128]{2,1,0:T(8,128)(2,1)S(1)}, bf16[2,512,128]{2,1,0:T(8,128)(2,1)S(1)}, u32[]{:S(2)}, u32[]{:S(2)}) collective-permute-start(bf16[2,512,128]{2,1,0:T(8,128)(2,1)S(1)} %get-tuple-element.87), channel_id=1, source_target_pairs={{1,4},{4,1},{3,6},{6,3},{9,12},{12,9},{11,14},{14,11},{17,20},{20,... | collective-permute-start | bytes 786440 | tf_op jit(solution)/shard_map/ppermute | solution.py:594
  54.2 5.5 %collective-permute-start.15 = (bf16[2,512,128]{2,1,0:T(8,128)(2,1)S(1)}, bf16[2,512,128]{2,1,0:T(8,128)(2,1)S(1)}, u32[]{:S(2)}, u32[]{:S(2)}) collective-permute-start(bf16[2,512,128]{2,1,0:T(8,128)(2,1)S(1)} %get-tuple-element.95), channel_id=1, source_target_pairs={{0,16},{4,20},{8,24},{12,28},{16,0},{20,4},{24,8},{28,12},{1,17},{... | collective-permute-start | bytes 786440 | tf_op jit(solution)/shard_map/ppermute | solution.py:460
  59.3 5.5 %collective-permute-start.20 = (bf16[512,128]{1,0:T(8,128)(2,1)S(1)}, bf16[512,128]{1,0:T(8,128)(2,1)S(1)}, u32[]{:S(2)}, u32[]{:S(2)}) collective-permute-start(bf16[512,128]{1,0:T(8,128)(2,1)S(1)} %get-tuple-element.90), channel_id=1, source_target_pairs={{0,8},{4,12},{8,0},{12,4},{16,24},{20,28},{24,16},{28,20},{1,9},{5... | collective-permute-start | bytes 393224 | tf_op jit(solution)/shard_map/ppermute | solution.py:460
  59.7 5.1 %collective-permute-start.16 = (bf16[512,128]{1,0:T(8,128)(2,1)S(1)}, bf16[512,128]{1,0:T(8,128)(2,1)S(1)}, u32[]{:S(2)}, u32[]{:S(2)}) collective-permute-start(bf16[512,128]{1,0:T(8,128)(2,1)S(1)} %bitcast.32), channel_id=1, source_target_pairs={{0,4},{5,1},{1,0},{4,5},{2,6},{7,3},{3,2},{6,7},{8,12},{13,9},{9,8... | collective-permute-start | bytes 393224 | tf_op jit(solution)/shard_map/ppermute | solution.py:617
  59.8 6.6 %collective-permute-start.17 = (bf16[512,128]{1,0:T(8,128)(2,1)S(1)}, bf16[512,128]{1,0:T(8,128)(2,1)S(1)}, u32[]{:S(2)}, u32[]{:S(2)}) collective-permute-start(bf16[512,128]{1,0:T(8,128)(2,1)S(1)} %bitcast.31), channel_id=1, source_target_pairs={{1,4},{4,1},{3,6},{6,3},{9,12},{12,9},{11,14},{14,11},{17,20},{20,... | collective-permute-start | bytes 393224 | tf_op jit(solution)/shard_map/ppermute | solution.py:618

commit v10 on v8

--- a/solution.py
+++ b/solution.py
@@ -338,14 +338,14 @@
     for head in range(width // HEAD_DIM):
         span = pl.ds(head * HEAD_DIM, HEAD_DIM)
         rows_h = query[span, :], key[span, :], value[span, :], lifted[span, :]
-        heads.append(rows_h + (tn(rows_h[1], rows_h[0]), tn(rows_h[2], rows_h[3])))
+        heads.append(rows_h + (tn(rows_h[1], rows_h[0]),))
     weighted = []
-    for _, _, _, _, scores, _ in heads:
+    for _, _, value_h, lifted_h, scores in heads:
         expo = jnp.exp(scores - jnp.max(scores, axis=0, keepdims=True))
         probs = expo * (1.0 / jnp.sum(expo, axis=0, keepdims=True))
-        weighted.append((probs, probs.astype(low)))
-    for head, (query_h, key_h, value_h, lifted_h, _, prob_grad) in enumerate(heads):
-        probs, probs_low = weighted[head]
+        weighted.append((probs, probs.astype(low), tn(value_h, lifted_h)))
+    for head, (query_h, key_h, value_h, lifted_h, _) in enumerate(heads):
+        probs, probs_low, prob_grad = weighted[head]
         spans = [pl.ds(part * width + head * HEAD_DIM, HEAD_DIM) for part in range(4)]
         attended = nn(value_h, probs_low)
         delta = jnp.sum(lifted_h.astype(jnp.float32) * attended, axis=0, keepdims=True)

time: 67.4 us -> 67.5 us (level)
  no operation moved by 1% of the time
where the time goes in v10:
time: 67.5 us; the launch traced here: 67.3 us
  starting transfers between devices  31.7 us (47%)
  Pallas kernels  16.6 us (25%)
  waiting for transfers between devices  15.3 us (23%)
  other arithmetic  2.76 us (4%)
  between operations  0.9 us (1%)
    ppermute x2, waiting for transfers between devices, fetch(): return (lax.ppermute(array, axes, first), two)  7.47 us
    ppermute x2, starting transfers between devices, fetch(): two = lax.ppermute(array, axes, second)  6.75 us
    ppermute x11, starting transfers between devices, across(): return lax.ppermute(array, 'dp', [(i, i ^ bit) for i in range(2 * chips)])  5.6 us
    pallas_call x1, Pallas kernels, column_shards(): pl.pallas_call(main_kernel, out_shape=(send_shape, keep_shape, send_shape...  5.24 us
    pallas_call x1, Pallas kernels, column_shards(): pl.pallas_call(weight_kernel, out_shape=(jax.ShapeDtypeStruct((features,...  4.31 us
    ppermute x1, starting transfers between devices, column_shards(): lax.ppermute(x_guest[0], axes, guests)  3.94 us
    ppermute x1, starting transfers between devices, column_shards(): home_one = lax.ppermute(back_one, axes, first_back)  3.69 us
    ppermute x2, starting transfers between devices, fetch(): return (lax.ppermute(array, axes, first), two)  3.56 us
  transfers between devices with their start and end apart: 21, of which 6 were waited for; matrix products, arithmetic and copies ran while one was open for 4% of the time, Pallas kernels for 16%

profile of v10, /device:TPU:1, one launch (start us, length us, event | category | flops | bytes accessed | tf_op | source)
XLA Modules:
  0.0 67.3 jit_solution(13099538462726220219)
XLA Ops:
  0.6 2.7 %collective-permute-start = (bf16[128,1024]{1,0:T(8,128)(2,1)}, bf16[128,1024]{1,0:T(8,128)(2,1)S(1)}, u32[]{:S(2)}, u32[]{:S(2)}) collective-permute-start(bf16[128,1024]{1,0:T(8,128)(2,1)} %bitcast.26), channel_id=1, source_target_pairs={{0,2},{1,0},{2,4},{3,6},{4,1},{5,7},{6,3},{7,5},{8,10},{9,8},{10,1... | collective-permute-start | bytes 786440 | tf_op jit(solution)/shard_map/ppermute | solution.py:463
  3.4 3.9 %collective-permute-start.1 = (bf16[128,1024]{1,0:T(8,128)(2,1)}, bf16[128,1024]{1,0:T(8,128)(2,1)S(1)}, u32[]{:S(2)}, u32[]{:S(2)}) collective-permute-start(bf16[128,1024]{1,0:T(8,128)(2,1)} %bitcast.27), channel_id=1, source_target_pairs={{4,3},{3,4},{1,6},{6,1},{0,0},{5,5},{2,2},{7,7},{12,11},{11,12},{9... | collective-permute-start | bytes 786440 | tf_op jit(solution)/shard_map/ppermute | solution.py:462
  7.3 2.9 %shard_map.114 = bf16[128,1024]{1,0:T(8,128)(2,1)} custom-call(s32[1,128]{1,0:T(1,128)} %places.1, bf16[128,1024]{1,0:T(8,128)(2,1)} %bitcast.33, f32[1,1024]{1,0:T(1,128)} %bitcast.34, f32[1,512]{1,0:T(1,128)} %constant.16.clone.freqs), custom_call_target="tpu_custom_call" | custom-call | tf_op jit(solution)/shard_map/pallas_call | solution.py:473
  10.2 0.8 %collective-permute-start.3 = (bf16[128,1024]{1,0:T(8,128)(2,1)}, bf16[128,1024]{1,0:T(8,128)(2,1)S(1)}, u32[]{:S(2)}, u32[]{:S(2)}) collective-permute-start(bf16[128,1024]{1,0:T(8,128)(2,1)} %shard_map.114), channel_id=1, source_target_pairs={{0,2},{1,0},{2,4},{3,6},{4,1},{5,7},{6,3},{7,5},{8,10},{9,8},{10,1... | collective-permute-start | bytes 786440 | tf_op jit(solution)/shard_map/ppermute | solution.py:463
  11.0 2.8 %collective-permute-start.4 = (bf16[128,1024]{1,0:T(8,128)(2,1)}, bf16[128,1024]{1,0:T(8,128)(2,1)S(1)}, u32[]{:S(2)}, u32[]{:S(2)}) collective-permute-start(bf16[128,1024]{1,0:T(8,128)(2,1)} %shard_map.114), channel_id=1, source_target_pairs={{4,3},{3,4},{1,6},{6,1},{0,0},{5,5},{2,2},{7,7},{12,11},{11,12},{9... | collective-permute-start | bytes 786440 | tf_op jit(solution)/shard_map/ppermute | solution.py:462
  13.8 0.0 copy-start.1
  13.9 0.0 copy-start.2
  13.9 0.0 copy-start.3
  13.9 0.1 collective-permute-start.2
  14.0 4.3 %shard_map.113 = (bf16[1024,256]{1,0:T(8,128)(2,1)S(1)}, bf16[768,1024]{1,0:T(8,128)(2,1)S(1)}, bf16[1536,1024]{1,0:T(8,128)(2,1)}) custom-call(bf16[1024,1024]{1,0:T(8,128)(2,1)} %w_out.1, bf16[3,1024,1024]{2,1,0:T(8,128)(2,1)} %w_qkv.1), custom_call_target="tpu_custom_call" | custom-call | bytes 4194304 | tf_op jit(solution)/shard_map/pallas_call | solution.py:481
  18.3 0.6 shard_map.112
  19.0 0.6 collective-permute-start.5
  19.5 0.1 collective-permute-start.6
  19.6 7.5 %collective-permute-done.3.t0 = bf16[128,1024]{1,0:T(8,128)(2,1)S(1)} collective-permute-done((bf16[128,1024]{1,0:T(8,128)(2,1)}, bf16[128,1024]{1,0:T(8,128)(2,1)S(1)}, u32[]{:S(2)}, u32[]{:S(2)}) %collective-permute-start.3) | collective-permute-done | bytes 262176 | tf_op jit(solution)/shard_map/ppermute | solution.py:463
  27.1 0.1 collective-permute-start.7
  27.2 0.5 collective-permute-start.8
  27.7 1.0 %shard_map.115 = (bf16[384,1024]{1,0:T(8,128)(2,1)S(1)}, bf16[256,384]{1,0:T(8,128)(2,1)S(1)}) custom-call(s32[1,512]{1,0:T(1,128)S(1)} %get-tuple-element.57.rank, bf16[128,1024]{1,0:T(8,128)(2,1)S(1)} %collective-permute-done.g0, bf16[128,1024]{1,0:T(8,128)(2,1)S(1)} %collective-permute-done.1.g1, bf16[128,1024]{1,0:T(8,128)(2,1)S(1)} %collective-permute-done.5.g2, ...), custom_call_target="tpu_custom_call" | custom-call | flops 603979776 | bytes 3145728 | tf_op jit(solution)/shard_map/pallas_call | solution.py:514
  28.6 0.0 collective-permute-done.7.t2
  28.7 0.4 collective-permute-done.8.t3
  29.1 5.2 %shard_map.116 = (bf16[2,2,512,128]{3,2,1,0:T(8,128)(2,1)S(1)}, f32[2,2,512,128]{3,2,1,0:T(8,128)S(1)}, bf16[2,2,512,128]{3,2,1,0:T(8,128)(2,1)S(1)}, f32[2,2,512,128]{3,2,1,0:T(8,128)S(1)}, bf16[768,384]{1,0:T(8,128)(2,1)S(1)}) custom-call(s32[1,512]{1,0:T(1,128)S(1)} %get-tuple-element.57.rank, bf16[128,1024]{1,0:T(8,128)(2,1)S(1)} %collective-permute-done.3.t0, ...), custom_call_target="tpu_custom_call" | custom-call | flops 2684354560 | bytes 8388608 | tf_op jit(solution)/shard_map/pallas_call | solution.py:533
  34.3 0.0 copy-start.6
  34.3 0.2 collective-permute-start.9
  34.5 1.2 %collective-permute-start.12 = (bf16[2,2,512,128]{3,2,1,0:T(8,128)(2,1)S(1)}, bf16[2,2,512,128]{3,2,1,0:T(8,128)(2,1)S(1)}, u32[]{:S(2)}, u32[]{:S(2)}) collective-permute-start(bf16[2,2,512,128]{3,2,1,0:T(8,128)(2,1)S(1)} %get-tuple-element.77), channel_id=1, source_target_pairs={{0,8},{4,12},{8,0},{12,4},{16,24},{20,28},{24,16},{28,20},{1,9},{5... | collective-permute-start | bytes 1572872 | tf_op jit(solution)/shard_map/ppermute | solution.py:459
  35.8 1.2 %collective-permute-start.13 = (bf16[2,2,512,128]{3,2,1,0:T(8,128)(2,1)S(1)}, bf16[2,2,512,128]{3,2,1,0:T(8,128)(2,1)S(1)}, u32[]{:S(2)}, u32[]{:S(2)}) collective-permute-start(bf16[2,2,512,128]{3,2,1,0:T(8,128)(2,1)S(1)} %get-tuple-element.78), channel_id=1, source_target_pairs={{0,16},{4,20},{8,24},{12,28},{16,0},{20,4},{24,8},{28,12},{1,17},{... | collective-permute-start | bytes 1572872 | tf_op jit(solution)/shard_map/ppermute | solution.py:459
  37.0 1.5 %shard_map.117 = (bf16[128,1024]{1,0:T(8,128)(2,1)S(1)}, bf16[128,1024]{1,0:T(8,128)(2,1)S(1)}) custom-call(s32[1,256]{1,0:T(1,128)S(1)} %get-tuple-element.55.own_rank, s32[1,256]{1,0:T(1,128)S(1)} %get-tuple-element.56.other_rank, bf16[768,384]{1,0:T(8,128)(2,1)S(1)} %get-tuple-element.70.own, bf16[768,384]{1,0:T(8,128)(2,1)S(1)} %collective-permute-done.9.other, ...), custom_call_target="tpu_custom_call" | custom-call | flops 805306368 | bytes 4194304 | tf_op jit(solution)/shard_map/pallas_call | solution.py:559
  38.5 0.0 copy-start.5
  38.5 3.7 %collective-permute-start.10 = (bf16[128,1024]{1,0:T(8,128)(2,1)S(1)}, bf16[128,1024]{1,0:T(8,128)(2,1)S(1)}, u32[]{:S(2)}, u32[]{:S(2)}) collective-permute-start(bf16[128,1024]{1,0:T(8,128)(2,1)S(1)} %get-tuple-element.74), channel_id=1, source_target_pairs={{2,0},{0,1},{4,2},{6,3},{1,4},{7,5},{3,6},{5,7},{10,8},{8,9},{12,1... | collective-permute-start | bytes 786440 | tf_op jit(solution)/shard_map/ppermute | solution.py:571
  42.2 2.7 %collective-permute-start.11 = (bf16[128,1024]{1,0:T(8,128)(2,1)S(1)}, bf16[128,1024]{1,0:T(8,128)(2,1)S(1)}, u32[]{:S(2)}, u32[]{:S(2)}) collective-permute-start(bf16[128,1024]{1,0:T(8,128)(2,1)S(1)} %get-tuple-element.75), channel_id=1, source_target_pairs={{4,3},{3,4},{1,6},{6,1},{0,0},{5,5},{2,2},{7,7},{12,11},{11,12},{9... | collective-permute-start | bytes 786440 | tf_op jit(solution)/shard_map/ppermute | solution.py:574
  44.9 1.0 %multiply_sine_fusion = (f32[128,512]{1,0:T(8,128)S(1)}, f32[128,512]{1,0:T(8,128)S(1)}) fusion(f32[512]{0:T(512)S(1)} %multiply_exponential_fusion, f32[128]{0:T(128)S(1)} %convert_bitcast_fusion), kind=kLoop, calls=%fused_computation.9 | loop fusion | flops 65536 | bytes 526848 | tf_op jit(solution)/shard_map/sin | solution.py:23
  45.9 0.1 fusion.3
  46.1 0.2 multiply_reduce_fusion.1
  46.3 1.4 %collective-permute-done.12 = bf16[2,2,512,128]{3,2,1,0:T(8,128)(2,1)S(1)} collective-permute-done((bf16[2,2,512,128]{3,2,1,0:T(8,128)(2,1)S(1)}, bf16[2,2,512,128]{3,2,1,0:T(8,128)(2,1)S(1)}, u32[]{:S(2)}, u32[]{:S(2)}) %collective-permute-start.12) | collective-permute-done | bytes 524320 | tf_op jit(solution)/shard_map/ppermute | solution.py:459
  47.7 0.9 %collective-permute-done.13.first = bf16[2,2,512,128]{3,2,1,0:T(8,128)(2,1)S(1)} collective-permute-done((bf16[2,2,512,128]{3,2,1,0:T(8,128)(2,1)S(1)}, bf16[2,2,512,128]{3,2,1,0:T(8,128)(2,1)S(1)}, u32[]{:S(2)}, u32[]{:S(2)}) %collective-permute-start.13) | collective-permute-done | bytes 524320 | tf_op jit(solution)/shard_map/ppermute | solution.py:459
  48.6 0.1 shard_map.119
  48.7 2.3 %collective-permute-start.18 = (bf16[2,512,128]{2,1,0:T(8,128)(2,1)S(1)}, bf16[2,512,128]{2,1,0:T(8,128)(2,1)S(1)}, u32[]{:S(2)}, u32[]{:S(2)}) collective-permute-start(bf16[2,512,128]{2,1,0:T(8,128)(2,1)S(1)} %get-tuple-element.86), channel_id=1, source_target_pairs={{0,4},{5,1},{1,0},{4,5},{2,6},{7,3},{3,2},{6,7},{8,12},{13,9},{9,8... | collective-permute-start | bytes 786440 | tf_op jit(solution)/shard_map/ppermute | solution.py:592
  51.0 3.1 %collective-permute-start.19 = (bf16[2,512,128]{2,1,0:T(8,128)(2,1)S(1)}, bf16[2,512,128]{2,1,0:T(8,128)(2,1)S(1)}, u32[]{:S(2)}, u32[]{:S(2)}) collective-permute-start(bf16[2,512,128]{2,1,0:T(8,128)(2,1)S(1)} %get-tuple-element.87), channel_id=1, source_target_pairs={{1,4},{4,1},{3,6},{6,3},{9,12},{12,9},{11,14},{14,11},{17,20},{20,... | collective-permute-start | bytes 786440 | tf_op jit(solution)/shard_map/ppermute | solution.py:593
  54.1 0.1 fusion.1
  54.2 1.3 %collective-permute-start.15 = (bf16[2,512,128]{2,1,0:T(8,128)(2,1)S(1)}, bf16[2,512,128]{2,1,0:T(8,128)(2,1)S(1)}, u32[]{:S(2)}, u32[]{:S(2)}) collective-permute-start(bf16[2,512,128]{2,1,0:T(8,128)(2,1)S(1)} %get-tuple-element.95), channel_id=1, source_target_pairs={{0,16},{4,20},{8,24},{12,28},{16,0},{20,4},{24,8},{28,12},{1,17},{... | collective-permute-start | bytes 786440 | tf_op jit(solution)/shard_map/ppermute | solution.py:459
  55.5 0.3 fusion
  55.8 3.4 %collective-permute-done.19.from_guest = bf16[2,512,128]{2,1,0:T(8,128)(2,1)S(1)} collective-permute-done((bf16[2,512,128]{2,1,0:T(8,128)(2,1)S(1)}, bf16[2,512,128]{2,1,0:T(8,128)(2,1)S(1)}, u32[]{:S(2)}, u32[]{:S(2)}) %collective-permute-start.19) | collective-permute-done | bytes 262176 | tf_op jit(solution)/shard_map/ppermute | solution.py:593
  59.2 0.1 shard_map.120
  59.3 0.4 collective-permute-start.20
  59.7 0.1 shard_map.118
  59.7 0.1 collective-permute-start.16
  59.8 3.9 %collective-permute-start.17 = (bf16[512,128]{1,0:T(8,128)(2,1)S(1)}, bf16[512,128]{1,0:T(8,128)(2,1)S(1)}, u32[]{:S(2)}, u32[]{:S(2)}) collective-permute-start(bf16[512,128]{1,0:T(8,128)(2,1)S(1)} %bitcast.31), channel_id=1, source_target_pairs={{1,4},{4,1},{3,6},{6,3},{9,12},{12,9},{11,14},{14,11},{17,20},{20,... | collective-permute-start | bytes 393224 | tf_op jit(solution)/shard_map/ppermute | solution.py:617
  63.8 1.0 %fusion.2 = bf16[1,128,1024]{2,1,0:T(8,128)(2,1)} fusion(f32[128]{0:T(128)S(1)} %get-tuple-element.99, f32[128]{0:T(128)S(1)} %broadcast_multiply_fusion.2, f32[128]{0:T(128)S(1)} %get-tuple-element.100, f32[1024]{0:T(1024)S(1)} %copy-done.5, bf16[128,1024]{1,0:T(8,128)(2,1)S(1)} %collective-permute-done.11, ...), kind=kLoop, calls=%fused_computation.11 | loop fusion | flops 2097152 | bytes 1841152 | tf_op jit(solution)/shard_map/broadcast_in_dim | solution.py:629
  64.8 1.6 %collective-permute-done.17.from_guest = bf16[512,128]{1,0:T(8,128)(2,1)S(1)} collective-permute-done((bf16[512,128]{1,0:T(8,128)(2,1)S(1)}, bf16[512,128]{1,0:T(8,128)(2,1)S(1)}, u32[]{:S(2)}, u32[]{:S(2)}) %collective-permute-start.17) | collective-permute-done | bytes 131104 | tf_op jit(solution)/shard_map/ppermute | solution.py:617
  66.4 0.9 %shard_map.121 = (f32[768,128]{1,0:T(8,128)}, f32[128,256]{1,0:T(8,128)}) custom-call(bf16[512,128]{1,0:T(8,128)(2,1)S(1)} %collective-permute-done.16.from_home, bf16[512,128]{1,0:T(8,128)(2,1)S(1)} %collective-permute-done.17.from_guest, f32[512,128]{1,0:T(8,128)S(1)} %bitcast.25, f32[512,128]{1,0:T(8,128)S(1)} %get-tuple-element.89.keep, ...), custom_call_target="tpu_custom_call" | custom-call | tf_op jit(solution)/shard_map/pallas_call | solution.py:606
  (30 shorter events, 0.1 us)
Async XLA Ops:
  0.6 18.3 %collective-permute-start = (bf16[128,1024]{1,0:T(8,128)(2,1)}, bf16[128,1024]{1,0:T(8,128)(2,1)S(1)}, u32[]{:S(2)}, u32[]{:S(2)}) collective-permute-start(bf16[128,1024]{1,0:T(8,128)(2,1)} %bitcast.26), channel_id=1, source_target_pairs={{0,2},{1,0},{2,4},{3,6},{4,1},{5,7},{6,3},{7,5},{8,10},{9,8},{10,1... | collective-permute-start | bytes 786440 | tf_op jit(solution)/shard_map/ppermute | solution.py:463
  3.4 15.6 %collective-permute-start.1 = (bf16[128,1024]{1,0:T(8,128)(2,1)}, bf16[128,1024]{1,0:T(8,128)(2,1)S(1)}, u32[]{:S(2)}, u32[]{:S(2)}) collective-permute-start(bf16[128,1024]{1,0:T(8,128)(2,1)} %bitcast.27), channel_id=1, source_target_pairs={{4,3},{3,4},{1,6},{6,1},{0,0},{5,5},{2,2},{7,7},{12,11},{11,12},{9... | collective-permute-start | bytes 786440 | tf_op jit(solution)/shard_map/ppermute | solution.py:462
  10.2 16.9 %collective-permute-start.3 = (bf16[128,1024]{1,0:T(8,128)(2,1)}, bf16[128,1024]{1,0:T(8,128)(2,1)S(1)}, u32[]{:S(2)}, u32[]{:S(2)}) collective-permute-start(bf16[128,1024]{1,0:T(8,128)(2,1)} %shard_map.114), channel_id=1, source_target_pairs={{0,2},{1,0},{2,4},{3,6},{4,1},{5,7},{6,3},{7,5},{8,10},{9,8},{10,1... | collective-permute-start | bytes 786440 | tf_op jit(solution)/shard_map/ppermute | solution.py:463
  11.0 16.1 %collective-permute-start.4 = (bf16[128,1024]{1,0:T(8,128)(2,1)}, bf16[128,1024]{1,0:T(8,128)(2,1)S(1)}, u32[]{:S(2)}, u32[]{:S(2)}) collective-permute-start(bf16[128,1024]{1,0:T(8,128)(2,1)} %shard_map.114), channel_id=1, source_target_pairs={{4,3},{3,4},{1,6},{6,1},{0,0},{5,5},{2,2},{7,7},{12,11},{11,12},{9... | collective-permute-start | bytes 786440 | tf_op jit(solution)/shard_map/ppermute | solution.py:462
  13.8 4.5 %copy-start.1 = (bf16[1,128,1024]{2,1,0:T(8,128)(2,1)S(1)}, bf16[1,128,1024]{2,1,0:T(8,128)(2,1)}, u32[]{:S(2)}) copy-start(bf16[1,128,1024]{2,1,0:T(8,128)(2,1)} %param.15) | copy-start | bytes 786436
  13.9 4.4 %copy-start.2 = (s32[1,4]{1,0:T(1,128)S(1)}, s32[1,4]{1,0:T(1,128)}, u32[]{:S(2)}) copy-start(s32[1,4]{1,0:T(1,128)} %param.11) | copy-start | bytes 52
  13.9 4.4 %copy-start.3 = (s32[16]{0:T(128)S(1)}, s32[16]{0:T(128)}, u32[]{:S(2)}) copy-start(s32[16]{0:T(128)} %constant.17.clone.table) | copy-start | bytes 196
  13.9 4.4 %collective-permute-start.2 = (s32[4]{0:T(128)}, s32[4]{0:T(128)S(1)}, u32[]{:S(2)}, u32[]{:S(2)}) collective-permute-start(s32[4]{0:T(128)} %bitcast.29), channel_id=1, source_target_pairs={{0,4},{4,0},{8,12},{12,8},{16,20},{20,16},{24,28},{28,24},{1,5},{5... | collective-permute-start | bytes 56 | tf_op jit(solution)/shard_map/ppermute | solution.py:459
  19.0 8.1 %collective-permute-start.5 = (bf16[128,1024]{1,0:T(8,128)(2,1)S(1)}, bf16[128,1024]{1,0:T(8,128)(2,1)S(1)}, u32[]{:S(2)}, u32[]{:S(2)}) collective-permute-start(bf16[128,1024]{1,0:T(8,128)(2,1)S(1)} %collective-permute-done.g0), channel_id=1, source_target_pairs={{0,4},{4,0},{8,12},{12,8},{16,20},{20,16},{24,28},{28,24},{1,5},{5... | collective-permute-start | bytes 786440 | tf_op jit(solution)/shard_map/ppermute | solution.py:459
  19.5 7.6 %collective-permute-start.6 = (bf16[128,1024]{1,0:T(8,128)(2,1)S(1)}, bf16[128,1024]{1,0:T(8,128)(2,1)S(1)}, u32[]{:S(2)}, u32[]{:S(2)}) collective-permute-start(bf16[128,1024]{1,0:T(8,128)(2,1)S(1)} %collective-permute-done.1.g1), channel_id=1, source_target_pairs={{0,4},{4,0},{8,12},{12,8},{16,20},{20,16},{24,28},{28,24},{1,5},{5... | collective-permute-start | bytes 786440 | tf_op jit(solution)/shard_map/ppermute | solution.py:459
  27.1 1.6 %collective-permute-start.7 = (bf16[128,1024]{1,0:T(8,128)(2,1)S(1)}, bf16[128,1024]{1,0:T(8,128)(2,1)S(1)}, u32[]{:S(2)}, u32[]{:S(2)}) collective-permute-start(bf16[128,1024]{1,0:T(8,128)(2,1)S(1)} %collective-permute-done.3.t0), channel_id=1, source_target_pairs={{0,4},{4,0},{8,12},{12,8},{16,20},{20,16},{24,28},{28,24},{1,5},{5... | collective-permute-start | bytes 786440 | tf_op jit(solution)/shard_map/ppermute | solution.py:459
  27.2 1.9 %collective-permute-start.8 = (bf16[128,1024]{1,0:T(8,128)(2,1)S(1)}, bf16[128,1024]{1,0:T(8,128)(2,1)S(1)}, u32[]{:S(2)}, u32[]{:S(2)}) collective-permute-start(bf16[128,1024]{1,0:T(8,128)(2,1)S(1)} %collective-permute-done.4.t1), channel_id=1, source_target_pairs={{0,4},{4,0},{8,12},{12,8},{16,20},{20,16},{24,28},{28,24},{1,5},{5... | collective-permute-start | bytes 786440 | tf_op jit(solution)/shard_map/ppermute | solution.py:459
  29.1 7.9 %copy-start = (bf16[1536,1024]{1,0:T(8,128)(2,1)S(1)}, bf16[1536,1024]{1,0:T(8,128)(2,1)}, u32[]{:S(2)}) copy-start(bf16[1536,1024]{1,0:T(8,128)(2,1)} %get-tuple-element.71.weight) | copy-start | bytes 9437188
  34.3 7.9 %copy-start.6 = (s32[1,128]{1,0:T(1,128)S(1)}, s32[1,128]{1,0:T(1,128)}, u32[]{:S(2)}) copy-start(s32[1,128]{1,0:T(1,128)} %places.1) | copy-start | bytes 1540
  34.3 11.6 %copy-start.4 = (bf16[1,128,1024]{2,1,0:T(8,128)(2,1)S(1)}, bf16[1,128,1024]{2,1,0:T(8,128)(2,1)}, u32[]{:S(2)}) copy-start(bf16[1,128,1024]{2,1,0:T(8,128)(2,1)} %param.9) | copy-start | bytes 786436
  34.3 2.7 %collective-permute-start.9 = (bf16[768,384]{1,0:T(8,128)(2,1)S(1)}, bf16[768,384]{1,0:T(8,128)(2,1)S(1)}, u32[]{:S(2)}, u32[]{:S(2)}) collective-permute-start(bf16[768,384]{1,0:T(8,128)(2,1)S(1)} %get-tuple-element.70.own), channel_id=1, source_target_pairs={{0,4},{4,0},{8,12},{12,8},{16,20},{20,16},{24,28},{28,24},{1,5},{5... | collective-permute-start | bytes 1769480 | tf_op jit(solution)/shard_map/ppermute | solution.py:459
  34.5 13.1 %collective-permute-start.12 = (bf16[2,2,512,128]{3,2,1,0:T(8,128)(2,1)S(1)}, bf16[2,2,512,128]{3,2,1,0:T(8,128)(2,1)S(1)}, u32[]{:S(2)}, u32[]{:S(2)}) collective-permute-start(bf16[2,2,512,128]{3,2,1,0:T(8,128)(2,1)S(1)} %get-tuple-element.77), channel_id=1, source_target_pairs={{0,8},{4,12},{8,0},{12,4},{16,24},{20,28},{24,16},{28,20},{1,9},{5... | collective-permute-start | bytes 1572872 | tf_op jit(solution)/shard_map/ppermute | solution.py:459
  35.8 12.8 %collective-permute-start.13 = (bf16[2,2,512,128]{3,2,1,0:T(8,128)(2,1)S(1)}, bf16[2,2,512,128]{3,2,1,0:T(8,128)(2,1)S(1)}, u32[]{:S(2)}, u32[]{:S(2)}) collective-permute-start(bf16[2,2,512,128]{3,2,1,0:T(8,128)(2,1)S(1)} %get-tuple-element.78), channel_id=1, source_target_pairs={{0,16},{4,20},{8,24},{12,28},{16,0},{20,4},{24,8},{28,12},{1,17},{... | collective-permute-start | bytes 1572872 | tf_op jit(solution)/shard_map/ppermute | solution.py:459
  38.5 17.0 %copy-start.5 = (f32[1024]{0:T(1024)S(1)}, f32[1024]{0:T(1024)}, u32[]{:S(2)}) copy-start(f32[1024]{0:T(1024)} %param.12) | copy-start | bytes 12292
  38.5 17.0 %collective-permute-start.10 = (bf16[128,1024]{1,0:T(8,128)(2,1)S(1)}, bf16[128,1024]{1,0:T(8,128)(2,1)S(1)}, u32[]{:S(2)}, u32[]{:S(2)}) collective-permute-start(bf16[128,1024]{1,0:T(8,128)(2,1)S(1)} %get-tuple-element.74), channel_id=1, source_target_pairs={{2,0},{0,1},{4,2},{6,3},{1,4},{7,5},{3,6},{5,7},{10,8},{8,9},{12,1... | collective-permute-start | bytes 786440 | tf_op jit(solution)/shard_map/ppermute | solution.py:571
  42.2 6.4 %collective-permute-start.14 = (bf16[16,1024]{1,0:T(8,128)(2,1)S(1)}, bf16[16,1024]{1,0:T(8,128)(2,1)S(1)}, u32[]{:S(2)}, u32[]{:S(2)}) collective-permute-start(bf16[16,1024]{1,0:T(8,128)(2,1)S(1)} %slice.16), channel_id=1, source_target_pairs={{0,4},{4,0},{8,12},{12,8},{16,20},{20,16},{24,28},{28,24},{1,5},{5... | collective-permute-start | bytes 98312 | tf_op jit(solution)/shard_map/ppermute | solution.py:459
  42.2 13.3 %collective-permute-start.11 = (bf16[128,1024]{1,0:T(8,128)(2,1)S(1)}, bf16[128,1024]{1,0:T(8,128)(2,1)S(1)}, u32[]{:S(2)}, u32[]{:S(2)}) collective-permute-start(bf16[128,1024]{1,0:T(8,128)(2,1)S(1)} %get-tuple-element.75), channel_id=1, source_target_pairs={{4,3},{3,4},{1,6},{6,1},{0,0},{5,5},{2,2},{7,7},{12,11},{11,12},{9... | collective-permute-start | bytes 786440 | tf_op jit(solution)/shard_map/ppermute | solution.py:574
  48.7 7.1 %collective-permute-start.18 = (bf16[2,512,128]{2,1,0:T(8,128)(2,1)S(1)}, bf16[2,512,128]{2,1,0:T(8,128)(2,1)S(1)}, u32[]{:S(2)}, u32[]{:S(2)}) collective-permute-start(bf16[2,512,128]{2,1,0:T(8,128)(2,1)S(1)} %get-tuple-element.86), channel_id=1, source_target_pairs={{0,4},{5,1},{1,0},{4,5},{2,6},{7,3},{3,2},{6,7},{8,12},{13,9},{9,8... | collective-permute-start | bytes 786440 | tf_op jit(solution)/shard_map/ppermute | solution.py:592
  51.0 8.2 %collective-permute-start.19 = (bf16[2,512,128]{2,1,0:T(8,128)(2,1)S(1)}, bf16[2,512,128]{2,1,0:T(8,128)(2,1)S(1)}, u32[]{:S(2)}, u32[]{:S(2)}) collective-permute-start(bf16[2,512,128]{2,1,0:T(8,128)(2,1)S(1)} %get-tuple-element.87), channel_id=1, source_target_pairs={{1,4},{4,1},{3,6},{6,3},{9,12},{12,9},{11,14},{14,11},{17,20},{20,... | collective-permute-start | bytes 786440 | tf_op jit(solution)/shard_map/ppermute | solution.py:593
  54.2 5.5 %collective-permute-start.15 = (bf16[2,512,128]{2,1,0:T(8,128)(2,1)S(1)}, bf16[2,512,128]{2,1,0:T(8,128)(2,1)S(1)}, u32[]{:S(2)}, u32[]{:S(2)}) collective-permute-start(bf16[2,512,128]{2,1,0:T(8,128)(2,1)S(1)} %get-tuple-element.95), channel_id=1, source_target_pairs={{0,16},{4,20},{8,24},{12,28},{16,0},{20,4},{24,8},{28,12},{1,17},{... | collective-permute-start | bytes 786440 | tf_op jit(solution)/shard_map/ppermute | solution.py:459
  59.3 5.5 %collective-permute-start.20 = (bf16[512,128]{1,0:T(8,128)(2,1)S(1)}, bf16[512,128]{1,0:T(8,128)(2,1)S(1)}, u32[]{:S(2)}, u32[]{:S(2)}) collective-permute-start(bf16[512,128]{1,0:T(8,128)(2,1)S(1)} %get-tuple-element.90), channel_id=1, source_target_pairs={{0,8},{4,12},{8,0},{12,4},{16,24},{20,28},{24,16},{28,20},{1,9},{5... | collective-permute-start | bytes 393224 | tf_op jit(solution)/shard_map/ppermute | solution.py:459
  59.7 5.0 %collective-permute-start.16 = (bf16[512,128]{1,0:T(8,128)(2,1)S(1)}, bf16[512,128]{1,0:T(8,128)(2,1)S(1)}, u32[]{:S(2)}, u32[]{:S(2)}) collective-permute-start(bf16[512,128]{1,0:T(8,128)(2,1)S(1)} %bitcast.32), channel_id=1, source_target_pairs={{0,4},{5,1},{1,0},{4,5},{2,6},{7,3},{3,2},{6,7},{8,12},{13,9},{9,8... | collective-permute-start | bytes 393224 | tf_op jit(solution)/shard_map/ppermute | solution.py:616
  59.8 6.6 %collective-permute-start.17 = (bf16[512,128]{1,0:T(8,128)(2,1)S(1)}, bf16[512,128]{1,0:T(8,128)(2,1)S(1)}, u32[]{:S(2)}, u32[]{:S(2)}) collective-permute-start(bf16[512,128]{1,0:T(8,128)(2,1)S(1)} %bitcast.31), channel_id=1, source_target_pairs={{1,4},{4,1},{3,6},{6,3},{9,12},{12,9},{11,14},{14,11},{17,20},{20,... | collective-permute-start | bytes 393224 | tf_op jit(solution)/shard_map/ppermute | solution.py:617
